TPU v7x, 32 devices: a whole 2x2x4 slice. The times are simulated.
32 devices in a mesh: grp: 2 (over y), seq: 4 (over x, core), sub: 4 (over z).
Axes of the slice: x: 2, y: 2, z: 4, core: 2. Of those that a mesh axis runs over, the one named last changes fastest.
Arguments:
- events: bfloat16 [4096, 1024], P(('grp', 'seq', 'sub')), parts along dimension 0, may hold values from -36 to 36
- offsets: int32 [4096], P(('grp', 'seq', 'sub')), parts along dimension 0, may hold values from 0 to 2047
- cotangent: bfloat16 [4096, 1024], P(('grp', 'seq', 'sub')), parts along dimension 0, may hold values from -6 to 6
- query_weight: bfloat16 [1024, 1024], P('sub'), may hold values from -0.1875 to 0.1875
- key_weight: bfloat16 [1024, 1024], P('sub'), may hold values from -0.1875 to 0.1875
- value_weight: bfloat16 [1024, 1024], P('sub'), may hold values from -0.1875 to 0.1875
- omega: bfloat16 [8, 128, 256], replicated, may hold values from -0.5 to 0.5
Outputs:
- grad_events: bfloat16 [4096, 1024], P(('grp', 'seq', 'sub')), parts along dimension 0
There are 2 independent parts, one for each index of `grp`. A program takes and returns all parts, laid end to end along the dimension named above; an argument that names none is the same for every part. Nothing has to cross between parts.
All inputs are finite; a program needn't handle non-finite values.
Results may differ from a plain program's by a relative error of at most 0.012.
Values may be sent and summed in bfloat16 or wider, within the bound.
No kernel may reach another device: no remote copies, remote signals or barrier semaphores. Data moves between devices by JAX's collectives and lax.ppermute only.
A program may use at most 64 MiB of HBM per device.

v0:
```python
import math

import jax
import jax.numpy as jnp
from jax import lax
from jax.sharding import PartitionSpec as P


def encode(events, offsets):
    half_width = events.shape[1] // 2
    indices = jnp.arange(half_width, dtype=jnp.float32)
    frequency = jnp.exp(indices * (-2.0 * math.log(10000.0) / events.shape[1]))
    angles = offsets.astype(jnp.float32)[:, None] * frequency[None, :]
    encoding = jnp.concatenate([jnp.sin(angles), jnp.cos(angles)], axis=1)
    return (events.astype(jnp.float32) + encoding).astype(jnp.bfloat16)


def split_heads(matrix, head_count):
    return matrix.reshape(matrix.shape[0], head_count, matrix.shape[1] // head_count)


def transposed(left, weight):
    return lax.dot_general(
        left, weight, (((1,), (1,)), ((), ())), preferred_element_type=jnp.float32
    )


def local(events, offsets, cotangent, query_weight, key_weight, value_weight, omega):
    widened_rows = jnp.float32
    head_count = omega.shape[0]
    local_rows = events.shape[0]
    model_width = events.shape[1]
    all_tokens = local_rows * lax.axis_size("seq") * lax.axis_size("sub")
    loss_scale = math.sqrt(all_tokens)
    inputs = encode(events, offsets)
    gathered = (
        lax.all_gather(query_weight, "sub", axis=0, tiled=True),
        lax.all_gather(key_weight, "sub", axis=0, tiled=True),
        lax.all_gather(value_weight, "sub", axis=0, tiled=True),
    )
    queries, key_act, value_act = [
        jnp.dot(inputs, weight, preferred_element_type=widened_rows).astype(jnp.bfloat16)
        for weight in gathered
    ]
    query_pre = jnp.einsum(
        "thd,hdm->thm", split_heads(queries, head_count), omega, preferred_element_type=widened_rows
    )
    key_pre = jnp.einsum(
        "thd,hdm->thm", split_heads(key_act, head_count), omega, preferred_element_type=widened_rows
    )
    query_feature_map = jax.nn.softplus(query_pre).astype(jnp.bfloat16)
    key_feature_map = jax.nn.softplus(key_pre).astype(jnp.bfloat16)
    value_per_head = split_heads(value_act, head_count)
    local_digest = jnp.einsum(
        "reb,rec->ebc", key_feature_map, value_per_head, preferred_element_type=widened_rows
    )
    local_total = jnp.sum(key_feature_map, axis=0, dtype=widened_rows)
    state_digest, key_total = lax.psum((local_digest, local_total), ("seq", "sub"))
    digest_halves = state_digest.astype(jnp.bfloat16)
    total_half = key_total.astype(jnp.bfloat16)
    numerator = jnp.einsum(
        "xls,lsk->xlk", query_feature_map, digest_halves, preferred_element_type=widened_rows
    )
    denom = jnp.einsum(
        "thm,hm->th", query_feature_map, total_half, preferred_element_type=widened_rows
    )
    attended = numerator / denom[..., None]
    upstream = split_heads(cotangent, head_count).astype(widened_rows) * loss_scale
    scaled_grad = upstream / denom[..., None]
    norm_grad = -jnp.sum(scaled_grad * attended, axis=-1)
    scaled_halves = scaled_grad.astype(jnp.bfloat16)
    norm_half = norm_grad.astype(jnp.bfloat16)
    local_gradient = jnp.einsum(
        "reb,rec->ebc", query_feature_map, scaled_halves, preferred_element_type=widened_rows
    )
    local_norm = jnp.einsum(
        "thm,th->hm", query_feature_map, norm_half, preferred_element_type=widened_rows
    )
    summary_grad, overall_gradient = lax.psum((local_gradient, local_norm), ("seq", "sub"))
    gradient_halves = summary_grad.astype(jnp.bfloat16)
    query_feature_gradient = jnp.einsum(
        "pfy,fly->pfl", scaled_halves, digest_halves, preferred_element_type=widened_rows
    )
    query_feature_gradient = (
        query_feature_gradient + norm_grad[..., None] * total_half.astype(widened_rows)[None]
    )
    key_feature_gradient = (
        jnp.einsum(
            "pfy,fly->pfl", value_per_head, gradient_halves, preferred_element_type=widened_rows
        )
        + overall_gradient[None]
    )
    value_gradient = jnp.einsum(
        "xls,lsk->xlk", key_feature_map, gradient_halves, preferred_element_type=widened_rows
    ).astype(jnp.bfloat16)
    query_pre_grad = (query_feature_gradient * jax.nn.sigmoid(query_pre)).astype(jnp.bfloat16)
    key_pre_grad = (key_feature_gradient * jax.nn.sigmoid(key_pre)).astype(jnp.bfloat16)
    query_grad = jnp.einsum(
        "thm,hdm->thd", query_pre_grad, omega, preferred_element_type=widened_rows
    ).astype(jnp.bfloat16)
    key_grad = jnp.einsum(
        "thm,hdm->thd", key_pre_grad, omega, preferred_element_type=widened_rows
    ).astype(jnp.bfloat16)
    query_flat = query_grad.reshape(local_rows, model_width)
    key_flat = key_grad.reshape(local_rows, model_width)
    value_flat = value_gradient.reshape(local_rows, model_width)
    summed = transposed(query_flat, gathered[0])
    summed = summed + transposed(key_flat, gathered[1])
    summed = summed + transposed(value_flat, gathered[2])
    return summed.astype(jnp.bfloat16)


def solution(mesh):
    in_specs = (
        P(("grp", "seq", "sub"), None),
        P(("grp", "seq", "sub")),
        P(("grp", "seq", "sub"), None),
        P("sub", None),
        P("sub", None),
        P("sub", None),
        P(),
    )
    out_specs = P(("grp", "seq", "sub"), None)
    return jax.shard_map(local, mesh=mesh, in_specs=in_specs, out_specs=out_specs, check_vma=False)
```

profile of v0, /device:TPU:0, one launch (start us, length us, event | category | flops | bytes accessed | tf_op | source)
XLA Modules:
  0.0 332.1 jit_solution(6996153496564950566)
XLA Ops:
  6.5 0.7 all-gather.4.cloned.1.call-update
  7.3 0.7 all-gather.8.cloned.1.call-update
  8.1 0.7 all-gather.6.cloned.1.call-update
  8.7 0.7 convert_element_type.77
  9.4 1.0 convert_multiply_fusion
  10.4 1.0 copy.11
  11.5 1.0 multiply_sine_fusion
  12.5 45.1 %all-gather.4.cloned.1.call-done = bf16[1024,1024]{1,0:T(8,128)(2,1)} async-done(((bf16[256,1024]{1,0:T(8,128)(2,1)}), bf16[1024,1024]{1,0:T(8,128)(2,1)}) %all-gather.4.cloned.1.call-update) | async-done | bytes 2097168 | tf_op jit(solution)/shard_map/all_gather | solution.py:38
  57.6 2.0 fusion.14
  59.7 1.7 convert_reduce_fusion
  61.3 42.5 %all-gather.8.cloned.1.call-done = bf16[1024,1024]{1,0:T(8,128)(2,1)} async-done(((bf16[256,1024]{1,0:T(8,128)(2,1)}), bf16[1024,1024]{1,0:T(8,128)(2,1)}) %all-gather.8.cloned.1.call-update) | async-done | bytes 2097168 | tf_op jit(solution)/shard_map/all_gather | solution.py:37
  103.9 2.0 fusion.15
  105.9 1.6 fusion.17
  107.5 42.6 %all-gather.6.cloned.1.call-done = bf16[1024,1024]{1,0:T(8,128)(2,1)} async-done(((bf16[256,1024]{1,0:T(8,128)(2,1)}), bf16[1024,1024]{1,0:T(8,128)(2,1)}) %all-gather.6.cloned.1.call-update) | async-done | bytes 2097168 | tf_op jit(solution)/shard_map/all_gather | solution.py:39
  150.1 2.0 convolution_convert_fusion.1
  152.7 81.4 %all-reduce.4 = (bf16[8,256]{1,0:T(8,128)(2,1)S(1)}, bf16[8,256,128]{2,1,0:T(8,128)(2,1)}) all-reduce(f32[8,256]{1,0:T(8,128)S(1)} %get-tuple-element.9, f32[8,256,128]{2,1,0:T(8,128)S(1)} %fusion.55), channel_id=1, replica_groups=mesh['grp'=2,'seq'=4,'sub'=4] {'seq','sub'}, use_global_device_ids=true, to_apply=%region_2.3 | all-reduce | flops 264192 | bytes 1585152 | tf_op jit(solution)/shard_map/psum | solution.py:58
  234.3 1.5 fusion.48
  236.3 80.4 %all-reduce.5 = (f32[8,256]{1,0:T(8,128)S(1)}, bf16[8,256,128]{2,1,0:T(8,128)(2,1)S(1)}) all-reduce(f32[8,256]{1,0:T(8,128)S(1)} %bitcast.110, f32[8,256,128]{2,1,0:T(8,128)S(1)} %fusion.48), channel_id=1, replica_groups=mesh['grp'=2,'seq'=4,'sub'=4] {'seq','sub'}, use_global_device_ids=true, to_apply=%region_5.6 | all-reduce | flops 264192 | bytes 1589248 | tf_op jit(solution)/shard_map/psum | solution.py:79
  317.1 1.9 fusion.11
  319.0 2.4 fusion.10
  321.4 0.8 fusion.56
  322.2 0.7 copy-done.3
  323.0 0.8 convolution_add_fusion.2
  324.0 1.6 fusion.12
  (27 shorter events, 2.0 us)
Async XLA Ops:
  6.5 53.1 %copy-start = (bf16[8,128,256]{2,1,0:T(8,128)(2,1)S(1)}, bf16[8,128,256]{2,1,0:T(8,128)(2,1)}, u32[]{:S(2)}) copy-start(bf16[8,128,256]{2,1,0:T(8,128)(2,1)} %param.13) | copy-start | bytes 1572868
  6.5 5.9 %copy-start.5 = (bf16[128,1024]{1,0:T(8,128)(2,1)S(1)}, bf16[128,1024]{1,0:T(8,128)(2,1)}, u32[]{:S(2)}) copy-start(bf16[128,1024]{1,0:T(8,128)(2,1)} %param.7) | copy-start | bytes 786436
  6.5 51.1 %all-gather.4.cloned.1.call-start = ((), (), s32[]{:S(2)}) async-start(), calls=%async_computation | async-start | bytes 2621440 | tf_op jit(solution)/shard_map/all_gather | solution.py:38
  7.3 96.6 %all-gather.8.cloned.1.call-start = ((), (), s32[]{:S(2)}) async-start(), calls=%async_computation.2 | async-start | bytes 2621440 | tf_op jit(solution)/shard_map/all_gather | solution.py:37
  8.0 142.1 %all-gather.6.cloned.1.call-start = ((), (), s32[]{:S(2)}) async-start(), calls=%async_computation.1 | async-start | bytes 2621440 | tf_op jit(solution)/shard_map/all_gather | solution.py:39
  234.0 1.7 copy-start.4
  234.0 1.7 copy-start.6
  319.0 2.4 copy-start.2
  321.4 1.6 copy-start.3
  322.2 1.7 copy-start.1
Sparse Core Ops, SparseCore 0:
  8.9 48.6 all-gather.3
  59.2 44.6 all-gather.7
  105.4 44.6 all-gather.5
where the time goes:
time: 334 us; the launch traced here: 332 us
  blocking collectives  162 us (49%)
  waiting for transfers between devices  132 us (40%)
  matrix products  19.8 us (6%)
  between operations  13.3 us (4%)
    psum x1, blocking collectives, local(): lax.psum((local_digest, local_total), ('seq', 'sub'))  81.4 us
    psum x1, blocking collectives, local(): lax.psum((local_gradient, local_norm), ('seq', 'sub'))  80.4 us
    all_gather x1, waiting for transfers between devices, local(): lax.all_gather(key_weight, 'sub', axis=0, tiled=True)  45.1 us
    all_gather x1, waiting for transfers between devices, local(): lax.all_gather(value_weight, 'sub', axis=0, tiled=True)  42.6 us
    all_gather x1, waiting for transfers between devices, local(): lax.all_gather(query_weight, 'sub', axis=0, tiled=True)  42.5 us
  transfers between devices with their start and end apart: 3, of which 3 were waited for; matrix products, arithmetic and copies ran while one was open for 3% of the time, Pallas kernels for 0%

commit v1 on v0

v1 whole, which is shorter than its diff:
```python
import functools
import math

import jax
import jax.numpy as jnp
from jax import lax
from jax.experimental import pallas as pl
from jax.experimental.pallas import tpu as pltpu
from jax.sharding import PartitionSpec as P

F32 = jnp.float32
BF16 = jnp.bfloat16


def encode(events, offsets):
    half_width = events.shape[1] // 2
    indices = jnp.arange(half_width, dtype=F32)
    frequency = jnp.exp(indices * (-2.0 * math.log(10000.0) / events.shape[1]))
    angles = offsets.astype(F32)[:, None] * frequency[None, :]
    encoding = jnp.concatenate([jnp.sin(angles), jnp.cos(angles)], axis=1)
    return (events.astype(F32) + encoding).astype(BF16)


def dot(a, b, ca=1, cb=0):
    return lax.dot_general(a, b, (((ca,), (cb,)), ((), ())), preferred_element_type=F32)


def soft_and_sigmoid(u):
    e = jnp.exp(-jnp.abs(u))
    series = e * (1.0 + e * (-0.5 + e * (1.0 / 3.0)))
    soft = jnp.maximum(u, 0.0) + jnp.where(e < 1e-3, series, jnp.log(1.0 + e))
    r = 1.0 / (1.0 + e)
    return soft, jnp.where(u >= 0.0, r, e * r)


def place_rows(full, parts):
    z = lax.axis_index("sub")
    rows = parts[0].shape[0]
    for k, part in enumerate(parts):
        full[pl.ds(pl.multiple_of((z ^ k) * rows, rows), rows), :] = part[...]


def call(body, outs, args, flops):
    nbytes = sum(a.size * a.dtype.itemsize for a in args)
    return pl.pallas_call(
        body,
        out_shape=[jax.ShapeDtypeStruct(s, d) for s, d in outs],
        compiler_params=pltpu.CompilerParams(vmem_limit_bytes=48 * 1024 * 1024),
        cost_estimate=pl.CostEstimate(flops=flops, bytes_accessed=nbytes, transcendentals=0),
    )(*args)


def features(xs, w_full, om, hp, feat, sig, total):
    hd, m = om.shape[1], om.shape[2]
    rows = xs[0].shape[0]
    sums = [jnp.zeros((1, m), F32) for _ in range(hp)]
    for i, x in enumerate(xs):
        act = dot(x[...], w_full[...]).astype(BF16)
        for h in range(hp):
            pre = dot(act[:, h * hd : (h + 1) * hd], om[h])
            soft, s = soft_and_sigmoid(pre)
            soft = soft.astype(BF16)
            at = (slice(i * rows, (i + 1) * rows), slice(h * m, (h + 1) * m))
            feat[at] = soft
            sig[at] = s
            if total is not None:
                sums[h] = sums[h] + jnp.sum(soft.astype(F32), axis=0, keepdims=True)
    if total is not None:
        for h in range(hp):
            total[:, h * m : (h + 1) * m] = sums[h]


def key_kernel(g, n, hp, *refs):
    xs, ws, om = refs[:g], refs[g : g + n], refs[g + n]
    w_full, feat, sig, total = refs[g + n + 1 :]
    place_rows(w_full, ws)
    features(xs, w_full, om, hp, feat, sig, total)


def query_kernel(g, n, hp, *refs):
    xs, ws, om = refs[:g], refs[g : g + n], refs[g + n]
    w_full, feat, sig = refs[g + n + 1 :]
    place_rows(w_full, ws)
    features(xs, w_full, om, hp, feat, sig, None)


def value_kernel(g, n, hp, *refs):
    xs, ws, feat = refs[:g], refs[g : g + n], refs[g + n]
    w_full, val, own, send = refs[g + n + 1 :]
    place_rows(w_full, ws)
    rows = xs[0].shape[0]
    for i, x in enumerate(xs):
        val[i * rows : (i + 1) * rows, :] = dot(x[...], w_full[...]).astype(BF16)
    m, hd = feat.shape[1] // hp, val.shape[1] // hp
    for h in range(hp):
        s = dot(feat[:, h * m : (h + 1) * m], val[:, h * hd : (h + 1) * hd], 0, 0)
        own[h * m : (h + 1) * m, :] = s
        send[h * m : (h + 1) * m, :] = s.astype(BF16)


def summed(parts):
    out = parts[0][...]
    for part in parts[1:]:
        out = out + part[...].astype(F32)
    return out


def scale_kernel(g, p, hp, loss_scale, *refs):
    tots, cots, feat = refs[:p], refs[p : p + g], refs[p + g]
    total_half, scaled_half, twice, own, send = refs[p + g + 1 :]
    total_half[...] = summed(tots).astype(BF16)
    m, hd = feat.shape[1] // hp, scaled_half.shape[1] // hp
    rows = cots[0].shape[0]
    for h in range(hp):
        spread = jnp.broadcast_to(total_half[:, h * m : (h + 1) * m].astype(F32), (hd, m)).astype(BF16)
        for i in range(g):
            tok = slice(i * rows, (i + 1) * rows)
            col = slice(h * hd, (h + 1) * hd)
            denom = dot(feat[tok, h * m : (h + 1) * m], spread, 1, 1)
            scaled = cots[i][:, col].astype(F32) * loss_scale / denom
            scaled_half[tok, col] = scaled.astype(BF16)
            twice[tok, col] = scaled / denom
        s = dot(feat[:, h * m : (h + 1) * m], scaled_half[:, h * hd : (h + 1) * hd], 0, 0)
        own[h * m : (h + 1) * m, :] = s
        send[h * m : (h + 1) * m, :] = s.astype(BF16)


def norm_kernel(p, hp, *refs):
    parts, feat, twice = refs[:p], refs[p], refs[p + 1]
    summary_half, norm, total = refs[p + 2 :]
    summary_half[...] = summed(parts).astype(BF16)
    m, hd = feat.shape[1] // hp, twice.shape[1] // hp
    for h in range(hp):
        qf = feat[:, h * m : (h + 1) * m]
        numer = dot(qf, summary_half[h * m : (h + 1) * m, :])
        ng = -jnp.sum(twice[:, h * hd : (h + 1) * hd] * numer, axis=1, keepdims=True)
        norm[:, h : h + 1] = ng
        half = ng.astype(BF16).astype(F32)
        total[:, h * m : (h + 1) * m] = jnp.sum(qf.astype(F32) * half, axis=0, keepdims=True)


def query_grad_kernel(hp, scaled_half, summary_half, norm, total_half, sig, om, out):
    hd, m = om.shape[1], om.shape[2]
    for h in range(hp):
        fg = dot(scaled_half[:, h * hd : (h + 1) * hd], summary_half[h * m : (h + 1) * m, :], 1, 1)
        fg = fg + norm[:, h : h + 1] * total_half[:, h * m : (h + 1) * m].astype(F32)
        pg = (fg * sig[:, h * m : (h + 1) * m]).astype(BF16)
        out[:, h * hd : (h + 1) * hd] = dot(pg, om[h], 1, 1).astype(BF16)


def final_kernel(g, p, hp, *refs):
    parts, tots = refs[:p], refs[p : 2 * p]
    val, feat, sig, om, qg, wq, wk, wv = refs[2 * p : 2 * p + 8]
    odd, even, kg, vg = refs[2 * p + 8 :]
    hd, m = om.shape[1], om.shape[2]
    grad_half = summed(parts).astype(BF16)
    total = summed(tots)
    for h in range(hp):
        gh = grad_half[h * m : (h + 1) * m, :]
        col = slice(h * hd, (h + 1) * hd)
        fg = dot(val[:, col], gh, 1, 1) + total[:, h * m : (h + 1) * m]
        vg[:, col] = dot(feat[:, h * m : (h + 1) * m], gh).astype(BF16)
        pg = (fg * sig[:, h * m : (h + 1) * m]).astype(BF16)
        kg[:, col] = dot(pg, om[h], 1, 1).astype(BF16)
    rows = val.shape[0] // g
    for i in range(g):
        tok = slice(i * rows, (i + 1) * rows)
        out = dot(qg[tok, :], wq[...], 1, 1)
        out = out + dot(kg[tok, :], wk[...], 1, 1)
        out = out + dot(vg[tok, :], wv[...], 1, 1)
        at = slice((i // 2) * rows, (i // 2 + 1) * rows)
        if i % 2:
            odd[at, :] = out.astype(BF16)
        else:
            even[at, :] = out


def local(events, offsets, cotangent, query_weight, key_weight, value_weight, omega):
    heads, hd, m = omega.shape
    n_seq, n_sub = lax.axis_size("seq"), lax.axis_size("sub")
    rows, width = events.shape
    loss_scale = math.sqrt(rows * n_seq * n_sub)
    g = math.gcd(heads, n_seq)
    r = n_seq // g
    hp = heads // g
    p = r * n_sub
    t = g * rows
    cols = hp * hd
    s = lax.axis_index("seq")
    mine = s % g

    def over_seq(x, k):
        return lax.ppermute(x, "seq", [(i, i ^ k) for i in range(n_seq)])

    def over_sub(x, k):
        return lax.ppermute(x, "sub", [(i, i ^ k) for i in range(n_sub)])

    def to_all(own, send):
        parts = [own]
        for j in range(r):
            for k in range(n_sub):
                if j or k:
                    perm = [
                        (a * n_sub + b, (a ^ (j * g)) * n_sub + (b ^ k))
                        for a in range(n_seq)
                        for b in range(n_sub)
                    ]
                    parts.append(lax.ppermute(send, ("seq", "sub"), perm))
        return parts

    def columns(w):
        return lax.dynamic_slice_in_dim(w, mine * cols, cols, 1)

    def weight_rows(w):
        w = columns(w)
        return [w] + [over_sub(w, k) for k in range(1, n_sub)]

    wk, wv, wq = weight_rows(key_weight), weight_rows(value_weight), weight_rows(query_weight)
    x0 = encode(events, offsets)
    xs = [x0] * g
    for k in range(2, g, 2):
        xs[k] = over_seq(x0, k)
    for k in range(1, g, 2):
        xs[k] = over_seq(xs[k ^ 1], 1)
    cots = [columns(cotangent)]
    for k in range(1, g):
        cots.append(over_seq(lax.dynamic_slice_in_dim(cotangent, (mine ^ k) * cols, cols, 1), k))
    om = lax.dynamic_slice_in_dim(omega, mine * hp, hp, 0)

    flop = 2 * t * width * cols
    wk_full, key_feat, key_sig, key_total = call(
        functools.partial(key_kernel, g, n_sub, hp),
        [((width, cols), BF16), ((t, hp * m), BF16), ((t, hp * m), F32), ((1, hp * m), F32)],
        [*xs, *wk, om],
        8 * flop,
    )
    tots = to_all(key_total, key_total)
    wv_full, val, own, send = call(
        functools.partial(value_kernel, g, n_sub, hp),
        [((width, cols), BF16), ((t, cols), BF16), ((hp * m, hd), F32), ((hp * m, hd), BF16)],
        [*xs, *wv, key_feat],
        4 * flop,
    )
    summary = to_all(own, send)
    wq_full, query_feat, query_sig = call(
        functools.partial(query_kernel, g, n_sub, hp),
        [((width, cols), BF16), ((t, hp * m), BF16), ((t, hp * m), F32)],
        [*xs, *wq, om],
        8 * flop,
    )
    total_half, scaled_half, twice, own, send = call(
        functools.partial(scale_kernel, g, p, hp, loss_scale),
        [((1, hp * m), BF16), ((t, cols), BF16), ((t, cols), F32), ((hp * m, hd), F32), ((hp * m, hd), BF16)],
        [*tots, *cots, query_feat],
        4 * flop,
    )
    summary_grad = to_all(own, send)
    summary_half, norm, total_part = call(
        functools.partial(norm_kernel, p, hp),
        [((hp * m, hd), BF16), ((t, hp), F32), ((1, hp * m), F32)],
        [*summary, query_feat, twice],
        4 * flop,
    )
    total_grad = to_all(total_part, total_part)
    (query_grad,) = call(
        functools.partial(query_grad_kernel, hp),
        [((t, cols), BF16)],
        [scaled_half, summary_half, norm, total_half, query_sig, om],
        4 * flop,
    )
    odd, even, _, _ = call(
        functools.partial(final_kernel, g, p, hp),
        [((t // 2, width), BF16), ((t // 2, width), F32), ((t, cols), BF16), ((t, cols), BF16)],
        [*summary_grad, *total_grad, val, key_feat, key_sig, om, query_grad, wq_full, wk_full, wv_full],
        8 * flop,
    )
    got = over_seq(odd, 1)
    both = even + got.astype(F32)
    out = both[:rows]
    for k in range(2, g, 2):
        at = (k // 2) * rows
        out = out + over_seq(both[at : at + rows].astype(BF16), k).astype(F32)
    return out.astype(BF16)


def solution(mesh):
    in_specs = (
        P(("grp", "seq", "sub"), None),
        P(("grp", "seq", "sub")),
        P(("grp", "seq", "sub"), None),
        P("sub", None),
        P("sub", None),
        P("sub", None),
        P(),
    )
    out_specs = P(("grp", "seq", "sub"), None)
    return jax.shard_map(local, mesh=mesh, in_specs=in_specs, out_specs=out_specs, check_vma=False)
```

time: 334 us -> 87.7 us (0.26)
  blocking collectives: 162 us -> 0 us
  waiting for transfers between devices: 132 us -> 27.8 us
  starting transfers between devices: 0.08 us -> 43.1 us
  matrix products: 19.8 us -> 0 us
  between operations: 13.3 us -> 0.2 us
  Pallas kernels: 0 us -> 9.79 us
    psum x2 -> x0, blocking collectives: 162 us -> none  [the longest x1 81.4 us: local(): lax.psum((local_digest, local_total), ('seq', 'sub'))]
    all_gather x3 -> x0, waiting for transfers between devices: 130 us -> none  [the longest x1 45.1 us: local(): lax.all_gather(key_weight, 'sub', axis=0, tiled=True)]
    ppermute x0 -> x29, starting transfers between devices: none -> 43.1 us  [the longest x9 19.1 us: over_sub(): return lax.ppermute(x, 'sub', [(i, i ^ k) for i in range(n_sub)])]
    ppermute x0 -> x29, waiting for transfers between devices: none -> 27.8 us  [the longest x8 11.3 us: over_seq(): return lax.ppermute(x, 'seq', [(i, i ^ k) for i in range(n_seq)])]
    dot_general x16 -> x0, matrix products: 19.8 us -> none  [the longest x3 6.1 us: local(): jnp.dot(inputs, weight, preferred_element_type=widened_rows)]
    pallas_call x0 -> x7, Pallas kernels: none -> 9.79 us  [call(): pl.pallas_call(body, out_shape=[jax.ShapeDtypeStruct(s, d) for s, d in ou...]
  transfers between devices with their start and end apart: 3 -> 29, of which waited for: 3 -> 11; matrix products, arithmetic and copies ran while one was open for 3% -> 3% of each run, Pallas kernels for 0% -> 7%
where the time goes in v1:
time: 87.7 us; the launch traced here: 87.4 us
  starting transfers between devices  43.1 us (49%)
  waiting for transfers between devices  27.8 us (32%)
  Pallas kernels  9.79 us (11%)
  local copies, waits for them, and re-layouts  4.53 us (5%)
  other arithmetic  1.99 us (2%)
    ppermute x9, starting transfers between devices, over_sub(): return lax.ppermute(x, 'sub', [(i, i ^ k) for i in range(n_sub)])  19.1 us
    ppermute x12, starting transfers between devices, to_all(): parts.append(lax.ppermute(send, ('seq', 'sub'), perm))  17.2 us
    ppermute x8, waiting for transfers between devices, over_seq(): return lax.ppermute(x, 'seq', [(i, i ^ k) for i in range(n_seq)])  11.3 us
    ppermute x12, waiting for transfers between devices, to_all(): parts.append(lax.ppermute(send, ('seq', 'sub'), perm))  10.5 us
    pallas_call x7, Pallas kernels, call(): pl.pallas_call(body, out_shape=[jax.ShapeDtypeStruct(s, d) for s, d in ou...  9.79 us
    ppermute x8, starting transfers between devices, over_seq(): return lax.ppermute(x, 'seq', [(i, i ^ k) for i in range(n_seq)])  6.76 us
    ppermute x9, waiting for transfers between devices, over_sub(): return lax.ppermute(x, 'sub', [(i, i ^ k) for i in range(n_sub)])  6.03 us
    dynamic_slice x3, local copies, waits for them, and re-layouts, columns(): return lax.dynamic_slice_in_dim(w, mine * cols, cols, 1)  1.84 us
  transfers between devices with their start and end apart: 29, of which 11 were waited for; matrix products, arithmetic and copies ran while one was open for 3% of the time, Pallas kernels for 7%

profile of v1, /device:TPU:0, one launch (start us, length us, event | category | flops | bytes accessed | tf_op | source)
XLA Modules:
  0.0 87.4 jit_solution(2797364907021379250)
XLA Ops:
  1.8 3.0 %collective-permute-start.1 = (bf16[128,1024]{1,0:T(8,128)(2,1)S(1)}, bf16[128,1024]{1,0:T(8,128)(2,1)S(1)}, u32[]{:S(2)}, u32[]{:S(2)}) collective-permute-start(bf16[128,1024]{1,0:T(8,128)(2,1)S(1)} %fusion.1.refs_0_), channel_id=1, source_target_pairs={{0,8},{4,12},{8,0},{12,4},{1,9},{5,13},{9,1},{13,5},{2,10},{6,14},... | collective-permute-start | bytes 786440 | tf_op jit(solution)/shard_map/ppermute | solution.py:193
  4.8 3.7 %collective-permute-start.20 = (bf16[256,256]{1,0:T(8,128)(2,1)S(1)}, bf16[256,256]{1,0:T(8,128)(2,1)S(1)}, u32[]{:S(2)}, u32[]{:S(2)}) collective-permute-start(bf16[256,256]{1,0:T(8,128)(2,1)S(1)} %constant_dynamic-slice_fusion.refs_4_), channel_id=1, source_target_pairs={{0,3},{1,2},{2,1},{3,0},{4,7},{5,6},{6,5},{7,4},{8,11},{9,10},{10,... | collective-permute-start | bytes 393224 | tf_op jit(solution)/shard_map/ppermute | solution.py:196
  9.3 1.9 %collective-permute-done.1.refs_2_ = bf16[128,1024]{1,0:T(8,128)(2,1)S(1)} collective-permute-done((bf16[128,1024]{1,0:T(8,128)(2,1)S(1)}, bf16[128,1024]{1,0:T(8,128)(2,1)S(1)}, u32[]{:S(2)}, u32[]{:S(2)}) %collective-permute-start.1) | collective-permute-done | bytes 262176 | tf_op jit(solution)/shard_map/ppermute | solution.py:193
  12.7 4.0 %collective-permute-start.5 = (bf16[256,256]{1,0:T(8,128)(2,1)S(1)}, bf16[256,256]{1,0:T(8,128)(2,1)S(1)}, u32[]{:S(2)}, u32[]{:S(2)}) collective-permute-start(bf16[256,256]{1,0:T(8,128)(2,1)S(1)} %constant_dynamic-slice_fusion.7.refs_4_), channel_id=1, source_target_pairs={{0,3},{1,2},{2,1},{3,0},{4,7},{5,6},{6,5},{7,4},{8,11},{9,10},{10,... | collective-permute-start | bytes 393224 | tf_op jit(solution)/shard_map/ppermute | solution.py:196
  19.2 1.9 %collective-permute-done.5.refs_7_ = bf16[256,256]{1,0:T(8,128)(2,1)S(1)} collective-permute-done((bf16[256,256]{1,0:T(8,128)(2,1)S(1)}, bf16[256,256]{1,0:T(8,128)(2,1)S(1)}, u32[]{:S(2)}, u32[]{:S(2)}) %collective-permute-start.5) | collective-permute-done | bytes 131104 | tf_op jit(solution)/shard_map/ppermute | solution.py:196
  21.1 6.4 %collective-permute-start.19 = (bf16[256,256]{1,0:T(8,128)(2,1)S(1)}, bf16[256,256]{1,0:T(8,128)(2,1)S(1)}, u32[]{:S(2)}, u32[]{:S(2)}) collective-permute-start(bf16[256,256]{1,0:T(8,128)(2,1)S(1)} %constant_dynamic-slice_fusion.refs_4_), channel_id=1, source_target_pairs={{0,2},{1,3},{2,0},{3,1},{4,6},{5,7},{6,4},{7,5},{8,10},{9,11},{10,... | collective-permute-start | bytes 393224 | tf_op jit(solution)/shard_map/ppermute | solution.py:196
  28.8 2.5 %collective-permute-start.14 = (bf16[256,256]{1,0:T(8,128)(2,1)S(1)}, bf16[256,256]{1,0:T(8,128)(2,1)S(1)}, u32[]{:S(2)}, u32[]{:S(2)}) collective-permute-start(bf16[256,256]{1,0:T(8,128)(2,1)S(1)} %constant_dynamic-slice_fusion.1.refs_4_), channel_id=1, source_target_pairs={{0,3},{1,2},{2,1},{3,0},{4,7},{5,6},{6,5},{7,4},{8,11},{9,10},{10,... | collective-permute-start | bytes 393224 | tf_op jit(solution)/shard_map/ppermute | solution.py:196
  33.2 1.6 %shard_map.73 = (bf16[1024,256]{1,0:T(8,128)(2,1)S(1)}, bf16[512,512]{1,0:T(8,128)(2,1)S(1)}, f32[512,512]{1,0:T(8,128)S(1)}, f32[1,512]{1,0:T(1,128)S(1)}) custom-call(bf16[128,1024]{1,0:T(8,128)(2,1)S(1)} %fusion.1.refs_0_, bf16[128,1024]{1,0:T(8,128)(2,1)S(1)} %collective-permute-done.refs_1_, bf16[128,1024]{1,0:T(8,128)(2,1)S(1)} %collective-permute-done.1.refs_2_, ...), custom_call_target="tpu_custom_call" | custom-call | flops 2147483648 | bytes 1703936 | tf_op jit(solution)/shard_map/pallas_call | solution.py:45
  37.3 2.5 %collective-permute-done.18.refs_5_ = bf16[256,256]{1,0:T(8,128)(2,1)S(1)} collective-permute-done((bf16[256,256]{1,0:T(8,128)(2,1)S(1)}, bf16[256,256]{1,0:T(8,128)(2,1)S(1)}, u32[]{:S(2)}, u32[]{:S(2)}) %collective-permute-start.18) | collective-permute-done | bytes 131104 | tf_op jit(solution)/shard_map/ppermute | solution.py:196
  39.8 1.9 %collective-permute-start.8 = (f32[1,512]{1,0:T(1,128)S(1)}, f32[1,512]{1,0:T(1,128)S(1)}, u32[]{:S(2)}, u32[]{:S(2)}) collective-permute-start(f32[1,512]{1,0:T(1,128)S(1)} %get-tuple-element.26.refs_0_), channel_id=1, source_target_pairs={{0,3},{1,2},{2,1},{3,0},{4,7},{5,6},{6,5},{7,4},{8,11},{9,10},{10,... | collective-permute-start | bytes 6152 | tf_op jit(solution)/shard_map/ppermute | solution.py:208
  42.6 2.4 %collective-permute-start.6 = (f32[1,512]{1,0:T(1,128)S(1)}, f32[1,512]{1,0:T(1,128)S(1)}, u32[]{:S(2)}, u32[]{:S(2)}) collective-permute-start(f32[1,512]{1,0:T(1,128)S(1)} %get-tuple-element.26.refs_0_), channel_id=1, source_target_pairs={{0,1},{1,0},{2,3},{3,2},{4,5},{5,4},{6,7},{7,6},{8,9},{9,8},{10,11... | collective-permute-start | bytes 6152 | tf_op jit(solution)/shard_map/ppermute | solution.py:208
  45.4 2.5 %collective-permute-start.23 = (bf16[512,128]{1,0:T(8,128)(2,1)S(1)}, bf16[512,128]{1,0:T(8,128)(2,1)S(1)}, u32[]{:S(2)}, u32[]{:S(2)}) collective-permute-start(bf16[512,128]{1,0:T(8,128)(2,1)S(1)} %get-tuple-element.32), channel_id=1, source_target_pairs={{0,3},{1,2},{2,1},{3,0},{4,7},{5,6},{6,5},{7,4},{8,11},{9,10},{10,... | collective-permute-start | bytes 393224 | tf_op jit(solution)/shard_map/ppermute | solution.py:208
  47.9 1.9 %collective-permute-start.21 = (bf16[512,128]{1,0:T(8,128)(2,1)S(1)}, bf16[512,128]{1,0:T(8,128)(2,1)S(1)}, u32[]{:S(2)}, u32[]{:S(2)}) collective-permute-start(bf16[512,128]{1,0:T(8,128)(2,1)S(1)} %get-tuple-element.32), channel_id=1, source_target_pairs={{0,1},{1,0},{2,3},{3,2},{4,5},{5,4},{6,7},{7,6},{8,9},{9,8},{10,11... | collective-permute-start | bytes 393224 | tf_op jit(solution)/shard_map/ppermute | solution.py:208
  49.8 1.5 %shard_map.74 = (bf16[1024,256]{1,0:T(8,128)(2,1)S(1)}, bf16[512,512]{1,0:T(8,128)(2,1)S(1)}, f32[512,512]{1,0:T(8,128)S(1)}) custom-call(bf16[128,1024]{1,0:T(8,128)(2,1)S(1)} %fusion.1.refs_0_, bf16[128,1024]{1,0:T(8,128)(2,1)S(1)} %collective-permute-done.refs_1_, bf16[128,1024]{1,0:T(8,128)(2,1)S(1)} %collective-permute-done.1.refs_2_, ...), custom_call_target="tpu_custom_call" | custom-call | flops 2147483648 | bytes 1703936 | tf_op jit(solution)/shard_map/pallas_call | solution.py:45
  52.1 2.5 %collective-permute-start.17 = (bf16[512,128]{1,0:T(8,128)(2,1)S(1)}, bf16[512,128]{1,0:T(8,128)(2,1)S(1)}, u32[]{:S(2)}, u32[]{:S(2)}) collective-permute-start(bf16[512,128]{1,0:T(8,128)(2,1)S(1)} %get-tuple-element.29), channel_id=1, source_target_pairs={{0,3},{1,2},{2,1},{3,0},{4,7},{5,6},{6,5},{7,4},{8,11},{9,10},{10,... | collective-permute-start | bytes 393224 | tf_op jit(solution)/shard_map/ppermute | solution.py:208
  54.7 1.9 %collective-permute-start.15 = (bf16[512,128]{1,0:T(8,128)(2,1)S(1)}, bf16[512,128]{1,0:T(8,128)(2,1)S(1)}, u32[]{:S(2)}, u32[]{:S(2)}) collective-permute-start(bf16[512,128]{1,0:T(8,128)(2,1)S(1)} %get-tuple-element.29), channel_id=1, source_target_pairs={{0,1},{1,0},{2,3},{3,2},{4,5},{5,4},{6,7},{7,6},{8,9},{9,8},{10,11... | collective-permute-start | bytes 393224 | tf_op jit(solution)/shard_map/ppermute | solution.py:208
  56.6 5.8 %collective-permute-done.22.refs_2_ = bf16[512,128]{1,0:T(8,128)(2,1)S(1)} collective-permute-done((bf16[512,128]{1,0:T(8,128)(2,1)S(1)}, bf16[512,128]{1,0:T(8,128)(2,1)S(1)}, u32[]{:S(2)}, u32[]{:S(2)}) %collective-permute-start.22) | collective-permute-done | bytes 131104 | tf_op jit(solution)/shard_map/ppermute | solution.py:208
  62.9 2.5 %collective-permute-start.26 = (f32[1,512]{1,0:T(1,128)S(1)}, f32[1,512]{1,0:T(1,128)S(1)}, u32[]{:S(2)}, u32[]{:S(2)}) collective-permute-start(f32[1,512]{1,0:T(1,128)S(1)} %get-tuple-element.34.refs_4_), channel_id=1, source_target_pairs={{0,3},{1,2},{2,1},{3,0},{4,7},{5,6},{6,5},{7,4},{8,11},{9,10},{10,... | collective-permute-start | bytes 6152 | tf_op jit(solution)/shard_map/ppermute | solution.py:208
  65.4 3.1 %collective-permute-done.26.refs_7_ = f32[1,512]{1,0:T(1,128)S(1)} collective-permute-done((f32[1,512]{1,0:T(1,128)S(1)}, f32[1,512]{1,0:T(1,128)S(1)}, u32[]{:S(2)}, u32[]{:S(2)}) %collective-permute-start.26) | collective-permute-done | bytes 2080 | tf_op jit(solution)/shard_map/ppermute | solution.py:208
  70.5 1.6 %collective-permute-done.24.refs_5_ = f32[1,512]{1,0:T(1,128)S(1)} collective-permute-done((f32[1,512]{1,0:T(1,128)S(1)}, f32[1,512]{1,0:T(1,128)S(1)}, u32[]{:S(2)}, u32[]{:S(2)}) %collective-permute-start.24) | collective-permute-done | bytes 2080 | tf_op jit(solution)/shard_map/ppermute | solution.py:208
  72.1 4.1 %shard_map.79 = (bf16[256,1024]{1,0:T(8,128)(2,1)S(1)}, f32[256,1024]{1,0:T(8,128)S(1)}, bf16[512,256]{1,0:T(8,128)(2,1)}, bf16[512,256]{1,0:T(8,128)(2,1)}) custom-call(f32[512,128]{1,0:T(8,128)S(1)} %get-tuple-element.28.refs_0_, bf16[512,128]{1,0:T(8,128)(2,1)S(1)} %collective-permute-done.15.refs_1_, ...), custom_call_target="tpu_custom_call" | custom-call | flops 2147483648 | bytes 4464640 | tf_op jit(solution)/shard_map/pallas_call | solution.py:45
  76.1 1.9 %collective-permute-done.27 = bf16[256,1024]{1,0:T(8,128)(2,1)S(1)} collective-permute-done((bf16[256,1024]{1,0:T(8,128)(2,1)S(1)}, bf16[256,1024]{1,0:T(8,128)(2,1)S(1)}, u32[]{:S(2)}, u32[]{:S(2)}) %collective-permute-start.27) | collective-permute-done | bytes 524320 | tf_op jit(solution)/shard_map/ppermute | solution.py:193
  78.3 1.5 %collective-permute-start.28 = (bf16[128,1024]{1,0:T(8,128)(2,1)S(1)}, bf16[128,1024]{1,0:T(8,128)(2,1)S(1)}, u32[]{:S(2)}, u32[]{:S(2)}) collective-permute-start(bf16[128,1024]{1,0:T(8,128)(2,1)S(1)} %slice.15), channel_id=1, source_target_pairs={{0,8},{4,12},{8,0},{12,4},{1,9},{5,13},{9,1},{13,5},{2,10},{6,14},... | collective-permute-start | bytes 786440 | tf_op jit(solution)/shard_map/ppermute | solution.py:193
  79.8 6.9 %collective-permute-done.28 = bf16[128,1024]{1,0:T(8,128)(2,1)S(1)} collective-permute-done((bf16[128,1024]{1,0:T(8,128)(2,1)S(1)}, bf16[128,1024]{1,0:T(8,128)(2,1)S(1)}, u32[]{:S(2)}, u32[]{:S(2)}) %collective-permute-start.28) | collective-permute-done | bytes 262176 | tf_op jit(solution)/shard_map/ppermute | solution.py:193
  (63 shorter events, 17.6 us)
Async XLA Ops:
  1.8 9.3 %collective-permute-start.1 = (bf16[128,1024]{1,0:T(8,128)(2,1)S(1)}, bf16[128,1024]{1,0:T(8,128)(2,1)S(1)}, u32[]{:S(2)}, u32[]{:S(2)}) collective-permute-start(bf16[128,1024]{1,0:T(8,128)(2,1)S(1)} %fusion.1.refs_0_), channel_id=1, source_target_pairs={{0,8},{4,12},{8,0},{12,4},{1,9},{5,13},{9,1},{13,5},{2,10},{6,14},... | collective-permute-start | bytes 786440 | tf_op jit(solution)/shard_map/ppermute | solution.py:193
  4.8 26.5 %collective-permute-start = (bf16[128,1024]{1,0:T(8,128)(2,1)S(1)}, bf16[128,1024]{1,0:T(8,128)(2,1)S(1)}, u32[]{:S(2)}, u32[]{:S(2)}) collective-permute-start(bf16[128,1024]{1,0:T(8,128)(2,1)S(1)} %fusion.1.refs_0_), channel_id=1, source_target_pairs={{0,4},{4,0},{8,12},{12,8},{1,5},{5,1},{9,13},{13,9},{2,6},{6,2},{1... | collective-permute-start | bytes 786440 | tf_op jit(solution)/shard_map/ppermute | solution.py:193
  4.8 11.8 %collective-permute-start.20 = (bf16[256,256]{1,0:T(8,128)(2,1)S(1)}, bf16[256,256]{1,0:T(8,128)(2,1)S(1)}, u32[]{:S(2)}, u32[]{:S(2)}) collective-permute-start(bf16[256,256]{1,0:T(8,128)(2,1)S(1)} %constant_dynamic-slice_fusion.refs_4_), channel_id=1, source_target_pairs={{0,3},{1,2},{2,1},{3,0},{4,7},{5,6},{6,5},{7,4},{8,11},{9,10},{10,... | collective-permute-start | bytes 393224 | tf_op jit(solution)/shard_map/ppermute | solution.py:196
  9.0 7.7 %collective-permute-start.9 = (bf16[128,256]{1,0:T(8,128)(2,1)S(1)}, bf16[128,256]{1,0:T(8,128)(2,1)S(1)}, u32[]{:S(2)}, u32[]{:S(2)}) collective-permute-start(bf16[128,256]{1,0:T(8,128)(2,1)S(1)} %get-tuple-element.48), channel_id=1, source_target_pairs={{0,4},{4,0},{8,12},{12,8},{1,5},{5,1},{9,13},{13,9},{2,6},{6,2},{1... | collective-permute-start | bytes 196616 | tf_op jit(solution)/shard_map/ppermute | solution.py:193
  11.1 21.2 %collective-permute-start.2 = (bf16[128,1024]{1,0:T(8,128)(2,1)S(1)}, bf16[128,1024]{1,0:T(8,128)(2,1)S(1)}, u32[]{:S(2)}, u32[]{:S(2)}) collective-permute-start(bf16[128,1024]{1,0:T(8,128)(2,1)S(1)} %collective-permute-done.1.refs_2_), channel_id=1, source_target_pairs={{0,4},{4,0},{8,12},{12,8},{1,5},{5,1},{9,13},{13,9},{2,6},{6,2},{1... | collective-permute-start | bytes 786440 | tf_op jit(solution)/shard_map/ppermute | solution.py:193
  12.7 8.4 %collective-permute-start.5 = (bf16[256,256]{1,0:T(8,128)(2,1)S(1)}, bf16[256,256]{1,0:T(8,128)(2,1)S(1)}, u32[]{:S(2)}, u32[]{:S(2)}) collective-permute-start(bf16[256,256]{1,0:T(8,128)(2,1)S(1)} %constant_dynamic-slice_fusion.7.refs_4_), channel_id=1, source_target_pairs={{0,3},{1,2},{2,1},{3,0},{4,7},{5,6},{6,5},{7,4},{8,11},{9,10},{10,... | collective-permute-start | bytes 393224 | tf_op jit(solution)/shard_map/ppermute | solution.py:196
  16.7 12.1 %collective-permute-start.4 = (bf16[256,256]{1,0:T(8,128)(2,1)S(1)}, bf16[256,256]{1,0:T(8,128)(2,1)S(1)}, u32[]{:S(2)}, u32[]{:S(2)}) collective-permute-start(bf16[256,256]{1,0:T(8,128)(2,1)S(1)} %constant_dynamic-slice_fusion.7.refs_4_), channel_id=1, source_target_pairs={{0,2},{1,3},{2,0},{3,1},{4,6},{5,7},{6,4},{7,5},{8,10},{9,11},{10,... | collective-permute-start | bytes 393224 | tf_op jit(solution)/shard_map/ppermute | solution.py:196
  16.7 12.1 %collective-permute-start.3 = (bf16[256,256]{1,0:T(8,128)(2,1)S(1)}, bf16[256,256]{1,0:T(8,128)(2,1)S(1)}, u32[]{:S(2)}, u32[]{:S(2)}) collective-permute-start(bf16[256,256]{1,0:T(8,128)(2,1)S(1)} %constant_dynamic-slice_fusion.7.refs_4_), channel_id=1, source_target_pairs={{0,1},{1,0},{2,3},{3,2},{4,5},{5,4},{6,7},{7,6},{8,9},{9,8},{10,11... | collective-permute-start | bytes 393224 | tf_op jit(solution)/shard_map/ppermute | solution.py:196
  21.1 14.7 %collective-permute-start.19 = (bf16[256,256]{1,0:T(8,128)(2,1)S(1)}, bf16[256,256]{1,0:T(8,128)(2,1)S(1)}, u32[]{:S(2)}, u32[]{:S(2)}) collective-permute-start(bf16[256,256]{1,0:T(8,128)(2,1)S(1)} %constant_dynamic-slice_fusion.refs_4_), channel_id=1, source_target_pairs={{0,2},{1,3},{2,0},{3,1},{4,6},{5,7},{6,4},{7,5},{8,10},{9,11},{10,... | collective-permute-start | bytes 393224 | tf_op jit(solution)/shard_map/ppermute | solution.py:196
  28.8 11.0 %collective-permute-start.18 = (bf16[256,256]{1,0:T(8,128)(2,1)S(1)}, bf16[256,256]{1,0:T(8,128)(2,1)S(1)}, u32[]{:S(2)}, u32[]{:S(2)}) collective-permute-start(bf16[256,256]{1,0:T(8,128)(2,1)S(1)} %constant_dynamic-slice_fusion.refs_4_), channel_id=1, source_target_pairs={{0,1},{1,0},{2,3},{3,2},{4,5},{5,4},{6,7},{7,6},{8,9},{9,8},{10,11... | collective-permute-start | bytes 393224 | tf_op jit(solution)/shard_map/ppermute | solution.py:196
  28.8 13.8 %collective-permute-start.14 = (bf16[256,256]{1,0:T(8,128)(2,1)S(1)}, bf16[256,256]{1,0:T(8,128)(2,1)S(1)}, u32[]{:S(2)}, u32[]{:S(2)}) collective-permute-start(bf16[256,256]{1,0:T(8,128)(2,1)S(1)} %constant_dynamic-slice_fusion.1.refs_4_), channel_id=1, source_target_pairs={{0,3},{1,2},{2,1},{3,0},{4,7},{5,6},{6,5},{7,4},{8,11},{9,10},{10,... | collective-permute-start | bytes 393224 | tf_op jit(solution)/shard_map/ppermute | solution.py:196
  31.3 14.1 %collective-permute-start.13 = (bf16[256,256]{1,0:T(8,128)(2,1)S(1)}, bf16[256,256]{1,0:T(8,128)(2,1)S(1)}, u32[]{:S(2)}, u32[]{:S(2)}) collective-permute-start(bf16[256,256]{1,0:T(8,128)(2,1)S(1)} %constant_dynamic-slice_fusion.1.refs_4_), channel_id=1, source_target_pairs={{0,2},{1,3},{2,0},{3,1},{4,6},{5,7},{6,4},{7,5},{8,10},{9,11},{10,... | collective-permute-start | bytes 393224 | tf_op jit(solution)/shard_map/ppermute | solution.py:196
  32.3 15.6 %collective-permute-start.12 = (bf16[256,256]{1,0:T(8,128)(2,1)S(1)}, bf16[256,256]{1,0:T(8,128)(2,1)S(1)}, u32[]{:S(2)}, u32[]{:S(2)}) collective-permute-start(bf16[256,256]{1,0:T(8,128)(2,1)S(1)} %constant_dynamic-slice_fusion.1.refs_4_), channel_id=1, source_target_pairs={{0,1},{1,0},{2,3},{3,2},{4,5},{5,4},{6,7},{7,6},{8,9},{9,8},{10,11... | collective-permute-start | bytes 393224 | tf_op jit(solution)/shard_map/ppermute | solution.py:196
  35.8 6.7 %collective-permute-start.10 = (bf16[128,256]{1,0:T(8,128)(2,1)S(1)}, bf16[128,256]{1,0:T(8,128)(2,1)S(1)}, u32[]{:S(2)}, u32[]{:S(2)}) collective-permute-start(bf16[128,256]{1,0:T(8,128)(2,1)S(1)} %get-tuple-element.50), channel_id=1, source_target_pairs={{0,8},{4,12},{8,0},{12,4},{1,9},{5,13},{9,1},{13,5},{2,10},{6,14},... | collective-permute-start | bytes 196616 | tf_op jit(solution)/shard_map/ppermute | solution.py:193
  39.8 8.1 %collective-permute-start.8 = (f32[1,512]{1,0:T(1,128)S(1)}, f32[1,512]{1,0:T(1,128)S(1)}, u32[]{:S(2)}, u32[]{:S(2)}) collective-permute-start(f32[1,512]{1,0:T(1,128)S(1)} %get-tuple-element.26.refs_0_), channel_id=1, source_target_pairs={{0,3},{1,2},{2,1},{3,0},{4,7},{5,6},{6,5},{7,4},{8,11},{9,10},{10,... | collective-permute-start | bytes 6152 | tf_op jit(solution)/shard_map/ppermute | solution.py:208
  42.5 8.8 %collective-permute-start.7 = (f32[1,512]{1,0:T(1,128)S(1)}, f32[1,512]{1,0:T(1,128)S(1)}, u32[]{:S(2)}, u32[]{:S(2)}) collective-permute-start(f32[1,512]{1,0:T(1,128)S(1)} %get-tuple-element.26.refs_0_), channel_id=1, source_target_pairs={{0,2},{1,3},{2,0},{3,1},{4,6},{5,7},{6,4},{7,5},{8,10},{9,11},{10,... | collective-permute-start | bytes 6152 | tf_op jit(solution)/shard_map/ppermute | solution.py:208
  42.6 8.8 %collective-permute-start.6 = (f32[1,512]{1,0:T(1,128)S(1)}, f32[1,512]{1,0:T(1,128)S(1)}, u32[]{:S(2)}, u32[]{:S(2)}) collective-permute-start(f32[1,512]{1,0:T(1,128)S(1)} %get-tuple-element.26.refs_0_), channel_id=1, source_target_pairs={{0,1},{1,0},{2,3},{3,2},{4,5},{5,4},{6,7},{7,6},{8,9},{9,8},{10,11... | collective-permute-start | bytes 6152 | tf_op jit(solution)/shard_map/ppermute | solution.py:208
  45.4 9.3 %collective-permute-start.23 = (bf16[512,128]{1,0:T(8,128)(2,1)S(1)}, bf16[512,128]{1,0:T(8,128)(2,1)S(1)}, u32[]{:S(2)}, u32[]{:S(2)}) collective-permute-start(bf16[512,128]{1,0:T(8,128)(2,1)S(1)} %get-tuple-element.32), channel_id=1, source_target_pairs={{0,3},{1,2},{2,1},{3,0},{4,7},{5,6},{6,5},{7,4},{8,11},{9,10},{10,... | collective-permute-start | bytes 393224 | tf_op jit(solution)/shard_map/ppermute | solution.py:208
  47.9 14.6 %collective-permute-start.22 = (bf16[512,128]{1,0:T(8,128)(2,1)S(1)}, bf16[512,128]{1,0:T(8,128)(2,1)S(1)}, u32[]{:S(2)}, u32[]{:S(2)}) collective-permute-start(bf16[512,128]{1,0:T(8,128)(2,1)S(1)} %get-tuple-element.32), channel_id=1, source_target_pairs={{0,2},{1,3},{2,0},{3,1},{4,6},{5,7},{6,4},{7,5},{8,10},{9,11},{10,... | collective-permute-start | bytes 393224 | tf_op jit(solution)/shard_map/ppermute | solution.py:208
  47.9 14.5 %collective-permute-start.21 = (bf16[512,128]{1,0:T(8,128)(2,1)S(1)}, bf16[512,128]{1,0:T(8,128)(2,1)S(1)}, u32[]{:S(2)}, u32[]{:S(2)}) collective-permute-start(bf16[512,128]{1,0:T(8,128)(2,1)S(1)} %get-tuple-element.32), channel_id=1, source_target_pairs={{0,1},{1,0},{2,3},{3,2},{4,5},{5,4},{6,7},{7,6},{8,9},{9,8},{10,11... | collective-permute-start | bytes 393224 | tf_op jit(solution)/shard_map/ppermute | solution.py:208
  52.1 19.9 %collective-permute-start.17 = (bf16[512,128]{1,0:T(8,128)(2,1)S(1)}, bf16[512,128]{1,0:T(8,128)(2,1)S(1)}, u32[]{:S(2)}, u32[]{:S(2)}) collective-permute-start(bf16[512,128]{1,0:T(8,128)(2,1)S(1)} %get-tuple-element.29), channel_id=1, source_target_pairs={{0,3},{1,2},{2,1},{3,0},{4,7},{5,6},{6,5},{7,4},{8,11},{9,10},{10,... | collective-permute-start | bytes 393224 | tf_op jit(solution)/shard_map/ppermute | solution.py:208
  54.7 17.4 %collective-permute-start.16 = (bf16[512,128]{1,0:T(8,128)(2,1)S(1)}, bf16[512,128]{1,0:T(8,128)(2,1)S(1)}, u32[]{:S(2)}, u32[]{:S(2)}) collective-permute-start(bf16[512,128]{1,0:T(8,128)(2,1)S(1)} %get-tuple-element.29), channel_id=1, source_target_pairs={{0,2},{1,3},{2,0},{3,1},{4,6},{5,7},{6,4},{7,5},{8,10},{9,11},{10,... | collective-permute-start | bytes 393224 | tf_op jit(solution)/shard_map/ppermute | solution.py:208
  54.7 17.4 %collective-permute-start.15 = (bf16[512,128]{1,0:T(8,128)(2,1)S(1)}, bf16[512,128]{1,0:T(8,128)(2,1)S(1)}, u32[]{:S(2)}, u32[]{:S(2)}) collective-permute-start(bf16[512,128]{1,0:T(8,128)(2,1)S(1)} %get-tuple-element.29), channel_id=1, source_target_pairs={{0,1},{1,0},{2,3},{3,2},{4,5},{5,4},{6,7},{7,6},{8,9},{9,8},{10,11... | collective-permute-start | bytes 393224 | tf_op jit(solution)/shard_map/ppermute | solution.py:208
  78.3 8.4 %collective-permute-start.28 = (bf16[128,1024]{1,0:T(8,128)(2,1)S(1)}, bf16[128,1024]{1,0:T(8,128)(2,1)S(1)}, u32[]{:S(2)}, u32[]{:S(2)}) collective-permute-start(bf16[128,1024]{1,0:T(8,128)(2,1)S(1)} %slice.15), channel_id=1, source_target_pairs={{0,8},{4,12},{8,0},{12,4},{1,9},{5,13},{9,1},{13,5},{2,10},{6,14},... | collective-permute-start | bytes 786440 | tf_op jit(solution)/shard_map/ppermute | solution.py:193
  (10 other events, 34.5 us)

commit v2 on v1

v2 whole, which is shorter than its diff:
```python
import functools
import math

import jax
import jax.numpy as jnp
from jax import lax
from jax.experimental import pallas as pl
from jax.experimental.pallas import tpu as pltpu
from jax.sharding import PartitionSpec as P

F32 = jnp.float32
BF16 = jnp.bfloat16
ANY = pl.BlockSpec(memory_space=pl.ANY)


def dot(a, b, ca=1, cb=0):
    return lax.dot_general(a, b, (((ca,), (cb,)), ((), ())), preferred_element_type=F32)


def soft_and_sigmoid(u):
    e = jnp.exp(-jnp.abs(u))
    series = e * (1.0 + e * (-0.5 + e * (1.0 / 3.0)))
    soft = jnp.maximum(u, 0.0) + jnp.where(e < 1e-3, series, jnp.log(1.0 + e))
    r = 1.0 / (1.0 + e)
    return soft, jnp.where(u >= 0.0, r, e * r)


def call(body, outs, args, flops, **kw):
    nbytes = sum(a.size * a.dtype.itemsize for a in args)
    return pl.pallas_call(
        body,
        out_shape=[jax.ShapeDtypeStruct(s, d) for s, d in outs],
        compiler_params=pltpu.CompilerParams(vmem_limit_bytes=24 * 1024 * 1024),
        cost_estimate=pl.CostEstimate(flops=flops, bytes_accessed=nbytes, transcendentals=0),
        **kw,
    )(*args)


def weight_kernel(g, cols, wk, wv, wq, kv, q, sems):
    at = pl.ds(pl.multiple_of((lax.axis_index("seq") % g) * cols, cols), cols)
    copies = [
        pltpu.make_async_copy(wk.at[:, at], kv.at[:, :cols], sems.at[0]),
        pltpu.make_async_copy(wv.at[:, at], kv.at[:, cols:], sems.at[1]),
        pltpu.make_async_copy(wq.at[:, at], q, sems.at[2]),
    ]
    for c in copies:
        c.start()
    for c in copies:
        c.wait()


def input_kernel(g, pair, events, sines, cosines, cot, *outs):
    width = events.shape[1]
    half = width // 2
    mine = (lax.axis_index("seq") % g) // 2
    left = (events[:, :half].astype(F32) + sines[...]).astype(BF16)
    right = (events[:, half:].astype(F32) + cosines[...]).astype(BF16)
    for k, out in enumerate(outs):
        out[:, :half] = left
        out[:, half:width] = right
        out[:, width:] = cot[:, pl.ds(pl.multiple_of((mine ^ k) * pair, pair), pair)]


def place_rows(full, parts):
    z = lax.axis_index("sub")
    rows = parts[0].shape[0]
    for k, part in enumerate(parts):
        full[pl.ds(pl.multiple_of((z ^ k) * rows, rows), rows), :] = part[...]


def features(act, om, h, i, feat, sig):
    hd, m = om.shape[1], om.shape[2]
    rows = act.shape[0]
    soft, s = soft_and_sigmoid(dot(act[:, h * hd : (h + 1) * hd], om[h]))
    soft = soft.astype(BF16)
    at = (slice(i * rows, (i + 1) * rows), slice(h * m, (h + 1) * m))
    feat[at] = soft
    sig[at] = s
    return soft


def put_total(own, send, base, extra, total):
    hd = own.shape[1]
    n = total.shape[1] // hd
    for j in range(n):
        piece = total[:, j * hd : (j + 1) * hd]
        high = piece.astype(BF16)
        own[base + j : base + j + 1, :] = piece
        send[base + j : base + j + 1, :] = high
        own[base + extra + j : base + extra + j + 1, :] = jnp.zeros_like(piece)
        send[base + extra + j : base + extra + j + 1, :] = (piece - high.astype(F32)).astype(BF16)


def get_total(tail, extra, h, m):
    hd = tail.shape[1]
    n = m // hd
    rows = [
        tail[h * n + j : h * n + j + 1, :] + tail[extra + h * n + j : extra + h * n + j + 1, :]
        for j in range(n)
    ]
    return jnp.concatenate(rows, axis=1)


def summed(parts, lo, hi):
    out = parts[0][lo:hi, :]
    for part in parts[1:]:
        out = out + part[lo:hi, :].astype(F32)
    return out


def key_value_kernel(g, n, hp, width, *refs):
    xs, ws, om = refs[:g], refs[g : g + n], refs[g + n]
    w_full, feat, sig, val, own, send = refs[g + n + 1 :]
    hd, m = om.shape[1], om.shape[2]
    cols = hp * hd
    place_rows(w_full, ws)
    rows = xs[0].shape[0]
    sums = [jnp.zeros((1, m), F32) for _ in range(hp)]
    for i, x in enumerate(xs):
        act = dot(x[:, :width], w_full[...]).astype(BF16)
        val[i * rows : (i + 1) * rows, :] = act[:, cols:]
        for h in range(hp):
            soft = features(act, om, h, i, feat, sig)
            sums[h] = sums[h] + jnp.sum(soft.astype(F32), axis=0, keepdims=True)
    base = hp * m
    own[base:, :] = jnp.zeros_like(own[base:, :])
    send[base:, :] = jnp.zeros_like(send[base:, :])
    for h in range(hp):
        s = dot(feat[:, h * m : (h + 1) * m], val[:, h * hd : (h + 1) * hd], 0, 0)
        own[h * m : (h + 1) * m, :] = s
        send[h * m : (h + 1) * m, :] = s.astype(BF16)
    put_total(own, send, base, hp * m // hd, jnp.concatenate(sums, axis=1))


def query_kernel(g, n, hp, width, *refs):
    xs, ws, om = refs[:g], refs[g : g + n], refs[g + n]
    w_full, feat, sig = refs[g + n + 1 :]
    place_rows(w_full, ws)
    for i, x in enumerate(xs):
        act = dot(x[:, :width], w_full[...]).astype(BF16)
        for h in range(hp):
            features(act, om, h, i, feat, sig)


def query_side_kernel(g, p, hp, m, width, loss_scale, *refs):
    parts, xs, feat = refs[:p], refs[p : p + g], refs[p + g]
    total_half, summary_half, scaled_half, norm, own, send = refs[p + g + 1 :]
    hd = summary_half.shape[1]
    cols = hp * hd
    base = hp * m
    extra = base // hd
    summary_half[...] = summed(parts, 0, base).astype(BF16)
    tail = summed(parts, base, parts[0].shape[0])
    core = lax.axis_index("seq") % 2
    rows = xs[0].shape[0]
    own[base:, :] = jnp.zeros_like(own[base:, :])
    send[base:, :] = jnp.zeros_like(send[base:, :])
    sums = []
    for h in range(hp):
        row = get_total(tail, extra, h, m).astype(BF16)
        total_half[:, h * m : (h + 1) * m] = row
        spread = jnp.broadcast_to(row.astype(F32), (hd, m)).astype(BF16)
        acc = jnp.zeros((1, m), F32)
        for i in range(g):
            tok = slice(i * rows, (i + 1) * rows)
            qf = feat[tok, h * m : (h + 1) * m]
            at = pl.multiple_of(width + core * cols + h * hd, hd)
            denom = dot(qf, spread, 1, 1)
            numer = dot(qf, summary_half[h * m : (h + 1) * m, :])
            scaled = xs[i][:, pl.ds(at, hd)].astype(F32) * loss_scale / denom
            scaled_half[tok, h * hd : (h + 1) * hd] = scaled.astype(BF16)
            ng = -jnp.sum(scaled * (numer / denom), axis=1, keepdims=True)
            norm[tok, h : h + 1] = ng
            acc = acc + jnp.sum(qf.astype(F32) * ng.astype(BF16).astype(F32), axis=0, keepdims=True)
        s = dot(feat[:, h * m : (h + 1) * m], scaled_half[:, h * hd : (h + 1) * hd], 0, 0)
        own[h * m : (h + 1) * m, :] = s
        send[h * m : (h + 1) * m, :] = s.astype(BF16)
        sums.append(acc)
    put_total(own, send, base, extra, jnp.concatenate(sums, axis=1))


def query_grad_kernel(hp, scaled_half, summary_half, norm, total_half, sig, om, out):
    hd, m = om.shape[1], om.shape[2]
    for h in range(hp):
        fg = dot(scaled_half[:, h * hd : (h + 1) * hd], summary_half[h * m : (h + 1) * m, :], 1, 1)
        fg = fg + norm[:, h : h + 1] * total_half[:, h * m : (h + 1) * m].astype(F32)
        pg = (fg * sig[:, h * m : (h + 1) * m]).astype(BF16)
        out[:, h * hd : (h + 1) * hd] = dot(pg, om[h], 1, 1).astype(BF16)


def products(g, start, qg, kvg, wq, wkv, out):
    rows = qg.shape[0] // g
    for i in range(start, g, 2):
        tok = slice(i * rows, (i + 1) * rows)
        o = dot(qg[tok, :], wq[...], 1, 1) + dot(kvg[tok, :], wkv[...], 1, 1)
        out[(i // 2) * rows : (i // 2 + 1) * rows, :] = o.astype(out.dtype)


def key_side_kernel(g, p, hp, *refs):
    parts = refs[:p]
    val, feat, sig, om, qg, wq, wkv = refs[p : p + 7]
    odd, kvg = refs[p + 7 :]
    hd, m = om.shape[1], om.shape[2]
    base = hp * m
    cols = hp * hd
    tail = summed(parts, base, parts[0].shape[0])
    for h in range(hp):
        gh = summed(parts, h * m, (h + 1) * m).astype(BF16)
        col = slice(h * hd, (h + 1) * hd)
        fg = dot(val[:, col], gh, 1, 1) + get_total(tail, base // hd, h, m)
        kvg[:, cols + h * hd : cols + (h + 1) * hd] = dot(feat[:, h * m : (h + 1) * m], gh).astype(BF16)
        pg = (fg * sig[:, h * m : (h + 1) * m]).astype(BF16)
        kvg[:, col] = dot(pg, om[h], 1, 1).astype(BF16)
    products(g, 1, qg, kvg, wq, wkv, odd)


def even_kernel(g, qg, kvg, wq, wkv, even):
    products(g, 0, qg, kvg, wq, wkv, even)


def local(events, offsets, cotangent, query_weight, key_weight, value_weight, omega):
    heads, hd, m = omega.shape
    n_seq, n_sub = lax.axis_size("seq"), lax.axis_size("sub")
    rows, width = events.shape
    loss_scale = math.sqrt(rows * n_seq * n_sub)
    g = math.gcd(heads, n_seq)
    r = n_seq // g
    hp = heads // g
    p = r * n_sub
    t = g * rows
    cols = hp * hd
    srows = hp * m + -(-2 * hp * m // hd // 16) * 16

    def over_seq(x, k):
        return lax.ppermute(x, "seq", [(i, i ^ k) for i in range(n_seq)])

    def over_sub(x, k):
        return lax.ppermute(x, "sub", [(i, i ^ k) for i in range(n_sub)])

    def to_all(own, send):
        parts = [own]
        for j in range(r):
            for k in range(n_sub):
                if j or k:
                    perm = [
                        (a * n_sub + b, (a ^ (j * g)) * n_sub + (b ^ k))
                        for a in range(n_seq)
                        for b in range(n_sub)
                    ]
                    parts.append(lax.ppermute(send, ("seq", "sub"), perm))
        return parts

    kv, q = call(
        functools.partial(weight_kernel, g, cols),
        [((key_weight.shape[0], 2 * cols), BF16), ((key_weight.shape[0], cols), BF16)],
        [key_weight, value_weight, query_weight],
        0,
        in_specs=[ANY] * 3,
        scratch_shapes=[pltpu.SemaphoreType.DMA((3,))],
    )
    kvs = [kv] + [over_sub(kv, k) for k in range(1, n_sub)]

    half = width // 2
    frequency = jnp.exp(jnp.arange(half, dtype=F32) * (-2.0 * math.log(10000.0) / width))
    angles = offsets.astype(F32)[:, None] * frequency[None, :]
    bufs = call(
        functools.partial(input_kernel, g, 2 * cols),
        [((rows, width + 2 * cols), BF16)] * (g // 2),
        [events, jnp.sin(angles), jnp.cos(angles), cotangent],
        0,
    )
    xs = [bufs[0]] * g
    for k in range(2, g, 2):
        xs[k] = over_seq(bufs[k // 2], k)
    for k in range(1, g, 2):
        xs[k] = over_seq(xs[k ^ 1], 1)
    qs = [q] + [over_sub(q, k) for k in range(1, n_sub)]
    om = lax.dynamic_slice_in_dim(omega, (lax.axis_index("seq") % g) * hp, hp, 0)

    flop = 2 * t * width * cols
    summary_out = [((srows, hd), F32), ((srows, hd), BF16)]
    wkv_full, key_feat, key_sig, val, own, send = call(
        functools.partial(key_value_kernel, g, n_sub, hp, width),
        [((width, 2 * cols), BF16), ((t, hp * m), BF16), ((t, hp * m), F32), ((t, cols), BF16)] + summary_out,
        [*xs, *kvs, om],
        8 * flop,
    )
    summary = to_all(own, send)
    wq_full, query_feat, query_sig = call(
        functools.partial(query_kernel, g, n_sub, hp, width),
        [((width, cols), BF16), ((t, hp * m), BF16), ((t, hp * m), F32)],
        [*xs, *qs, om],
        8 * flop,
    )
    total_half, summary_half, scaled_half, norm, own, send = call(
        functools.partial(query_side_kernel, g, p, hp, m, width, loss_scale),
        [((1, hp * m), BF16), ((hp * m, hd), BF16), ((t, cols), BF16), ((t, hp), F32)] + summary_out,
        [*summary, *xs, query_feat],
        8 * flop,
    )
    summary_grad = to_all(own, send)
    (query_grad,) = call(
        functools.partial(query_grad_kernel, hp),
        [((t, cols), BF16)],
        [scaled_half, summary_half, norm, total_half, query_sig, om],
        4 * flop,
    )
    odd, key_value_grad = call(
        functools.partial(key_side_kernel, g, p, hp),
        [((t // 2, width), BF16), ((t, 2 * cols), BF16)],
        [*summary_grad, val, key_feat, key_sig, om, query_grad, wq_full, wkv_full],
        8 * flop,
    )
    got = over_seq(odd, 1)
    (even,) = call(
        functools.partial(even_kernel, g),
        [((t // 2, width), F32)],
        [query_grad, key_value_grad, wq_full, wkv_full],
        8 * flop,
    )
    both = even + got.astype(F32)
    out = both[:rows]
    for k in range(2, g, 2):
        at = (k // 2) * rows
        out = out + over_seq(both[at : at + rows].astype(BF16), k).astype(F32)
    return out.astype(BF16)


def solution(mesh):
    in_specs = (
        P(("grp", "seq", "sub"), None),
        P(("grp", "seq", "sub")),
        P(("grp", "seq", "sub"), None),
        P("sub", None),
        P("sub", None),
        P("sub", None),
        P(),
    )
    out_specs = P(("grp", "seq", "sub"), None)
    return jax.shard_map(local, mesh=mesh, in_specs=in_specs, out_specs=out_specs, check_vma=False)
```

time: 87.7 us -> 92.9 us (1.059)
  waiting for transfers between devices: 27.8 us -> 55.5 us
  starting transfers between devices: 43.1 us -> 24.9 us
  Pallas kernels: 9.79 us -> 7.71 us
  local copies, waits for them, and re-layouts: 4.53 us -> 2.65 us
    ppermute x9 -> x6, waiting for transfers between devices: 6.03 us -> 24.6 us  [over_sub(): return lax.ppermute(x, 'sub', [(i, i ^ k) for i in range(n_sub)])]
    ppermute x12 -> x6, starting transfers between devices: 17.2 us -> 8.91 us  [to_all(): parts.append(lax.ppermute(send, ('seq', 'sub'), perm))]
    ppermute x9 -> x6, starting transfers between devices: 19.1 us -> 11.3 us  [over_sub(): return lax.ppermute(x, 'sub', [(i, i ^ k) for i in range(n_sub)])]
    ppermute x8 -> x5, waiting for transfers between devices: 11.3 us -> 16.7 us  [over_seq(): return lax.ppermute(x, 'seq', [(i, i ^ k) for i in range(n_seq)])]
    ppermute x12 -> x6, waiting for transfers between devices: 10.5 us -> 14.2 us  [to_all(): parts.append(lax.ppermute(send, ('seq', 'sub'), perm))]
    dynamic_slice x5 -> x1, local copies, waits for them, and re-layouts: 2.8 us -> 0.01 us  [local(): om = lax.dynamic_slice_in_dim(omega, lax.axis_index('seq') % g * hp, hp, 0)]
    ppermute x8 -> x5, starting transfers between devices: 6.76 us -> 4.66 us  [over_seq(): return lax.ppermute(x, 'seq', [(i, i ^ k) for i in range(n_seq)])]
    pallas_call x7 -> x8, Pallas kernels: 9.79 us -> 7.71 us  [call(): pl.pallas_call(body, out_shape=[jax.ShapeDtypeStruct(s, d) for s, d in ou...]
  transfers between devices with their start and end apart: 29 -> 17, of which waited for: 11 -> 9; matrix products, arithmetic and copies ran while one was open for 3% -> 0% of each run, Pallas kernels for 7% -> 6%
where the time goes in v2:
time: 92.9 us; the launch traced here: 92.8 us
  waiting for transfers between devices  55.5 us (60%)
  starting transfers between devices  24.9 us (27%)
  Pallas kernels  7.71 us (8%)
  local copies, waits for them, and re-layouts  2.65 us (3%)
  other arithmetic  1.89 us (2%)
    ppermute x6, waiting for transfers between devices, over_sub(): return lax.ppermute(x, 'sub', [(i, i ^ k) for i in range(n_sub)])  24.6 us
    ppermute x5, waiting for transfers between devices, over_seq(): return lax.ppermute(x, 'seq', [(i, i ^ k) for i in range(n_seq)])  16.7 us
    ppermute x6, waiting for transfers between devices, to_all(): parts.append(lax.ppermute(send, ('seq', 'sub'), perm))  14.2 us
    ppermute x6, starting transfers between devices, over_sub(): return lax.ppermute(x, 'sub', [(i, i ^ k) for i in range(n_sub)])  11.3 us
    ppermute x6, starting transfers between devices, to_all(): parts.append(lax.ppermute(send, ('seq', 'sub'), perm))  8.91 us
    pallas_call x8, Pallas kernels, call(): pl.pallas_call(body, out_shape=[jax.ShapeDtypeStruct(s, d) for s, d in ou...  7.71 us
    ppermute x5, starting transfers between devices, over_seq(): return lax.ppermute(x, 'seq', [(i, i ^ k) for i in range(n_seq)])  4.66 us
    unnamed x14, local copies, waits for them, and re-layouts  2.61 us
  transfers between devices with their start and end apart: 17, of which 9 were waited for; matrix products, arithmetic and copies ran while one was open for 0% of the time, Pallas kernels for 6%

profile of v2, /device:TPU:0, one launch (start us, length us, event | category | flops | bytes accessed | tf_op | source)
XLA Modules:
  0.0 92.8 jit_solution(2859387316197757766)
XLA Ops:
  0.7 1.0 %multiply_cosine_fusion = (f32[128,512]{1,0:T(8,128)S(1)}, f32[128,512]{1,0:T(8,128)S(1)}) fusion(f32[512]{0:T(512)S(1)} %multiply_exponential_fusion, f32[128]{0:T(128)S(1)} %convert_element_type.13), kind=kLoop, calls=%fused_computation.4 | loop fusion | flops 65536 | bytes 526848 | tf_op jit(solution)/shard_map/cos | solution.py:269
  1.7 0.9 %copy-done.4 = bf16[128,1024]{1,0:T(8,128)(2,1)S(1)} copy-done((bf16[128,1024]{1,0:T(8,128)(2,1)S(1)}, bf16[128,1024]{1,0:T(8,128)(2,1)}, u32[]{:S(2)}) %copy-start.4) | copy-done | bytes 262168
  2.7 0.9 %copy-done.5 = bf16[128,1024]{1,0:T(8,128)(2,1)S(1)} copy-done((bf16[128,1024]{1,0:T(8,128)(2,1)S(1)}, bf16[128,1024]{1,0:T(8,128)(2,1)}, u32[]{:S(2)}) %copy-start.5) | copy-done | bytes 262168
  3.7 3.0 %collective-permute-start.1 = (bf16[128,1536]{1,0:T(8,128)(2,1)S(1)}, bf16[128,1536]{1,0:T(8,128)(2,1)S(1)}, u32[]{:S(2)}, u32[]{:S(2)}) collective-permute-start(bf16[128,1536]{1,0:T(8,128)(2,1)S(1)} %get-tuple-element.27), channel_id=1, source_target_pairs={{0,8},{4,12},{8,0},{12,4},{1,9},{5,13},{9,1},{13,5},{2,10},{6,14},... | collective-permute-start | bytes 1179656 | tf_op jit(solution)/shard_map/ppermute | solution.py:235
  6.7 9.1 %collective-permute-done.1.refs_2_.refs_6_ = bf16[128,1536]{1,0:T(8,128)(2,1)S(1)} collective-permute-done((bf16[128,1536]{1,0:T(8,128)(2,1)S(1)}, bf16[128,1536]{1,0:T(8,128)(2,1)S(1)}, u32[]{:S(2)}, u32[]{:S(2)}) %collective-permute-start.1) | collective-permute-done | bytes 393248 | tf_op jit(solution)/shard_map/ppermute | solution.py:235
  15.9 3.9 %collective-permute-start.5 = (bf16[256,512]{1,0:T(8,128)(2,1)S(1)}, bf16[256,512]{1,0:T(8,128)(2,1)S(1)}, u32[]{:S(2)}, u32[]{:S(2)}) collective-permute-start(bf16[256,512]{1,0:T(8,128)(2,1)S(1)} %get-tuple-element.28.refs_4_), channel_id=1, source_target_pairs={{0,3},{1,2},{2,1},{3,0},{4,7},{5,6},{6,5},{7,4},{8,11},{9,10},{10,... | collective-permute-start | bytes 786440 | tf_op jit(solution)/shard_map/ppermute | solution.py:238
  20.5 6.6 %collective-permute-done.5.refs_7_ = bf16[256,512]{1,0:T(8,128)(2,1)S(1)} collective-permute-done((bf16[256,512]{1,0:T(8,128)(2,1)S(1)}, bf16[256,512]{1,0:T(8,128)(2,1)S(1)}, u32[]{:S(2)}, u32[]{:S(2)}) %collective-permute-start.5) | collective-permute-done | bytes 262176 | tf_op jit(solution)/shard_map/ppermute | solution.py:238
  27.2 3.7 %collective-permute-start.11 = (bf16[256,256]{1,0:T(8,128)(2,1)S(1)}, bf16[256,256]{1,0:T(8,128)(2,1)S(1)}, u32[]{:S(2)}, u32[]{:S(2)}) collective-permute-start(bf16[256,256]{1,0:T(8,128)(2,1)S(1)} %get-tuple-element.31.refs_4_), channel_id=1, source_target_pairs={{0,3},{1,2},{2,1},{3,0},{4,7},{5,6},{6,5},{7,4},{8,11},{9,10},{10,... | collective-permute-start | bytes 393224 | tf_op jit(solution)/shard_map/ppermute | solution.py:238
  30.9 15.1 %collective-permute-done.4.refs_6_ = bf16[256,512]{1,0:T(8,128)(2,1)S(1)} collective-permute-done((bf16[256,512]{1,0:T(8,128)(2,1)S(1)}, bf16[256,512]{1,0:T(8,128)(2,1)S(1)}, u32[]{:S(2)}, u32[]{:S(2)}) %collective-permute-start.4) | collective-permute-done | bytes 262176 | tf_op jit(solution)/shard_map/ppermute | solution.py:238
  46.0 3.0 %collective-permute-start.9 = (bf16[256,256]{1,0:T(8,128)(2,1)S(1)}, bf16[256,256]{1,0:T(8,128)(2,1)S(1)}, u32[]{:S(2)}, u32[]{:S(2)}) collective-permute-start(bf16[256,256]{1,0:T(8,128)(2,1)S(1)} %get-tuple-element.31.refs_4_), channel_id=1, source_target_pairs={{0,1},{1,0},{2,3},{3,2},{4,5},{5,4},{6,7},{7,6},{8,9},{9,8},{10,11... | collective-permute-start | bytes 393224 | tf_op jit(solution)/shard_map/ppermute | solution.py:238
  49.1 2.0 %shard_map.75 = (bf16[1024,512]{1,0:T(8,128)(2,1)S(1)}, bf16[512,512]{1,0:T(8,128)(2,1)S(1)}, f32[512,512]{1,0:T(8,128)S(1)}, bf16[512,256]{1,0:T(8,128)(2,1)S(1...) custom-call(bf16[128,1536]{1,0:T(8,128)(2,1)S(1)} %get-tuple-element.26.refs_0_.refs_4_, ...), custom_call_target="tpu_custom_call" | custom-call | flops 2147483648 | bytes 2752512 | tf_op jit(solution)/shard_map/pallas_call | solution.py:30
  51.1 1.4 %collective-permute-start.8 = (bf16[528,128]{1,0:T(8,128)(2,1)S(1)}, bf16[528,128]{1,0:T(8,128)(2,1)S(1)}, u32[]{:S(2)}, u32[]{:S(2)}) collective-permute-start(bf16[528,128]{1,0:T(8,128)(2,1)S(1)} %get-tuple-element.30), channel_id=1, source_target_pairs={{0,3},{1,2},{2,1},{3,0},{4,7},{5,6},{6,5},{7,4},{8,11},{9,10},{10,... | collective-permute-start | bytes 405512 | tf_op jit(solution)/shard_map/ppermute | solution.py:250
  52.7 2.9 %collective-permute-start.6 = (bf16[528,128]{1,0:T(8,128)(2,1)S(1)}, bf16[528,128]{1,0:T(8,128)(2,1)S(1)}, u32[]{:S(2)}, u32[]{:S(2)}) collective-permute-start(bf16[528,128]{1,0:T(8,128)(2,1)S(1)} %get-tuple-element.30), channel_id=1, source_target_pairs={{0,1},{1,0},{2,3},{3,2},{4,5},{5,4},{6,7},{7,6},{8,9},{9,8},{10,11... | collective-permute-start | bytes 405512 | tf_op jit(solution)/shard_map/ppermute | solution.py:250
  55.6 2.8 %collective-permute-done.10.refs_6_ = bf16[256,256]{1,0:T(8,128)(2,1)S(1)} collective-permute-done((bf16[256,256]{1,0:T(8,128)(2,1)S(1)}, bf16[256,256]{1,0:T(8,128)(2,1)S(1)}, u32[]{:S(2)}, u32[]{:S(2)}) %collective-permute-start.10) | collective-permute-done | bytes 131104 | tf_op jit(solution)/shard_map/ppermute | solution.py:238
  58.3 1.4 %shard_map.76 = (bf16[1024,256]{1,0:T(8,128)(2,1)S(1)}, bf16[512,512]{1,0:T(8,128)(2,1)S(1)}, f32[512,512]{1,0:T(8,128)S(1)}) custom-call(bf16[128,1536]{1,0:T(8,128)(2,1)S(1)} %get-tuple-element.26.refs_0_.refs_4_, bf16[128,1536]{1,0:T(8,128)(2,1)S(1)} %collective-permute-done.refs_1_.refs_5_, bf16[128,1536]{1,0:T(8,128)(2,1)S(1)} %collective-permute-done.1.refs_2_.refs_6_, ...), custom_call_target="tpu_custom_call" | custom-call | flops 2147483648 | bytes 2228224 | tf_op jit(solution)/shard_map/pallas_call | solution.py:30
  59.8 6.1 %collective-permute-done.7.refs_2_ = bf16[528,128]{1,0:T(8,128)(2,1)S(1)} collective-permute-done((bf16[528,128]{1,0:T(8,128)(2,1)S(1)}, bf16[528,128]{1,0:T(8,128)(2,1)S(1)}, u32[]{:S(2)}, u32[]{:S(2)}) %collective-permute-start.7) | collective-permute-done | bytes 135200 | tf_op jit(solution)/shard_map/ppermute | solution.py:250
  66.8 2.3 %collective-permute-start.14 = (bf16[528,128]{1,0:T(8,128)(2,1)S(1)}, bf16[528,128]{1,0:T(8,128)(2,1)S(1)}, u32[]{:S(2)}, u32[]{:S(2)}) collective-permute-start(bf16[528,128]{1,0:T(8,128)(2,1)S(1)} %get-tuple-element.39), channel_id=1, source_target_pairs={{0,3},{1,2},{2,1},{3,0},{4,7},{5,6},{6,5},{7,4},{8,11},{9,10},{10,... | collective-permute-start | bytes 405512 | tf_op jit(solution)/shard_map/ppermute | solution.py:250
  69.1 2.2 %collective-permute-start.12 = (bf16[528,128]{1,0:T(8,128)(2,1)S(1)}, bf16[528,128]{1,0:T(8,128)(2,1)S(1)}, u32[]{:S(2)}, u32[]{:S(2)}) collective-permute-start(bf16[528,128]{1,0:T(8,128)(2,1)S(1)} %get-tuple-element.39), channel_id=1, source_target_pairs={{0,1},{1,0},{2,3},{3,2},{4,5},{5,4},{6,7},{7,6},{8,9},{9,8},{10,11... | collective-permute-start | bytes 405512 | tf_op jit(solution)/shard_map/ppermute | solution.py:250
  71.8 3.5 %collective-permute-done.14.refs_3_ = bf16[528,128]{1,0:T(8,128)(2,1)S(1)} collective-permute-done((bf16[528,128]{1,0:T(8,128)(2,1)S(1)}, bf16[528,128]{1,0:T(8,128)(2,1)S(1)}, u32[]{:S(2)}, u32[]{:S(2)}) %collective-permute-start.14) | collective-permute-done | bytes 135200 | tf_op jit(solution)/shard_map/ppermute | solution.py:250
  75.2 4.6 %collective-permute-done.13.refs_2_ = bf16[528,128]{1,0:T(8,128)(2,1)S(1)} collective-permute-done((bf16[528,128]{1,0:T(8,128)(2,1)S(1)}, bf16[528,128]{1,0:T(8,128)(2,1)S(1)}, u32[]{:S(2)}, u32[]{:S(2)}) %collective-permute-start.13) | collective-permute-done | bytes 135200 | tf_op jit(solution)/shard_map/ppermute | solution.py:250
  79.8 1.6 %shard_map.79 = (bf16[256,1024]{1,0:T(8,128)(2,1)S(1)}, bf16[512,512]{1,0:T(8,128)(2,1)S(1)}) custom-call(f32[528,128]{1,0:T(8,128)S(1)} %get-tuple-element.38.refs_0_, bf16[528,128]{1,0:T(8,128)(2,1)S(1)} %collective-permute-done.12.refs_1_, bf16[528,128]{1,0:T(8,128)(2,1)S(1)} %collective-permute-done.13.refs_2_, ...), custom_call_target="tpu_custom_call" | custom-call | flops 2147483648 | bytes 4476928 | tf_op jit(solution)/shard_map/pallas_call | solution.py:30
  81.5 1.1 %shard_map.80 = f32[256,1024]{1,0:T(8,128)S(1)} custom-call(bf16[512,256]{1,0:T(8,128)(2,1)S(1)} %shard_map.78.refs_8_.qg, bf16[512,512]{1,0:T(8,128)(2,1)S(1)} %get-tuple-element.45.kvg, bf16[1024,256]{1,0:T(8,128)(2,1)S(1)} %get-tuple-element.43.refs_9_.wq, bf16[1024,512]{1,0:T(8,128)(2,1)S(1)} %get-tuple-element.44.refs_10_.wkv), custom_call_target="tpu_custom_call" | custom-call | flops 2147483648 | bytes 2359296 | tf_op jit(solution)/shard_map/pallas_call | solution.py:30
  83.6 1.6 %collective-permute-start.16 = (bf16[128,1024]{1,0:T(8,128)(2,1)S(1)}, bf16[128,1024]{1,0:T(8,128)(2,1)S(1)}, u32[]{:S(2)}, u32[]{:S(2)}) collective-permute-start(bf16[128,1024]{1,0:T(8,128)(2,1)S(1)} %slice.15), channel_id=1, source_target_pairs={{0,8},{4,12},{8,0},{12,4},{1,9},{5,13},{9,1},{13,5},{2,10},{6,14},... | collective-permute-start | bytes 786440 | tf_op jit(solution)/shard_map/ppermute | solution.py:235
  85.2 6.8 %collective-permute-done.16 = bf16[128,1024]{1,0:T(8,128)(2,1)S(1)} collective-permute-done((bf16[128,1024]{1,0:T(8,128)(2,1)S(1)}, bf16[128,1024]{1,0:T(8,128)(2,1)S(1)}, u32[]{:S(2)}, u32[]{:S(2)}) %collective-permute-start.16) | collective-permute-done | bytes 262176 | tf_op jit(solution)/shard_map/ppermute | solution.py:235
  (39 shorter events, 4.9 us)
Async XLA Ops:
  0.0 20.5 %copy-start = (bf16[8,128,256]{2,1,0:T(8,128)(2,1)S(1)}, bf16[8,128,256]{2,1,0:T(8,128)(2,1)}, u32[]{:S(2)}) copy-start(bf16[8,128,256]{2,1,0:T(8,128)(2,1)} %param.13) | copy-start | bytes 1572868
  0.0 0.7 copy-start.6
  0.7 15.1 %copy-start.3 = (bf16[256,1024]{1,0:T(8,128)(2,1)S(1)}, bf16[256,1024]{1,0:T(8,128)(2,1)}, u32[]{:S(2)}) copy-start(bf16[256,1024]{1,0:T(8,128)(2,1)} %wq.1) | copy-start | bytes 1572868
  1.7 1.0 %copy-start.4 = (bf16[128,1024]{1,0:T(8,128)(2,1)S(1)}, bf16[128,1024]{1,0:T(8,128)(2,1)}, u32[]{:S(2)}) copy-start(bf16[128,1024]{1,0:T(8,128)(2,1)} %events.1) | copy-start | bytes 786436
  2.7 0.9 %copy-start.5 = (bf16[128,1024]{1,0:T(8,128)(2,1)S(1)}, bf16[128,1024]{1,0:T(8,128)(2,1)}, u32[]{:S(2)}) copy-start(bf16[128,1024]{1,0:T(8,128)(2,1)} %cot.1) | copy-start | bytes 786436
  3.6 12.2 %copy-start.1 = (bf16[256,1024]{1,0:T(8,128)(2,1)S(1)}, bf16[256,1024]{1,0:T(8,128)(2,1)}, u32[]{:S(2)}) copy-start(bf16[256,1024]{1,0:T(8,128)(2,1)} %wk.1) | copy-start | bytes 1572868
  3.6 12.2 %copy-start.2 = (bf16[256,1024]{1,0:T(8,128)(2,1)S(1)}, bf16[256,1024]{1,0:T(8,128)(2,1)}, u32[]{:S(2)}) copy-start(bf16[256,1024]{1,0:T(8,128)(2,1)} %wv.1) | copy-start | bytes 1572868
  3.7 12.1 %collective-permute-start.1 = (bf16[128,1536]{1,0:T(8,128)(2,1)S(1)}, bf16[128,1536]{1,0:T(8,128)(2,1)S(1)}, u32[]{:S(2)}, u32[]{:S(2)}) collective-permute-start(bf16[128,1536]{1,0:T(8,128)(2,1)S(1)} %get-tuple-element.27), channel_id=1, source_target_pairs={{0,8},{4,12},{8,0},{12,4},{1,9},{5,13},{9,1},{13,5},{2,10},{6,14},... | collective-permute-start | bytes 1179656 | tf_op jit(solution)/shard_map/ppermute | solution.py:235
  6.7 42.4 %collective-permute-start = (bf16[128,1536]{1,0:T(8,128)(2,1)S(1)}, bf16[128,1536]{1,0:T(8,128)(2,1)S(1)}, u32[]{:S(2)}, u32[]{:S(2)}) collective-permute-start(bf16[128,1536]{1,0:T(8,128)(2,1)S(1)} %get-tuple-element.26.refs_0_.refs_4_), channel_id=1, source_target_pairs={{0,4},{4,0},{8,12},{12,8},{1,5},{5,1},{9,13},{13,9},{2,6},{6,2},{1... | collective-permute-start | bytes 1179656 | tf_op jit(solution)/shard_map/ppermute | solution.py:235
  15.8 33.3 %collective-permute-start.2 = (bf16[128,1536]{1,0:T(8,128)(2,1)S(1)}, bf16[128,1536]{1,0:T(8,128)(2,1)S(1)}, u32[]{:S(2)}, u32[]{:S(2)}) collective-permute-start(bf16[128,1536]{1,0:T(8,128)(2,1)S(1)} %collective-permute-done.1.refs_2_.refs_6_), channel_id=1, source_target_pairs={{0,4},{4,0},{8,12},{12,8},{1,5},{5,1},{9,13},{13,9},{2,6},{6,2},{1... | collective-permute-start | bytes 1179656 | tf_op jit(solution)/shard_map/ppermute | solution.py:235
  15.9 11.2 %collective-permute-start.5 = (bf16[256,512]{1,0:T(8,128)(2,1)S(1)}, bf16[256,512]{1,0:T(8,128)(2,1)S(1)}, u32[]{:S(2)}, u32[]{:S(2)}) collective-permute-start(bf16[256,512]{1,0:T(8,128)(2,1)S(1)} %get-tuple-element.28.refs_4_), channel_id=1, source_target_pairs={{0,3},{1,2},{2,1},{3,0},{4,7},{5,6},{6,5},{7,4},{8,11},{9,10},{10,... | collective-permute-start | bytes 786440 | tf_op jit(solution)/shard_map/ppermute | solution.py:238
  19.9 26.2 %collective-permute-start.4 = (bf16[256,512]{1,0:T(8,128)(2,1)S(1)}, bf16[256,512]{1,0:T(8,128)(2,1)S(1)}, u32[]{:S(2)}, u32[]{:S(2)}) collective-permute-start(bf16[256,512]{1,0:T(8,128)(2,1)S(1)} %get-tuple-element.28.refs_4_), channel_id=1, source_target_pairs={{0,2},{1,3},{2,0},{3,1},{4,6},{5,7},{6,4},{7,5},{8,10},{9,11},{10,... | collective-permute-start | bytes 786440 | tf_op jit(solution)/shard_map/ppermute | solution.py:238
  19.9 26.2 %collective-permute-start.3 = (bf16[256,512]{1,0:T(8,128)(2,1)S(1)}, bf16[256,512]{1,0:T(8,128)(2,1)S(1)}, u32[]{:S(2)}, u32[]{:S(2)}) collective-permute-start(bf16[256,512]{1,0:T(8,128)(2,1)S(1)} %get-tuple-element.28.refs_4_), channel_id=1, source_target_pairs={{0,1},{1,0},{2,3},{3,2},{4,5},{5,4},{6,7},{7,6},{8,9},{9,8},{10,11... | collective-permute-start | bytes 786440 | tf_op jit(solution)/shard_map/ppermute | solution.py:238
  27.2 25.5 %collective-permute-start.11 = (bf16[256,256]{1,0:T(8,128)(2,1)S(1)}, bf16[256,256]{1,0:T(8,128)(2,1)S(1)}, u32[]{:S(2)}, u32[]{:S(2)}) collective-permute-start(bf16[256,256]{1,0:T(8,128)(2,1)S(1)} %get-tuple-element.31.refs_4_), channel_id=1, source_target_pairs={{0,3},{1,2},{2,1},{3,0},{4,7},{5,6},{6,5},{7,4},{8,11},{9,10},{10,... | collective-permute-start | bytes 393224 | tf_op jit(solution)/shard_map/ppermute | solution.py:238
  46.0 12.3 %collective-permute-start.10 = (bf16[256,256]{1,0:T(8,128)(2,1)S(1)}, bf16[256,256]{1,0:T(8,128)(2,1)S(1)}, u32[]{:S(2)}, u32[]{:S(2)}) collective-permute-start(bf16[256,256]{1,0:T(8,128)(2,1)S(1)} %get-tuple-element.31.refs_4_), channel_id=1, source_target_pairs={{0,2},{1,3},{2,0},{3,1},{4,6},{5,7},{6,4},{7,5},{8,10},{9,11},{10,... | collective-permute-start | bytes 393224 | tf_op jit(solution)/shard_map/ppermute | solution.py:238
  46.0 12.3 %collective-permute-start.9 = (bf16[256,256]{1,0:T(8,128)(2,1)S(1)}, bf16[256,256]{1,0:T(8,128)(2,1)S(1)}, u32[]{:S(2)}, u32[]{:S(2)}) collective-permute-start(bf16[256,256]{1,0:T(8,128)(2,1)S(1)} %get-tuple-element.31.refs_4_), channel_id=1, source_target_pairs={{0,1},{1,0},{2,3},{3,2},{4,5},{5,4},{6,7},{7,6},{8,9},{9,8},{10,11... | collective-permute-start | bytes 393224 | tf_op jit(solution)/shard_map/ppermute | solution.py:238
  51.1 8.7 %collective-permute-start.8 = (bf16[528,128]{1,0:T(8,128)(2,1)S(1)}, bf16[528,128]{1,0:T(8,128)(2,1)S(1)}, u32[]{:S(2)}, u32[]{:S(2)}) collective-permute-start(bf16[528,128]{1,0:T(8,128)(2,1)S(1)} %get-tuple-element.30), channel_id=1, source_target_pairs={{0,3},{1,2},{2,1},{3,0},{4,7},{5,6},{6,5},{7,4},{8,11},{9,10},{10,... | collective-permute-start | bytes 405512 | tf_op jit(solution)/shard_map/ppermute | solution.py:250
  52.5 13.4 %collective-permute-start.7 = (bf16[528,128]{1,0:T(8,128)(2,1)S(1)}, bf16[528,128]{1,0:T(8,128)(2,1)S(1)}, u32[]{:S(2)}, u32[]{:S(2)}) collective-permute-start(bf16[528,128]{1,0:T(8,128)(2,1)S(1)} %get-tuple-element.30), channel_id=1, source_target_pairs={{0,2},{1,3},{2,0},{3,1},{4,6},{5,7},{6,4},{7,5},{8,10},{9,11},{10,... | collective-permute-start | bytes 405512 | tf_op jit(solution)/shard_map/ppermute | solution.py:250
  52.7 13.3 %collective-permute-start.6 = (bf16[528,128]{1,0:T(8,128)(2,1)S(1)}, bf16[528,128]{1,0:T(8,128)(2,1)S(1)}, u32[]{:S(2)}, u32[]{:S(2)}) collective-permute-start(bf16[528,128]{1,0:T(8,128)(2,1)S(1)} %get-tuple-element.30), channel_id=1, source_target_pairs={{0,1},{1,0},{2,3},{3,2},{4,5},{5,4},{6,7},{7,6},{8,9},{9,8},{10,11... | collective-permute-start | bytes 405512 | tf_op jit(solution)/shard_map/ppermute | solution.py:250
  66.8 8.4 %collective-permute-start.14 = (bf16[528,128]{1,0:T(8,128)(2,1)S(1)}, bf16[528,128]{1,0:T(8,128)(2,1)S(1)}, u32[]{:S(2)}, u32[]{:S(2)}) collective-permute-start(bf16[528,128]{1,0:T(8,128)(2,1)S(1)} %get-tuple-element.39), channel_id=1, source_target_pairs={{0,3},{1,2},{2,1},{3,0},{4,7},{5,6},{6,5},{7,4},{8,11},{9,10},{10,... | collective-permute-start | bytes 405512 | tf_op jit(solution)/shard_map/ppermute | solution.py:250
  69.1 10.8 %collective-permute-start.13 = (bf16[528,128]{1,0:T(8,128)(2,1)S(1)}, bf16[528,128]{1,0:T(8,128)(2,1)S(1)}, u32[]{:S(2)}, u32[]{:S(2)}) collective-permute-start(bf16[528,128]{1,0:T(8,128)(2,1)S(1)} %get-tuple-element.39), channel_id=1, source_target_pairs={{0,2},{1,3},{2,0},{3,1},{4,6},{5,7},{6,4},{7,5},{8,10},{9,11},{10,... | collective-permute-start | bytes 405512 | tf_op jit(solution)/shard_map/ppermute | solution.py:250
  69.1 10.8 %collective-permute-start.12 = (bf16[528,128]{1,0:T(8,128)(2,1)S(1)}, bf16[528,128]{1,0:T(8,128)(2,1)S(1)}, u32[]{:S(2)}, u32[]{:S(2)}) collective-permute-start(bf16[528,128]{1,0:T(8,128)(2,1)S(1)} %get-tuple-element.39), channel_id=1, source_target_pairs={{0,1},{1,0},{2,3},{3,2},{4,5},{5,4},{6,7},{7,6},{8,9},{9,8},{10,11... | collective-permute-start | bytes 405512 | tf_op jit(solution)/shard_map/ppermute | solution.py:250
  81.4 2.0 %collective-permute-start.15 = (bf16[256,1024]{1,0:T(8,128)(2,1)S(1)}, bf16[256,1024]{1,0:T(8,128)(2,1)S(1)}, u32[]{:S(2)}, u32[]{:S(2)}) collective-permute-start(bf16[256,1024]{1,0:T(8,128)(2,1)S(1)} %get-tuple-element.46), channel_id=1, source_target_pairs={{0,4},{4,0},{8,12},{12,8},{1,5},{5,1},{9,13},{13,9},{2,6},{6,2},{1... | collective-permute-start | bytes 1572872 | tf_op jit(solution)/shard_map/ppermute | solution.py:235
  83.6 8.4 %collective-permute-start.16 = (bf16[128,1024]{1,0:T(8,128)(2,1)S(1)}, bf16[128,1024]{1,0:T(8,128)(2,1)S(1)}, u32[]{:S(2)}, u32[]{:S(2)}) collective-permute-start(bf16[128,1024]{1,0:T(8,128)(2,1)S(1)} %slice.15), channel_id=1, source_target_pairs={{0,8},{4,12},{8,0},{12,4},{1,9},{5,13},{9,1},{13,5},{2,10},{6,14},... | collective-permute-start | bytes 786440 | tf_op jit(solution)/shard_map/ppermute | solution.py:235

commit v3 on v2

--- a/solution.py
+++ b/solution.py
@@ -10,7 +10,7 @@
 
 F32 = jnp.float32
 BF16 = jnp.bfloat16
-ANY = pl.BlockSpec(memory_space=pl.ANY)
+HBM = pl.BlockSpec(memory_space=pltpu.HBM)
 
 
 def dot(a, b, ca=1, cb=0):
@@ -36,13 +36,18 @@
     )(*args)
 
 
-def weight_kernel(g, cols, wk, wv, wq, kv, q, sems):
+def weight_kernel(g, cols, split, wk, wv, wq, *refs):
+    outs, sems = refs[:-1], refs[-1]
     at = pl.ds(pl.multiple_of((lax.axis_index("seq") % g) * cols, cols), cols)
-    copies = [
-        pltpu.make_async_copy(wk.at[:, at], kv.at[:, :cols], sems.at[0]),
-        pltpu.make_async_copy(wv.at[:, at], kv.at[:, cols:], sems.at[1]),
-        pltpu.make_async_copy(wq.at[:, at], q, sems.at[2]),
-    ]
+    pairs = [(wk.at[:, at], outs[0].at[:, :cols]), (wv.at[:, at], outs[0].at[:, cols:]), (wq.at[:, at], outs[1])]
+    if split:
+        half = wk.shape[0] // 2
+        rows = pl.ds(pl.multiple_of(lax.axis_index("grp") * half, half), half)
+        pairs += [
+            (wk.at[rows, at], outs[2].at[:, :cols]),
+            (wv.at[rows, at], outs[2].at[:, cols:]),
+        ]
+    copies = [pltpu.make_async_copy(a, b, sems.at[i]) for i, (a, b) in enumerate(pairs)]
     for c in copies:
         c.start()
     for c in copies:
@@ -61,11 +66,18 @@
         out[:, width:] = cot[:, pl.ds(pl.multiple_of((mine ^ k) * pair, pair), pair)]
 
 
-def place_rows(full, parts):
+def place_rows(full, parts, n):
     z = lax.axis_index("sub")
     rows = parts[0].shape[0]
-    for k, part in enumerate(parts):
-        full[pl.ds(pl.multiple_of((z ^ k) * rows, rows), rows), :] = part[...]
+    spots = [(k, 0) for k in range(n)]
+    if len(parts) > n:
+        half, mine = rows // 2, lax.axis_index("grp")
+        spots = [(0, 0), (1, 0)]
+        for k in range(2, n):
+            spots += [(k, mine * half), (k, half - mine * half)]
+    for (k, start), part in zip(spots, parts):
+        size = part.shape[0]
+        full[pl.ds(pl.multiple_of((z ^ k) * rows + start, size), size), :] = part[...]
 
 
 def features(act, om, h, i, feat, sig):
@@ -108,12 +120,12 @@
     return out
 
 
-def key_value_kernel(g, n, hp, width, *refs):
-    xs, ws, om = refs[:g], refs[g : g + n], refs[g + n]
-    w_full, feat, sig, val, own, send = refs[g + n + 1 :]
+def key_value_kernel(g, n, nw, hp, width, *refs):
+    xs, ws, om = refs[:g], refs[g : g + nw], refs[g + nw]
+    w_full, feat, sig, val, own, send = refs[g + nw + 1 :]
     hd, m = om.shape[1], om.shape[2]
     cols = hp * hd
-    place_rows(w_full, ws)
+    place_rows(w_full, ws, n)
     rows = xs[0].shape[0]
     sums = [jnp.zeros((1, m), F32) for _ in range(hp)]
     for i, x in enumerate(xs):
@@ -132,10 +144,10 @@
     put_total(own, send, base, hp * m // hd, jnp.concatenate(sums, axis=1))
 
 
-def query_kernel(g, n, hp, width, *refs):
-    xs, ws, om = refs[:g], refs[g : g + n], refs[g + n]
-    w_full, feat, sig = refs[g + n + 1 :]
-    place_rows(w_full, ws)
+def query_kernel(g, n, nw, hp, width, *refs):
+    xs, ws, om = refs[:g], refs[g : g + nw], refs[g + nw]
+    w_full, feat, sig = refs[g + nw + 1 :]
+    place_rows(w_full, ws, n)
     for i, x in enumerate(xs):
         act = dot(x[:, :width], w_full[...]).astype(BF16)
         for h in range(hp):
@@ -250,16 +262,32 @@
                     parts.append(lax.ppermute(send, ("seq", "sub"), perm))
         return parts
 
-    kv, q = call(
-        functools.partial(weight_kernel, g, cols),
-        [((key_weight.shape[0], 2 * cols), BF16), ((key_weight.shape[0], cols), BF16)],
+    wrows = key_weight.shape[0]
+    split = lax.axis_size("grp") == 2 and wrows % 32 == 0
+    wouts = [((wrows, 2 * cols), BF16), ((wrows, cols), BF16)]
+    if split:
+        wouts.append(((wrows // 2, 2 * cols), BF16))
+    pieces = list(call(
+        functools.partial(weight_kernel, g, cols, split),
+        wouts,
         [key_weight, value_weight, query_weight],
         0,
-        in_specs=[ANY] * 3,
-        scratch_shapes=[pltpu.SemaphoreType.DMA((3,))],
-    )
-    kvs = [kv] + [over_sub(kv, k) for k in range(1, n_sub)]
-
+        in_specs=[HBM] * 3,
+        scratch_shapes=[pltpu.SemaphoreType.DMA((5 if split else 3,))],
+    ))
+
+    def weight_rows(i, split):
+        if not split:
+            return [pieces[i]] + [over_sub(pieces[i], k) for k in range(1, n_sub)]
+        far = []
+        for k in range(2, n_sub):
+            part = over_sub(pieces[i + 2], k)
+            far += [part, lax.ppermute(part, "grp", [(0, 1), (1, 0)])]
+        return [pieces[i], over_sub(pieces[i], 1)] + far
+
+    kvs = weight_rows(0, split)
+
+    events, offsets, _ = lax.optimization_barrier((events, offsets, pieces[0]))
     half = width // 2
     frequency = jnp.exp(jnp.arange(half, dtype=F32) * (-2.0 * math.log(10000.0) / width))
     angles = offsets.astype(F32)[:, None] * frequency[None, :]
@@ -267,27 +295,31 @@
         functools.partial(input_kernel, g, 2 * cols),
         [((rows, width + 2 * cols), BF16)] * (g // 2),
         [events, jnp.sin(angles), jnp.cos(angles), cotangent],
-        0,
+        16 * 2**30,
     )
     xs = [bufs[0]] * g
     for k in range(2, g, 2):
         xs[k] = over_seq(bufs[k // 2], k)
-    for k in range(1, g, 2):
+    xs[1] = over_seq(bufs[0], 1)
+    arrived = kvs[1:2] + kvs[2::2] if split else kvs[1:]
+    xs[2:], _ = lax.optimization_barrier((xs[2:], arrived[1:]))
+    for k in range(3, g, 2):
         xs[k] = over_seq(xs[k ^ 1], 1)
-    qs = [q] + [over_sub(q, k) for k in range(1, n_sub)]
+    pieces, _ = lax.optimization_barrier((pieces, arrived + xs[1:2]))
+    qs = weight_rows(1, False)
     om = lax.dynamic_slice_in_dim(omega, (lax.axis_index("seq") % g) * hp, hp, 0)
 
     flop = 2 * t * width * cols
     summary_out = [((srows, hd), F32), ((srows, hd), BF16)]
     wkv_full, key_feat, key_sig, val, own, send = call(
-        functools.partial(key_value_kernel, g, n_sub, hp, width),
+        functools.partial(key_value_kernel, g, n_sub, len(kvs), hp, width),
         [((width, 2 * cols), BF16), ((t, hp * m), BF16), ((t, hp * m), F32), ((t, cols), BF16)] + summary_out,
         [*xs, *kvs, om],
         8 * flop,
     )
     summary = to_all(own, send)
     wq_full, query_feat, query_sig = call(
-        functools.partial(query_kernel, g, n_sub, hp, width),
+        functools.partial(query_kernel, g, n_sub, len(qs), hp, width),
         [((width, cols), BF16), ((t, hp * m), BF16), ((t, hp * m), F32)],
         [*xs, *qs, om],
         8 * flop,

time: 92.9 us -> 83.2 us (0.90)
  waiting for transfers between devices: 55.5 us -> 45.4 us
  local copies, waits for them, and re-layouts: 2.65 us -> 3.9 us
  starting transfers between devices: 24.9 us -> 23.9 us
    ppermute x5, waiting for transfers between devices: 16.7 us -> 8.58 us  [over_seq(): return lax.ppermute(x, 'seq', [(i, i ^ k) for i in range(n_seq)])]
    ppermute x6, starting transfers between devices: 11.3 us -> 8 us  [over_sub(): return lax.ppermute(x, 'sub', [(i, i ^ k) for i in range(n_sub)])]
    ppermute x6, waiting for transfers between devices: 14.2 us -> 11.5 us  [to_all(): parts.append(lax.ppermute(send, ('seq', 'sub'), perm))]
    ppermute x0 -> x2, starting transfers between devices: none -> 2.09 us  [weight_rows(): far += [part, lax.ppermute(part, 'grp', [(0, 1), (1, 0)])]]
    unnamed x14, local copies, waits for them, and re-layouts: 2.61 us -> 3.86 us
    ppermute x6, starting transfers between devices: 8.91 us -> 10.1 us  [to_all(): parts.append(lax.ppermute(send, ('seq', 'sub'), perm))]
    ppermute x5, starting transfers between devices: 4.66 us -> 3.68 us  [over_seq(): return lax.ppermute(x, 'seq', [(i, i ^ k) for i in range(n_seq)])]
  transfers between devices with their start and end apart: 17 -> 19, of which waited for: 9 -> 9; matrix products, arithmetic and copies ran while one was open for 0% -> 0% of each run, Pallas kernels for 6% -> 6%
where the time goes in v3:
time: 83.2 us; the launch traced here: 82.9 us
  waiting for transfers between devices  45.4 us (55%)
  starting transfers between devices  23.9 us (29%)
  Pallas kernels  7.73 us (9%)
  local copies, waits for them, and re-layouts  3.9 us (5%)
  other arithmetic  1.89 us (2%)
    ppermute x6, waiting for transfers between devices, over_sub(): return lax.ppermute(x, 'sub', [(i, i ^ k) for i in range(n_sub)])  25.4 us
    ppermute x6, waiting for transfers between devices, to_all(): parts.append(lax.ppermute(send, ('seq', 'sub'), perm))  11.5 us
    ppermute x6, starting transfers between devices, to_all(): parts.append(lax.ppermute(send, ('seq', 'sub'), perm))  10.1 us
    ppermute x5, waiting for transfers between devices, over_seq(): return lax.ppermute(x, 'seq', [(i, i ^ k) for i in range(n_seq)])  8.58 us
    ppermute x6, starting transfers between devices, over_sub(): return lax.ppermute(x, 'sub', [(i, i ^ k) for i in range(n_sub)])  8 us
    pallas_call x8, Pallas kernels, call(): pl.pallas_call(body, out_shape=[jax.ShapeDtypeStruct(s, d) for s, d in ou...  7.73 us
    unnamed x14, local copies, waits for them, and re-layouts  3.86 us
    ppermute x5, starting transfers between devices, over_seq(): return lax.ppermute(x, 'seq', [(i, i ^ k) for i in range(n_seq)])  3.68 us
  transfers between devices with their start and end apart: 19, of which 9 were waited for; matrix products, arithmetic and copies ran while one was open for 0% of the time, Pallas kernels for 6%

profile of v3, /device:TPU:0, one launch (start us, length us, event | category | flops | bytes accessed | tf_op | source)
XLA Modules:
  0.0 82.9 jit_solution(10856677060567854844)
XLA Ops:
  0.0 1.1 %copy-done.1 = bf16[256,1024]{1,0:T(8,128)(2,1)S(1)} copy-done((bf16[256,1024]{1,0:T(8,128)(2,1)S(1)}, bf16[256,1024]{1,0:T(8,128)(2,1)}, u32[]{:S(2)}) %copy-start.1) | copy-done | bytes 524312
  1.1 1.0 %copy-done.2 = bf16[256,1024]{1,0:T(8,128)(2,1)S(1)} copy-done((bf16[256,1024]{1,0:T(8,128)(2,1)S(1)}, bf16[256,1024]{1,0:T(8,128)(2,1)}, u32[]{:S(2)}) %copy-start.2) | copy-done | bytes 524312
  2.2 1.0 %copy-done.3 = bf16[256,1024]{1,0:T(8,128)(2,1)S(1)} copy-done((bf16[256,1024]{1,0:T(8,128)(2,1)S(1)}, bf16[256,1024]{1,0:T(8,128)(2,1)}, u32[]{:S(2)}) %copy-start.3) | copy-done | bytes 524312
  5.1 3.0 %collective-permute-start.1 = (bf16[128,1536]{1,0:T(8,128)(2,1)S(1)}, bf16[128,1536]{1,0:T(8,128)(2,1)S(1)}, u32[]{:S(2)}, u32[]{:S(2)}) collective-permute-start(bf16[128,1536]{1,0:T(8,128)(2,1)S(1)} %get-tuple-element.35), channel_id=1, source_target_pairs={{0,8},{4,12},{8,0},{12,4},{1,9},{5,13},{9,1},{13,5},{2,10},{6,14},... | collective-permute-start | bytes 1179656 | tf_op jit(solution)/shard_map/ppermute | solution.py:247
  8.1 3.6 %collective-permute-start.3 = (bf16[128,512]{1,0:T(8,128)(2,1)S(1)}, bf16[128,512]{1,0:T(8,128)(2,1)S(1)}, u32[]{:S(2)}, u32[]{:S(2)}) collective-permute-start(bf16[128,512]{1,0:T(8,128)(2,1)S(1)} %get-tuple-element.36), channel_id=1, source_target_pairs={{0,3},{1,2},{2,1},{3,0},{4,7},{5,6},{6,5},{7,4},{8,11},{9,10},{10,... | collective-permute-start | bytes 393224 | tf_op jit(solution)/shard_map/ppermute | solution.py:250
  11.7 4.7 %collective-permute-done.3.refs_8_ = bf16[128,512]{1,0:T(8,128)(2,1)S(1)} collective-permute-done((bf16[128,512]{1,0:T(8,128)(2,1)S(1)}, bf16[128,512]{1,0:T(8,128)(2,1)S(1)}, u32[]{:S(2)}, u32[]{:S(2)}) %collective-permute-start.3) | collective-permute-done | bytes 131104 | tf_op jit(solution)/shard_map/ppermute | solution.py:250
  16.4 6.1 %collective-permute-done.2.refs_6_ = bf16[128,512]{1,0:T(8,128)(2,1)S(1)} collective-permute-done((bf16[128,512]{1,0:T(8,128)(2,1)S(1)}, bf16[128,512]{1,0:T(8,128)(2,1)S(1)}, u32[]{:S(2)}, u32[]{:S(2)}) %collective-permute-start.2) | collective-permute-done | bytes 131104 | tf_op jit(solution)/shard_map/ppermute | solution.py:250
  22.5 1.6 %collective-permute-start.7 = (bf16[128,512]{1,0:T(8,128)(2,1)S(1)}, bf16[128,512]{1,0:T(8,128)(2,1)S(1)}, u32[]{:S(2)}, u32[]{:S(2)}) collective-permute-start(bf16[128,512]{1,0:T(8,128)(2,1)S(1)} %collective-permute-done.3.refs_8_), channel_id=1, source_target_pairs={{0,16},{16,0},{1,17},{17,1},{2,18},{18,2},{3,19},{19,3},{4,20},{20... | collective-permute-start | bytes 393224 | tf_op jit(solution)/shard_map/ppermute | solution.py:285
  24.6 6.6 %collective-permute-done.5.refs_5_ = bf16[256,512]{1,0:T(8,128)(2,1)S(1)} collective-permute-done((bf16[256,512]{1,0:T(8,128)(2,1)S(1)}, bf16[256,512]{1,0:T(8,128)(2,1)S(1)}, u32[]{:S(2)}, u32[]{:S(2)}) %collective-permute-start.5) | collective-permute-done | bytes 262176 | tf_op jit(solution)/shard_map/ppermute | solution.py:250
  31.2 2.5 %collective-permute-start.13 = (bf16[256,256]{1,0:T(8,128)(2,1)S(1)}, bf16[256,256]{1,0:T(8,128)(2,1)S(1)}, u32[]{:S(2)}, u32[]{:S(2)}) collective-permute-start(bf16[256,256]{1,0:T(8,128)(2,1)S(1)} %get-tuple-element.41.refs_4_), channel_id=1, source_target_pairs={{0,3},{1,2},{2,1},{3,0},{4,7},{5,6},{6,5},{7,4},{8,11},{9,10},{10,... | collective-permute-start | bytes 393224 | tf_op jit(solution)/shard_map/ppermute | solution.py:250
  33.7 1.9 %collective-permute-start.11 = (bf16[256,256]{1,0:T(8,128)(2,1)S(1)}, bf16[256,256]{1,0:T(8,128)(2,1)S(1)}, u32[]{:S(2)}, u32[]{:S(2)}) collective-permute-start(bf16[256,256]{1,0:T(8,128)(2,1)S(1)} %get-tuple-element.41.refs_4_), channel_id=1, source_target_pairs={{0,1},{1,0},{2,3},{3,2},{4,5},{5,4},{6,7},{7,6},{8,9},{9,8},{10,11... | collective-permute-start | bytes 393224 | tf_op jit(solution)/shard_map/ppermute | solution.py:250
  35.6 2.0 %shard_map.75 = (bf16[1024,512]{1,0:T(8,128)(2,1)S(1)}, bf16[512,512]{1,0:T(8,128)(2,1)S(1)}, f32[512,512]{1,0:T(8,128)S(1)}, bf16[512,256]{1,0:T(8,128)(2,1)S(1...) custom-call(bf16[128,1536]{1,0:T(8,128)(2,1)S(1)} %get-tuple-element.34.refs_0_.refs_4_, ...), custom_call_target="tpu_custom_call" | custom-call | flops 2147483648 | bytes 2752512 | tf_op jit(solution)/shard_map/pallas_call | solution.py:30
  37.6 2.5 %collective-permute-start.10 = (bf16[528,128]{1,0:T(8,128)(2,1)S(1)}, bf16[528,128]{1,0:T(8,128)(2,1)S(1)}, u32[]{:S(2)}, u32[]{:S(2)}) collective-permute-start(bf16[528,128]{1,0:T(8,128)(2,1)S(1)} %get-tuple-element.39), channel_id=1, source_target_pairs={{0,3},{1,2},{2,1},{3,0},{4,7},{5,6},{6,5},{7,4},{8,11},{9,10},{10,... | collective-permute-start | bytes 405512 | tf_op jit(solution)/shard_map/ppermute | solution.py:262
  40.2 3.1 %collective-permute-start.8 = (bf16[528,128]{1,0:T(8,128)(2,1)S(1)}, bf16[528,128]{1,0:T(8,128)(2,1)S(1)}, u32[]{:S(2)}, u32[]{:S(2)}) collective-permute-start(bf16[528,128]{1,0:T(8,128)(2,1)S(1)} %get-tuple-element.39), channel_id=1, source_target_pairs={{0,1},{1,0},{2,3},{3,2},{4,5},{5,4},{6,7},{7,6},{8,9},{9,8},{10,11... | collective-permute-start | bytes 405512 | tf_op jit(solution)/shard_map/ppermute | solution.py:262
  43.3 8.0 %collective-permute-done.12.refs_6_ = bf16[256,256]{1,0:T(8,128)(2,1)S(1)} collective-permute-done((bf16[256,256]{1,0:T(8,128)(2,1)S(1)}, bf16[256,256]{1,0:T(8,128)(2,1)S(1)}, u32[]{:S(2)}, u32[]{:S(2)}) %collective-permute-start.12) | collective-permute-done | bytes 131104 | tf_op jit(solution)/shard_map/ppermute | solution.py:250
  51.3 1.4 %shard_map.76 = (bf16[1024,256]{1,0:T(8,128)(2,1)S(1)}, bf16[512,512]{1,0:T(8,128)(2,1)S(1)}, f32[512,512]{1,0:T(8,128)S(1)}) custom-call(bf16[128,1536]{1,0:T(8,128)(2,1)S(1)} %get-tuple-element.34.refs_0_.refs_4_, bf16[128,1536]{1,0:T(8,128)(2,1)S(1)} %collective-permute-done.refs_1_.refs_5_, bf16[128,1536]{1,0:T(8,128)(2,1)S(1)} %collective-permute-done.1.refs_2_.refs_6_, ...), custom_call_target="tpu_custom_call" | custom-call | flops 2147483648 | bytes 2228224 | tf_op jit(solution)/shard_map/pallas_call | solution.py:30
  52.7 3.6 %collective-permute-done.9.refs_2_ = bf16[528,128]{1,0:T(8,128)(2,1)S(1)} collective-permute-done((bf16[528,128]{1,0:T(8,128)(2,1)S(1)}, bf16[528,128]{1,0:T(8,128)(2,1)S(1)}, u32[]{:S(2)}, u32[]{:S(2)}) %collective-permute-start.9) | collective-permute-done | bytes 135200 | tf_op jit(solution)/shard_map/ppermute | solution.py:262
  57.2 2.5 %collective-permute-start.16 = (bf16[528,128]{1,0:T(8,128)(2,1)S(1)}, bf16[528,128]{1,0:T(8,128)(2,1)S(1)}, u32[]{:S(2)}, u32[]{:S(2)}) collective-permute-start(bf16[528,128]{1,0:T(8,128)(2,1)S(1)} %get-tuple-element.49), channel_id=1, source_target_pairs={{0,3},{1,2},{2,1},{3,0},{4,7},{5,6},{6,5},{7,4},{8,11},{9,10},{10,... | collective-permute-start | bytes 405512 | tf_op jit(solution)/shard_map/ppermute | solution.py:262
  59.7 1.9 %collective-permute-start.14 = (bf16[528,128]{1,0:T(8,128)(2,1)S(1)}, bf16[528,128]{1,0:T(8,128)(2,1)S(1)}, u32[]{:S(2)}, u32[]{:S(2)}) collective-permute-start(bf16[528,128]{1,0:T(8,128)(2,1)S(1)} %get-tuple-element.49), channel_id=1, source_target_pairs={{0,1},{1,0},{2,3},{3,2},{4,5},{5,4},{6,7},{7,6},{8,9},{9,8},{10,11... | collective-permute-start | bytes 405512 | tf_op jit(solution)/shard_map/ppermute | solution.py:262
  62.2 3.4 %collective-permute-done.16.refs_3_ = bf16[528,128]{1,0:T(8,128)(2,1)S(1)} collective-permute-done((bf16[528,128]{1,0:T(8,128)(2,1)S(1)}, bf16[528,128]{1,0:T(8,128)(2,1)S(1)}, u32[]{:S(2)}, u32[]{:S(2)}) %collective-permute-start.16) | collective-permute-done | bytes 135200 | tf_op jit(solution)/shard_map/ppermute | solution.py:262
  65.5 4.5 %collective-permute-done.15.refs_2_ = bf16[528,128]{1,0:T(8,128)(2,1)S(1)} collective-permute-done((bf16[528,128]{1,0:T(8,128)(2,1)S(1)}, bf16[528,128]{1,0:T(8,128)(2,1)S(1)}, u32[]{:S(2)}, u32[]{:S(2)}) %collective-permute-start.15) | collective-permute-done | bytes 135200 | tf_op jit(solution)/shard_map/ppermute | solution.py:262
  70.0 1.6 %shard_map.79 = (bf16[256,1024]{1,0:T(8,128)(2,1)S(1)}, bf16[512,512]{1,0:T(8,128)(2,1)S(1)}) custom-call(f32[528,128]{1,0:T(8,128)S(1)} %get-tuple-element.48.refs_0_, bf16[528,128]{1,0:T(8,128)(2,1)S(1)} %collective-permute-done.14.refs_1_, bf16[528,128]{1,0:T(8,128)(2,1)S(1)} %collective-permute-done.15.refs_2_, ...), custom_call_target="tpu_custom_call" | custom-call | flops 2147483648 | bytes 4476928 | tf_op jit(solution)/shard_map/pallas_call | solution.py:30
  71.7 1.1 %shard_map.80 = f32[256,1024]{1,0:T(8,128)S(1)} custom-call(bf16[512,256]{1,0:T(8,128)(2,1)S(1)} %shard_map.78.refs_8_.qg, bf16[512,512]{1,0:T(8,128)(2,1)S(1)} %get-tuple-element.55.kvg, bf16[1024,256]{1,0:T(8,128)(2,1)S(1)} %get-tuple-element.53.refs_9_.wq, bf16[1024,512]{1,0:T(8,128)(2,1)S(1)} %get-tuple-element.54.refs_10_.wkv), custom_call_target="tpu_custom_call" | custom-call | flops 2147483648 | bytes 2359296 | tf_op jit(solution)/shard_map/pallas_call | solution.py:30
  74.4 7.8 %collective-permute-done.18 = bf16[128,1024]{1,0:T(8,128)(2,1)S(1)} collective-permute-done((bf16[128,1024]{1,0:T(8,128)(2,1)S(1)}, bf16[128,1024]{1,0:T(8,128)(2,1)S(1)}, u32[]{:S(2)}, u32[]{:S(2)}) %collective-permute-start.18) | collective-permute-done | bytes 262176 | tf_op jit(solution)/shard_map/ppermute | solution.py:247
  (43 shorter events, 6.2 us)
Async XLA Ops:
  0.0 24.6 %copy-start = (bf16[8,128,256]{2,1,0:T(8,128)(2,1)S(1)}, bf16[8,128,256]{2,1,0:T(8,128)(2,1)}, u32[]{:S(2)}) copy-start(bf16[8,128,256]{2,1,0:T(8,128)(2,1)} %param.13) | copy-start | bytes 1572868
  0.0 1.1 %copy-start.1 = (bf16[256,1024]{1,0:T(8,128)(2,1)S(1)}, bf16[256,1024]{1,0:T(8,128)(2,1)}, u32[]{:S(2)}) copy-start(bf16[256,1024]{1,0:T(8,128)(2,1)} %wk.1) | copy-start | bytes 1572868
  1.1 1.0 %copy-start.2 = (bf16[256,1024]{1,0:T(8,128)(2,1)S(1)}, bf16[256,1024]{1,0:T(8,128)(2,1)}, u32[]{:S(2)}) copy-start(bf16[256,1024]{1,0:T(8,128)(2,1)} %wv.1) | copy-start | bytes 1572868
  2.2 1.0 %copy-start.3 = (bf16[256,1024]{1,0:T(8,128)(2,1)S(1)}, bf16[256,1024]{1,0:T(8,128)(2,1)}, u32[]{:S(2)}) copy-start(bf16[256,1024]{1,0:T(8,128)(2,1)} %wq.1) | copy-start | bytes 1572868
  4.0 1.0 %copy-start.5 = (bf16[128,1024]{1,0:T(8,128)(2,1)S(1)}, bf16[128,1024]{1,0:T(8,128)(2,1)}, u32[]{:S(2)}) copy-start(bf16[128,1024]{1,0:T(8,128)(2,1)} %cot.1) | copy-start | bytes 786436
  5.1 17.4 %collective-permute-start.1 = (bf16[128,1536]{1,0:T(8,128)(2,1)S(1)}, bf16[128,1536]{1,0:T(8,128)(2,1)S(1)}, u32[]{:S(2)}, u32[]{:S(2)}) collective-permute-start(bf16[128,1536]{1,0:T(8,128)(2,1)S(1)} %get-tuple-element.35), channel_id=1, source_target_pairs={{0,8},{4,12},{8,0},{12,4},{1,9},{5,13},{9,1},{13,5},{2,10},{6,14},... | collective-permute-start | bytes 1179656 | tf_op jit(solution)/shard_map/ppermute | solution.py:247
  8.1 8.3 %collective-permute-start.3 = (bf16[128,512]{1,0:T(8,128)(2,1)S(1)}, bf16[128,512]{1,0:T(8,128)(2,1)S(1)}, u32[]{:S(2)}, u32[]{:S(2)}) collective-permute-start(bf16[128,512]{1,0:T(8,128)(2,1)S(1)} %get-tuple-element.36), channel_id=1, source_target_pairs={{0,3},{1,2},{2,1},{3,0},{4,7},{5,6},{6,5},{7,4},{8,11},{9,10},{10,... | collective-permute-start | bytes 393224 | tf_op jit(solution)/shard_map/ppermute | solution.py:250
  11.7 10.8 %collective-permute-start.2 = (bf16[128,512]{1,0:T(8,128)(2,1)S(1)}, bf16[128,512]{1,0:T(8,128)(2,1)S(1)}, u32[]{:S(2)}, u32[]{:S(2)}) collective-permute-start(bf16[128,512]{1,0:T(8,128)(2,1)S(1)} %get-tuple-element.36), channel_id=1, source_target_pairs={{0,2},{1,3},{2,0},{3,1},{4,6},{5,7},{6,4},{7,5},{8,10},{9,11},{10,... | collective-permute-start | bytes 393224 | tf_op jit(solution)/shard_map/ppermute | solution.py:250
  11.7 19.5 %collective-permute-start = (bf16[128,1536]{1,0:T(8,128)(2,1)S(1)}, bf16[128,1536]{1,0:T(8,128)(2,1)S(1)}, u32[]{:S(2)}, u32[]{:S(2)}) collective-permute-start(bf16[128,1536]{1,0:T(8,128)(2,1)S(1)} %get-tuple-element.34.refs_0_.refs_4_), channel_id=1, source_target_pairs={{0,4},{4,0},{8,12},{12,8},{1,5},{5,1},{9,13},{13,9},{2,6},{6,2},{1... | collective-permute-start | bytes 1179656 | tf_op jit(solution)/shard_map/ppermute | solution.py:247
  22.5 13.1 %collective-permute-start.4 = (bf16[128,1536]{1,0:T(8,128)(2,1)S(1)}, bf16[128,1536]{1,0:T(8,128)(2,1)S(1)}, u32[]{:S(2)}, u32[]{:S(2)}) collective-permute-start(bf16[128,1536]{1,0:T(8,128)(2,1)S(1)} %collective-permute-done.1.refs_2_.refs_6_), channel_id=1, source_target_pairs={{0,4},{4,0},{8,12},{12,8},{1,5},{5,1},{9,13},{13,9},{2,6},{6,2},{1... | collective-permute-start | bytes 1179656 | tf_op jit(solution)/shard_map/ppermute | solution.py:247
  22.5 8.7 %collective-permute-start.5 = (bf16[256,512]{1,0:T(8,128)(2,1)S(1)}, bf16[256,512]{1,0:T(8,128)(2,1)S(1)}, u32[]{:S(2)}, u32[]{:S(2)}) collective-permute-start(bf16[256,512]{1,0:T(8,128)(2,1)S(1)} %get-tuple-element.31.refs_4_), channel_id=1, source_target_pairs={{0,1},{1,0},{2,3},{3,2},{4,5},{5,4},{6,7},{7,6},{8,9},{9,8},{10,11... | collective-permute-start | bytes 786440 | tf_op jit(solution)/shard_map/ppermute | solution.py:250
  22.5 11.2 %collective-permute-start.7 = (bf16[128,512]{1,0:T(8,128)(2,1)S(1)}, bf16[128,512]{1,0:T(8,128)(2,1)S(1)}, u32[]{:S(2)}, u32[]{:S(2)}) collective-permute-start(bf16[128,512]{1,0:T(8,128)(2,1)S(1)} %collective-permute-done.3.refs_8_), channel_id=1, source_target_pairs={{0,16},{16,0},{1,17},{17,1},{2,18},{18,2},{3,19},{19,3},{4,20},{20... | collective-permute-start | bytes 393224 | tf_op jit(solution)/shard_map/ppermute | solution.py:285
  24.1 11.5 %collective-permute-start.6 = (bf16[128,512]{1,0:T(8,128)(2,1)S(1)}, bf16[128,512]{1,0:T(8,128)(2,1)S(1)}, u32[]{:S(2)}, u32[]{:S(2)}) collective-permute-start(bf16[128,512]{1,0:T(8,128)(2,1)S(1)} %collective-permute-done.2.refs_6_), channel_id=1, source_target_pairs={{0,16},{16,0},{1,17},{17,1},{2,18},{18,2},{3,19},{19,3},{4,20},{20... | collective-permute-start | bytes 393224 | tf_op jit(solution)/shard_map/ppermute | solution.py:285
  31.2 9.0 %collective-permute-start.13 = (bf16[256,256]{1,0:T(8,128)(2,1)S(1)}, bf16[256,256]{1,0:T(8,128)(2,1)S(1)}, u32[]{:S(2)}, u32[]{:S(2)}) collective-permute-start(bf16[256,256]{1,0:T(8,128)(2,1)S(1)} %get-tuple-element.41.refs_4_), channel_id=1, source_target_pairs={{0,3},{1,2},{2,1},{3,0},{4,7},{5,6},{6,5},{7,4},{8,11},{9,10},{10,... | collective-permute-start | bytes 393224 | tf_op jit(solution)/shard_map/ppermute | solution.py:250
  33.7 17.6 %collective-permute-start.12 = (bf16[256,256]{1,0:T(8,128)(2,1)S(1)}, bf16[256,256]{1,0:T(8,128)(2,1)S(1)}, u32[]{:S(2)}, u32[]{:S(2)}) collective-permute-start(bf16[256,256]{1,0:T(8,128)(2,1)S(1)} %get-tuple-element.41.refs_4_), channel_id=1, source_target_pairs={{0,2},{1,3},{2,0},{3,1},{4,6},{5,7},{6,4},{7,5},{8,10},{9,11},{10,... | collective-permute-start | bytes 393224 | tf_op jit(solution)/shard_map/ppermute | solution.py:250
  33.7 17.6 %collective-permute-start.11 = (bf16[256,256]{1,0:T(8,128)(2,1)S(1)}, bf16[256,256]{1,0:T(8,128)(2,1)S(1)}, u32[]{:S(2)}, u32[]{:S(2)}) collective-permute-start(bf16[256,256]{1,0:T(8,128)(2,1)S(1)} %get-tuple-element.41.refs_4_), channel_id=1, source_target_pairs={{0,1},{1,0},{2,3},{3,2},{4,5},{5,4},{6,7},{7,6},{8,9},{9,8},{10,11... | collective-permute-start | bytes 393224 | tf_op jit(solution)/shard_map/ppermute | solution.py:250
  37.6 15.0 %collective-permute-start.10 = (bf16[528,128]{1,0:T(8,128)(2,1)S(1)}, bf16[528,128]{1,0:T(8,128)(2,1)S(1)}, u32[]{:S(2)}, u32[]{:S(2)}) collective-permute-start(bf16[528,128]{1,0:T(8,128)(2,1)S(1)} %get-tuple-element.39), channel_id=1, source_target_pairs={{0,3},{1,2},{2,1},{3,0},{4,7},{5,6},{6,5},{7,4},{8,11},{9,10},{10,... | collective-permute-start | bytes 405512 | tf_op jit(solution)/shard_map/ppermute | solution.py:262
  40.2 16.1 %collective-permute-start.9 = (bf16[528,128]{1,0:T(8,128)(2,1)S(1)}, bf16[528,128]{1,0:T(8,128)(2,1)S(1)}, u32[]{:S(2)}, u32[]{:S(2)}) collective-permute-start(bf16[528,128]{1,0:T(8,128)(2,1)S(1)} %get-tuple-element.39), channel_id=1, source_target_pairs={{0,2},{1,3},{2,0},{3,1},{4,6},{5,7},{6,4},{7,5},{8,10},{9,11},{10,... | collective-permute-start | bytes 405512 | tf_op jit(solution)/shard_map/ppermute | solution.py:262
  40.2 16.1 %collective-permute-start.8 = (bf16[528,128]{1,0:T(8,128)(2,1)S(1)}, bf16[528,128]{1,0:T(8,128)(2,1)S(1)}, u32[]{:S(2)}, u32[]{:S(2)}) collective-permute-start(bf16[528,128]{1,0:T(8,128)(2,1)S(1)} %get-tuple-element.39), channel_id=1, source_target_pairs={{0,1},{1,0},{2,3},{3,2},{4,5},{5,4},{6,7},{7,6},{8,9},{9,8},{10,11... | collective-permute-start | bytes 405512 | tf_op jit(solution)/shard_map/ppermute | solution.py:262
  57.2 8.4 %collective-permute-start.16 = (bf16[528,128]{1,0:T(8,128)(2,1)S(1)}, bf16[528,128]{1,0:T(8,128)(2,1)S(1)}, u32[]{:S(2)}, u32[]{:S(2)}) collective-permute-start(bf16[528,128]{1,0:T(8,128)(2,1)S(1)} %get-tuple-element.49), channel_id=1, source_target_pairs={{0,3},{1,2},{2,1},{3,0},{4,7},{5,6},{6,5},{7,4},{8,11},{9,10},{10,... | collective-permute-start | bytes 405512 | tf_op jit(solution)/shard_map/ppermute | solution.py:262
  59.7 10.3 %collective-permute-start.15 = (bf16[528,128]{1,0:T(8,128)(2,1)S(1)}, bf16[528,128]{1,0:T(8,128)(2,1)S(1)}, u32[]{:S(2)}, u32[]{:S(2)}) collective-permute-start(bf16[528,128]{1,0:T(8,128)(2,1)S(1)} %get-tuple-element.49), channel_id=1, source_target_pairs={{0,2},{1,3},{2,0},{3,1},{4,6},{5,7},{6,4},{7,5},{8,10},{9,11},{10,... | collective-permute-start | bytes 405512 | tf_op jit(solution)/shard_map/ppermute | solution.py:262
  59.7 10.3 %collective-permute-start.14 = (bf16[528,128]{1,0:T(8,128)(2,1)S(1)}, bf16[528,128]{1,0:T(8,128)(2,1)S(1)}, u32[]{:S(2)}, u32[]{:S(2)}) collective-permute-start(bf16[528,128]{1,0:T(8,128)(2,1)S(1)} %get-tuple-element.49), channel_id=1, source_target_pairs={{0,1},{1,0},{2,3},{3,2},{4,5},{5,4},{6,7},{7,6},{8,9},{9,8},{10,11... | collective-permute-start | bytes 405512 | tf_op jit(solution)/shard_map/ppermute | solution.py:262
  71.6 2.0 %collective-permute-start.17 = (bf16[256,1024]{1,0:T(8,128)(2,1)S(1)}, bf16[256,1024]{1,0:T(8,128)(2,1)S(1)}, u32[]{:S(2)}, u32[]{:S(2)}) collective-permute-start(bf16[256,1024]{1,0:T(8,128)(2,1)S(1)} %get-tuple-element.56), channel_id=1, source_target_pairs={{0,4},{4,0},{8,12},{12,8},{1,5},{5,1},{9,13},{13,9},{2,6},{6,2},{1... | collective-permute-start | bytes 1572872 | tf_op jit(solution)/shard_map/ppermute | solution.py:247
  73.8 8.4 %collective-permute-start.18 = (bf16[128,1024]{1,0:T(8,128)(2,1)S(1)}, bf16[128,1024]{1,0:T(8,128)(2,1)S(1)}, u32[]{:S(2)}, u32[]{:S(2)}) collective-permute-start(bf16[128,1024]{1,0:T(8,128)(2,1)S(1)} %slice.15), channel_id=1, source_target_pairs={{0,8},{4,12},{8,0},{12,4},{1,9},{5,13},{9,1},{13,5},{2,10},{6,14},... | collective-permute-start | bytes 786440 | tf_op jit(solution)/shard_map/ppermute | solution.py:247
  (2 other events, 1.7 us)

commit v4 on v3

--- a/solution.py
+++ b/solution.py
@@ -25,29 +25,30 @@
     return soft, jnp.where(u >= 0.0, r, e * r)
 
 
-def call(body, outs, args, flops, **kw):
+def call(body, outs, args, flops, vmem=24, **kw):
     nbytes = sum(a.size * a.dtype.itemsize for a in args)
     return pl.pallas_call(
         body,
         out_shape=[jax.ShapeDtypeStruct(s, d) for s, d in outs],
-        compiler_params=pltpu.CompilerParams(vmem_limit_bytes=24 * 1024 * 1024),
+        compiler_params=pltpu.CompilerParams(vmem_limit_bytes=vmem * 2**20),
         cost_estimate=pl.CostEstimate(flops=flops, bytes_accessed=nbytes, transcendentals=0),
         **kw,
     )(*args)
 
 
-def weight_kernel(g, cols, split, wk, wv, wq, *refs):
-    outs, sems = refs[:-1], refs[-1]
+def weight_kernel(g, cols, split, *refs):
+    ws, outs, sems = refs[:3], refs[3:-1], refs[-1]
     at = pl.ds(pl.multiple_of((lax.axis_index("seq") % g) * cols, cols), cols)
-    pairs = [(wk.at[:, at], outs[0].at[:, :cols]), (wv.at[:, at], outs[0].at[:, cols:]), (wq.at[:, at], outs[1])]
-    if split:
-        half = wk.shape[0] // 2
-        rows = pl.ds(pl.multiple_of(lax.axis_index("grp") * half, half), half)
-        pairs += [
-            (wk.at[rows, at], outs[2].at[:, :cols]),
-            (wv.at[rows, at], outs[2].at[:, cols:]),
-        ]
-    copies = [pltpu.make_async_copy(a, b, sems.at[i]) for i, (a, b) in enumerate(pairs)]
+    half = ws[0].shape[0] // 2
+    copies = []
+    for i, w in enumerate(ws):
+        to = slice(i * cols, (i + 1) * cols)
+        pairs = [(w.at[:, at], outs[0].at[:, to])]
+        if split:
+            rows = pl.ds(pl.multiple_of(lax.axis_index("grp") * half, half), half)
+            pairs.append((w.at[rows, at], outs[1].at[:, to]))
+        copies += pairs
+    copies = [pltpu.make_async_copy(a, b, sems.at[i]) for i, (a, b) in enumerate(copies)]
     for c in copies:
         c.start()
     for c in copies:
@@ -129,7 +130,7 @@
     rows = xs[0].shape[0]
     sums = [jnp.zeros((1, m), F32) for _ in range(hp)]
     for i, x in enumerate(xs):
-        act = dot(x[:, :width], w_full[...]).astype(BF16)
+        act = dot(x[:, :width], w_full[:, : 2 * cols]).astype(BF16)
         val[i * rows : (i + 1) * rows, :] = act[:, cols:]
         for h in range(hp):
             soft = features(act, om, h, i, feat, sig)
@@ -144,12 +145,12 @@
     put_total(own, send, base, hp * m // hd, jnp.concatenate(sums, axis=1))
 
 
-def query_kernel(g, n, nw, hp, width, *refs):
-    xs, ws, om = refs[:g], refs[g : g + nw], refs[g + nw]
-    w_full, feat, sig = refs[g + nw + 1 :]
-    place_rows(w_full, ws, n)
+def query_kernel(g, hp, width, *refs):
+    xs, w_full, om = refs[:g], refs[g], refs[g + 1]
+    feat, sig = refs[g + 2 :]
+    cols = hp * om.shape[1]
     for i, x in enumerate(xs):
-        act = dot(x[:, :width], w_full[...]).astype(BF16)
+        act = dot(x[:, :width], w_full[:, 2 * cols :]).astype(BF16)
         for h in range(hp):
             features(act, om, h, i, feat, sig)
 
@@ -200,18 +201,19 @@
         out[:, h * hd : (h + 1) * hd] = dot(pg, om[h], 1, 1).astype(BF16)
 
 
-def products(g, start, qg, kvg, wq, wkv, out):
+def products(g, start, qg, kvg, w, out):
     rows = qg.shape[0] // g
+    two = kvg.shape[1]
     for i in range(start, g, 2):
         tok = slice(i * rows, (i + 1) * rows)
-        o = dot(qg[tok, :], wq[...], 1, 1) + dot(kvg[tok, :], wkv[...], 1, 1)
+        o = dot(kvg[tok, :], w[:, :two], 1, 1) + dot(qg[tok, :], w[:, two:], 1, 1)
         out[(i // 2) * rows : (i // 2 + 1) * rows, :] = o.astype(out.dtype)
 
 
 def key_side_kernel(g, p, hp, *refs):
     parts = refs[:p]
-    val, feat, sig, om, qg, wq, wkv = refs[p : p + 7]
-    odd, kvg = refs[p + 7 :]
+    val, feat, sig, om, qg, w = refs[p : p + 6]
+    odd, kvg = refs[p + 6 :]
     hd, m = om.shape[1], om.shape[2]
     base = hp * m
     cols = hp * hd
@@ -223,11 +225,11 @@
         kvg[:, cols + h * hd : cols + (h + 1) * hd] = dot(feat[:, h * m : (h + 1) * m], gh).astype(BF16)
         pg = (fg * sig[:, h * m : (h + 1) * m]).astype(BF16)
         kvg[:, col] = dot(pg, om[h], 1, 1).astype(BF16)
-    products(g, 1, qg, kvg, wq, wkv, odd)
-
-
-def even_kernel(g, qg, kvg, wq, wkv, even):
-    products(g, 0, qg, kvg, wq, wkv, even)
+    products(g, 1, qg, kvg, w, odd)
+
+
+def even_kernel(g, qg, kvg, w, even):
+    products(g, 0, qg, kvg, w, even)
 
 
 def local(events, offsets, cotangent, query_weight, key_weight, value_weight, omega):
@@ -264,28 +266,24 @@
 
     wrows = key_weight.shape[0]
     split = lax.axis_size("grp") == 2 and wrows % 32 == 0
-    wouts = [((wrows, 2 * cols), BF16), ((wrows, cols), BF16)]
-    if split:
-        wouts.append(((wrows // 2, 2 * cols), BF16))
-    pieces = list(call(
+    wouts = [((wrows, 3 * cols), BF16), ((wrows // 2, 3 * cols), BF16)]
+    pieces = call(
         functools.partial(weight_kernel, g, cols, split),
-        wouts,
+        wouts if split else wouts[:1],
         [key_weight, value_weight, query_weight],
         0,
+        vmem=56,
         in_specs=[HBM] * 3,
-        scratch_shapes=[pltpu.SemaphoreType.DMA((5 if split else 3,))],
-    ))
-
-    def weight_rows(i, split):
-        if not split:
-            return [pieces[i]] + [over_sub(pieces[i], k) for k in range(1, n_sub)]
-        far = []
-        for k in range(2, n_sub):
-            part = over_sub(pieces[i + 2], k)
-            far += [part, lax.ppermute(part, "grp", [(0, 1), (1, 0)])]
-        return [pieces[i], over_sub(pieces[i], 1)] + far
-
-    kvs = weight_rows(0, split)
+        scratch_shapes=[pltpu.SemaphoreType.DMA((6 if split else 3,))],
+    )
+    if split:
+        arrived = [over_sub(pieces[0], 1)] + [over_sub(pieces[1], k) for k in range(2, n_sub)]
+        ws = [pieces[0], arrived[0]]
+        for part in arrived[1:]:
+            ws += [part, lax.ppermute(part, "grp", [(0, 1), (1, 0)])]
+    else:
+        arrived = [over_sub(pieces[0], k) for k in range(1, n_sub)]
+        ws = [pieces[0]] + arrived
 
     events, offsets, _ = lax.optimization_barrier((events, offsets, pieces[0]))
     half = width // 2
@@ -301,27 +299,24 @@
     for k in range(2, g, 2):
         xs[k] = over_seq(bufs[k // 2], k)
     xs[1] = over_seq(bufs[0], 1)
-    arrived = kvs[1:2] + kvs[2::2] if split else kvs[1:]
-    xs[2:], _ = lax.optimization_barrier((xs[2:], arrived[1:]))
+    xs[2:], _ = lax.optimization_barrier((xs[2:], arrived))
     for k in range(3, g, 2):
         xs[k] = over_seq(xs[k ^ 1], 1)
-    pieces, _ = lax.optimization_barrier((pieces, arrived + xs[1:2]))
-    qs = weight_rows(1, False)
     om = lax.dynamic_slice_in_dim(omega, (lax.axis_index("seq") % g) * hp, hp, 0)
 
     flop = 2 * t * width * cols
     summary_out = [((srows, hd), F32), ((srows, hd), BF16)]
-    wkv_full, key_feat, key_sig, val, own, send = call(
-        functools.partial(key_value_kernel, g, n_sub, len(kvs), hp, width),
-        [((width, 2 * cols), BF16), ((t, hp * m), BF16), ((t, hp * m), F32), ((t, cols), BF16)] + summary_out,
-        [*xs, *kvs, om],
+    w_full, key_feat, key_sig, val, own, send = call(
+        functools.partial(key_value_kernel, g, n_sub, len(ws), hp, width),
+        [((width, 3 * cols), BF16), ((t, hp * m), BF16), ((t, hp * m), F32), ((t, cols), BF16)] + summary_out,
+        [*xs, *ws, om],
         8 * flop,
     )
     summary = to_all(own, send)
-    wq_full, query_feat, query_sig = call(
-        functools.partial(query_kernel, g, n_sub, len(qs), hp, width),
-        [((width, cols), BF16), ((t, hp * m), BF16), ((t, hp * m), F32)],
-        [*xs, *qs, om],
+    query_feat, query_sig = call(
+        functools.partial(query_kernel, g, hp, width),
+        [((t, hp * m), BF16), ((t, hp * m), F32)],
+        [*xs, w_full, om],
         8 * flop,
     )
     total_half, summary_half, scaled_half, norm, own, send = call(
@@ -340,14 +335,14 @@
     odd, key_value_grad = call(
         functools.partial(key_side_kernel, g, p, hp),
         [((t // 2, width), BF16), ((t, 2 * cols), BF16)],
-        [*summary_grad, val, key_feat, key_sig, om, query_grad, wq_full, wkv_full],
+        [*summary_grad, val, key_feat, key_sig, om, query_grad, w_full],
         8 * flop,
     )
     got = over_seq(odd, 1)
     (even,) = call(
         functools.partial(even_kernel, g),
         [((t // 2, width), F32)],
-        [query_grad, key_value_grad, wq_full, wkv_full],
+        [query_grad, key_value_grad, w_full],
         8 * flop,
     )
     both = even + got.astype(F32)

time: 83.2 us -> 82.9 us (level)
  waiting for transfers between devices: 45.4 us -> 50.6 us
  starting transfers between devices: 23.9 us -> 19.4 us
  local copies, waits for them, and re-layouts: 3.9 us -> 0.07 us
  Pallas kernels: 7.73 us -> 10.5 us
    ppermute x2, waiting for transfers between devices: 0.01 us -> 9.52 us  [local(): ws += [part, lax.ppermute(part, 'grp', [(0, 1), (1, 0)])]]
    ppermute x6 -> x3, waiting for transfers between devices: 25.4 us -> 17 us  [over_sub(): return lax.ppermute(x, 'sub', [(i, i ^ k) for i in range(n_sub)])]
    ppermute x6, waiting for transfers between devices: 11.5 us -> 16.1 us  [to_all(): parts.append(lax.ppermute(send, ('seq', 'sub'), perm))]
    unnamed x14 -> x12, local copies, waits for them, and re-layouts: 3.86 us -> 0.03 us
    pallas_call x8, Pallas kernels: 7.73 us -> 10.5 us  [call(): pl.pallas_call(body, out_shape=[jax.ShapeDtypeStruct(s, d) for s, d in ou...]
    ppermute x6 -> x3, starting transfers between devices: 8 us -> 5.69 us  [over_sub(): return lax.ppermute(x, 'sub', [(i, i ^ k) for i in range(n_sub)])]
    ppermute x6, starting transfers between devices: 10.1 us -> 8.91 us  [to_all(): parts.append(lax.ppermute(send, ('seq', 'sub'), perm))]
    ppermute x5, starting transfers between devices: 3.68 us -> 2.75 us  [over_seq(): return lax.ppermute(x, 'seq', [(i, i ^ k) for i in range(n_seq)])]
  transfers between devices with their start and end apart: 19 -> 16, of which waited for: 9 -> 10; matrix products, arithmetic and copies ran while one was open for 0% -> 1% of each run, Pallas kernels for 6% -> 4%
where the time goes in v4:
time: 82.9 us; the launch traced here: 82.7 us
  waiting for transfers between devices  50.6 us (61%)
  starting transfers between devices  19.4 us (23%)
  Pallas kernels  10.5 us (13%)
  other arithmetic  1.91 us (2%)
    ppermute x3, waiting for transfers between devices, over_sub(): return lax.ppermute(x, 'sub', [(i, i ^ k) for i in range(n_sub)])  17 us
    ppermute x6, waiting for transfers between devices, to_all(): parts.append(lax.ppermute(send, ('seq', 'sub'), perm))  16.1 us
    pallas_call x8, Pallas kernels, call(): pl.pallas_call(body, out_shape=[jax.ShapeDtypeStruct(s, d) for s, d in ou...  10.5 us
    ppermute x2, waiting for transfers between devices, local(): ws += [part, lax.ppermute(part, 'grp', [(0, 1), (1, 0)])]  9.52 us
    ppermute x6, starting transfers between devices, to_all(): parts.append(lax.ppermute(send, ('seq', 'sub'), perm))  8.91 us
    ppermute x5, waiting for transfers between devices, over_seq(): return lax.ppermute(x, 'seq', [(i, i ^ k) for i in range(n_seq)])  8.06 us
    ppermute x3, starting transfers between devices, over_sub(): return lax.ppermute(x, 'sub', [(i, i ^ k) for i in range(n_sub)])  5.69 us
    ppermute x5, starting transfers between devices, over_seq(): return lax.ppermute(x, 'seq', [(i, i ^ k) for i in range(n_seq)])  2.75 us
  transfers between devices with their start and end apart: 16, of which 10 were waited for; matrix products, arithmetic and copies ran while one was open for 1% of the time, Pallas kernels for 4%

profile of v4, /device:TPU:0, one launch (start us, length us, event | category | flops | bytes accessed | tf_op | source)
XLA Modules:
  0.0 82.7 jit_solution(14917427094405670780)
XLA Ops:
  0.0 2.1 %shard_map.73 = (bf16[256,768]{1,0:T(8,128)(2,1)}, bf16[128,768]{1,0:T(8,128)(2,1)}) custom-call(bf16[256,1024]{1,0:T(8,128)(2,1)} %refs_0_.1, bf16[256,1024]{1,0:T(8,128)(2,1)} %refs_1_.1, bf16[256,1024]{1,0:T(8,128)(2,1)} %refs_2_.1), custom_call_target="tpu_custom_call" | custom-call | bytes 1572864 | tf_op jit(solution)/shard_map/pallas_call | solution.py:30
  2.1 3.1 %collective-permute-start.2 = (bf16[256,768]{1,0:T(8,128)(2,1)}, bf16[256,768]{1,0:T(8,128)(2,1)S(1)}, u32[]{:S(2)}, u32[]{:S(2)}) collective-permute-start(bf16[256,768]{1,0:T(8,128)(2,1)} %get-tuple-element.28.refs_4_), channel_id=1, source_target_pairs={{0,1},{1,0},{2,3},{3,2},{4,5},{5,4},{6,7},{7,6},{8,9},{9,8},{10,11... | collective-permute-start | bytes 1179656 | tf_op jit(solution)/shard_map/ppermute | solution.py:252
  5.2 1.0 %multiply_cosine_fusion = (f32[128,512]{1,0:T(8,128)S(1)}, f32[128,512]{1,0:T(8,128)S(1)}) fusion(f32[512]{0:T(512)S(1)} %multiply_exponential_fusion, f32[128]{0:T(128)S(1)} %convert_element_type.13), kind=kLoop, calls=%fused_computation.4 | loop fusion | flops 65536 | bytes 526848 | tf_op jit(solution)/shard_map/cos | solution.py:295
  6.3 1.6 %collective-permute-start.1 = (bf16[128,1536]{1,0:T(8,128)(2,1)S(1)}, bf16[128,1536]{1,0:T(8,128)(2,1)S(1)}, u32[]{:S(2)}, u32[]{:S(2)}) collective-permute-start(bf16[128,1536]{1,0:T(8,128)(2,1)S(1)} %get-tuple-element.32), channel_id=1, source_target_pairs={{0,8},{4,12},{8,0},{12,4},{1,9},{5,13},{9,1},{13,5},{2,10},{6,14},... | collective-permute-start | bytes 1179656 | tf_op jit(solution)/shard_map/ppermute | solution.py:249
  7.9 2.5 %collective-permute-start.4 = (bf16[128,768]{1,0:T(8,128)(2,1)S(1)}, bf16[128,768]{1,0:T(8,128)(2,1)S(1)}, u32[]{:S(2)}, u32[]{:S(2)}) collective-permute-start(bf16[128,768]{1,0:T(8,128)(2,1)S(1)} %copy-done.4), channel_id=1, source_target_pairs={{0,3},{1,2},{2,1},{3,0},{4,7},{5,6},{6,5},{7,4},{8,11},{9,10},{10,... | collective-permute-start | bytes 589832 | tf_op jit(solution)/shard_map/ppermute | solution.py:252
  10.5 11.7 %collective-permute-done.4.refs_8_ = bf16[128,768]{1,0:T(8,128)(2,1)S(1)} collective-permute-done((bf16[128,768]{1,0:T(8,128)(2,1)S(1)}, bf16[128,768]{1,0:T(8,128)(2,1)S(1)}, u32[]{:S(2)}, u32[]{:S(2)}) %collective-permute-start.4) | collective-permute-done | bytes 196640 | tf_op jit(solution)/shard_map/ppermute | solution.py:252
  22.1 5.3 %collective-permute-done.3.refs_6_ = bf16[128,768]{1,0:T(8,128)(2,1)S(1)} collective-permute-done((bf16[128,768]{1,0:T(8,128)(2,1)S(1)}, bf16[128,768]{1,0:T(8,128)(2,1)S(1)}, u32[]{:S(2)}, u32[]{:S(2)}) %collective-permute-start.3) | collective-permute-done | bytes 196640 | tf_op jit(solution)/shard_map/ppermute | solution.py:252
  27.4 1.6 %collective-permute-start.7 = (bf16[128,768]{1,0:T(8,128)(2,1)S(1)}, bf16[128,768]{1,0:T(8,128)(2,1)S(1)}, u32[]{:S(2)}, u32[]{:S(2)}) collective-permute-start(bf16[128,768]{1,0:T(8,128)(2,1)S(1)} %collective-permute-done.4.refs_8_), channel_id=1, source_target_pairs={{0,16},{16,0},{1,17},{17,1},{2,18},{18,2},{3,19},{19,3},{4,20},{20... | collective-permute-start | bytes 589832 | tf_op jit(solution)/shard_map/ppermute | solution.py:283
  29.6 5.7 %collective-permute-done.7.refs_9_ = bf16[128,768]{1,0:T(8,128)(2,1)S(1)} collective-permute-done((bf16[128,768]{1,0:T(8,128)(2,1)S(1)}, bf16[128,768]{1,0:T(8,128)(2,1)S(1)}, u32[]{:S(2)}, u32[]{:S(2)}) %collective-permute-start.7) | collective-permute-done | bytes 196640 | tf_op jit(solution)/shard_map/ppermute | solution.py:283
  35.2 3.9 %collective-permute-done.6.refs_7_ = bf16[128,768]{1,0:T(8,128)(2,1)} collective-permute-done((bf16[128,768]{1,0:T(8,128)(2,1)S(1)}, bf16[128,768]{1,0:T(8,128)(2,1)}, u32[]{:S(2)}, u32[]{:S(2)}) %collective-permute-start.6) | collective-permute-done | bytes 196640 | tf_op jit(solution)/shard_map/ppermute | solution.py:283
  39.1 3.0 %shard_map.75 = (bf16[1024,768]{1,0:T(8,128)(2,1)S(1)}, bf16[512,512]{1,0:T(8,128)(2,1)S(1)}, f32[512,512]{1,0:T(8,128)S(1)}, bf16[512,256]{1,0:T(8,128)(2,1)S(1...) custom-call(bf16[128,1536]{1,0:T(8,128)(2,1)S(1)} %get-tuple-element.31.refs_0_.refs_4_, ...), custom_call_target="tpu_custom_call" | custom-call | flops 2147483648 | bytes 3276800 | tf_op jit(solution)/shard_map/pallas_call | solution.py:30
  42.0 2.7 %collective-permute-start.10 = (bf16[528,128]{1,0:T(8,128)(2,1)S(1)}, bf16[528,128]{1,0:T(8,128)(2,1)S(1)}, u32[]{:S(2)}, u32[]{:S(2)}) collective-permute-start(bf16[528,128]{1,0:T(8,128)(2,1)S(1)} %get-tuple-element.36), channel_id=1, source_target_pairs={{0,3},{1,2},{2,1},{3,0},{4,7},{5,6},{6,5},{7,4},{8,11},{9,10},{10,... | collective-permute-start | bytes 405512 | tf_op jit(solution)/shard_map/ppermute | solution.py:264
  44.8 1.7 %collective-permute-start.8 = (bf16[528,128]{1,0:T(8,128)(2,1)S(1)}, bf16[528,128]{1,0:T(8,128)(2,1)S(1)}, u32[]{:S(2)}, u32[]{:S(2)}) collective-permute-start(bf16[528,128]{1,0:T(8,128)(2,1)S(1)} %get-tuple-element.36), channel_id=1, source_target_pairs={{0,1},{1,0},{2,3},{3,2},{4,5},{5,4},{6,7},{7,6},{8,9},{9,8},{10,11... | collective-permute-start | bytes 405512 | tf_op jit(solution)/shard_map/ppermute | solution.py:264
  46.5 1.4 %shard_map.76 = (bf16[512,512]{1,0:T(8,128)(2,1)S(1)}, f32[512,512]{1,0:T(8,128)S(1)}) custom-call(bf16[128,1536]{1,0:T(8,128)(2,1)S(1)} %get-tuple-element.31.refs_0_.refs_4_, bf16[128,1536]{1,0:T(8,128)(2,1)S(1)} %collective-permute-done.refs_1_.refs_5_, bf16[128,1536]{1,0:T(8,128)(2,1)S(1)} %collective-permute-done.1.refs_2_.refs_6_, ...), custom_call_target="tpu_custom_call" | custom-call | flops 2147483648 | bytes 3276800 | tf_op jit(solution)/shard_map/pallas_call | solution.py:30
  47.9 2.6 %collective-permute-done.10.refs_3_ = bf16[528,128]{1,0:T(8,128)(2,1)S(1)} collective-permute-done((bf16[528,128]{1,0:T(8,128)(2,1)S(1)}, bf16[528,128]{1,0:T(8,128)(2,1)S(1)}, u32[]{:S(2)}, u32[]{:S(2)}) %collective-permute-start.10) | collective-permute-done | bytes 135200 | tf_op jit(solution)/shard_map/ppermute | solution.py:264
  50.5 4.7 %collective-permute-done.9.refs_2_ = bf16[528,128]{1,0:T(8,128)(2,1)S(1)} collective-permute-done((bf16[528,128]{1,0:T(8,128)(2,1)S(1)}, bf16[528,128]{1,0:T(8,128)(2,1)S(1)}, u32[]{:S(2)}, u32[]{:S(2)}) %collective-permute-start.9) | collective-permute-done | bytes 135200 | tf_op jit(solution)/shard_map/ppermute | solution.py:264
  56.1 2.3 %collective-permute-start.13 = (bf16[528,128]{1,0:T(8,128)(2,1)S(1)}, bf16[528,128]{1,0:T(8,128)(2,1)S(1)}, u32[]{:S(2)}, u32[]{:S(2)}) collective-permute-start(bf16[528,128]{1,0:T(8,128)(2,1)S(1)} %get-tuple-element.45), channel_id=1, source_target_pairs={{0,3},{1,2},{2,1},{3,0},{4,7},{5,6},{6,5},{7,4},{8,11},{9,10},{10,... | collective-permute-start | bytes 405512 | tf_op jit(solution)/shard_map/ppermute | solution.py:264
  58.4 2.1 %collective-permute-start.11 = (bf16[528,128]{1,0:T(8,128)(2,1)S(1)}, bf16[528,128]{1,0:T(8,128)(2,1)S(1)}, u32[]{:S(2)}, u32[]{:S(2)}) collective-permute-start(bf16[528,128]{1,0:T(8,128)(2,1)S(1)} %get-tuple-element.45), channel_id=1, source_target_pairs={{0,1},{1,0},{2,3},{3,2},{4,5},{5,4},{6,7},{7,6},{8,9},{9,8},{10,11... | collective-permute-start | bytes 405512 | tf_op jit(solution)/shard_map/ppermute | solution.py:264
  61.1 3.4 %collective-permute-done.13.refs_3_ = bf16[528,128]{1,0:T(8,128)(2,1)S(1)} collective-permute-done((bf16[528,128]{1,0:T(8,128)(2,1)S(1)}, bf16[528,128]{1,0:T(8,128)(2,1)S(1)}, u32[]{:S(2)}, u32[]{:S(2)}) %collective-permute-start.13) | collective-permute-done | bytes 135200 | tf_op jit(solution)/shard_map/ppermute | solution.py:264
  64.5 5.3 %collective-permute-done.12.refs_2_ = bf16[528,128]{1,0:T(8,128)(2,1)S(1)} collective-permute-done((bf16[528,128]{1,0:T(8,128)(2,1)S(1)}, bf16[528,128]{1,0:T(8,128)(2,1)S(1)}, u32[]{:S(2)}, u32[]{:S(2)}) %collective-permute-start.12) | collective-permute-done | bytes 135200 | tf_op jit(solution)/shard_map/ppermute | solution.py:264
  69.8 1.5 %shard_map.79 = (bf16[256,1024]{1,0:T(8,128)(2,1)S(1)}, bf16[512,512]{1,0:T(8,128)(2,1)S(1)}) custom-call(f32[528,128]{1,0:T(8,128)S(1)} %get-tuple-element.44.refs_0_, bf16[528,128]{1,0:T(8,128)(2,1)S(1)} %collective-permute-done.11.refs_1_, bf16[528,128]{1,0:T(8,128)(2,1)S(1)} %collective-permute-done.12.refs_2_, ...), custom_call_target="tpu_custom_call" | custom-call | flops 2147483648 | bytes 4476928 | tf_op jit(solution)/shard_map/pallas_call | solution.py:30
  71.4 1.1 %shard_map.80 = f32[256,1024]{1,0:T(8,128)S(1)} custom-call(bf16[512,256]{1,0:T(8,128)(2,1)S(1)} %shard_map.78.refs_8_.qg, bf16[512,512]{1,0:T(8,128)(2,1)S(1)} %get-tuple-element.49.kvg, bf16[1024,768]{1,0:T(8,128)(2,1)S(1)} %get-tuple-element.37.refs_4_.refs_9_.w), custom_call_target="tpu_custom_call" | custom-call | flops 2147483648 | bytes 2359296 | tf_op jit(solution)/shard_map/pallas_call | solution.py:30
  73.5 1.1 %collective-permute-start.15 = (bf16[128,1024]{1,0:T(8,128)(2,1)S(1)}, bf16[128,1024]{1,0:T(8,128)(2,1)S(1)}, u32[]{:S(2)}, u32[]{:S(2)}) collective-permute-start(bf16[128,1024]{1,0:T(8,128)(2,1)S(1)} %slice.15), channel_id=1, source_target_pairs={{0,8},{4,12},{8,0},{12,4},{1,9},{5,13},{9,1},{13,5},{2,10},{6,14},... | collective-permute-start | bytes 786440 | tf_op jit(solution)/shard_map/ppermute | solution.py:249
  74.6 7.3 %collective-permute-done.15 = bf16[128,1024]{1,0:T(8,128)(2,1)S(1)} collective-permute-done((bf16[128,1024]{1,0:T(8,128)(2,1)S(1)}, bf16[128,1024]{1,0:T(8,128)(2,1)S(1)}, u32[]{:S(2)}, u32[]{:S(2)}) %collective-permute-start.15) | collective-permute-done | bytes 262176 | tf_op jit(solution)/shard_map/ppermute | solution.py:249
  (35 shorter events, 4.0 us)
Async XLA Ops:
  0.0 29.5 %copy-start = (bf16[8,128,256]{2,1,0:T(8,128)(2,1)S(1)}, bf16[8,128,256]{2,1,0:T(8,128)(2,1)}, u32[]{:S(2)}) copy-start(bf16[8,128,256]{2,1,0:T(8,128)(2,1)} %param.13) | copy-start | bytes 1572868
  0.0 5.2 %copy-start.5 = (s32[128]{0:T(128)S(1)}, s32[128]{0:T(128)}, u32[]{:S(2)}) copy-start(s32[128]{0:T(128)} %param.8) | copy-start | bytes 1540
  0.0 6.2 %copy-start.2 = (bf16[128,1024]{1,0:T(8,128)(2,1)S(1)}, bf16[128,1024]{1,0:T(8,128)(2,1)}, u32[]{:S(2)}) copy-start(bf16[128,1024]{1,0:T(8,128)(2,1)} %events) | copy-start | bytes 786436
  0.0 6.2 %copy-start.3 = (bf16[128,1024]{1,0:T(8,128)(2,1)S(1)}, bf16[128,1024]{1,0:T(8,128)(2,1)}, u32[]{:S(2)}) copy-start(bf16[128,1024]{1,0:T(8,128)(2,1)} %cot.1) | copy-start | bytes 786436
  2.1 25.4 %collective-permute-start.2 = (bf16[256,768]{1,0:T(8,128)(2,1)}, bf16[256,768]{1,0:T(8,128)(2,1)S(1)}, u32[]{:S(2)}, u32[]{:S(2)}) collective-permute-start(bf16[256,768]{1,0:T(8,128)(2,1)} %get-tuple-element.28.refs_4_), channel_id=1, source_target_pairs={{0,1},{1,0},{2,3},{3,2},{4,5},{5,4},{6,7},{7,6},{8,9},{9,8},{10,11... | collective-permute-start | bytes 1179656 | tf_op jit(solution)/shard_map/ppermute | solution.py:252
  6.2 1.7 %copy-start.4 = (bf16[128,768]{1,0:T(8,128)(2,1)S(1)}, bf16[128,768]{1,0:T(8,128)(2,1)}, u32[]{:S(2)}) copy-start(bf16[128,768]{1,0:T(8,128)(2,1)} %get-tuple-element.33) | copy-start | bytes 589828
  6.2 32.9 %copy-start.1 = (bf16[256,768]{1,0:T(8,128)(2,1)S(1)}, bf16[256,768]{1,0:T(8,128)(2,1)}, u32[]{:S(2)}) copy-start(bf16[256,768]{1,0:T(8,128)(2,1)} %get-tuple-element.28.refs_4_) | copy-start | bytes 1179652
  6.3 21.1 %collective-permute-start.1 = (bf16[128,1536]{1,0:T(8,128)(2,1)S(1)}, bf16[128,1536]{1,0:T(8,128)(2,1)S(1)}, u32[]{:S(2)}, u32[]{:S(2)}) collective-permute-start(bf16[128,1536]{1,0:T(8,128)(2,1)S(1)} %get-tuple-element.32), channel_id=1, source_target_pairs={{0,8},{4,12},{8,0},{12,4},{1,9},{5,13},{9,1},{13,5},{2,10},{6,14},... | collective-permute-start | bytes 1179656 | tf_op jit(solution)/shard_map/ppermute | solution.py:249
  7.9 14.3 %collective-permute-start.4 = (bf16[128,768]{1,0:T(8,128)(2,1)S(1)}, bf16[128,768]{1,0:T(8,128)(2,1)S(1)}, u32[]{:S(2)}, u32[]{:S(2)}) collective-permute-start(bf16[128,768]{1,0:T(8,128)(2,1)S(1)} %copy-done.4), channel_id=1, source_target_pairs={{0,3},{1,2},{2,1},{3,0},{4,7},{5,6},{6,5},{7,4},{8,11},{9,10},{10,... | collective-permute-start | bytes 589832 | tf_op jit(solution)/shard_map/ppermute | solution.py:252
  10.3 17.1 %collective-permute-start.3 = (bf16[128,768]{1,0:T(8,128)(2,1)S(1)}, bf16[128,768]{1,0:T(8,128)(2,1)S(1)}, u32[]{:S(2)}, u32[]{:S(2)}) collective-permute-start(bf16[128,768]{1,0:T(8,128)(2,1)S(1)} %copy-done.4), channel_id=1, source_target_pairs={{0,2},{1,3},{2,0},{3,1},{4,6},{5,7},{6,4},{7,5},{8,10},{9,11},{10,... | collective-permute-start | bytes 589832 | tf_op jit(solution)/shard_map/ppermute | solution.py:252
  10.5 28.6 %collective-permute-start = (bf16[128,1536]{1,0:T(8,128)(2,1)S(1)}, bf16[128,1536]{1,0:T(8,128)(2,1)S(1)}, u32[]{:S(2)}, u32[]{:S(2)}) collective-permute-start(bf16[128,1536]{1,0:T(8,128)(2,1)S(1)} %get-tuple-element.31.refs_0_.refs_4_), channel_id=1, source_target_pairs={{0,4},{4,0},{8,12},{12,8},{1,5},{5,1},{9,13},{13,9},{2,6},{6,2},{1... | collective-permute-start | bytes 1179656 | tf_op jit(solution)/shard_map/ppermute | solution.py:249
  27.4 11.6 %collective-permute-start.5 = (bf16[128,1536]{1,0:T(8,128)(2,1)S(1)}, bf16[128,1536]{1,0:T(8,128)(2,1)S(1)}, u32[]{:S(2)}, u32[]{:S(2)}) collective-permute-start(bf16[128,1536]{1,0:T(8,128)(2,1)S(1)} %collective-permute-done.1.refs_2_.refs_6_), channel_id=1, source_target_pairs={{0,4},{4,0},{8,12},{12,8},{1,5},{5,1},{9,13},{13,9},{2,6},{6,2},{1... | collective-permute-start | bytes 1179656 | tf_op jit(solution)/shard_map/ppermute | solution.py:249
  27.4 7.8 %collective-permute-start.7 = (bf16[128,768]{1,0:T(8,128)(2,1)S(1)}, bf16[128,768]{1,0:T(8,128)(2,1)S(1)}, u32[]{:S(2)}, u32[]{:S(2)}) collective-permute-start(bf16[128,768]{1,0:T(8,128)(2,1)S(1)} %collective-permute-done.4.refs_8_), channel_id=1, source_target_pairs={{0,16},{16,0},{1,17},{17,1},{2,18},{18,2},{3,19},{19,3},{4,20},{20... | collective-permute-start | bytes 589832 | tf_op jit(solution)/shard_map/ppermute | solution.py:283
  29.0 10.0 %collective-permute-start.6 = (bf16[128,768]{1,0:T(8,128)(2,1)S(1)}, bf16[128,768]{1,0:T(8,128)(2,1)}, u32[]{:S(2)}, u32[]{:S(2)}) collective-permute-start(bf16[128,768]{1,0:T(8,128)(2,1)S(1)} %collective-permute-done.3.refs_6_), channel_id=1, source_target_pairs={{0,16},{16,0},{1,17},{17,1},{2,18},{18,2},{3,19},{19,3},{4,20},{20... | collective-permute-start | bytes 589832 | tf_op jit(solution)/shard_map/ppermute | solution.py:283
  42.0 8.4 %collective-permute-start.10 = (bf16[528,128]{1,0:T(8,128)(2,1)S(1)}, bf16[528,128]{1,0:T(8,128)(2,1)S(1)}, u32[]{:S(2)}, u32[]{:S(2)}) collective-permute-start(bf16[528,128]{1,0:T(8,128)(2,1)S(1)} %get-tuple-element.36), channel_id=1, source_target_pairs={{0,3},{1,2},{2,1},{3,0},{4,7},{5,6},{6,5},{7,4},{8,11},{9,10},{10,... | collective-permute-start | bytes 405512 | tf_op jit(solution)/shard_map/ppermute | solution.py:264
  44.8 10.4 %collective-permute-start.9 = (bf16[528,128]{1,0:T(8,128)(2,1)S(1)}, bf16[528,128]{1,0:T(8,128)(2,1)S(1)}, u32[]{:S(2)}, u32[]{:S(2)}) collective-permute-start(bf16[528,128]{1,0:T(8,128)(2,1)S(1)} %get-tuple-element.36), channel_id=1, source_target_pairs={{0,2},{1,3},{2,0},{3,1},{4,6},{5,7},{6,4},{7,5},{8,10},{9,11},{10,... | collective-permute-start | bytes 405512 | tf_op jit(solution)/shard_map/ppermute | solution.py:264
  44.8 10.4 %collective-permute-start.8 = (bf16[528,128]{1,0:T(8,128)(2,1)S(1)}, bf16[528,128]{1,0:T(8,128)(2,1)S(1)}, u32[]{:S(2)}, u32[]{:S(2)}) collective-permute-start(bf16[528,128]{1,0:T(8,128)(2,1)S(1)} %get-tuple-element.36), channel_id=1, source_target_pairs={{0,1},{1,0},{2,3},{3,2},{4,5},{5,4},{6,7},{7,6},{8,9},{9,8},{10,11... | collective-permute-start | bytes 405512 | tf_op jit(solution)/shard_map/ppermute | solution.py:264
  56.1 8.4 %collective-permute-start.13 = (bf16[528,128]{1,0:T(8,128)(2,1)S(1)}, bf16[528,128]{1,0:T(8,128)(2,1)S(1)}, u32[]{:S(2)}, u32[]{:S(2)}) collective-permute-start(bf16[528,128]{1,0:T(8,128)(2,1)S(1)} %get-tuple-element.45), channel_id=1, source_target_pairs={{0,3},{1,2},{2,1},{3,0},{4,7},{5,6},{6,5},{7,4},{8,11},{9,10},{10,... | collective-permute-start | bytes 405512 | tf_op jit(solution)/shard_map/ppermute | solution.py:264
  58.4 11.4 %collective-permute-start.12 = (bf16[528,128]{1,0:T(8,128)(2,1)S(1)}, bf16[528,128]{1,0:T(8,128)(2,1)S(1)}, u32[]{:S(2)}, u32[]{:S(2)}) collective-permute-start(bf16[528,128]{1,0:T(8,128)(2,1)S(1)} %get-tuple-element.45), channel_id=1, source_target_pairs={{0,2},{1,3},{2,0},{3,1},{4,6},{5,7},{6,4},{7,5},{8,10},{9,11},{10,... | collective-permute-start | bytes 405512 | tf_op jit(solution)/shard_map/ppermute | solution.py:264
  58.4 11.4 %collective-permute-start.11 = (bf16[528,128]{1,0:T(8,128)(2,1)S(1)}, bf16[528,128]{1,0:T(8,128)(2,1)S(1)}, u32[]{:S(2)}, u32[]{:S(2)}) collective-permute-start(bf16[528,128]{1,0:T(8,128)(2,1)S(1)} %get-tuple-element.45), channel_id=1, source_target_pairs={{0,1},{1,0},{2,3},{3,2},{4,5},{5,4},{6,7},{7,6},{8,9},{9,8},{10,11... | collective-permute-start | bytes 405512 | tf_op jit(solution)/shard_map/ppermute | solution.py:264
  71.4 2.0 %collective-permute-start.14 = (bf16[256,1024]{1,0:T(8,128)(2,1)S(1)}, bf16[256,1024]{1,0:T(8,128)(2,1)S(1)}, u32[]{:S(2)}, u32[]{:S(2)}) collective-permute-start(bf16[256,1024]{1,0:T(8,128)(2,1)S(1)} %get-tuple-element.50), channel_id=1, source_target_pairs={{0,4},{4,0},{8,12},{12,8},{1,5},{5,1},{9,13},{13,9},{2,6},{6,2},{1... | collective-permute-start | bytes 1572872 | tf_op jit(solution)/shard_map/ppermute | solution.py:249
  73.5 8.4 %collective-permute-start.15 = (bf16[128,1024]{1,0:T(8,128)(2,1)S(1)}, bf16[128,1024]{1,0:T(8,128)(2,1)S(1)}, u32[]{:S(2)}, u32[]{:S(2)}) collective-permute-start(bf16[128,1024]{1,0:T(8,128)(2,1)S(1)} %slice.15), channel_id=1, source_target_pairs={{0,8},{4,12},{8,0},{12,4},{1,9},{5,13},{9,1},{13,5},{2,10},{6,14},... | collective-permute-start | bytes 786440 | tf_op jit(solution)/shard_map/ppermute | solution.py:249

commit v5 on v3

--- a/solution.py
+++ b/solution.py
@@ -25,12 +25,12 @@
     return soft, jnp.where(u >= 0.0, r, e * r)
 
 
-def call(body, outs, args, flops, **kw):
+def call(body, outs, args, flops, vmem=24, **kw):
     nbytes = sum(a.size * a.dtype.itemsize for a in args)
     return pl.pallas_call(
         body,
         out_shape=[jax.ShapeDtypeStruct(s, d) for s, d in outs],
-        compiler_params=pltpu.CompilerParams(vmem_limit_bytes=24 * 1024 * 1024),
+        compiler_params=pltpu.CompilerParams(vmem_limit_bytes=vmem * 2**20),
         cost_estimate=pl.CostEstimate(flops=flops, bytes_accessed=nbytes, transcendentals=0),
         **kw,
     )(*args)
@@ -272,6 +272,7 @@
         wouts,
         [key_weight, value_weight, query_weight],
         0,
+        vmem=56,
         in_specs=[HBM] * 3,
         scratch_shapes=[pltpu.SemaphoreType.DMA((5 if split else 3,))],
     ))
@@ -302,7 +303,7 @@
         xs[k] = over_seq(bufs[k // 2], k)
     xs[1] = over_seq(bufs[0], 1)
     arrived = kvs[1:2] + kvs[2::2] if split else kvs[1:]
-    xs[2:], _ = lax.optimization_barrier((xs[2:], arrived[1:]))
+    xs[2:], _ = lax.optimization_barrier((xs[2:], arrived))
     for k in range(3, g, 2):
         xs[k] = over_seq(xs[k ^ 1], 1)
     pieces, _ = lax.optimization_barrier((pieces, arrived + xs[1:2]))

time: 83.2 us -> 77.1 us (0.927)
  waiting for transfers between devices: 45.4 us -> 40.5 us
  local copies, waits for them, and re-layouts: 3.9 us -> 1.62 us
  Pallas kernels: 7.73 us -> 9.56 us
    ppermute x6, waiting for transfers between devices: 25.4 us -> 19.5 us  [over_sub(): return lax.ppermute(x, 'sub', [(i, i ^ k) for i in range(n_sub)])]
    unnamed x14, local copies, waits for them, and re-layouts: 3.86 us -> 1.58 us
    ppermute x2, waiting for transfers between devices: 0.01 us -> 2.05 us  [weight_rows(): far += [part, lax.ppermute(part, 'grp', [(0, 1), (1, 0)])]]
    pallas_call x8, Pallas kernels: 7.73 us -> 9.56 us  [call(): pl.pallas_call(body, out_shape=[jax.ShapeDtypeStruct(s, d) for s, d in ou...]
    ppermute x6, starting transfers between devices: 10.1 us -> 8.97 us  [to_all(): parts.append(lax.ppermute(send, ('seq', 'sub'), perm))]
  transfers between devices with their start and end apart: 19 -> 19, of which waited for: 9 -> 10; matrix products, arithmetic and copies ran while one was open for 0% -> 0% of each run, Pallas kernels for 6% -> 7%
where the time goes in v5:
time: 77.1 us; the launch traced here: 76.9 us
  waiting for transfers between devices  40.5 us (53%)
  starting transfers between devices  23.2 us (30%)
  Pallas kernels  9.56 us (12%)
  other arithmetic  1.89 us (2%)
  local copies, waits for them, and re-layouts  1.62 us (2%)
    ppermute x6, waiting for transfers between devices, over_sub(): return lax.ppermute(x, 'sub', [(i, i ^ k) for i in range(n_sub)])  19.5 us
    ppermute x6, waiting for transfers between devices, to_all(): parts.append(lax.ppermute(send, ('seq', 'sub'), perm))  11 us
    pallas_call x8, Pallas kernels, call(): pl.pallas_call(body, out_shape=[jax.ShapeDtypeStruct(s, d) for s, d in ou...  9.56 us
    ppermute x6, starting transfers between devices, to_all(): parts.append(lax.ppermute(send, ('seq', 'sub'), perm))  8.97 us
    ppermute x5, waiting for transfers between devices, over_seq(): return lax.ppermute(x, 'seq', [(i, i ^ k) for i in range(n_seq)])  8 us
    ppermute x6, starting transfers between devices, over_sub(): return lax.ppermute(x, 'sub', [(i, i ^ k) for i in range(n_sub)])  7.83 us
    ppermute x5, starting transfers between devices, over_seq(): return lax.ppermute(x, 'seq', [(i, i ^ k) for i in range(n_seq)])  4.27 us
    ppermute x2, starting transfers between devices, weight_rows(): far += [part, lax.ppermute(part, 'grp', [(0, 1), (1, 0)])]  2.09 us
  transfers between devices with their start and end apart: 19, of which 10 were waited for; matrix products, arithmetic and copies ran while one was open for 0% of the time, Pallas kernels for 7%

profile of v5, /device:TPU:0, one launch (start us, length us, event | category | flops | bytes accessed | tf_op | source)
XLA Modules:
  0.0 76.9 jit_solution(13266772611046223095)
XLA Ops:
  0.0 2.0 %shard_map.73 = (bf16[256,512]{1,0:T(8,128)(2,1)}, bf16[256,256]{1,0:T(8,128)(2,1)}, bf16[128,512]{1,0:T(8,128)(2,1)}) custom-call(bf16[256,1024]{1,0:T(8,128)(2,1)} %wk.1, bf16[256,1024]{1,0:T(8,128)(2,1)} %wv.1, bf16[256,1024]{1,0:T(8,128)(2,1)} %wq.1), custom_call_target="tpu_custom_call" | custom-call | bytes 1572864 | tf_op jit(solution)/shard_map/pallas_call | solution.py:30
  3.7 3.0 %collective-permute-start.1 = (bf16[128,1536]{1,0:T(8,128)(2,1)S(1)}, bf16[128,1536]{1,0:T(8,128)(2,1)S(1)}, u32[]{:S(2)}, u32[]{:S(2)}) collective-permute-start(bf16[128,1536]{1,0:T(8,128)(2,1)S(1)} %get-tuple-element.35), channel_id=1, source_target_pairs={{0,8},{4,12},{8,0},{12,4},{1,9},{5,13},{9,1},{13,5},{2,10},{6,14},... | collective-permute-start | bytes 1179656 | tf_op jit(solution)/shard_map/ppermute | solution.py:247
  6.8 1.6 %collective-permute-start.2 = (bf16[256,512]{1,0:T(8,128)(2,1)S(1)}, bf16[256,512]{1,0:T(8,128)(2,1)S(1)}, u32[]{:S(2)}, u32[]{:S(2)}) collective-permute-start(bf16[256,512]{1,0:T(8,128)(2,1)S(1)} %copy-done.3), channel_id=1, source_target_pairs={{0,1},{1,0},{2,3},{3,2},{4,5},{5,4},{6,7},{7,6},{8,9},{9,8},{10,11... | collective-permute-start | bytes 786440 | tf_op jit(solution)/shard_map/ppermute | solution.py:250
  8.3 2.5 %collective-permute-start.4 = (bf16[128,512]{1,0:T(8,128)(2,1)S(1)}, bf16[128,512]{1,0:T(8,128)(2,1)S(1)}, u32[]{:S(2)}, u32[]{:S(2)}) collective-permute-start(bf16[128,512]{1,0:T(8,128)(2,1)S(1)} %copy-done.5), channel_id=1, source_target_pairs={{0,3},{1,2},{2,1},{3,0},{4,7},{5,6},{6,5},{7,4},{8,11},{9,10},{10,... | collective-permute-start | bytes 393224 | tf_op jit(solution)/shard_map/ppermute | solution.py:250
  10.9 9.9 %collective-permute-done.4.refs_8_ = bf16[128,512]{1,0:T(8,128)(2,1)S(1)} collective-permute-done((bf16[128,512]{1,0:T(8,128)(2,1)S(1)}, bf16[128,512]{1,0:T(8,128)(2,1)S(1)}, u32[]{:S(2)}, u32[]{:S(2)}) %collective-permute-start.4) | collective-permute-done | bytes 131104 | tf_op jit(solution)/shard_map/ppermute | solution.py:250
  20.9 1.4 %collective-permute-done.3.refs_6_ = bf16[128,512]{1,0:T(8,128)(2,1)S(1)} collective-permute-done((bf16[128,512]{1,0:T(8,128)(2,1)S(1)}, bf16[128,512]{1,0:T(8,128)(2,1)S(1)}, u32[]{:S(2)}, u32[]{:S(2)}) %collective-permute-start.3) | collective-permute-done | bytes 131104 | tf_op jit(solution)/shard_map/ppermute | solution.py:250
  22.3 1.6 %collective-permute-start.7 = (bf16[128,512]{1,0:T(8,128)(2,1)S(1)}, bf16[128,512]{1,0:T(8,128)(2,1)S(1)}, u32[]{:S(2)}, u32[]{:S(2)}) collective-permute-start(bf16[128,512]{1,0:T(8,128)(2,1)S(1)} %collective-permute-done.4.refs_8_), channel_id=1, source_target_pairs={{0,16},{16,0},{1,17},{17,1},{2,18},{18,2},{3,19},{19,3},{4,20},{20... | collective-permute-start | bytes 393224 | tf_op jit(solution)/shard_map/ppermute | solution.py:286
  25.3 2.6 %collective-permute-start.13 = (bf16[256,256]{1,0:T(8,128)(2,1)S(1)}, bf16[256,256]{1,0:T(8,128)(2,1)S(1)}, u32[]{:S(2)}, u32[]{:S(2)}) collective-permute-start(bf16[256,256]{1,0:T(8,128)(2,1)S(1)} %copy-done.4), channel_id=1, source_target_pairs={{0,3},{1,2},{2,1},{3,0},{4,7},{5,6},{6,5},{7,4},{8,11},{9,10},{10,... | collective-permute-start | bytes 393224 | tf_op jit(solution)/shard_map/ppermute | solution.py:250
  28.7 1.0 %collective-permute-start.11 = (bf16[256,256]{1,0:T(8,128)(2,1)S(1)}, bf16[256,256]{1,0:T(8,128)(2,1)S(1)}, u32[]{:S(2)}, u32[]{:S(2)}) collective-permute-start(bf16[256,256]{1,0:T(8,128)(2,1)S(1)} %copy-done.4), channel_id=1, source_target_pairs={{0,1},{1,0},{2,3},{3,2},{4,5},{5,4},{6,7},{7,6},{8,9},{9,8},{10,11... | collective-permute-start | bytes 393224 | tf_op jit(solution)/shard_map/ppermute | solution.py:250
  29.7 1.3 %collective-permute-done.6.refs_7_ = bf16[128,512]{1,0:T(8,128)(2,1)S(1)} collective-permute-done((bf16[128,512]{1,0:T(8,128)(2,1)S(1)}, bf16[128,512]{1,0:T(8,128)(2,1)S(1)}, u32[]{:S(2)}, u32[]{:S(2)}) %collective-permute-start.6) | collective-permute-done | bytes 131104 | tf_op jit(solution)/shard_map/ppermute | solution.py:286
  31.0 2.0 %shard_map.75 = (bf16[1024,512]{1,0:T(8,128)(2,1)S(1)}, bf16[512,512]{1,0:T(8,128)(2,1)S(1)}, f32[512,512]{1,0:T(8,128)S(1)}, bf16[512,256]{1,0:T(8,128)(2,1)S(1...) custom-call(bf16[128,1536]{1,0:T(8,128)(2,1)S(1)} %get-tuple-element.34.refs_0_.refs_4_, ...), custom_call_target="tpu_custom_call" | custom-call | flops 2147483648 | bytes 2752512 | tf_op jit(solution)/shard_map/pallas_call | solution.py:30
  33.0 2.7 %collective-permute-start.10 = (bf16[528,128]{1,0:T(8,128)(2,1)S(1)}, bf16[528,128]{1,0:T(8,128)(2,1)S(1)}, u32[]{:S(2)}, u32[]{:S(2)}) collective-permute-start(bf16[528,128]{1,0:T(8,128)(2,1)S(1)} %get-tuple-element.39), channel_id=1, source_target_pairs={{0,3},{1,2},{2,1},{3,0},{4,7},{5,6},{6,5},{7,4},{8,11},{9,10},{10,... | collective-permute-start | bytes 405512 | tf_op jit(solution)/shard_map/ppermute | solution.py:262
  35.8 1.8 %collective-permute-start.8 = (bf16[528,128]{1,0:T(8,128)(2,1)S(1)}, bf16[528,128]{1,0:T(8,128)(2,1)S(1)}, u32[]{:S(2)}, u32[]{:S(2)}) collective-permute-start(bf16[528,128]{1,0:T(8,128)(2,1)S(1)} %get-tuple-element.39), channel_id=1, source_target_pairs={{0,1},{1,0},{2,3},{3,2},{4,5},{5,4},{6,7},{7,6},{8,9},{9,8},{10,11... | collective-permute-start | bytes 405512 | tf_op jit(solution)/shard_map/ppermute | solution.py:262
  37.6 8.1 %collective-permute-done.12.refs_6_ = bf16[256,256]{1,0:T(8,128)(2,1)S(1)} collective-permute-done((bf16[256,256]{1,0:T(8,128)(2,1)S(1)}, bf16[256,256]{1,0:T(8,128)(2,1)S(1)}, u32[]{:S(2)}, u32[]{:S(2)}) %collective-permute-start.12) | collective-permute-done | bytes 131104 | tf_op jit(solution)/shard_map/ppermute | solution.py:250
  45.6 1.4 %shard_map.76 = (bf16[1024,256]{1,0:T(8,128)(2,1)S(1)}, bf16[512,512]{1,0:T(8,128)(2,1)S(1)}, f32[512,512]{1,0:T(8,128)S(1)}) custom-call(bf16[128,1536]{1,0:T(8,128)(2,1)S(1)} %get-tuple-element.34.refs_0_.refs_4_, bf16[128,1536]{1,0:T(8,128)(2,1)S(1)} %collective-permute-done.refs_1_.refs_5_, bf16[128,1536]{1,0:T(8,128)(2,1)S(1)} %collective-permute-done.1.refs_2_.refs_6_, ...), custom_call_target="tpu_custom_call" | custom-call | flops 2147483648 | bytes 2228224 | tf_op jit(solution)/shard_map/pallas_call | solution.py:30
  47.1 3.5 %collective-permute-done.9.refs_2_ = bf16[528,128]{1,0:T(8,128)(2,1)S(1)} collective-permute-done((bf16[528,128]{1,0:T(8,128)(2,1)S(1)}, bf16[528,128]{1,0:T(8,128)(2,1)S(1)}, u32[]{:S(2)}, u32[]{:S(2)}) %collective-permute-start.9) | collective-permute-done | bytes 135200 | tf_op jit(solution)/shard_map/ppermute | solution.py:262
  51.5 1.7 %collective-permute-start.16 = (bf16[528,128]{1,0:T(8,128)(2,1)S(1)}, bf16[528,128]{1,0:T(8,128)(2,1)S(1)}, u32[]{:S(2)}, u32[]{:S(2)}) collective-permute-start(bf16[528,128]{1,0:T(8,128)(2,1)S(1)} %get-tuple-element.49), channel_id=1, source_target_pairs={{0,3},{1,2},{2,1},{3,0},{4,7},{5,6},{6,5},{7,4},{8,11},{9,10},{10,... | collective-permute-start | bytes 405512 | tf_op jit(solution)/shard_map/ppermute | solution.py:262
  53.2 2.8 %collective-permute-start.14 = (bf16[528,128]{1,0:T(8,128)(2,1)S(1)}, bf16[528,128]{1,0:T(8,128)(2,1)S(1)}, u32[]{:S(2)}, u32[]{:S(2)}) collective-permute-start(bf16[528,128]{1,0:T(8,128)(2,1)S(1)} %get-tuple-element.49), channel_id=1, source_target_pairs={{0,1},{1,0},{2,3},{3,2},{4,5},{5,4},{6,7},{7,6},{8,9},{9,8},{10,11... | collective-permute-start | bytes 405512 | tf_op jit(solution)/shard_map/ppermute | solution.py:262
  56.5 3.5 %collective-permute-done.16.refs_3_ = bf16[528,128]{1,0:T(8,128)(2,1)S(1)} collective-permute-done((bf16[528,128]{1,0:T(8,128)(2,1)S(1)}, bf16[528,128]{1,0:T(8,128)(2,1)S(1)}, u32[]{:S(2)}, u32[]{:S(2)}) %collective-permute-start.16) | collective-permute-done | bytes 135200 | tf_op jit(solution)/shard_map/ppermute | solution.py:262
  60.0 4.0 %collective-permute-done.15.refs_2_ = bf16[528,128]{1,0:T(8,128)(2,1)S(1)} collective-permute-done((bf16[528,128]{1,0:T(8,128)(2,1)S(1)}, bf16[528,128]{1,0:T(8,128)(2,1)S(1)}, u32[]{:S(2)}, u32[]{:S(2)}) %collective-permute-start.15) | collective-permute-done | bytes 135200 | tf_op jit(solution)/shard_map/ppermute | solution.py:262
  64.0 1.6 %shard_map.79 = (bf16[256,1024]{1,0:T(8,128)(2,1)S(1)}, bf16[512,512]{1,0:T(8,128)(2,1)S(1)}) custom-call(f32[528,128]{1,0:T(8,128)S(1)} %get-tuple-element.48.refs_0_, bf16[528,128]{1,0:T(8,128)(2,1)S(1)} %collective-permute-done.14.refs_1_, bf16[528,128]{1,0:T(8,128)(2,1)S(1)} %collective-permute-done.15.refs_2_, ...), custom_call_target="tpu_custom_call" | custom-call | flops 2147483648 | bytes 4476928 | tf_op jit(solution)/shard_map/pallas_call | solution.py:30
  65.7 1.1 %shard_map.80 = f32[256,1024]{1,0:T(8,128)S(1)} custom-call(bf16[512,256]{1,0:T(8,128)(2,1)S(1)} %shard_map.78.refs_8_.qg, bf16[512,512]{1,0:T(8,128)(2,1)S(1)} %get-tuple-element.55.kvg, bf16[1024,256]{1,0:T(8,128)(2,1)S(1)} %get-tuple-element.53.refs_9_.wq, bf16[1024,512]{1,0:T(8,128)(2,1)S(1)} %get-tuple-element.54.refs_10_.wkv), custom_call_target="tpu_custom_call" | custom-call | flops 2147483648 | bytes 2359296 | tf_op jit(solution)/shard_map/pallas_call | solution.py:30
  67.7 1.1 %collective-permute-start.18 = (bf16[128,1024]{1,0:T(8,128)(2,1)S(1)}, bf16[128,1024]{1,0:T(8,128)(2,1)S(1)}, u32[]{:S(2)}, u32[]{:S(2)}) collective-permute-start(bf16[128,1024]{1,0:T(8,128)(2,1)S(1)} %slice.15), channel_id=1, source_target_pairs={{0,8},{4,12},{8,0},{12,4},{1,9},{5,13},{9,1},{13,5},{2,10},{6,14},... | collective-permute-start | bytes 786440 | tf_op jit(solution)/shard_map/ppermute | solution.py:247
  68.9 7.3 %collective-permute-done.18 = bf16[128,1024]{1,0:T(8,128)(2,1)S(1)} collective-permute-done((bf16[128,1024]{1,0:T(8,128)(2,1)S(1)}, bf16[128,1024]{1,0:T(8,128)(2,1)S(1)}, u32[]{:S(2)}, u32[]{:S(2)}) %collective-permute-start.18) | collective-permute-done | bytes 262176 | tf_op jit(solution)/shard_map/ppermute | solution.py:247
  (43 shorter events, 7.2 us)
Async XLA Ops:
  0.0 24.4 %copy-start = (bf16[8,128,256]{2,1,0:T(8,128)(2,1)S(1)}, bf16[8,128,256]{2,1,0:T(8,128)(2,1)}, u32[]{:S(2)}) copy-start(bf16[8,128,256]{2,1,0:T(8,128)(2,1)} %param.13) | copy-start | bytes 1572868
  2.6 1.0 %copy-start.1 = (bf16[128,1024]{1,0:T(8,128)(2,1)S(1)}, bf16[128,1024]{1,0:T(8,128)(2,1)}, u32[]{:S(2)}) copy-start(bf16[128,1024]{1,0:T(8,128)(2,1)} %events) | copy-start | bytes 786436
  2.6 1.0 %copy-start.2 = (bf16[128,1024]{1,0:T(8,128)(2,1)S(1)}, bf16[128,1024]{1,0:T(8,128)(2,1)}, u32[]{:S(2)}) copy-start(bf16[128,1024]{1,0:T(8,128)(2,1)} %cot.1) | copy-start | bytes 786436
  3.7 3.1 %copy-start.3 = (bf16[256,512]{1,0:T(8,128)(2,1)S(1)}, bf16[256,512]{1,0:T(8,128)(2,1)}, u32[]{:S(2)}) copy-start(bf16[256,512]{1,0:T(8,128)(2,1)} %get-tuple-element.31.refs_4_) | copy-start | bytes 786436
  3.7 4.7 %copy-start.5 = (bf16[128,512]{1,0:T(8,128)(2,1)S(1)}, bf16[128,512]{1,0:T(8,128)(2,1)}, u32[]{:S(2)}) copy-start(bf16[128,512]{1,0:T(8,128)(2,1)} %get-tuple-element.36) | copy-start | bytes 393220
  3.7 18.6 %collective-permute-start.1 = (bf16[128,1536]{1,0:T(8,128)(2,1)S(1)}, bf16[128,1536]{1,0:T(8,128)(2,1)S(1)}, u32[]{:S(2)}, u32[]{:S(2)}) collective-permute-start(bf16[128,1536]{1,0:T(8,128)(2,1)S(1)} %get-tuple-element.35), channel_id=1, source_target_pairs={{0,8},{4,12},{8,0},{12,4},{1,9},{5,13},{9,1},{13,5},{2,10},{6,14},... | collective-permute-start | bytes 1179656 | tf_op jit(solution)/shard_map/ppermute | solution.py:247
  6.8 15.5 %collective-permute-start.2 = (bf16[256,512]{1,0:T(8,128)(2,1)S(1)}, bf16[256,512]{1,0:T(8,128)(2,1)S(1)}, u32[]{:S(2)}, u32[]{:S(2)}) collective-permute-start(bf16[256,512]{1,0:T(8,128)(2,1)S(1)} %copy-done.3), channel_id=1, source_target_pairs={{0,1},{1,0},{2,3},{3,2},{4,5},{5,4},{6,7},{7,6},{8,9},{9,8},{10,11... | collective-permute-start | bytes 786440 | tf_op jit(solution)/shard_map/ppermute | solution.py:250
  8.3 12.5 %collective-permute-start.4 = (bf16[128,512]{1,0:T(8,128)(2,1)S(1)}, bf16[128,512]{1,0:T(8,128)(2,1)S(1)}, u32[]{:S(2)}, u32[]{:S(2)}) collective-permute-start(bf16[128,512]{1,0:T(8,128)(2,1)S(1)} %copy-done.5), channel_id=1, source_target_pairs={{0,3},{1,2},{2,1},{3,0},{4,7},{5,6},{6,5},{7,4},{8,11},{9,10},{10,... | collective-permute-start | bytes 393224 | tf_op jit(solution)/shard_map/ppermute | solution.py:250
  10.8 11.5 %collective-permute-start.3 = (bf16[128,512]{1,0:T(8,128)(2,1)S(1)}, bf16[128,512]{1,0:T(8,128)(2,1)S(1)}, u32[]{:S(2)}, u32[]{:S(2)}) collective-permute-start(bf16[128,512]{1,0:T(8,128)(2,1)S(1)} %copy-done.5), channel_id=1, source_target_pairs={{0,2},{1,3},{2,0},{3,1},{4,6},{5,7},{6,4},{7,5},{8,10},{9,11},{10,... | collective-permute-start | bytes 393224 | tf_op jit(solution)/shard_map/ppermute | solution.py:250
  10.9 13.5 %collective-permute-start = (bf16[128,1536]{1,0:T(8,128)(2,1)S(1)}, bf16[128,1536]{1,0:T(8,128)(2,1)S(1)}, u32[]{:S(2)}, u32[]{:S(2)}) collective-permute-start(bf16[128,1536]{1,0:T(8,128)(2,1)S(1)} %get-tuple-element.34.refs_0_.refs_4_), channel_id=1, source_target_pairs={{0,4},{4,0},{8,12},{12,8},{1,5},{5,1},{9,13},{13,9},{2,6},{6,2},{1... | collective-permute-start | bytes 1179656 | tf_op jit(solution)/shard_map/ppermute | solution.py:247
  22.3 8.7 %collective-permute-start.5 = (bf16[128,1536]{1,0:T(8,128)(2,1)S(1)}, bf16[128,1536]{1,0:T(8,128)(2,1)S(1)}, u32[]{:S(2)}, u32[]{:S(2)}) collective-permute-start(bf16[128,1536]{1,0:T(8,128)(2,1)S(1)} %collective-permute-done.1.refs_2_.refs_6_), channel_id=1, source_target_pairs={{0,4},{4,0},{8,12},{12,8},{1,5},{5,1},{9,13},{13,9},{2,6},{6,2},{1... | collective-permute-start | bytes 1179656 | tf_op jit(solution)/shard_map/ppermute | solution.py:247
  22.3 6.4 %collective-permute-start.7 = (bf16[128,512]{1,0:T(8,128)(2,1)S(1)}, bf16[128,512]{1,0:T(8,128)(2,1)S(1)}, u32[]{:S(2)}, u32[]{:S(2)}) collective-permute-start(bf16[128,512]{1,0:T(8,128)(2,1)S(1)} %collective-permute-done.4.refs_8_), channel_id=1, source_target_pairs={{0,16},{16,0},{1,17},{17,1},{2,18},{18,2},{3,19},{19,3},{4,20},{20... | collective-permute-start | bytes 393224 | tf_op jit(solution)/shard_map/ppermute | solution.py:286
  23.9 7.1 %collective-permute-start.6 = (bf16[128,512]{1,0:T(8,128)(2,1)S(1)}, bf16[128,512]{1,0:T(8,128)(2,1)S(1)}, u32[]{:S(2)}, u32[]{:S(2)}) collective-permute-start(bf16[128,512]{1,0:T(8,128)(2,1)S(1)} %collective-permute-done.3.refs_6_), channel_id=1, source_target_pairs={{0,16},{16,0},{1,17},{17,1},{2,18},{18,2},{3,19},{19,3},{4,20},{20... | collective-permute-start | bytes 393224 | tf_op jit(solution)/shard_map/ppermute | solution.py:286
  25.3 10.4 %collective-permute-start.13 = (bf16[256,256]{1,0:T(8,128)(2,1)S(1)}, bf16[256,256]{1,0:T(8,128)(2,1)S(1)}, u32[]{:S(2)}, u32[]{:S(2)}) collective-permute-start(bf16[256,256]{1,0:T(8,128)(2,1)S(1)} %copy-done.4), channel_id=1, source_target_pairs={{0,3},{1,2},{2,1},{3,0},{4,7},{5,6},{6,5},{7,4},{8,11},{9,10},{10,... | collective-permute-start | bytes 393224 | tf_op jit(solution)/shard_map/ppermute | solution.py:250
  27.9 17.7 %collective-permute-start.12 = (bf16[256,256]{1,0:T(8,128)(2,1)S(1)}, bf16[256,256]{1,0:T(8,128)(2,1)S(1)}, u32[]{:S(2)}, u32[]{:S(2)}) collective-permute-start(bf16[256,256]{1,0:T(8,128)(2,1)S(1)} %copy-done.4), channel_id=1, source_target_pairs={{0,2},{1,3},{2,0},{3,1},{4,6},{5,7},{6,4},{7,5},{8,10},{9,11},{10,... | collective-permute-start | bytes 393224 | tf_op jit(solution)/shard_map/ppermute | solution.py:250
  28.7 17.0 %collective-permute-start.11 = (bf16[256,256]{1,0:T(8,128)(2,1)S(1)}, bf16[256,256]{1,0:T(8,128)(2,1)S(1)}, u32[]{:S(2)}, u32[]{:S(2)}) collective-permute-start(bf16[256,256]{1,0:T(8,128)(2,1)S(1)} %copy-done.4), channel_id=1, source_target_pairs={{0,1},{1,0},{2,3},{3,2},{4,5},{5,4},{6,7},{7,6},{8,9},{9,8},{10,11... | collective-permute-start | bytes 393224 | tf_op jit(solution)/shard_map/ppermute | solution.py:250
  33.0 14.0 %collective-permute-start.10 = (bf16[528,128]{1,0:T(8,128)(2,1)S(1)}, bf16[528,128]{1,0:T(8,128)(2,1)S(1)}, u32[]{:S(2)}, u32[]{:S(2)}) collective-permute-start(bf16[528,128]{1,0:T(8,128)(2,1)S(1)} %get-tuple-element.39), channel_id=1, source_target_pairs={{0,3},{1,2},{2,1},{3,0},{4,7},{5,6},{6,5},{7,4},{8,11},{9,10},{10,... | collective-permute-start | bytes 405512 | tf_op jit(solution)/shard_map/ppermute | solution.py:262
  35.7 14.9 %collective-permute-start.9 = (bf16[528,128]{1,0:T(8,128)(2,1)S(1)}, bf16[528,128]{1,0:T(8,128)(2,1)S(1)}, u32[]{:S(2)}, u32[]{:S(2)}) collective-permute-start(bf16[528,128]{1,0:T(8,128)(2,1)S(1)} %get-tuple-element.39), channel_id=1, source_target_pairs={{0,2},{1,3},{2,0},{3,1},{4,6},{5,7},{6,4},{7,5},{8,10},{9,11},{10,... | collective-permute-start | bytes 405512 | tf_op jit(solution)/shard_map/ppermute | solution.py:262
  35.8 14.9 %collective-permute-start.8 = (bf16[528,128]{1,0:T(8,128)(2,1)S(1)}, bf16[528,128]{1,0:T(8,128)(2,1)S(1)}, u32[]{:S(2)}, u32[]{:S(2)}) collective-permute-start(bf16[528,128]{1,0:T(8,128)(2,1)S(1)} %get-tuple-element.39), channel_id=1, source_target_pairs={{0,1},{1,0},{2,3},{3,2},{4,5},{5,4},{6,7},{7,6},{8,9},{9,8},{10,11... | collective-permute-start | bytes 405512 | tf_op jit(solution)/shard_map/ppermute | solution.py:262
  51.5 8.5 %collective-permute-start.16 = (bf16[528,128]{1,0:T(8,128)(2,1)S(1)}, bf16[528,128]{1,0:T(8,128)(2,1)S(1)}, u32[]{:S(2)}, u32[]{:S(2)}) collective-permute-start(bf16[528,128]{1,0:T(8,128)(2,1)S(1)} %get-tuple-element.49), channel_id=1, source_target_pairs={{0,3},{1,2},{2,1},{3,0},{4,7},{5,6},{6,5},{7,4},{8,11},{9,10},{10,... | collective-permute-start | bytes 405512 | tf_op jit(solution)/shard_map/ppermute | solution.py:262
  53.2 10.8 %collective-permute-start.15 = (bf16[528,128]{1,0:T(8,128)(2,1)S(1)}, bf16[528,128]{1,0:T(8,128)(2,1)S(1)}, u32[]{:S(2)}, u32[]{:S(2)}) collective-permute-start(bf16[528,128]{1,0:T(8,128)(2,1)S(1)} %get-tuple-element.49), channel_id=1, source_target_pairs={{0,2},{1,3},{2,0},{3,1},{4,6},{5,7},{6,4},{7,5},{8,10},{9,11},{10,... | collective-permute-start | bytes 405512 | tf_op jit(solution)/shard_map/ppermute | solution.py:262
  53.2 10.8 %collective-permute-start.14 = (bf16[528,128]{1,0:T(8,128)(2,1)S(1)}, bf16[528,128]{1,0:T(8,128)(2,1)S(1)}, u32[]{:S(2)}, u32[]{:S(2)}) collective-permute-start(bf16[528,128]{1,0:T(8,128)(2,1)S(1)} %get-tuple-element.49), channel_id=1, source_target_pairs={{0,1},{1,0},{2,3},{3,2},{4,5},{5,4},{6,7},{7,6},{8,9},{9,8},{10,11... | collective-permute-start | bytes 405512 | tf_op jit(solution)/shard_map/ppermute | solution.py:262
  65.6 2.0 %collective-permute-start.17 = (bf16[256,1024]{1,0:T(8,128)(2,1)S(1)}, bf16[256,1024]{1,0:T(8,128)(2,1)S(1)}, u32[]{:S(2)}, u32[]{:S(2)}) collective-permute-start(bf16[256,1024]{1,0:T(8,128)(2,1)S(1)} %get-tuple-element.56), channel_id=1, source_target_pairs={{0,4},{4,0},{8,12},{12,8},{1,5},{5,1},{9,13},{13,9},{2,6},{6,2},{1... | collective-permute-start | bytes 1572872 | tf_op jit(solution)/shard_map/ppermute | solution.py:247
  67.7 8.4 %collective-permute-start.18 = (bf16[128,1024]{1,0:T(8,128)(2,1)S(1)}, bf16[128,1024]{1,0:T(8,128)(2,1)S(1)}, u32[]{:S(2)}, u32[]{:S(2)}) collective-permute-start(bf16[128,1024]{1,0:T(8,128)(2,1)S(1)} %slice.15), channel_id=1, source_target_pairs={{0,8},{4,12},{8,0},{12,4},{1,9},{5,13},{9,1},{13,5},{2,10},{6,14},... | collective-permute-start | bytes 786440 | tf_op jit(solution)/shard_map/ppermute | solution.py:247
  (2 other events, 1.6 us)

commit v6 on v5

--- a/solution.py
+++ b/solution.py
@@ -36,34 +36,39 @@
     )(*args)
 
 
-def weight_kernel(g, cols, split, wk, wv, wq, *refs):
-    outs, sems = refs[:-1], refs[-1]
-    at = pl.ds(pl.multiple_of((lax.axis_index("seq") % g) * cols, cols), cols)
-    pairs = [(wk.at[:, at], outs[0].at[:, :cols]), (wv.at[:, at], outs[0].at[:, cols:]), (wq.at[:, at], outs[1])]
+def first_kernel(g, cols, split, *refs):
+    wk, wv, wq, events, offsets, frequency, cot = refs[:7]
+    n = 4 if split else 2
+    pieces, bufs, sems = refs[7 : 7 + n], refs[7 + n : -1], refs[-1]
+    mine = lax.axis_index("seq") % g
+    at = pl.ds(pl.multiple_of(mine * cols, cols), cols)
+    pairs = [(wk.at[:, at], pieces[0].at[:, :cols]), (wv.at[:, at], pieces[0].at[:, cols:]), (wq.at[:, at], pieces[1])]
     if split:
         half = wk.shape[0] // 2
         rows = pl.ds(pl.multiple_of(lax.axis_index("grp") * half, half), half)
         pairs += [
-            (wk.at[rows, at], outs[2].at[:, :cols]),
-            (wv.at[rows, at], outs[2].at[:, cols:]),
+            (wk.at[rows, at], pieces[2].at[:, :cols]),
+            (wv.at[rows, at], pieces[2].at[:, cols:]),
+            (wq.at[rows, at], pieces[3]),
         ]
     copies = [pltpu.make_async_copy(a, b, sems.at[i]) for i, (a, b) in enumerate(pairs)]
     for c in copies:
         c.start()
+    tokens, width = events.shape
+    half = width // 2
+    lanes = 128
+    column = jnp.transpose(jnp.broadcast_to(offsets[...].astype(F32), (lanes, tokens)))
+    for j in range(0, half, lanes):
+        angle = column * frequency[:, j : j + lanes]
+        for value, start in ((jnp.sin(angle), j), (jnp.cos(angle), half + j)):
+            to = slice(start, start + lanes)
+            x = (events[:, to].astype(F32) + value).astype(BF16)
+            for buf in bufs:
+                buf[:, to] = x
+    for k, buf in enumerate(bufs):
+        buf[:, width:] = cot[:, pl.ds(pl.multiple_of(((mine // 2) ^ k) * 2 * cols, 2 * cols), 2 * cols)]
     for c in copies:
         c.wait()
-
-
-def input_kernel(g, pair, events, sines, cosines, cot, *outs):
-    width = events.shape[1]
-    half = width // 2
-    mine = (lax.axis_index("seq") % g) // 2
-    left = (events[:, :half].astype(F32) + sines[...]).astype(BF16)
-    right = (events[:, half:].astype(F32) + cosines[...]).astype(BF16)
-    for k, out in enumerate(outs):
-        out[:, :half] = left
-        out[:, half:width] = right
-        out[:, width:] = cot[:, pl.ds(pl.multiple_of((mine ^ k) * pair, pair), pair)]
 
 
 def place_rows(full, parts, n):
@@ -264,50 +269,45 @@
 
     wrows = key_weight.shape[0]
     split = lax.axis_size("grp") == 2 and wrows % 32 == 0
-    wouts = [((wrows, 2 * cols), BF16), ((wrows, cols), BF16)]
-    if split:
-        wouts.append(((wrows // 2, 2 * cols), BF16))
-    pieces = list(call(
-        functools.partial(weight_kernel, g, cols, split),
-        wouts,
-        [key_weight, value_weight, query_weight],
+    wouts = [((wrows, 2 * cols), BF16), ((wrows, cols), BF16), ((wrows // 2, 2 * cols), BF16), ((wrows // 2, cols), BF16)]
+    wouts = wouts if split else wouts[:2]
+    n = len(wouts)
+    frequency = jnp.exp(jnp.arange(width // 2, dtype=F32) * (-2.0 * math.log(10000.0) / width))
+    whole = pl.BlockSpec(memory_space=pltpu.VMEM)
+    firsts = call(
+        functools.partial(first_kernel, g, cols, split),
+        wouts + [((rows, width + 2 * cols), BF16)] * (g // 2),
+        [key_weight, value_weight, query_weight, events, offsets[None], frequency[None], cotangent],
         0,
         vmem=56,
-        in_specs=[HBM] * 3,
-        scratch_shapes=[pltpu.SemaphoreType.DMA((5 if split else 3,))],
-    ))
-
-    def weight_rows(i, split):
+        in_specs=[HBM] * 3 + [whole] * 4,
+        out_specs=[HBM] * n + [whole] * (g // 2),
+        scratch_shapes=[pltpu.SemaphoreType.DMA((6 if split else 3,))],
+    )
+    pieces, bufs = firsts[:n], firsts[n:]
+
+    def from_sub(i):
+        return [over_sub(pieces[i], 1)] + [over_sub(pieces[i + 2 if split else i], k) for k in range(2, n_sub)]
+
+    def weight_rows(i, arrived):
         if not split:
-            return [pieces[i]] + [over_sub(pieces[i], k) for k in range(1, n_sub)]
+            return [pieces[i]] + arrived
         far = []
-        for k in range(2, n_sub):
-            part = over_sub(pieces[i + 2], k)
+        for part in arrived[1:]:
             far += [part, lax.ppermute(part, "grp", [(0, 1), (1, 0)])]
-        return [pieces[i], over_sub(pieces[i], 1)] + far
-
-    kvs = weight_rows(0, split)
-
-    events, offsets, _ = lax.optimization_barrier((events, offsets, pieces[0]))
-    half = width // 2
-    frequency = jnp.exp(jnp.arange(half, dtype=F32) * (-2.0 * math.log(10000.0) / width))
-    angles = offsets.astype(F32)[:, None] * frequency[None, :]
-    bufs = call(
-        functools.partial(input_kernel, g, 2 * cols),
-        [((rows, width + 2 * cols), BF16)] * (g // 2),
-        [events, jnp.sin(angles), jnp.cos(angles), cotangent],
-        16 * 2**30,
-    )
+        return [pieces[i], arrived[0]] + far
+
+    arrived = from_sub(0)
+    kvs = weight_rows(0, arrived)
     xs = [bufs[0]] * g
     for k in range(2, g, 2):
         xs[k] = over_seq(bufs[k // 2], k)
     xs[1] = over_seq(bufs[0], 1)
-    arrived = kvs[1:2] + kvs[2::2] if split else kvs[1:]
     xs[2:], _ = lax.optimization_barrier((xs[2:], arrived))
     for k in range(3, g, 2):
         xs[k] = over_seq(xs[k ^ 1], 1)
     pieces, _ = lax.optimization_barrier((pieces, arrived + xs[1:2]))
-    qs = weight_rows(1, False)
+    query_rows = from_sub(1)
     om = lax.dynamic_slice_in_dim(omega, (lax.axis_index("seq") % g) * hp, hp, 0)
 
     flop = 2 * t * width * cols
@@ -319,6 +319,8 @@
         8 * flop,
     )
     summary = to_all(own, send)
+    query_rows, _ = lax.optimization_barrier((query_rows, val))
+    qs = weight_rows(1, query_rows)
     wq_full, query_feat, query_sig = call(
         functools.partial(query_kernel, g, n_sub, len(qs), hp, width),
         [((width, cols), BF16), ((t, hp * m), BF16), ((t, hp * m), F32)],

time: 77.1 us -> 95.4 us (1.24)
  Pallas kernels: 9.56 us -> 28.5 us
    pallas_call x8 -> x7, Pallas kernels: 9.56 us -> 28.5 us  [call(): pl.pallas_call(body, out_shape=[jax.ShapeDtypeStruct(s, d) for s, d in ou...]
    ppermute x6, waiting for transfers between devices: 19.5 us -> 12.8 us  [over_sub(): return lax.ppermute(x, 'sub', [(i, i ^ k) for i in range(n_sub)])]
    ppermute x6, waiting for transfers between devices: 11 us -> 15.3 us  [to_all(): parts.append(lax.ppermute(send, ('seq', 'sub'), perm))]
    ppermute x2 -> x4, starting transfers between devices: 2.09 us -> 4.12 us  [weight_rows(): far += [part, lax.ppermute(part, 'grp', [(0, 1), (1, 0)])]]
    ppermute x2 -> x4, waiting for transfers between devices: 2.05 us -> 3.36 us  [weight_rows(): far += [part, lax.ppermute(part, 'grp', [(0, 1), (1, 0)])]]
    cos x1 -> x0, other arithmetic: 0.98 us -> none  [local(): jnp.cos(angles)]
  transfers between devices with their start and end apart: 19 -> 21, of which waited for: 10 -> 11; matrix products, arithmetic and copies ran while one was open for 0% -> 0% of each run, Pallas kernels for 7% -> 5%
where the time goes in v6:
time: 95.4 us; the launch traced here: 95.3 us
  waiting for transfers between devices  40 us (42%)
  Pallas kernels  28.5 us (30%)
  starting transfers between devices  24 us (25%)
  other arithmetic  1.51 us (2%)
  local copies, waits for them, and re-layouts  1.05 us (1%)
    pallas_call x7, Pallas kernels, call(): pl.pallas_call(body, out_shape=[jax.ShapeDtypeStruct(s, d) for s, d in ou...  28.5 us
    ppermute x6, waiting for transfers between devices, to_all(): parts.append(lax.ppermute(send, ('seq', 'sub'), perm))  15.3 us
    ppermute x6, waiting for transfers between devices, over_sub(): return lax.ppermute(x, 'sub', [(i, i ^ k) for i in range(n_sub)])  12.8 us
    ppermute x6, starting transfers between devices, to_all(): parts.append(lax.ppermute(send, ('seq', 'sub'), perm))  8.84 us
    ppermute x5, waiting for transfers between devices, over_seq(): return lax.ppermute(x, 'seq', [(i, i ^ k) for i in range(n_seq)])  8.57 us
    ppermute x6, starting transfers between devices, over_sub(): return lax.ppermute(x, 'sub', [(i, i ^ k) for i in range(n_sub)])  7.4 us
    ppermute x4, starting transfers between devices, weight_rows(): far += [part, lax.ppermute(part, 'grp', [(0, 1), (1, 0)])]  4.12 us
    ppermute x5, starting transfers between devices, over_seq(): return lax.ppermute(x, 'seq', [(i, i ^ k) for i in range(n_seq)])  3.68 us
  transfers between devices with their start and end apart: 21, of which 11 were waited for; matrix products, arithmetic and copies ran while one was open for 0% of the time, Pallas kernels for 5%

profile of v6, /device:TPU:0, one launch (start us, length us, event | category | flops | bytes accessed | tf_op | source)
XLA Modules:
  0.0 95.3 jit_solution(7537728059345386509)
XLA Ops:
  0.6 21.0 %shard_map.73 = (bf16[256,512]{1,0:T(8,128)(2,1)}, bf16[256,256]{1,0:T(8,128)(2,1)}, bf16[128,512]{1,0:T(8,128)(2,1)}, bf16[128,256]{1,0:T(8,128)(2,1)}, bf16[12...) custom-call(bf16[256,1024]{1,0:T(8,128)(2,1)} %refs_0_.1, bf16[256,1024]{1,0:T(8,128)(2,1)} %refs_1_.1, ...), custom_call_target="tpu_custom_call" | custom-call | bytes 2099712 | tf_op jit(solution)/shard_map/pallas_call | solution.py:30
  21.6 3.0 %collective-permute-start.1 = (bf16[128,1536]{1,0:T(8,128)(2,1)}, bf16[128,1536]{1,0:T(8,128)(2,1)S(1)}, u32[]{:S(2)}, u32[]{:S(2)}) collective-permute-start(bf16[128,1536]{1,0:T(8,128)(2,1)} %get-tuple-element.35), channel_id=1, source_target_pairs={{0,8},{4,12},{8,0},{12,4},{1,9},{5,13},{9,1},{13,5},{2,10},{6,14},... | collective-permute-start | bytes 1179656 | tf_op jit(solution)/shard_map/ppermute | solution.py:252
  24.6 1.6 %collective-permute-start.2 = (bf16[256,512]{1,0:T(8,128)(2,1)}, bf16[256,512]{1,0:T(8,128)(2,1)S(1)}, u32[]{:S(2)}, u32[]{:S(2)}) collective-permute-start(bf16[256,512]{1,0:T(8,128)(2,1)} %get-tuple-element.36.refs_4_), channel_id=1, source_target_pairs={{0,1},{1,0},{2,3},{3,2},{4,5},{5,4},{6,7},{7,6},{8,9},{9,8},{10,11... | collective-permute-start | bytes 786440 | tf_op jit(solution)/shard_map/ppermute | solution.py:255
  26.2 2.5 %collective-permute-start.4 = (bf16[128,512]{1,0:T(8,128)(2,1)}, bf16[128,512]{1,0:T(8,128)(2,1)S(1)}, u32[]{:S(2)}, u32[]{:S(2)}) collective-permute-start(bf16[128,512]{1,0:T(8,128)(2,1)} %get-tuple-element.37), channel_id=1, source_target_pairs={{0,3},{1,2},{2,1},{3,0},{4,7},{5,6},{6,5},{7,4},{8,11},{9,10},{10,... | collective-permute-start | bytes 393224 | tf_op jit(solution)/shard_map/ppermute | solution.py:255
  28.8 10.1 %collective-permute-done.4.refs_8_ = bf16[128,512]{1,0:T(8,128)(2,1)S(1)} collective-permute-done((bf16[128,512]{1,0:T(8,128)(2,1)}, bf16[128,512]{1,0:T(8,128)(2,1)S(1)}, u32[]{:S(2)}, u32[]{:S(2)}) %collective-permute-start.4) | collective-permute-done | bytes 131104 | tf_op jit(solution)/shard_map/ppermute | solution.py:255
  38.9 1.4 %collective-permute-done.3.refs_6_ = bf16[128,512]{1,0:T(8,128)(2,1)S(1)} collective-permute-done((bf16[128,512]{1,0:T(8,128)(2,1)}, bf16[128,512]{1,0:T(8,128)(2,1)S(1)}, u32[]{:S(2)}, u32[]{:S(2)}) %collective-permute-start.3) | collective-permute-done | bytes 131104 | tf_op jit(solution)/shard_map/ppermute | solution.py:255
  40.4 1.6 %collective-permute-start.7 = (bf16[128,512]{1,0:T(8,128)(2,1)S(1)}, bf16[128,512]{1,0:T(8,128)(2,1)S(1)}, u32[]{:S(2)}, u32[]{:S(2)}) collective-permute-start(bf16[128,512]{1,0:T(8,128)(2,1)S(1)} %collective-permute-done.4.refs_8_), channel_id=1, source_target_pairs={{0,16},{16,0},{1,17},{17,1},{2,18},{18,2},{3,19},{19,3},{4,20},{20... | collective-permute-start | bytes 393224 | tf_op jit(solution)/shard_map/ppermute | solution.py:297
  42.5 2.7 %collective-permute-start.13 = (bf16[128,256]{1,0:T(8,128)(2,1)}, bf16[128,256]{1,0:T(8,128)(2,1)S(1)}, u32[]{:S(2)}, u32[]{:S(2)}) collective-permute-start(bf16[128,256]{1,0:T(8,128)(2,1)} %get-tuple-element.44), channel_id=1, source_target_pairs={{0,3},{1,2},{2,1},{3,0},{4,7},{5,6},{6,5},{7,4},{8,11},{9,10},{10,... | collective-permute-start | bytes 196616 | tf_op jit(solution)/shard_map/ppermute | solution.py:255
  45.2 1.5 %collective-permute-done.7.refs_9_ = bf16[128,512]{1,0:T(8,128)(2,1)S(1)} collective-permute-done((bf16[128,512]{1,0:T(8,128)(2,1)S(1)}, bf16[128,512]{1,0:T(8,128)(2,1)S(1)}, u32[]{:S(2)}, u32[]{:S(2)}) %collective-permute-start.7) | collective-permute-done | bytes 131104 | tf_op jit(solution)/shard_map/ppermute | solution.py:297
  47.3 1.8 %collective-permute-done.6.refs_7_ = bf16[128,512]{1,0:T(8,128)(2,1)S(1)} collective-permute-done((bf16[128,512]{1,0:T(8,128)(2,1)S(1)}, bf16[128,512]{1,0:T(8,128)(2,1)S(1)}, u32[]{:S(2)}, u32[]{:S(2)}) %collective-permute-start.6) | collective-permute-done | bytes 131104 | tf_op jit(solution)/shard_map/ppermute | solution.py:297
  50.1 2.0 %shard_map.74 = (bf16[1024,512]{1,0:T(8,128)(2,1)S(1)}, bf16[512,512]{1,0:T(8,128)(2,1)S(1)}, f32[512,512]{1,0:T(8,128)S(1)}, bf16[512,256]{1,0:T(8,128)(2,1)S(1...) custom-call(bf16[128,1536]{1,0:T(8,128)(2,1)S(1)} %copy-done.1, ...), custom_call_target="tpu_custom_call" | custom-call | flops 2147483648 | bytes 2752512 | tf_op jit(solution)/shard_map/pallas_call | solution.py:30
  52.1 1.2 %collective-permute-done.11.refs_5_ = bf16[256,256]{1,0:T(8,128)(2,1)S(1)} collective-permute-done((bf16[256,256]{1,0:T(8,128)(2,1)}, bf16[256,256]{1,0:T(8,128)(2,1)S(1)}, u32[]{:S(2)}, u32[]{:S(2)}) %collective-permute-start.11) | collective-permute-done | bytes 131104 | tf_op jit(solution)/shard_map/ppermute | solution.py:255
  53.3 1.5 %collective-permute-start.14 = (bf16[128,256]{1,0:T(8,128)(2,1)S(1)}, bf16[128,256]{1,0:T(8,128)(2,1)S(1)}, u32[]{:S(2)}, u32[]{:S(2)}) collective-permute-start(bf16[128,256]{1,0:T(8,128)(2,1)S(1)} %collective-permute-done.12.refs_6_), channel_id=1, source_target_pairs={{0,16},{16,0},{1,17},{17,1},{2,18},{18,2},{3,19},{19,3},{4,20},{20... | collective-permute-start | bytes 196616 | tf_op jit(solution)/shard_map/ppermute | solution.py:297
  55.4 2.6 %collective-permute-start.10 = (bf16[528,128]{1,0:T(8,128)(2,1)S(1)}, bf16[528,128]{1,0:T(8,128)(2,1)S(1)}, u32[]{:S(2)}, u32[]{:S(2)}) collective-permute-start(bf16[528,128]{1,0:T(8,128)(2,1)S(1)} %get-tuple-element.40), channel_id=1, source_target_pairs={{0,3},{1,2},{2,1},{3,0},{4,7},{5,6},{6,5},{7,4},{8,11},{9,10},{10,... | collective-permute-start | bytes 405512 | tf_op jit(solution)/shard_map/ppermute | solution.py:267
  57.9 1.8 %collective-permute-start.8 = (bf16[528,128]{1,0:T(8,128)(2,1)S(1)}, bf16[528,128]{1,0:T(8,128)(2,1)S(1)}, u32[]{:S(2)}, u32[]{:S(2)}) collective-permute-start(bf16[528,128]{1,0:T(8,128)(2,1)S(1)} %get-tuple-element.40), channel_id=1, source_target_pairs={{0,1},{1,0},{2,3},{3,2},{4,5},{5,4},{6,7},{7,6},{8,9},{9,8},{10,11... | collective-permute-start | bytes 405512 | tf_op jit(solution)/shard_map/ppermute | solution.py:267
  59.8 1.4 %shard_map.75 = (bf16[1024,256]{1,0:T(8,128)(2,1)S(1)}, bf16[512,512]{1,0:T(8,128)(2,1)S(1)}, f32[512,512]{1,0:T(8,128)S(1)}) custom-call(bf16[128,1536]{1,0:T(8,128)(2,1)S(1)} %copy-done.2, bf16[128,1536]{1,0:T(8,128)(2,1)S(1)} %collective-permute-done.refs_1_.refs_5_, bf16[128,1536]{1,0:T(8,128)(2,1)S(1)} %collective-permute-done.1.refs_2_.refs_6_, ...), custom_call_target="tpu_custom_call" | custom-call | flops 2147483648 | bytes 2228224 | tf_op jit(solution)/shard_map/pallas_call | solution.py:30
  61.2 2.5 %collective-permute-done.10.refs_3_ = bf16[528,128]{1,0:T(8,128)(2,1)S(1)} collective-permute-done((bf16[528,128]{1,0:T(8,128)(2,1)S(1)}, bf16[528,128]{1,0:T(8,128)(2,1)S(1)}, u32[]{:S(2)}, u32[]{:S(2)}) %collective-permute-start.10) | collective-permute-done | bytes 135200 | tf_op jit(solution)/shard_map/ppermute | solution.py:267
  63.7 4.9 %collective-permute-done.9.refs_2_ = bf16[528,128]{1,0:T(8,128)(2,1)S(1)} collective-permute-done((bf16[528,128]{1,0:T(8,128)(2,1)S(1)}, bf16[528,128]{1,0:T(8,128)(2,1)S(1)}, u32[]{:S(2)}, u32[]{:S(2)}) %collective-permute-start.9) | collective-permute-done | bytes 135200 | tf_op jit(solution)/shard_map/ppermute | solution.py:267
  69.4 2.2 %collective-permute-start.18 = (bf16[528,128]{1,0:T(8,128)(2,1)S(1)}, bf16[528,128]{1,0:T(8,128)(2,1)S(1)}, u32[]{:S(2)}, u32[]{:S(2)}) collective-permute-start(bf16[528,128]{1,0:T(8,128)(2,1)S(1)} %get-tuple-element.56), channel_id=1, source_target_pairs={{0,3},{1,2},{2,1},{3,0},{4,7},{5,6},{6,5},{7,4},{8,11},{9,10},{10,... | collective-permute-start | bytes 405512 | tf_op jit(solution)/shard_map/ppermute | solution.py:267
  71.7 2.2 %collective-permute-start.16 = (bf16[528,128]{1,0:T(8,128)(2,1)S(1)}, bf16[528,128]{1,0:T(8,128)(2,1)S(1)}, u32[]{:S(2)}, u32[]{:S(2)}) collective-permute-start(bf16[528,128]{1,0:T(8,128)(2,1)S(1)} %get-tuple-element.56), channel_id=1, source_target_pairs={{0,1},{1,0},{2,3},{3,2},{4,5},{5,4},{6,7},{7,6},{8,9},{9,8},{10,11... | collective-permute-start | bytes 405512 | tf_op jit(solution)/shard_map/ppermute | solution.py:267
  74.4 3.4 %collective-permute-done.18.refs_3_ = bf16[528,128]{1,0:T(8,128)(2,1)S(1)} collective-permute-done((bf16[528,128]{1,0:T(8,128)(2,1)S(1)}, bf16[528,128]{1,0:T(8,128)(2,1)S(1)}, u32[]{:S(2)}, u32[]{:S(2)}) %collective-permute-start.18) | collective-permute-done | bytes 135200 | tf_op jit(solution)/shard_map/ppermute | solution.py:267
  77.8 4.5 %collective-permute-done.17.refs_2_ = bf16[528,128]{1,0:T(8,128)(2,1)S(1)} collective-permute-done((bf16[528,128]{1,0:T(8,128)(2,1)S(1)}, bf16[528,128]{1,0:T(8,128)(2,1)S(1)}, u32[]{:S(2)}, u32[]{:S(2)}) %collective-permute-start.17) | collective-permute-done | bytes 135200 | tf_op jit(solution)/shard_map/ppermute | solution.py:267
  82.3 1.6 %shard_map.78 = (bf16[256,1024]{1,0:T(8,128)(2,1)S(1)}, bf16[512,512]{1,0:T(8,128)(2,1)S(1)}) custom-call(f32[528,128]{1,0:T(8,128)S(1)} %get-tuple-element.55.refs_0_, bf16[528,128]{1,0:T(8,128)(2,1)S(1)} %collective-permute-done.16.refs_1_, bf16[528,128]{1,0:T(8,128)(2,1)S(1)} %collective-permute-done.17.refs_2_, ...), custom_call_target="tpu_custom_call" | custom-call | flops 2147483648 | bytes 4476928 | tf_op jit(solution)/shard_map/pallas_call | solution.py:30
  86.7 7.8 %collective-permute-done.20 = bf16[128,1024]{1,0:T(8,128)(2,1)S(1)} collective-permute-done((bf16[128,1024]{1,0:T(8,128)(2,1)S(1)}, bf16[128,1024]{1,0:T(8,128)(2,1)S(1)}, u32[]{:S(2)}, u32[]{:S(2)}) %collective-permute-start.20) | collective-permute-done | bytes 262176 | tf_op jit(solution)/shard_map/ppermute | solution.py:252
  (40 shorter events, 8.3 us)
Async XLA Ops:
  0.0 42.5 %copy-start = (bf16[8,128,256]{2,1,0:T(8,128)(2,1)S(1)}, bf16[8,128,256]{2,1,0:T(8,128)(2,1)}, u32[]{:S(2)}) copy-start(bf16[8,128,256]{2,1,0:T(8,128)(2,1)} %param.13) | copy-start | bytes 1572868
  21.6 27.5 %copy-start.3 = (bf16[256,512]{1,0:T(8,128)(2,1)S(1)}, bf16[256,512]{1,0:T(8,128)(2,1)}, u32[]{:S(2)}) copy-start(bf16[256,512]{1,0:T(8,128)(2,1)} %get-tuple-element.36.refs_4_) | copy-start | bytes 786436
  21.6 18.8 %collective-permute-start.1 = (bf16[128,1536]{1,0:T(8,128)(2,1)}, bf16[128,1536]{1,0:T(8,128)(2,1)S(1)}, u32[]{:S(2)}, u32[]{:S(2)}) collective-permute-start(bf16[128,1536]{1,0:T(8,128)(2,1)} %get-tuple-element.35), channel_id=1, source_target_pairs={{0,8},{4,12},{8,0},{12,4},{1,9},{5,13},{9,1},{13,5},{2,10},{6,14},... | collective-permute-start | bytes 1179656 | tf_op jit(solution)/shard_map/ppermute | solution.py:252
  24.6 15.8 %collective-permute-start.2 = (bf16[256,512]{1,0:T(8,128)(2,1)}, bf16[256,512]{1,0:T(8,128)(2,1)S(1)}, u32[]{:S(2)}, u32[]{:S(2)}) collective-permute-start(bf16[256,512]{1,0:T(8,128)(2,1)} %get-tuple-element.36.refs_4_), channel_id=1, source_target_pairs={{0,1},{1,0},{2,3},{3,2},{4,5},{5,4},{6,7},{7,6},{8,9},{9,8},{10,11... | collective-permute-start | bytes 786440 | tf_op jit(solution)/shard_map/ppermute | solution.py:255
  26.2 12.7 %collective-permute-start.4 = (bf16[128,512]{1,0:T(8,128)(2,1)}, bf16[128,512]{1,0:T(8,128)(2,1)S(1)}, u32[]{:S(2)}, u32[]{:S(2)}) collective-permute-start(bf16[128,512]{1,0:T(8,128)(2,1)} %get-tuple-element.37), channel_id=1, source_target_pairs={{0,3},{1,2},{2,1},{3,0},{4,7},{5,6},{6,5},{7,4},{8,11},{9,10},{10,... | collective-permute-start | bytes 393224 | tf_op jit(solution)/shard_map/ppermute | solution.py:255
  28.6 11.7 %collective-permute-start.3 = (bf16[128,512]{1,0:T(8,128)(2,1)}, bf16[128,512]{1,0:T(8,128)(2,1)S(1)}, u32[]{:S(2)}, u32[]{:S(2)}) collective-permute-start(bf16[128,512]{1,0:T(8,128)(2,1)} %get-tuple-element.37), channel_id=1, source_target_pairs={{0,2},{1,3},{2,0},{3,1},{4,6},{5,7},{6,4},{7,5},{8,10},{9,11},{10,... | collective-permute-start | bytes 393224 | tf_op jit(solution)/shard_map/ppermute | solution.py:255
  28.8 13.7 %collective-permute-start = (bf16[128,1536]{1,0:T(8,128)(2,1)}, bf16[128,1536]{1,0:T(8,128)(2,1)S(1)}, u32[]{:S(2)}, u32[]{:S(2)}) collective-permute-start(bf16[128,1536]{1,0:T(8,128)(2,1)} %get-tuple-element.34.refs_0_.refs_4_), channel_id=1, source_target_pairs={{0,4},{4,0},{8,12},{12,8},{1,5},{5,1},{9,13},{13,9},{2,6},{6,2},{1... | collective-permute-start | bytes 1179656 | tf_op jit(solution)/shard_map/ppermute | solution.py:252
  40.3 8.7 %collective-permute-start.5 = (bf16[128,1536]{1,0:T(8,128)(2,1)S(1)}, bf16[128,1536]{1,0:T(8,128)(2,1)S(1)}, u32[]{:S(2)}, u32[]{:S(2)}) collective-permute-start(bf16[128,1536]{1,0:T(8,128)(2,1)S(1)} %collective-permute-done.1.refs_2_.refs_6_), channel_id=1, source_target_pairs={{0,4},{4,0},{8,12},{12,8},{1,5},{5,1},{9,13},{13,9},{2,6},{6,2},{1... | collective-permute-start | bytes 1179656 | tf_op jit(solution)/shard_map/ppermute | solution.py:252
  40.4 6.4 %collective-permute-start.7 = (bf16[128,512]{1,0:T(8,128)(2,1)S(1)}, bf16[128,512]{1,0:T(8,128)(2,1)S(1)}, u32[]{:S(2)}, u32[]{:S(2)}) collective-permute-start(bf16[128,512]{1,0:T(8,128)(2,1)S(1)} %collective-permute-done.4.refs_8_), channel_id=1, source_target_pairs={{0,16},{16,0},{1,17},{17,1},{2,18},{18,2},{3,19},{19,3},{4,20},{20... | collective-permute-start | bytes 393224 | tf_op jit(solution)/shard_map/ppermute | solution.py:297
  41.9 7.1 %collective-permute-start.6 = (bf16[128,512]{1,0:T(8,128)(2,1)S(1)}, bf16[128,512]{1,0:T(8,128)(2,1)S(1)}, u32[]{:S(2)}, u32[]{:S(2)}) collective-permute-start(bf16[128,512]{1,0:T(8,128)(2,1)S(1)} %collective-permute-done.3.refs_6_), channel_id=1, source_target_pairs={{0,16},{16,0},{1,17},{17,1},{2,18},{18,2},{3,19},{19,3},{4,20},{20... | collective-permute-start | bytes 393224 | tf_op jit(solution)/shard_map/ppermute | solution.py:297
  42.5 9.6 %collective-permute-start.13 = (bf16[128,256]{1,0:T(8,128)(2,1)}, bf16[128,256]{1,0:T(8,128)(2,1)S(1)}, u32[]{:S(2)}, u32[]{:S(2)}) collective-permute-start(bf16[128,256]{1,0:T(8,128)(2,1)} %get-tuple-element.44), channel_id=1, source_target_pairs={{0,3},{1,2},{2,1},{3,0},{4,7},{5,6},{6,5},{7,4},{8,11},{9,10},{10,... | collective-permute-start | bytes 196616 | tf_op jit(solution)/shard_map/ppermute | solution.py:255
  45.2 6.9 %collective-permute-start.12 = (bf16[128,256]{1,0:T(8,128)(2,1)}, bf16[128,256]{1,0:T(8,128)(2,1)S(1)}, u32[]{:S(2)}, u32[]{:S(2)}) collective-permute-start(bf16[128,256]{1,0:T(8,128)(2,1)} %get-tuple-element.44), channel_id=1, source_target_pairs={{0,2},{1,3},{2,0},{3,1},{4,6},{5,7},{6,4},{7,5},{8,10},{9,11},{10,... | collective-permute-start | bytes 196616 | tf_op jit(solution)/shard_map/ppermute | solution.py:255
  46.7 6.6 %collective-permute-start.11 = (bf16[256,256]{1,0:T(8,128)(2,1)}, bf16[256,256]{1,0:T(8,128)(2,1)S(1)}, u32[]{:S(2)}, u32[]{:S(2)}) collective-permute-start(bf16[256,256]{1,0:T(8,128)(2,1)} %get-tuple-element.43.refs_4_), channel_id=1, source_target_pairs={{0,1},{1,0},{2,3},{3,2},{4,5},{5,4},{6,7},{7,6},{8,9},{9,8},{10,11... | collective-permute-start | bytes 393224 | tf_op jit(solution)/shard_map/ppermute | solution.py:255
  50.1 9.7 %copy-start.4 = (bf16[256,256]{1,0:T(8,128)(2,1)S(1)}, bf16[256,256]{1,0:T(8,128)(2,1)}, u32[]{:S(2)}) copy-start(bf16[256,256]{1,0:T(8,128)(2,1)} %get-tuple-element.43.refs_4_) | copy-start | bytes 393220
  53.3 6.4 %collective-permute-start.14 = (bf16[128,256]{1,0:T(8,128)(2,1)S(1)}, bf16[128,256]{1,0:T(8,128)(2,1)S(1)}, u32[]{:S(2)}, u32[]{:S(2)}) collective-permute-start(bf16[128,256]{1,0:T(8,128)(2,1)S(1)} %collective-permute-done.12.refs_6_), channel_id=1, source_target_pairs={{0,16},{16,0},{1,17},{17,1},{2,18},{18,2},{3,19},{19,3},{4,20},{20... | collective-permute-start | bytes 196616 | tf_op jit(solution)/shard_map/ppermute | solution.py:297
  54.8 4.9 %collective-permute-start.15 = (bf16[128,256]{1,0:T(8,128)(2,1)S(1)}, bf16[128,256]{1,0:T(8,128)(2,1)S(1)}, u32[]{:S(2)}, u32[]{:S(2)}) collective-permute-start(bf16[128,256]{1,0:T(8,128)(2,1)S(1)} %collective-permute-done.13.refs_8_), channel_id=1, source_target_pairs={{0,16},{16,0},{1,17},{17,1},{2,18},{18,2},{3,19},{19,3},{4,20},{20... | collective-permute-start | bytes 196616 | tf_op jit(solution)/shard_map/ppermute | solution.py:297
  55.4 8.3 %collective-permute-start.10 = (bf16[528,128]{1,0:T(8,128)(2,1)S(1)}, bf16[528,128]{1,0:T(8,128)(2,1)S(1)}, u32[]{:S(2)}, u32[]{:S(2)}) collective-permute-start(bf16[528,128]{1,0:T(8,128)(2,1)S(1)} %get-tuple-element.40), channel_id=1, source_target_pairs={{0,3},{1,2},{2,1},{3,0},{4,7},{5,6},{6,5},{7,4},{8,11},{9,10},{10,... | collective-permute-start | bytes 405512 | tf_op jit(solution)/shard_map/ppermute | solution.py:267
  57.9 10.6 %collective-permute-start.9 = (bf16[528,128]{1,0:T(8,128)(2,1)S(1)}, bf16[528,128]{1,0:T(8,128)(2,1)S(1)}, u32[]{:S(2)}, u32[]{:S(2)}) collective-permute-start(bf16[528,128]{1,0:T(8,128)(2,1)S(1)} %get-tuple-element.40), channel_id=1, source_target_pairs={{0,2},{1,3},{2,0},{3,1},{4,6},{5,7},{6,4},{7,5},{8,10},{9,11},{10,... | collective-permute-start | bytes 405512 | tf_op jit(solution)/shard_map/ppermute | solution.py:267
  57.9 10.6 %collective-permute-start.8 = (bf16[528,128]{1,0:T(8,128)(2,1)S(1)}, bf16[528,128]{1,0:T(8,128)(2,1)S(1)}, u32[]{:S(2)}, u32[]{:S(2)}) collective-permute-start(bf16[528,128]{1,0:T(8,128)(2,1)S(1)} %get-tuple-element.40), channel_id=1, source_target_pairs={{0,1},{1,0},{2,3},{3,2},{4,5},{5,4},{6,7},{7,6},{8,9},{9,8},{10,11... | collective-permute-start | bytes 405512 | tf_op jit(solution)/shard_map/ppermute | solution.py:267
  69.4 8.4 %collective-permute-start.18 = (bf16[528,128]{1,0:T(8,128)(2,1)S(1)}, bf16[528,128]{1,0:T(8,128)(2,1)S(1)}, u32[]{:S(2)}, u32[]{:S(2)}) collective-permute-start(bf16[528,128]{1,0:T(8,128)(2,1)S(1)} %get-tuple-element.56), channel_id=1, source_target_pairs={{0,3},{1,2},{2,1},{3,0},{4,7},{5,6},{6,5},{7,4},{8,11},{9,10},{10,... | collective-permute-start | bytes 405512 | tf_op jit(solution)/shard_map/ppermute | solution.py:267
  71.7 10.6 %collective-permute-start.17 = (bf16[528,128]{1,0:T(8,128)(2,1)S(1)}, bf16[528,128]{1,0:T(8,128)(2,1)S(1)}, u32[]{:S(2)}, u32[]{:S(2)}) collective-permute-start(bf16[528,128]{1,0:T(8,128)(2,1)S(1)} %get-tuple-element.56), channel_id=1, source_target_pairs={{0,2},{1,3},{2,0},{3,1},{4,6},{5,7},{6,4},{7,5},{8,10},{9,11},{10,... | collective-permute-start | bytes 405512 | tf_op jit(solution)/shard_map/ppermute | solution.py:267
  71.7 10.6 %collective-permute-start.16 = (bf16[528,128]{1,0:T(8,128)(2,1)S(1)}, bf16[528,128]{1,0:T(8,128)(2,1)S(1)}, u32[]{:S(2)}, u32[]{:S(2)}) collective-permute-start(bf16[528,128]{1,0:T(8,128)(2,1)S(1)} %get-tuple-element.56), channel_id=1, source_target_pairs={{0,1},{1,0},{2,3},{3,2},{4,5},{5,4},{6,7},{7,6},{8,9},{9,8},{10,11... | collective-permute-start | bytes 405512 | tf_op jit(solution)/shard_map/ppermute | solution.py:267
  83.9 2.0 %collective-permute-start.19 = (bf16[256,1024]{1,0:T(8,128)(2,1)S(1)}, bf16[256,1024]{1,0:T(8,128)(2,1)S(1)}, u32[]{:S(2)}, u32[]{:S(2)}) collective-permute-start(bf16[256,1024]{1,0:T(8,128)(2,1)S(1)} %get-tuple-element.62), channel_id=1, source_target_pairs={{0,4},{4,0},{8,12},{12,8},{1,5},{5,1},{9,13},{13,9},{2,6},{6,2},{1... | collective-permute-start | bytes 1572872 | tf_op jit(solution)/shard_map/ppermute | solution.py:252
  86.1 8.4 %collective-permute-start.20 = (bf16[128,1024]{1,0:T(8,128)(2,1)S(1)}, bf16[128,1024]{1,0:T(8,128)(2,1)S(1)}, u32[]{:S(2)}, u32[]{:S(2)}) collective-permute-start(bf16[128,1024]{1,0:T(8,128)(2,1)S(1)} %slice.15), channel_id=1, source_target_pairs={{0,8},{4,12},{8,0},{12,4},{1,9},{5,13},{9,1},{13,5},{2,10},{6,14},... | collective-permute-start | bytes 786440 | tf_op jit(solution)/shard_map/ppermute | solution.py:252
  (2 other events, 10.7 us)

commit v7 on v6

--- a/solution.py
+++ b/solution.py
@@ -26,7 +26,7 @@
 
 
 def call(body, outs, args, flops, vmem=24, **kw):
-    nbytes = sum(a.size * a.dtype.itemsize for a in args)
+    nbytes = sum(a.size * a.dtype.itemsize for a in args) if flops else 0
     return pl.pallas_call(
         body,
         out_shape=[jax.ShapeDtypeStruct(s, d) for s, d in outs],
@@ -36,22 +36,21 @@
     )(*args)
 
 
-def first_kernel(g, cols, split, *refs):
-    wk, wv, wq, events, offsets, frequency, cot = refs[:7]
-    n = 4 if split else 2
-    pieces, bufs, sems = refs[7 : 7 + n], refs[7 + n : -1], refs[-1]
+def first_kernel(g, cols, *refs):
+    ws, (events, offsets, frequency, cot) = refs[:3], refs[3:7]
+    (near, far, far_query), bufs, sems = refs[7:10], refs[10:-1], refs[-1]
     mine = lax.axis_index("seq") % g
     at = pl.ds(pl.multiple_of(mine * cols, cols), cols)
-    pairs = [(wk.at[:, at], pieces[0].at[:, :cols]), (wv.at[:, at], pieces[0].at[:, cols:]), (wq.at[:, at], pieces[1])]
-    if split:
-        half = wk.shape[0] // 2
-        rows = pl.ds(pl.multiple_of(lax.axis_index("grp") * half, half), half)
-        pairs += [
-            (wk.at[rows, at], pieces[2].at[:, :cols]),
-            (wv.at[rows, at], pieces[2].at[:, cols:]),
-            (wq.at[rows, at], pieces[3]),
-        ]
-    copies = [pltpu.make_async_copy(a, b, sems.at[i]) for i, (a, b) in enumerate(pairs)]
+    size = far.shape[0]
+    rows = slice(None)
+    if size < near.shape[0]:
+        rows = pl.ds(pl.multiple_of(lax.axis_index("grp") * size, size), size)
+    copies = []
+    for i, w in enumerate(ws):
+        to = slice(i * cols, (i + 1) * cols)
+        copies.append((w.at[:, at], near.at[:, to]))
+        copies.append((w.at[rows, at], far.at[:, to] if i < 2 else far_query))
+    copies = [pltpu.make_async_copy(a, b, sems.at[i]) for i, (a, b) in enumerate(copies)]
     for c in copies:
         c.start()
     tokens, width = events.shape
@@ -71,18 +70,21 @@
         c.wait()
 
 
-def place_rows(full, parts, n):
+def place_rows(full, parts, n, start):
     z = lax.axis_index("sub")
-    rows = parts[0].shape[0]
-    spots = [(k, 0) for k in range(n)]
-    if len(parts) > n:
-        half, mine = rows // 2, lax.axis_index("grp")
-        spots = [(0, 0), (1, 0)]
-        for k in range(2, n):
-            spots += [(k, mine * half), (k, half - mine * half)]
-    for (k, start), part in zip(spots, parts):
-        size = part.shape[0]
-        full[pl.ds(pl.multiple_of((z ^ k) * rows + start, size), size), :] = part[...]
+    rows, cols = parts[0].shape[0], full.shape[1]
+    full[pl.ds(pl.multiple_of(z * rows, rows), rows), :] = parts[0][:, start : start + cols]
+    full[pl.ds(pl.multiple_of((z ^ 1) * rows, rows), rows), :] = parts[1][:, start : start + cols]
+    far = parts[2:]
+    halves = len(far) // (n - 2)
+    size = rows // halves
+    for i, part in enumerate(far):
+        k = 2 + i // halves
+        where = (z ^ k) * rows
+        if halves == 2:
+            mine = lax.axis_index("grp") * size
+            where = where + (size - mine if i % 2 else mine)
+        full[pl.ds(pl.multiple_of(where, size), size), :] = part[...]
 
 
 def features(act, om, h, i, feat, sig):
@@ -130,7 +132,7 @@
     w_full, feat, sig, val, own, send = refs[g + nw + 1 :]
     hd, m = om.shape[1], om.shape[2]
     cols = hp * hd
-    place_rows(w_full, ws, n)
+    place_rows(w_full, ws, n, 0)
     rows = xs[0].shape[0]
     sums = [jnp.zeros((1, m), F32) for _ in range(hp)]
     for i, x in enumerate(xs):
@@ -152,7 +154,7 @@
 def query_kernel(g, n, nw, hp, width, *refs):
     xs, ws, om = refs[:g], refs[g : g + nw], refs[g + nw]
     w_full, feat, sig = refs[g + nw + 1 :]
-    place_rows(w_full, ws, n)
+    place_rows(w_full, ws, n, 2 * w_full.shape[1])
     for i, x in enumerate(xs):
         act = dot(x[:, :width], w_full[...]).astype(BF16)
         for h in range(hp):
@@ -269,36 +271,29 @@
 
     wrows = key_weight.shape[0]
     split = lax.axis_size("grp") == 2 and wrows % 32 == 0
-    wouts = [((wrows, 2 * cols), BF16), ((wrows, cols), BF16), ((wrows // 2, 2 * cols), BF16), ((wrows // 2, cols), BF16)]
-    wouts = wouts if split else wouts[:2]
-    n = len(wouts)
+    size = wrows // 2 if split else wrows
+    wouts = [((wrows, 3 * cols), BF16), ((size, 2 * cols), BF16), ((size, cols), BF16)]
     frequency = jnp.exp(jnp.arange(width // 2, dtype=F32) * (-2.0 * math.log(10000.0) / width))
     whole = pl.BlockSpec(memory_space=pltpu.VMEM)
     firsts = call(
-        functools.partial(first_kernel, g, cols, split),
+        functools.partial(first_kernel, g, cols),
         wouts + [((rows, width + 2 * cols), BF16)] * (g // 2),
         [key_weight, value_weight, query_weight, events, offsets[None], frequency[None], cotangent],
         0,
-        vmem=56,
+        vmem=52,
         in_specs=[HBM] * 3 + [whole] * 4,
-        out_specs=[HBM] * n + [whole] * (g // 2),
-        scratch_shapes=[pltpu.SemaphoreType.DMA((6 if split else 3,))],
-    )
-    pieces, bufs = firsts[:n], firsts[n:]
-
-    def from_sub(i):
-        return [over_sub(pieces[i], 1)] + [over_sub(pieces[i + 2 if split else i], k) for k in range(2, n_sub)]
-
-    def weight_rows(i, arrived):
+        scratch_shapes=[pltpu.SemaphoreType.DMA((6,))],
+    )
+    (near, far, far_query), bufs = firsts[:3], firsts[3:]
+
+    def swapped(parts):
         if not split:
-            return [pieces[i]] + arrived
-        far = []
-        for part in arrived[1:]:
-            far += [part, lax.ppermute(part, "grp", [(0, 1), (1, 0)])]
-        return [pieces[i], arrived[0]] + far
-
-    arrived = from_sub(0)
-    kvs = weight_rows(0, arrived)
+            return parts
+        return [x for part in parts for x in (part, lax.ppermute(part, "grp", [(0, 1), (1, 0)]))]
+
+    nearest = over_sub(near, 1)
+    arrived = [over_sub(far, k) for k in range(2, n_sub)]
+    kvs = [near, nearest] + swapped(arrived)
     xs = [bufs[0]] * g
     for k in range(2, g, 2):
         xs[k] = over_seq(bufs[k // 2], k)
@@ -306,8 +301,9 @@
     xs[2:], _ = lax.optimization_barrier((xs[2:], arrived))
     for k in range(3, g, 2):
         xs[k] = over_seq(xs[k ^ 1], 1)
-    pieces, _ = lax.optimization_barrier((pieces, arrived + xs[1:2]))
-    query_rows = from_sub(1)
+    far_query, _ = lax.optimization_barrier((far_query, arrived + xs[1:2]))
+    query_rows = [over_sub(far_query, k) for k in range(2, n_sub)]
+    kvs, _ = lax.optimization_barrier((kvs, query_rows))
     om = lax.dynamic_slice_in_dim(omega, (lax.axis_index("seq") % g) * hp, hp, 0)
 
     flop = 2 * t * width * cols
@@ -320,12 +316,12 @@
     )
     summary = to_all(own, send)
     query_rows, _ = lax.optimization_barrier((query_rows, val))
-    qs = weight_rows(1, query_rows)
+    qs = [near, nearest] + swapped(query_rows)
     wq_full, query_feat, query_sig = call(
         functools.partial(query_kernel, g, n_sub, len(qs), hp, width),
         [((width, cols), BF16), ((t, hp * m), BF16), ((t, hp * m), F32)],
         [*xs, *qs, om],
-        8 * flop,
+        0,
     )
     total_half, summary_half, scaled_half, norm, own, send = call(
         functools.partial(query_side_kernel, g, p, hp, m, width, loss_scale),

time: 95.4 us -> 74.7 us (0.78)
  Pallas kernels: 28.5 us -> 8.72 us
  local copies, waits for them, and re-layouts: 1.05 us -> 2.65 us
  waiting for transfers between devices: 40 us -> 38.5 us
    pallas_call x7, Pallas kernels: 28.5 us -> 8.72 us  [call(): pl.pallas_call(body, out_shape=[jax.ShapeDtypeStruct(s, d) for s, d in ou...]
    ppermute x6, waiting for transfers between devices: 15.3 us -> 8.98 us  [to_all(): parts.append(lax.ppermute(send, ('seq', 'sub'), perm))]
    ppermute x4, waiting for transfers between devices: 3.36 us -> 7.86 us  [swapped(): lax.ppermute(part, 'grp', [(0, 1), (1, 0)])]
    unnamed x10 -> x8, local copies, waits for them, and re-layouts: 1.01 us -> 2.61 us
    ppermute x6 -> x5, starting transfers between devices: 7.4 us -> 6.96 us  [over_sub(): return lax.ppermute(x, 'sub', [(i, i ^ k) for i in range(n_sub)])]
    ppermute x6 -> x5, waiting for transfers between devices: 12.8 us -> 13.1 us  [over_sub(): return lax.ppermute(x, 'sub', [(i, i ^ k) for i in range(n_sub)])]
  transfers between devices with their start and end apart: 21 -> 20, of which waited for: 11 -> 12; matrix products, arithmetic and copies ran while one was open for 0% -> 0% of each run, Pallas kernels for 5% -> 4%
where the time goes in v7:
time: 74.7 us; the launch traced here: 74.5 us
  waiting for transfers between devices  38.5 us (52%)
  starting transfers between devices  23.6 us (32%)
  Pallas kernels  8.72 us (12%)
  local copies, waits for them, and re-layouts  2.65 us (4%)
  other arithmetic  0.92 us (1%)
    ppermute x5, waiting for transfers between devices, over_sub(): return lax.ppermute(x, 'sub', [(i, i ^ k) for i in range(n_sub)])  13.1 us
    ppermute x6, waiting for transfers between devices, to_all(): parts.append(lax.ppermute(send, ('seq', 'sub'), perm))  8.98 us
    ppermute x6, starting transfers between devices, to_all(): parts.append(lax.ppermute(send, ('seq', 'sub'), perm))  8.91 us
    pallas_call x7, Pallas kernels, call(): pl.pallas_call(body, out_shape=[jax.ShapeDtypeStruct(s, d) for s, d in ou...  8.72 us
    ppermute x5, waiting for transfers between devices, over_seq(): return lax.ppermute(x, 'seq', [(i, i ^ k) for i in range(n_seq)])  8.58 us
    ppermute x4, waiting for transfers between devices, swapped(): lax.ppermute(part, 'grp', [(0, 1), (1, 0)])  7.86 us
    ppermute x5, starting transfers between devices, over_sub(): return lax.ppermute(x, 'sub', [(i, i ^ k) for i in range(n_sub)])  6.96 us
    ppermute x4, starting transfers between devices, swapped(): lax.ppermute(part, 'grp', [(0, 1), (1, 0)])  4.05 us
  transfers between devices with their start and end apart: 20, of which 12 were waited for; matrix products, arithmetic and copies ran while one was open for 0% of the time, Pallas kernels for 4%

profile of v7, /device:TPU:0, one launch (start us, length us, event | category | flops | bytes accessed | tf_op | source)
XLA Modules:
  0.0 74.5 jit_solution(7066457151033931323)
XLA Ops:
  2.6 1.2 %shard_map.73 = (bf16[256,768]{1,0:T(8,128)(2,1)S(1)}, bf16[128,512]{1,0:T(8,128)(2,1)S(1)}, bf16[128,256]{1,0:T(8,128)(2,1)S(1)}, bf16[128,1536]{1,0:T(8,128)(2,1)S(1)}, bf16[128,1536]{1,0:T(8,128)(2,1)S(1)}) custom-call(bf16[256,1024]{1,0:T(8,128)(2,1)} %refs_0_.1, bf16[256,1024]{1,0:T(8,128)(2,1)} %refs_1_.1, bf16[256,1024]{1,0:T(8,128)(2,1)} %refs_2_.1, ...), custom_call_target="tpu_custom_call" | custom-call | tf_op jit(solution)/shard_map/pallas_call | solution.py:30
  3.8 3.0 %collective-permute-start.1 = (bf16[128,1536]{1,0:T(8,128)(2,1)S(1)}, bf16[128,1536]{1,0:T(8,128)(2,1)S(1)}, u32[]{:S(2)}, u32[]{:S(2)}) collective-permute-start(bf16[128,1536]{1,0:T(8,128)(2,1)S(1)} %get-tuple-element.38), channel_id=1, source_target_pairs={{0,8},{4,12},{8,0},{12,4},{1,9},{5,13},{9,1},{13,5},{2,10},{6,14},... | collective-permute-start | bytes 1179656 | tf_op jit(solution)/shard_map/ppermute | solution.py:254
  6.8 3.6 %collective-permute-start.3 = (bf16[128,512]{1,0:T(8,128)(2,1)S(1)}, bf16[128,512]{1,0:T(8,128)(2,1)S(1)}, u32[]{:S(2)}, u32[]{:S(2)}) collective-permute-start(bf16[128,512]{1,0:T(8,128)(2,1)S(1)} %get-tuple-element.39), channel_id=1, source_target_pairs={{0,3},{1,2},{2,1},{3,0},{4,7},{5,6},{6,5},{7,4},{8,11},{9,10},{10,... | collective-permute-start | bytes 393224 | tf_op jit(solution)/shard_map/ppermute | solution.py:257
  11.2 3.9 %collective-permute-done.3.refs_8_ = bf16[128,512]{1,0:T(8,128)(2,1)S(1)} collective-permute-done((bf16[128,512]{1,0:T(8,128)(2,1)S(1)}, bf16[128,512]{1,0:T(8,128)(2,1)S(1)}, u32[]{:S(2)}, u32[]{:S(2)}) %collective-permute-start.3) | collective-permute-done | bytes 131104 | tf_op jit(solution)/shard_map/ppermute | solution.py:257
  15.1 6.2 %collective-permute-done.2.refs_6_ = bf16[128,512]{1,0:T(8,128)(2,1)S(1)} collective-permute-done((bf16[128,512]{1,0:T(8,128)(2,1)S(1)}, bf16[128,512]{1,0:T(8,128)(2,1)S(1)}, u32[]{:S(2)}, u32[]{:S(2)}) %collective-permute-start.2) | collective-permute-done | bytes 131104 | tf_op jit(solution)/shard_map/ppermute | solution.py:257
  21.3 1.5 %collective-permute-start.7 = (bf16[128,512]{1,0:T(8,128)(2,1)S(1)}, bf16[128,512]{1,0:T(8,128)(2,1)S(1)}, u32[]{:S(2)}, u32[]{:S(2)}) collective-permute-start(bf16[128,512]{1,0:T(8,128)(2,1)S(1)} %collective-permute-done.3.refs_8_), channel_id=1, source_target_pairs={{0,16},{16,0},{1,17},{17,1},{2,18},{18,2},{3,19},{19,3},{4,20},{20... | collective-permute-start | bytes 393224 | tf_op jit(solution)/shard_map/ppermute | solution.py:292
  23.4 2.4 %collective-permute-start.9 = (bf16[128,256]{1,0:T(8,128)(2,1)S(1)}, bf16[128,256]{1,0:T(8,128)(2,1)S(1)}, u32[]{:S(2)}, u32[]{:S(2)}) collective-permute-start(bf16[128,256]{1,0:T(8,128)(2,1)S(1)} %get-tuple-element.43), channel_id=1, source_target_pairs={{0,3},{1,2},{2,1},{3,0},{4,7},{5,6},{6,5},{7,4},{8,11},{9,10},{10,... | collective-permute-start | bytes 196616 | tf_op jit(solution)/shard_map/ppermute | solution.py:257
  25.8 1.8 %collective-permute-done.7.refs_9_ = bf16[128,512]{1,0:T(8,128)(2,1)S(1)} collective-permute-done((bf16[128,512]{1,0:T(8,128)(2,1)S(1)}, bf16[128,512]{1,0:T(8,128)(2,1)S(1)}, u32[]{:S(2)}, u32[]{:S(2)}) %collective-permute-start.7) | collective-permute-done | bytes 131104 | tf_op jit(solution)/shard_map/ppermute | solution.py:292
  27.8 2.3 %collective-permute-done.6.refs_7_ = bf16[128,512]{1,0:T(8,128)(2,1)S(1)} collective-permute-done((bf16[128,512]{1,0:T(8,128)(2,1)S(1)}, bf16[128,512]{1,0:T(8,128)(2,1)S(1)}, u32[]{:S(2)}, u32[]{:S(2)}) %collective-permute-start.6) | collective-permute-done | bytes 131104 | tf_op jit(solution)/shard_map/ppermute | solution.py:292
  30.1 3.0 %collective-permute-done.8.refs_6_ = bf16[128,256]{1,0:T(8,128)(2,1)S(1)} collective-permute-done((bf16[128,256]{1,0:T(8,128)(2,1)S(1)}, bf16[128,256]{1,0:T(8,128)(2,1)S(1)}, u32[]{:S(2)}, u32[]{:S(2)}) %collective-permute-start.8) | collective-permute-done | bytes 65568 | tf_op jit(solution)/shard_map/ppermute | solution.py:257
  33.1 2.0 %shard_map.74 = (bf16[1024,512]{1,0:T(8,128)(2,1)S(1)}, bf16[512,512]{1,0:T(8,128)(2,1)S(1)}, f32[512,512]{1,0:T(8,128)S(1)}, bf16[512,256]{1,0:T(8,128)(2,1)S(1...) custom-call(bf16[128,1536]{1,0:T(8,128)(2,1)S(1)} %get-tuple-element.37.refs_0_.refs_4_, ...), custom_call_target="tpu_custom_call" | custom-call | flops 2147483648 | bytes 3014656 | tf_op jit(solution)/shard_map/pallas_call | solution.py:30
  35.1 2.2 %collective-permute-start.12 = (bf16[528,128]{1,0:T(8,128)(2,1)S(1)}, bf16[528,128]{1,0:T(8,128)(2,1)S(1)}, u32[]{:S(2)}, u32[]{:S(2)}) collective-permute-start(bf16[528,128]{1,0:T(8,128)(2,1)S(1)} %get-tuple-element.51), channel_id=1, source_target_pairs={{0,3},{1,2},{2,1},{3,0},{4,7},{5,6},{6,5},{7,4},{8,11},{9,10},{10,... | collective-permute-start | bytes 405512 | tf_op jit(solution)/shard_map/ppermute | solution.py:269
  37.3 2.2 %collective-permute-start.10 = (bf16[528,128]{1,0:T(8,128)(2,1)S(1)}, bf16[528,128]{1,0:T(8,128)(2,1)S(1)}, u32[]{:S(2)}, u32[]{:S(2)}) collective-permute-start(bf16[528,128]{1,0:T(8,128)(2,1)S(1)} %get-tuple-element.51), channel_id=1, source_target_pairs={{0,1},{1,0},{2,3},{3,2},{4,5},{5,4},{6,7},{7,6},{8,9},{9,8},{10,11... | collective-permute-start | bytes 405512 | tf_op jit(solution)/shard_map/ppermute | solution.py:269
  39.5 1.5 %collective-permute-start.13 = (bf16[128,256]{1,0:T(8,128)(2,1)S(1)}, bf16[128,256]{1,0:T(8,128)(2,1)S(1)}, u32[]{:S(2)}, u32[]{:S(2)}) collective-permute-start(bf16[128,256]{1,0:T(8,128)(2,1)S(1)} %collective-permute-done.8.refs_6_), channel_id=1, source_target_pairs={{0,16},{16,0},{1,17},{17,1},{2,18},{18,2},{3,19},{19,3},{4,20},{20... | collective-permute-start | bytes 196616 | tf_op jit(solution)/shard_map/ppermute | solution.py:292
  41.6 2.2 %collective-permute-done.13.refs_7_ = bf16[128,256]{1,0:T(8,128)(2,1)S(1)} collective-permute-done((bf16[128,256]{1,0:T(8,128)(2,1)S(1)}, bf16[128,256]{1,0:T(8,128)(2,1)S(1)}, u32[]{:S(2)}, u32[]{:S(2)}) %collective-permute-start.13) | collective-permute-done | bytes 65568 | tf_op jit(solution)/shard_map/ppermute | solution.py:292
  43.8 1.5 %collective-permute-done.14.refs_9_ = bf16[128,256]{1,0:T(8,128)(2,1)S(1)} collective-permute-done((bf16[128,256]{1,0:T(8,128)(2,1)S(1)}, bf16[128,256]{1,0:T(8,128)(2,1)S(1)}, u32[]{:S(2)}, u32[]{:S(2)}) %collective-permute-start.14) | collective-permute-done | bytes 65568 | tf_op jit(solution)/shard_map/ppermute | solution.py:292
  45.3 1.4 %shard_map.75 = (bf16[1024,256]{1,0:T(8,128)(2,1)S(1)}, bf16[512,512]{1,0:T(8,128)(2,1)S(1)}, f32[512,512]{1,0:T(8,128)S(1)}) custom-call(bf16[128,1536]{1,0:T(8,128)(2,1)S(1)} %get-tuple-element.37.refs_0_.refs_4_, bf16[128,1536]{1,0:T(8,128)(2,1)S(1)} %collective-permute-done.refs_1_.refs_5_, bf16[128,1536]{1,0:T(8,128)(2,1)S(1)} %collective-permute-done.1.refs_2_.refs_6_, ...), custom_call_target="tpu_custom_call" | custom-call | tf_op jit(solution)/shard_map/pallas_call | solution.py:30
  46.7 1.3 %collective-permute-done.11.refs_2_ = bf16[528,128]{1,0:T(8,128)(2,1)S(1)} collective-permute-done((bf16[528,128]{1,0:T(8,128)(2,1)S(1)}, bf16[528,128]{1,0:T(8,128)(2,1)S(1)}, u32[]{:S(2)}, u32[]{:S(2)}) %collective-permute-start.11) | collective-permute-done | bytes 135200 | tf_op jit(solution)/shard_map/ppermute | solution.py:269
  49.0 1.7 %collective-permute-start.17 = (bf16[528,128]{1,0:T(8,128)(2,1)S(1)}, bf16[528,128]{1,0:T(8,128)(2,1)S(1)}, u32[]{:S(2)}, u32[]{:S(2)}) collective-permute-start(bf16[528,128]{1,0:T(8,128)(2,1)S(1)} %get-tuple-element.62), channel_id=1, source_target_pairs={{0,3},{1,2},{2,1},{3,0},{4,7},{5,6},{6,5},{7,4},{8,11},{9,10},{10,... | collective-permute-start | bytes 405512 | tf_op jit(solution)/shard_map/ppermute | solution.py:269
  50.7 2.8 %collective-permute-start.15 = (bf16[528,128]{1,0:T(8,128)(2,1)S(1)}, bf16[528,128]{1,0:T(8,128)(2,1)S(1)}, u32[]{:S(2)}, u32[]{:S(2)}) collective-permute-start(bf16[528,128]{1,0:T(8,128)(2,1)S(1)} %get-tuple-element.62), channel_id=1, source_target_pairs={{0,1},{1,0},{2,3},{3,2},{4,5},{5,4},{6,7},{7,6},{8,9},{9,8},{10,11... | collective-permute-start | bytes 405512 | tf_op jit(solution)/shard_map/ppermute | solution.py:269
  54.0 3.4 %collective-permute-done.17.refs_3_ = bf16[528,128]{1,0:T(8,128)(2,1)S(1)} collective-permute-done((bf16[528,128]{1,0:T(8,128)(2,1)S(1)}, bf16[528,128]{1,0:T(8,128)(2,1)S(1)}, u32[]{:S(2)}, u32[]{:S(2)}) %collective-permute-start.17) | collective-permute-done | bytes 135200 | tf_op jit(solution)/shard_map/ppermute | solution.py:269
  57.4 4.2 %collective-permute-done.16.refs_2_ = bf16[528,128]{1,0:T(8,128)(2,1)S(1)} collective-permute-done((bf16[528,128]{1,0:T(8,128)(2,1)S(1)}, bf16[528,128]{1,0:T(8,128)(2,1)S(1)}, u32[]{:S(2)}, u32[]{:S(2)}) %collective-permute-start.16) | collective-permute-done | bytes 135200 | tf_op jit(solution)/shard_map/ppermute | solution.py:269
  61.6 1.6 %shard_map.78 = (bf16[256,1024]{1,0:T(8,128)(2,1)S(1)}, bf16[512,512]{1,0:T(8,128)(2,1)S(1)}) custom-call(f32[528,128]{1,0:T(8,128)S(1)} %get-tuple-element.61.refs_0_, bf16[528,128]{1,0:T(8,128)(2,1)S(1)} %collective-permute-done.15.refs_1_, bf16[528,128]{1,0:T(8,128)(2,1)S(1)} %collective-permute-done.16.refs_2_, ...), custom_call_target="tpu_custom_call" | custom-call | flops 2147483648 | bytes 4476928 | tf_op jit(solution)/shard_map/pallas_call | solution.py:30
  65.9 7.8 %collective-permute-done.19 = bf16[128,1024]{1,0:T(8,128)(2,1)S(1)} collective-permute-done((bf16[128,1024]{1,0:T(8,128)(2,1)S(1)}, bf16[128,1024]{1,0:T(8,128)(2,1)S(1)}, u32[]{:S(2)}, u32[]{:S(2)}) %collective-permute-start.19) | collective-permute-done | bytes 262176 | tf_op jit(solution)/shard_map/ppermute | solution.py:254
  (36 shorter events, 9.5 us)
Async XLA Ops:
  0.0 27.8 %copy-start = (bf16[8,128,256]{2,1,0:T(8,128)(2,1)S(1)}, bf16[8,128,256]{2,1,0:T(8,128)(2,1)}, u32[]{:S(2)}) copy-start(bf16[8,128,256]{2,1,0:T(8,128)(2,1)} %param.13) | copy-start | bytes 1572868
  0.0 0.7 copy-start.3
  0.7 0.9 %copy-start.1 = (bf16[128,1024]{1,0:T(8,128)(2,1)S(1)}, bf16[128,1024]{1,0:T(8,128)(2,1)}, u32[]{:S(2)}) copy-start(bf16[128,1024]{1,0:T(8,128)(2,1)} %refs_3_.1) | copy-start | bytes 786436
  1.7 0.9 %copy-start.2 = (bf16[128,1024]{1,0:T(8,128)(2,1)S(1)}, bf16[128,1024]{1,0:T(8,128)(2,1)}, u32[]{:S(2)}) copy-start(bf16[128,1024]{1,0:T(8,128)(2,1)} %refs_6_.1) | copy-start | bytes 786436
  3.8 17.5 %collective-permute-start.1 = (bf16[128,1536]{1,0:T(8,128)(2,1)S(1)}, bf16[128,1536]{1,0:T(8,128)(2,1)S(1)}, u32[]{:S(2)}, u32[]{:S(2)}) collective-permute-start(bf16[128,1536]{1,0:T(8,128)(2,1)S(1)} %get-tuple-element.38), channel_id=1, source_target_pairs={{0,8},{4,12},{8,0},{12,4},{1,9},{5,13},{9,1},{13,5},{2,10},{6,14},... | collective-permute-start | bytes 1179656 | tf_op jit(solution)/shard_map/ppermute | solution.py:254
  6.8 8.3 %collective-permute-start.3 = (bf16[128,512]{1,0:T(8,128)(2,1)S(1)}, bf16[128,512]{1,0:T(8,128)(2,1)S(1)}, u32[]{:S(2)}, u32[]{:S(2)}) collective-permute-start(bf16[128,512]{1,0:T(8,128)(2,1)S(1)} %get-tuple-element.39), channel_id=1, source_target_pairs={{0,3},{1,2},{2,1},{3,0},{4,7},{5,6},{6,5},{7,4},{8,11},{9,10},{10,... | collective-permute-start | bytes 393224 | tf_op jit(solution)/shard_map/ppermute | solution.py:257
  10.4 10.9 %collective-permute-start.2 = (bf16[128,512]{1,0:T(8,128)(2,1)S(1)}, bf16[128,512]{1,0:T(8,128)(2,1)S(1)}, u32[]{:S(2)}, u32[]{:S(2)}) collective-permute-start(bf16[128,512]{1,0:T(8,128)(2,1)S(1)} %get-tuple-element.39), channel_id=1, source_target_pairs={{0,2},{1,3},{2,0},{3,1},{4,6},{5,7},{6,4},{7,5},{8,10},{9,11},{10,... | collective-permute-start | bytes 393224 | tf_op jit(solution)/shard_map/ppermute | solution.py:257
  10.4 12.9 %collective-permute-start = (bf16[128,1536]{1,0:T(8,128)(2,1)S(1)}, bf16[128,1536]{1,0:T(8,128)(2,1)S(1)}, u32[]{:S(2)}, u32[]{:S(2)}) collective-permute-start(bf16[128,1536]{1,0:T(8,128)(2,1)S(1)} %get-tuple-element.37.refs_0_.refs_4_), channel_id=1, source_target_pairs={{0,4},{4,0},{8,12},{12,8},{1,5},{5,1},{9,13},{13,9},{2,6},{6,2},{1... | collective-permute-start | bytes 1179656 | tf_op jit(solution)/shard_map/ppermute | solution.py:254
  10.4 19.6 %collective-permute-start.5 = (bf16[256,768]{1,0:T(8,128)(2,1)S(1)}, bf16[256,768]{1,0:T(8,128)(2,1)S(1)}, u32[]{:S(2)}, u32[]{:S(2)}) collective-permute-start(bf16[256,768]{1,0:T(8,128)(2,1)S(1)} %get-tuple-element.44.refs_4_), channel_id=1, source_target_pairs={{0,1},{1,0},{2,3},{3,2},{4,5},{5,4},{6,7},{7,6},{8,9},{9,8},{10,11... | collective-permute-start | bytes 1179656 | tf_op jit(solution)/shard_map/ppermute | solution.py:257
  21.3 11.7 %collective-permute-start.4 = (bf16[128,1536]{1,0:T(8,128)(2,1)S(1)}, bf16[128,1536]{1,0:T(8,128)(2,1)S(1)}, u32[]{:S(2)}, u32[]{:S(2)}) collective-permute-start(bf16[128,1536]{1,0:T(8,128)(2,1)S(1)} %collective-permute-done.1.refs_2_.refs_6_), channel_id=1, source_target_pairs={{0,4},{4,0},{8,12},{12,8},{1,5},{5,1},{9,13},{13,9},{2,6},{6,2},{1... | collective-permute-start | bytes 1179656 | tf_op jit(solution)/shard_map/ppermute | solution.py:254
  21.3 6.3 %collective-permute-start.7 = (bf16[128,512]{1,0:T(8,128)(2,1)S(1)}, bf16[128,512]{1,0:T(8,128)(2,1)S(1)}, u32[]{:S(2)}, u32[]{:S(2)}) collective-permute-start(bf16[128,512]{1,0:T(8,128)(2,1)S(1)} %collective-permute-done.3.refs_8_), channel_id=1, source_target_pairs={{0,16},{16,0},{1,17},{17,1},{2,18},{18,2},{3,19},{19,3},{4,20},{20... | collective-permute-start | bytes 393224 | tf_op jit(solution)/shard_map/ppermute | solution.py:292
  22.8 7.2 %collective-permute-start.6 = (bf16[128,512]{1,0:T(8,128)(2,1)S(1)}, bf16[128,512]{1,0:T(8,128)(2,1)S(1)}, u32[]{:S(2)}, u32[]{:S(2)}) collective-permute-start(bf16[128,512]{1,0:T(8,128)(2,1)S(1)} %collective-permute-done.2.refs_6_), channel_id=1, source_target_pairs={{0,16},{16,0},{1,17},{17,1},{2,18},{18,2},{3,19},{19,3},{4,20},{20... | collective-permute-start | bytes 393224 | tf_op jit(solution)/shard_map/ppermute | solution.py:292
  23.4 6.7 %collective-permute-start.9 = (bf16[128,256]{1,0:T(8,128)(2,1)S(1)}, bf16[128,256]{1,0:T(8,128)(2,1)S(1)}, u32[]{:S(2)}, u32[]{:S(2)}) collective-permute-start(bf16[128,256]{1,0:T(8,128)(2,1)S(1)} %get-tuple-element.43), channel_id=1, source_target_pairs={{0,3},{1,2},{2,1},{3,0},{4,7},{5,6},{6,5},{7,4},{8,11},{9,10},{10,... | collective-permute-start | bytes 196616 | tf_op jit(solution)/shard_map/ppermute | solution.py:257
  27.6 5.4 %collective-permute-start.8 = (bf16[128,256]{1,0:T(8,128)(2,1)S(1)}, bf16[128,256]{1,0:T(8,128)(2,1)S(1)}, u32[]{:S(2)}, u32[]{:S(2)}) collective-permute-start(bf16[128,256]{1,0:T(8,128)(2,1)S(1)} %get-tuple-element.43), channel_id=1, source_target_pairs={{0,2},{1,3},{2,0},{3,1},{4,6},{5,7},{6,4},{7,5},{8,10},{9,11},{10,... | collective-permute-start | bytes 196616 | tf_op jit(solution)/shard_map/ppermute | solution.py:257
  35.1 11.7 %collective-permute-start.12 = (bf16[528,128]{1,0:T(8,128)(2,1)S(1)}, bf16[528,128]{1,0:T(8,128)(2,1)S(1)}, u32[]{:S(2)}, u32[]{:S(2)}) collective-permute-start(bf16[528,128]{1,0:T(8,128)(2,1)S(1)} %get-tuple-element.51), channel_id=1, source_target_pairs={{0,3},{1,2},{2,1},{3,0},{4,7},{5,6},{6,5},{7,4},{8,11},{9,10},{10,... | collective-permute-start | bytes 405512 | tf_op jit(solution)/shard_map/ppermute | solution.py:269
  37.3 10.8 %collective-permute-start.11 = (bf16[528,128]{1,0:T(8,128)(2,1)S(1)}, bf16[528,128]{1,0:T(8,128)(2,1)S(1)}, u32[]{:S(2)}, u32[]{:S(2)}) collective-permute-start(bf16[528,128]{1,0:T(8,128)(2,1)S(1)} %get-tuple-element.51), channel_id=1, source_target_pairs={{0,2},{1,3},{2,0},{3,1},{4,6},{5,7},{6,4},{7,5},{8,10},{9,11},{10,... | collective-permute-start | bytes 405512 | tf_op jit(solution)/shard_map/ppermute | solution.py:269
  37.3 10.8 %collective-permute-start.10 = (bf16[528,128]{1,0:T(8,128)(2,1)S(1)}, bf16[528,128]{1,0:T(8,128)(2,1)S(1)}, u32[]{:S(2)}, u32[]{:S(2)}) collective-permute-start(bf16[528,128]{1,0:T(8,128)(2,1)S(1)} %get-tuple-element.51), channel_id=1, source_target_pairs={{0,1},{1,0},{2,3},{3,2},{4,5},{5,4},{6,7},{7,6},{8,9},{9,8},{10,11... | collective-permute-start | bytes 405512 | tf_op jit(solution)/shard_map/ppermute | solution.py:269
  39.5 4.3 %collective-permute-start.13 = (bf16[128,256]{1,0:T(8,128)(2,1)S(1)}, bf16[128,256]{1,0:T(8,128)(2,1)S(1)}, u32[]{:S(2)}, u32[]{:S(2)}) collective-permute-start(bf16[128,256]{1,0:T(8,128)(2,1)S(1)} %collective-permute-done.8.refs_6_), channel_id=1, source_target_pairs={{0,16},{16,0},{1,17},{17,1},{2,18},{18,2},{3,19},{19,3},{4,20},{20... | collective-permute-start | bytes 196616 | tf_op jit(solution)/shard_map/ppermute | solution.py:292
  41.0 4.3 %collective-permute-start.14 = (bf16[128,256]{1,0:T(8,128)(2,1)S(1)}, bf16[128,256]{1,0:T(8,128)(2,1)S(1)}, u32[]{:S(2)}, u32[]{:S(2)}) collective-permute-start(bf16[128,256]{1,0:T(8,128)(2,1)S(1)} %collective-permute-done.9.refs_8_), channel_id=1, source_target_pairs={{0,16},{16,0},{1,17},{17,1},{2,18},{18,2},{3,19},{19,3},{4,20},{20... | collective-permute-start | bytes 196616 | tf_op jit(solution)/shard_map/ppermute | solution.py:292
  49.0 8.4 %collective-permute-start.17 = (bf16[528,128]{1,0:T(8,128)(2,1)S(1)}, bf16[528,128]{1,0:T(8,128)(2,1)S(1)}, u32[]{:S(2)}, u32[]{:S(2)}) collective-permute-start(bf16[528,128]{1,0:T(8,128)(2,1)S(1)} %get-tuple-element.62), channel_id=1, source_target_pairs={{0,3},{1,2},{2,1},{3,0},{4,7},{5,6},{6,5},{7,4},{8,11},{9,10},{10,... | collective-permute-start | bytes 405512 | tf_op jit(solution)/shard_map/ppermute | solution.py:269
  50.7 10.9 %collective-permute-start.16 = (bf16[528,128]{1,0:T(8,128)(2,1)S(1)}, bf16[528,128]{1,0:T(8,128)(2,1)S(1)}, u32[]{:S(2)}, u32[]{:S(2)}) collective-permute-start(bf16[528,128]{1,0:T(8,128)(2,1)S(1)} %get-tuple-element.62), channel_id=1, source_target_pairs={{0,2},{1,3},{2,0},{3,1},{4,6},{5,7},{6,4},{7,5},{8,10},{9,11},{10,... | collective-permute-start | bytes 405512 | tf_op jit(solution)/shard_map/ppermute | solution.py:269
  50.7 10.9 %collective-permute-start.15 = (bf16[528,128]{1,0:T(8,128)(2,1)S(1)}, bf16[528,128]{1,0:T(8,128)(2,1)S(1)}, u32[]{:S(2)}, u32[]{:S(2)}) collective-permute-start(bf16[528,128]{1,0:T(8,128)(2,1)S(1)} %get-tuple-element.62), channel_id=1, source_target_pairs={{0,1},{1,0},{2,3},{3,2},{4,5},{5,4},{6,7},{7,6},{8,9},{9,8},{10,11... | collective-permute-start | bytes 405512 | tf_op jit(solution)/shard_map/ppermute | solution.py:269
  63.2 2.0 %collective-permute-start.18 = (bf16[256,1024]{1,0:T(8,128)(2,1)S(1)}, bf16[256,1024]{1,0:T(8,128)(2,1)S(1)}, u32[]{:S(2)}, u32[]{:S(2)}) collective-permute-start(bf16[256,1024]{1,0:T(8,128)(2,1)S(1)} %get-tuple-element.68), channel_id=1, source_target_pairs={{0,4},{4,0},{8,12},{12,8},{1,5},{5,1},{9,13},{13,9},{2,6},{6,2},{1... | collective-permute-start | bytes 1572872 | tf_op jit(solution)/shard_map/ppermute | solution.py:254
  65.3 8.4 %collective-permute-start.19 = (bf16[128,1024]{1,0:T(8,128)(2,1)S(1)}, bf16[128,1024]{1,0:T(8,128)(2,1)S(1)}, u32[]{:S(2)}, u32[]{:S(2)}) collective-permute-start(bf16[128,1024]{1,0:T(8,128)(2,1)S(1)} %slice.15), channel_id=1, source_target_pairs={{0,8},{4,12},{8,0},{12,4},{1,9},{5,13},{9,1},{13,5},{2,10},{6,14},... | collective-permute-start | bytes 786440 | tf_op jit(solution)/shard_map/ppermute | solution.py:254

commit v8 on v7

--- a/solution.py
+++ b/solution.py
@@ -30,15 +30,14 @@
     return pl.pallas_call(
         body,
         out_shape=[jax.ShapeDtypeStruct(s, d) for s, d in outs],
-        compiler_params=pltpu.CompilerParams(vmem_limit_bytes=vmem * 2**20),
+        compiler_params=pltpu.CompilerParams(vmem_limit_bytes=int(vmem * 2**20)),
         cost_estimate=pl.CostEstimate(flops=flops, bytes_accessed=nbytes, transcendentals=0),
         **kw,
     )(*args)
 
 
-def first_kernel(g, cols, *refs):
-    ws, (events, offsets, frequency, cot) = refs[:3], refs[3:7]
-    (near, far, far_query), bufs, sems = refs[7:10], refs[10:-1], refs[-1]
+def weight_kernel(g, cols, *refs):
+    ws, (near, far, far_query), sems = refs[:3], refs[3:6], refs[6]
     mine = lax.axis_index("seq") % g
     at = pl.ds(pl.multiple_of(mine * cols, cols), cols)
     size = far.shape[0]
@@ -53,6 +52,12 @@
     copies = [pltpu.make_async_copy(a, b, sems.at[i]) for i, (a, b) in enumerate(copies)]
     for c in copies:
         c.start()
+    for c in copies:
+        c.wait()
+
+
+def input_kernel(g, cols, events, offsets, frequency, cot, *bufs):
+    mine = (lax.axis_index("seq") % g) // 2
     tokens, width = events.shape
     half = width // 2
     lanes = 128
@@ -65,9 +70,7 @@
             for buf in bufs:
                 buf[:, to] = x
     for k, buf in enumerate(bufs):
-        buf[:, width:] = cot[:, pl.ds(pl.multiple_of(((mine // 2) ^ k) * 2 * cols, 2 * cols), 2 * cols)]
-    for c in copies:
-        c.wait()
+        buf[:, width:] = cot[:, pl.ds(pl.multiple_of((mine ^ k) * 2 * cols, 2 * cols), 2 * cols)]
 
 
 def place_rows(full, parts, n, start):
@@ -207,18 +210,18 @@
         out[:, h * hd : (h + 1) * hd] = dot(pg, om[h], 1, 1).astype(BF16)
 
 
-def products(g, start, qg, kvg, wq, wkv, out):
+def products(g, blocks, qg, kvg, wq, wkv, out):
     rows = qg.shape[0] // g
-    for i in range(start, g, 2):
+    for j, i in enumerate(blocks):
         tok = slice(i * rows, (i + 1) * rows)
         o = dot(qg[tok, :], wq[...], 1, 1) + dot(kvg[tok, :], wkv[...], 1, 1)
-        out[(i // 2) * rows : (i // 2 + 1) * rows, :] = o.astype(out.dtype)
+        out[j * rows : (j + 1) * rows, :] = o.astype(out.dtype)
 
 
 def key_side_kernel(g, p, hp, *refs):
     parts = refs[:p]
     val, feat, sig, om, qg, wq, wkv = refs[p : p + 7]
-    odd, kvg = refs[p + 7 :]
+    odd, one, kvg = refs[p + 7 :]
     hd, m = om.shape[1], om.shape[2]
     base = hp * m
     cols = hp * hd
@@ -230,11 +233,12 @@
         kvg[:, cols + h * hd : cols + (h + 1) * hd] = dot(feat[:, h * m : (h + 1) * m], gh).astype(BF16)
         pg = (fg * sig[:, h * m : (h + 1) * m]).astype(BF16)
         kvg[:, col] = dot(pg, om[h], 1, 1).astype(BF16)
-    products(g, 1, qg, kvg, wq, wkv, odd)
-
-
-def even_kernel(g, qg, kvg, wq, wkv, even):
-    products(g, 0, qg, kvg, wq, wkv, even)
+    products(g, range(3, g, 2), qg, kvg, wq, wkv, odd)
+    products(g, [1], qg, kvg, wq, wkv, one)
+
+
+def even_kernel(g, blocks, qg, kvg, wq, wkv, even):
+    products(g, blocks, qg, kvg, wq, wkv, even)
 
 
 def local(events, offsets, cotangent, query_weight, key_weight, value_weight, omega):
@@ -274,17 +278,22 @@
     size = wrows // 2 if split else wrows
     wouts = [((wrows, 3 * cols), BF16), ((size, 2 * cols), BF16), ((size, cols), BF16)]
     frequency = jnp.exp(jnp.arange(width // 2, dtype=F32) * (-2.0 * math.log(10000.0) / width))
-    whole = pl.BlockSpec(memory_space=pltpu.VMEM)
-    firsts = call(
-        functools.partial(first_kernel, g, cols),
-        wouts + [((rows, width + 2 * cols), BF16)] * (g // 2),
-        [key_weight, value_weight, query_weight, events, offsets[None], frequency[None], cotangent],
+    near, far, far_query = call(
+        functools.partial(weight_kernel, g, cols),
+        wouts,
+        [key_weight, value_weight, query_weight],
         0,
-        vmem=52,
-        in_specs=[HBM] * 3 + [whole] * 4,
+        vmem=53,
+        in_specs=[HBM] * 3,
         scratch_shapes=[pltpu.SemaphoreType.DMA((6,))],
     )
-    (near, far, far_query), bufs = firsts[:3], firsts[3:]
+    offsets, _ = lax.optimization_barrier((offsets, near))
+    bufs = call(
+        functools.partial(input_kernel, g, cols),
+        [((rows, width + 2 * cols), BF16)] * (g // 2),
+        [events, offsets[None], frequency[None], cotangent],
+        0,
+    )
 
     def swapped(parts):
         if not split:
@@ -336,24 +345,29 @@
         [scaled_half, summary_half, norm, total_half, query_sig, om],
         4 * flop,
     )
-    odd, key_value_grad = call(
+    others = g // 2 - 1
+    odd, one, key_value_grad = call(
         functools.partial(key_side_kernel, g, p, hp),
-        [((t // 2, width), BF16), ((t, 2 * cols), BF16)],
+        [((others * rows, width), BF16), ((rows, width), BF16), ((t, 2 * cols), BF16)],
         [*summary_grad, val, key_feat, key_sig, om, query_grad, wq_full, wkv_full],
         8 * flop,
     )
     got = over_seq(odd, 1)
-    (even,) = call(
-        functools.partial(even_kernel, g),
-        [((t // 2, width), F32)],
-        [query_grad, key_value_grad, wq_full, wkv_full],
-        8 * flop,
-    )
-    both = even + got.astype(F32)
-    out = both[:rows]
+    got_one = over_seq(one, 1)
+
+    def even_blocks(blocks):
+        return call(
+            functools.partial(even_kernel, g, blocks),
+            [((len(blocks) * rows, width), F32)],
+            [query_grad, key_value_grad, wq_full, wkv_full],
+            8 * flop,
+        )[0]
+
+    both = (even_blocks(range(2, g, 2)) + got.astype(F32)).astype(BF16)
+    out = even_blocks([0]) + got_one.astype(F32)
     for k in range(2, g, 2):
-        at = (k // 2) * rows
-        out = out + over_seq(both[at : at + rows].astype(BF16), k).astype(F32)
+        at = (k // 2 - 1) * rows
+        out = out + over_seq(both[at : at + rows], k).astype(F32)
     return out.astype(BF16)
 
 

time: 74.7 us -> 73.6 us (0.985)
  local copies, waits for them, and re-layouts: 2.65 us -> 0.68 us
  Pallas kernels: 8.72 us -> 10.1 us
  waiting for transfers between devices: 38.5 us -> 37.5 us
    unnamed x8, local copies, waits for them, and re-layouts: 2.61 us -> 0.67 us
    pallas_call x7 -> x9, Pallas kernels: 8.72 us -> 10.1 us  [call(): pl.pallas_call(body, out_shape=[jax.ShapeDtypeStruct(s, d) for s, d in ou...]
    ppermute x5 -> x6, waiting for transfers between devices: 8.58 us -> 7.54 us  [over_seq(): return lax.ppermute(x, 'seq', [(i, i ^ k) for i in range(n_seq)])]
    ppermute x5 -> x6, starting transfers between devices: 3.67 us -> 4.19 us  [over_seq(): return lax.ppermute(x, 'seq', [(i, i ^ k) for i in range(n_seq)])]
  transfers between devices with their start and end apart: 20 -> 21, of which waited for: 12 -> 12; matrix products, arithmetic and copies ran while one was open for 0% -> 0% of each run, Pallas kernels for 4% -> 4%
where the time goes in v8:
time: 73.6 us; the launch traced here: 73.4 us
  waiting for transfers between devices  37.5 us (51%)
  starting transfers between devices  24.1 us (33%)
  Pallas kernels  10.1 us (14%)
  other arithmetic  0.89 us (1%)
    ppermute x5, waiting for transfers between devices, over_sub(): return lax.ppermute(x, 'sub', [(i, i ^ k) for i in range(n_sub)])  13.1 us
    pallas_call x9, Pallas kernels, call(): pl.pallas_call(body, out_shape=[jax.ShapeDtypeStruct(s, d) for s, d in ou...  10.1 us
    ppermute x6, waiting for transfers between devices, to_all(): parts.append(lax.ppermute(send, ('seq', 'sub'), perm))  8.98 us
    ppermute x6, starting transfers between devices, to_all(): parts.append(lax.ppermute(send, ('seq', 'sub'), perm))  8.91 us
    ppermute x4, waiting for transfers between devices, swapped(): lax.ppermute(part, 'grp', [(0, 1), (1, 0)])  7.86 us
    ppermute x6, waiting for transfers between devices, over_seq(): return lax.ppermute(x, 'seq', [(i, i ^ k) for i in range(n_seq)])  7.54 us
    ppermute x5, starting transfers between devices, over_sub(): return lax.ppermute(x, 'sub', [(i, i ^ k) for i in range(n_sub)])  6.96 us
    ppermute x6, starting transfers between devices, over_seq(): return lax.ppermute(x, 'seq', [(i, i ^ k) for i in range(n_seq)])  4.19 us
  transfers between devices with their start and end apart: 21, of which 12 were waited for; matrix products, arithmetic and copies ran while one was open for 0% of the time, Pallas kernels for 4%

profile of v8, /device:TPU:0, one launch (start us, length us, event | category | flops | bytes accessed | tf_op | source)
XLA Modules:
  0.0 73.4 jit_solution(15939309203503448712)
XLA Ops:
  0.0 1.2 %shard_map.73 = (bf16[256,768]{1,0:T(8,128)(2,1)S(1)}, bf16[128,512]{1,0:T(8,128)(2,1)S(1)}, bf16[128,256]{1,0:T(8,128)(2,1)S(1)}) custom-call(bf16[256,1024]{1,0:T(8,128)(2,1)} %refs_0_.1, bf16[256,1024]{1,0:T(8,128)(2,1)} %refs_1_.1, bf16[256,1024]{1,0:T(8,128)(2,1)} %refs_2_.1), custom_call_target="tpu_custom_call" | custom-call | tf_op jit(solution)/shard_map/pallas_call | solution.py:30
  3.1 3.0 %collective-permute-start.1 = (bf16[128,1536]{1,0:T(8,128)(2,1)S(1)}, bf16[128,1536]{1,0:T(8,128)(2,1)S(1)}, u32[]{:S(2)}, u32[]{:S(2)}) collective-permute-start(bf16[128,1536]{1,0:T(8,128)(2,1)S(1)} %get-tuple-element.42), channel_id=1, source_target_pairs={{0,8},{4,12},{8,0},{12,4},{1,9},{5,13},{9,1},{13,5},{2,10},{6,14},... | collective-permute-start | bytes 1179656 | tf_op jit(solution)/shard_map/ppermute | solution.py:258
  6.1 3.6 %collective-permute-start.3 = (bf16[128,512]{1,0:T(8,128)(2,1)S(1)}, bf16[128,512]{1,0:T(8,128)(2,1)S(1)}, u32[]{:S(2)}, u32[]{:S(2)}) collective-permute-start(bf16[128,512]{1,0:T(8,128)(2,1)S(1)} %get-tuple-element.43), channel_id=1, source_target_pairs={{0,3},{1,2},{2,1},{3,0},{4,7},{5,6},{6,5},{7,4},{8,11},{9,10},{10,... | collective-permute-start | bytes 393224 | tf_op jit(solution)/shard_map/ppermute | solution.py:261
  10.5 3.9 %collective-permute-done.3.refs_8_ = bf16[128,512]{1,0:T(8,128)(2,1)S(1)} collective-permute-done((bf16[128,512]{1,0:T(8,128)(2,1)S(1)}, bf16[128,512]{1,0:T(8,128)(2,1)S(1)}, u32[]{:S(2)}, u32[]{:S(2)}) %collective-permute-start.3) | collective-permute-done | bytes 131104 | tf_op jit(solution)/shard_map/ppermute | solution.py:261
  14.4 6.2 %collective-permute-done.2.refs_6_ = bf16[128,512]{1,0:T(8,128)(2,1)S(1)} collective-permute-done((bf16[128,512]{1,0:T(8,128)(2,1)S(1)}, bf16[128,512]{1,0:T(8,128)(2,1)S(1)}, u32[]{:S(2)}, u32[]{:S(2)}) %collective-permute-start.2) | collective-permute-done | bytes 131104 | tf_op jit(solution)/shard_map/ppermute | solution.py:261
  20.6 1.5 %collective-permute-start.7 = (bf16[128,512]{1,0:T(8,128)(2,1)S(1)}, bf16[128,512]{1,0:T(8,128)(2,1)S(1)}, u32[]{:S(2)}, u32[]{:S(2)}) collective-permute-start(bf16[128,512]{1,0:T(8,128)(2,1)S(1)} %collective-permute-done.3.refs_8_), channel_id=1, source_target_pairs={{0,16},{16,0},{1,17},{17,1},{2,18},{18,2},{3,19},{19,3},{4,20},{20... | collective-permute-start | bytes 393224 | tf_op jit(solution)/shard_map/ppermute | solution.py:301
  22.6 2.4 %collective-permute-start.9 = (bf16[128,256]{1,0:T(8,128)(2,1)S(1)}, bf16[128,256]{1,0:T(8,128)(2,1)S(1)}, u32[]{:S(2)}, u32[]{:S(2)}) collective-permute-start(bf16[128,256]{1,0:T(8,128)(2,1)S(1)} %get-tuple-element.46), channel_id=1, source_target_pairs={{0,3},{1,2},{2,1},{3,0},{4,7},{5,6},{6,5},{7,4},{8,11},{9,10},{10,... | collective-permute-start | bytes 196616 | tf_op jit(solution)/shard_map/ppermute | solution.py:261
  25.0 1.8 %collective-permute-done.7.refs_9_ = bf16[128,512]{1,0:T(8,128)(2,1)S(1)} collective-permute-done((bf16[128,512]{1,0:T(8,128)(2,1)S(1)}, bf16[128,512]{1,0:T(8,128)(2,1)S(1)}, u32[]{:S(2)}, u32[]{:S(2)}) %collective-permute-start.7) | collective-permute-done | bytes 131104 | tf_op jit(solution)/shard_map/ppermute | solution.py:301
  27.0 2.3 %collective-permute-done.6.refs_7_ = bf16[128,512]{1,0:T(8,128)(2,1)S(1)} collective-permute-done((bf16[128,512]{1,0:T(8,128)(2,1)S(1)}, bf16[128,512]{1,0:T(8,128)(2,1)S(1)}, u32[]{:S(2)}, u32[]{:S(2)}) %collective-permute-start.6) | collective-permute-done | bytes 131104 | tf_op jit(solution)/shard_map/ppermute | solution.py:301
  29.3 3.0 %collective-permute-done.8.refs_6_ = bf16[128,256]{1,0:T(8,128)(2,1)S(1)} collective-permute-done((bf16[128,256]{1,0:T(8,128)(2,1)S(1)}, bf16[128,256]{1,0:T(8,128)(2,1)S(1)}, u32[]{:S(2)}, u32[]{:S(2)}) %collective-permute-start.8) | collective-permute-done | bytes 65568 | tf_op jit(solution)/shard_map/ppermute | solution.py:261
  32.3 2.0 %shard_map.75 = (bf16[1024,512]{1,0:T(8,128)(2,1)S(1)}, bf16[512,512]{1,0:T(8,128)(2,1)S(1)}, f32[512,512]{1,0:T(8,128)S(1)}, bf16[512,256]{1,0:T(8,128)(2,1)S(1...) custom-call(bf16[128,1536]{1,0:T(8,128)(2,1)S(1)} %get-tuple-element.41.refs_0_.refs_4_, ...), custom_call_target="tpu_custom_call" | custom-call | flops 2147483648 | bytes 3014656 | tf_op jit(solution)/shard_map/pallas_call | solution.py:30
  34.3 2.2 %collective-permute-start.12 = (bf16[528,128]{1,0:T(8,128)(2,1)S(1)}, bf16[528,128]{1,0:T(8,128)(2,1)S(1)}, u32[]{:S(2)}, u32[]{:S(2)}) collective-permute-start(bf16[528,128]{1,0:T(8,128)(2,1)S(1)} %get-tuple-element.54), channel_id=1, source_target_pairs={{0,3},{1,2},{2,1},{3,0},{4,7},{5,6},{6,5},{7,4},{8,11},{9,10},{10,... | collective-permute-start | bytes 405512 | tf_op jit(solution)/shard_map/ppermute | solution.py:273
  36.6 2.2 %collective-permute-start.10 = (bf16[528,128]{1,0:T(8,128)(2,1)S(1)}, bf16[528,128]{1,0:T(8,128)(2,1)S(1)}, u32[]{:S(2)}, u32[]{:S(2)}) collective-permute-start(bf16[528,128]{1,0:T(8,128)(2,1)S(1)} %get-tuple-element.54), channel_id=1, source_target_pairs={{0,1},{1,0},{2,3},{3,2},{4,5},{5,4},{6,7},{7,6},{8,9},{9,8},{10,11... | collective-permute-start | bytes 405512 | tf_op jit(solution)/shard_map/ppermute | solution.py:273
  38.8 1.5 %collective-permute-start.13 = (bf16[128,256]{1,0:T(8,128)(2,1)S(1)}, bf16[128,256]{1,0:T(8,128)(2,1)S(1)}, u32[]{:S(2)}, u32[]{:S(2)}) collective-permute-start(bf16[128,256]{1,0:T(8,128)(2,1)S(1)} %collective-permute-done.8.refs_6_), channel_id=1, source_target_pairs={{0,16},{16,0},{1,17},{17,1},{2,18},{18,2},{3,19},{19,3},{4,20},{20... | collective-permute-start | bytes 196616 | tf_op jit(solution)/shard_map/ppermute | solution.py:301
  40.8 2.2 %collective-permute-done.13.refs_7_ = bf16[128,256]{1,0:T(8,128)(2,1)S(1)} collective-permute-done((bf16[128,256]{1,0:T(8,128)(2,1)S(1)}, bf16[128,256]{1,0:T(8,128)(2,1)S(1)}, u32[]{:S(2)}, u32[]{:S(2)}) %collective-permute-start.13) | collective-permute-done | bytes 65568 | tf_op jit(solution)/shard_map/ppermute | solution.py:301
  43.0 1.5 %collective-permute-done.14.refs_9_ = bf16[128,256]{1,0:T(8,128)(2,1)S(1)} collective-permute-done((bf16[128,256]{1,0:T(8,128)(2,1)S(1)}, bf16[128,256]{1,0:T(8,128)(2,1)S(1)}, u32[]{:S(2)}, u32[]{:S(2)}) %collective-permute-start.14) | collective-permute-done | bytes 65568 | tf_op jit(solution)/shard_map/ppermute | solution.py:301
  44.6 1.4 %shard_map.76 = (bf16[1024,256]{1,0:T(8,128)(2,1)S(1)}, bf16[512,512]{1,0:T(8,128)(2,1)S(1)}, f32[512,512]{1,0:T(8,128)S(1)}) custom-call(bf16[128,1536]{1,0:T(8,128)(2,1)S(1)} %get-tuple-element.41.refs_0_.refs_4_, bf16[128,1536]{1,0:T(8,128)(2,1)S(1)} %collective-permute-done.refs_1_.refs_5_, bf16[128,1536]{1,0:T(8,128)(2,1)S(1)} %collective-permute-done.1.refs_2_.refs_6_, ...), custom_call_target="tpu_custom_call" | custom-call | tf_op jit(solution)/shard_map/pallas_call | solution.py:30
  46.0 1.4 %collective-permute-done.11.refs_2_ = bf16[528,128]{1,0:T(8,128)(2,1)S(1)} collective-permute-done((bf16[528,128]{1,0:T(8,128)(2,1)S(1)}, bf16[528,128]{1,0:T(8,128)(2,1)S(1)}, u32[]{:S(2)}, u32[]{:S(2)}) %collective-permute-start.11) | collective-permute-done | bytes 135200 | tf_op jit(solution)/shard_map/ppermute | solution.py:273
  48.2 1.7 %collective-permute-start.17 = (bf16[528,128]{1,0:T(8,128)(2,1)S(1)}, bf16[528,128]{1,0:T(8,128)(2,1)S(1)}, u32[]{:S(2)}, u32[]{:S(2)}) collective-permute-start(bf16[528,128]{1,0:T(8,128)(2,1)S(1)} %get-tuple-element.65), channel_id=1, source_target_pairs={{0,3},{1,2},{2,1},{3,0},{4,7},{5,6},{6,5},{7,4},{8,11},{9,10},{10,... | collective-permute-start | bytes 405512 | tf_op jit(solution)/shard_map/ppermute | solution.py:273
  49.9 2.8 %collective-permute-start.15 = (bf16[528,128]{1,0:T(8,128)(2,1)S(1)}, bf16[528,128]{1,0:T(8,128)(2,1)S(1)}, u32[]{:S(2)}, u32[]{:S(2)}) collective-permute-start(bf16[528,128]{1,0:T(8,128)(2,1)S(1)} %get-tuple-element.65), channel_id=1, source_target_pairs={{0,1},{1,0},{2,3},{3,2},{4,5},{5,4},{6,7},{7,6},{8,9},{9,8},{10,11... | collective-permute-start | bytes 405512 | tf_op jit(solution)/shard_map/ppermute | solution.py:273
  53.2 3.4 %collective-permute-done.17.refs_3_ = bf16[528,128]{1,0:T(8,128)(2,1)S(1)} collective-permute-done((bf16[528,128]{1,0:T(8,128)(2,1)S(1)}, bf16[528,128]{1,0:T(8,128)(2,1)S(1)}, u32[]{:S(2)}, u32[]{:S(2)}) %collective-permute-start.17) | collective-permute-done | bytes 135200 | tf_op jit(solution)/shard_map/ppermute | solution.py:273
  56.6 4.2 %collective-permute-done.16.refs_2_ = bf16[528,128]{1,0:T(8,128)(2,1)S(1)} collective-permute-done((bf16[528,128]{1,0:T(8,128)(2,1)S(1)}, bf16[528,128]{1,0:T(8,128)(2,1)S(1)}, u32[]{:S(2)}, u32[]{:S(2)}) %collective-permute-start.16) | collective-permute-done | bytes 135200 | tf_op jit(solution)/shard_map/ppermute | solution.py:273
  60.9 1.7 %shard_map.79 = (bf16[128,1024]{1,0:T(8,128)(2,1)S(1)}, bf16[128,1024]{1,0:T(8,128)(2,1)S(1)}, bf16[512,512]{1,0:T(8,128)(2,1)S(1)}) custom-call(f32[528,128]{1,0:T(8,128)S(1)} %get-tuple-element.64.refs_0_, bf16[528,128]{1,0:T(8,128)(2,1)S(1)} %collective-permute-done.15.refs_1_, bf16[528,128]{1,0:T(8,128)(2,1)S(1)} %collective-permute-done.16.refs_2_, ...), custom_call_target="tpu_custom_call" | custom-call | flops 2147483648 | bytes 4476928 | tf_op jit(solution)/shard_map/pallas_call | solution.py:30
  65.5 7.1 %collective-permute-done.20 = bf16[128,1024]{1,0:T(8,128)(2,1)S(1)} collective-permute-done((bf16[128,1024]{1,0:T(8,128)(2,1)S(1)}, bf16[128,1024]{1,0:T(8,128)(2,1)S(1)}, u32[]{:S(2)}, u32[]{:S(2)}) %collective-permute-start.20) | collective-permute-done | bytes 262176 | tf_op jit(solution)/shard_map/ppermute | solution.py:258
  (39 shorter events, 8.9 us)
Async XLA Ops:
  0.0 27.0 %copy-start = (bf16[8,128,256]{2,1,0:T(8,128)(2,1)S(1)}, bf16[8,128,256]{2,1,0:T(8,128)(2,1)}, u32[]{:S(2)}) copy-start(bf16[8,128,256]{2,1,0:T(8,128)(2,1)} %param.13) | copy-start | bytes 1572868
  0.0 1.3 %copy-start.1 = (bf16[128,1024]{1,0:T(8,128)(2,1)S(1)}, bf16[128,1024]{1,0:T(8,128)(2,1)}, u32[]{:S(2)}) copy-start(bf16[128,1024]{1,0:T(8,128)(2,1)} %events.1) | copy-start | bytes 786436
  0.0 1.4 %copy-start.2 = (bf16[128,1024]{1,0:T(8,128)(2,1)S(1)}, bf16[128,1024]{1,0:T(8,128)(2,1)}, u32[]{:S(2)}) copy-start(bf16[128,1024]{1,0:T(8,128)(2,1)} %cot.1) | copy-start | bytes 786436
  3.1 17.5 %collective-permute-start.1 = (bf16[128,1536]{1,0:T(8,128)(2,1)S(1)}, bf16[128,1536]{1,0:T(8,128)(2,1)S(1)}, u32[]{:S(2)}, u32[]{:S(2)}) collective-permute-start(bf16[128,1536]{1,0:T(8,128)(2,1)S(1)} %get-tuple-element.42), channel_id=1, source_target_pairs={{0,8},{4,12},{8,0},{12,4},{1,9},{5,13},{9,1},{13,5},{2,10},{6,14},... | collective-permute-start | bytes 1179656 | tf_op jit(solution)/shard_map/ppermute | solution.py:258
  6.1 8.3 %collective-permute-start.3 = (bf16[128,512]{1,0:T(8,128)(2,1)S(1)}, bf16[128,512]{1,0:T(8,128)(2,1)S(1)}, u32[]{:S(2)}, u32[]{:S(2)}) collective-permute-start(bf16[128,512]{1,0:T(8,128)(2,1)S(1)} %get-tuple-element.43), channel_id=1, source_target_pairs={{0,3},{1,2},{2,1},{3,0},{4,7},{5,6},{6,5},{7,4},{8,11},{9,10},{10,... | collective-permute-start | bytes 393224 | tf_op jit(solution)/shard_map/ppermute | solution.py:261
  9.7 10.9 %collective-permute-start.2 = (bf16[128,512]{1,0:T(8,128)(2,1)S(1)}, bf16[128,512]{1,0:T(8,128)(2,1)S(1)}, u32[]{:S(2)}, u32[]{:S(2)}) collective-permute-start(bf16[128,512]{1,0:T(8,128)(2,1)S(1)} %get-tuple-element.43), channel_id=1, source_target_pairs={{0,2},{1,3},{2,0},{3,1},{4,6},{5,7},{6,4},{7,5},{8,10},{9,11},{10,... | collective-permute-start | bytes 393224 | tf_op jit(solution)/shard_map/ppermute | solution.py:261
  9.7 12.9 %collective-permute-start = (bf16[128,1536]{1,0:T(8,128)(2,1)S(1)}, bf16[128,1536]{1,0:T(8,128)(2,1)S(1)}, u32[]{:S(2)}, u32[]{:S(2)}) collective-permute-start(bf16[128,1536]{1,0:T(8,128)(2,1)S(1)} %get-tuple-element.41.refs_0_.refs_4_), channel_id=1, source_target_pairs={{0,4},{4,0},{8,12},{12,8},{1,5},{5,1},{9,13},{13,9},{2,6},{6,2},{1... | collective-permute-start | bytes 1179656 | tf_op jit(solution)/shard_map/ppermute | solution.py:258
  9.7 19.6 %collective-permute-start.5 = (bf16[256,768]{1,0:T(8,128)(2,1)S(1)}, bf16[256,768]{1,0:T(8,128)(2,1)S(1)}, u32[]{:S(2)}, u32[]{:S(2)}) collective-permute-start(bf16[256,768]{1,0:T(8,128)(2,1)S(1)} %get-tuple-element.47.refs_4_), channel_id=1, source_target_pairs={{0,1},{1,0},{2,3},{3,2},{4,5},{5,4},{6,7},{7,6},{8,9},{9,8},{10,11... | collective-permute-start | bytes 1179656 | tf_op jit(solution)/shard_map/ppermute | solution.py:261
  20.6 11.7 %collective-permute-start.4 = (bf16[128,1536]{1,0:T(8,128)(2,1)S(1)}, bf16[128,1536]{1,0:T(8,128)(2,1)S(1)}, u32[]{:S(2)}, u32[]{:S(2)}) collective-permute-start(bf16[128,1536]{1,0:T(8,128)(2,1)S(1)} %collective-permute-done.1.refs_2_.refs_6_), channel_id=1, source_target_pairs={{0,4},{4,0},{8,12},{12,8},{1,5},{5,1},{9,13},{13,9},{2,6},{6,2},{1... | collective-permute-start | bytes 1179656 | tf_op jit(solution)/shard_map/ppermute | solution.py:258
  20.6 6.3 %collective-permute-start.7 = (bf16[128,512]{1,0:T(8,128)(2,1)S(1)}, bf16[128,512]{1,0:T(8,128)(2,1)S(1)}, u32[]{:S(2)}, u32[]{:S(2)}) collective-permute-start(bf16[128,512]{1,0:T(8,128)(2,1)S(1)} %collective-permute-done.3.refs_8_), channel_id=1, source_target_pairs={{0,16},{16,0},{1,17},{17,1},{2,18},{18,2},{3,19},{19,3},{4,20},{20... | collective-permute-start | bytes 393224 | tf_op jit(solution)/shard_map/ppermute | solution.py:301
  22.1 7.2 %collective-permute-start.6 = (bf16[128,512]{1,0:T(8,128)(2,1)S(1)}, bf16[128,512]{1,0:T(8,128)(2,1)S(1)}, u32[]{:S(2)}, u32[]{:S(2)}) collective-permute-start(bf16[128,512]{1,0:T(8,128)(2,1)S(1)} %collective-permute-done.2.refs_6_), channel_id=1, source_target_pairs={{0,16},{16,0},{1,17},{17,1},{2,18},{18,2},{3,19},{19,3},{4,20},{20... | collective-permute-start | bytes 393224 | tf_op jit(solution)/shard_map/ppermute | solution.py:301
  22.6 6.7 %collective-permute-start.9 = (bf16[128,256]{1,0:T(8,128)(2,1)S(1)}, bf16[128,256]{1,0:T(8,128)(2,1)S(1)}, u32[]{:S(2)}, u32[]{:S(2)}) collective-permute-start(bf16[128,256]{1,0:T(8,128)(2,1)S(1)} %get-tuple-element.46), channel_id=1, source_target_pairs={{0,3},{1,2},{2,1},{3,0},{4,7},{5,6},{6,5},{7,4},{8,11},{9,10},{10,... | collective-permute-start | bytes 196616 | tf_op jit(solution)/shard_map/ppermute | solution.py:261
  26.9 5.4 %collective-permute-start.8 = (bf16[128,256]{1,0:T(8,128)(2,1)S(1)}, bf16[128,256]{1,0:T(8,128)(2,1)S(1)}, u32[]{:S(2)}, u32[]{:S(2)}) collective-permute-start(bf16[128,256]{1,0:T(8,128)(2,1)S(1)} %get-tuple-element.46), channel_id=1, source_target_pairs={{0,2},{1,3},{2,0},{3,1},{4,6},{5,7},{6,4},{7,5},{8,10},{9,11},{10,... | collective-permute-start | bytes 196616 | tf_op jit(solution)/shard_map/ppermute | solution.py:261
  34.3 11.7 %collective-permute-start.12 = (bf16[528,128]{1,0:T(8,128)(2,1)S(1)}, bf16[528,128]{1,0:T(8,128)(2,1)S(1)}, u32[]{:S(2)}, u32[]{:S(2)}) collective-permute-start(bf16[528,128]{1,0:T(8,128)(2,1)S(1)} %get-tuple-element.54), channel_id=1, source_target_pairs={{0,3},{1,2},{2,1},{3,0},{4,7},{5,6},{6,5},{7,4},{8,11},{9,10},{10,... | collective-permute-start | bytes 405512 | tf_op jit(solution)/shard_map/ppermute | solution.py:273
  36.6 10.8 %collective-permute-start.11 = (bf16[528,128]{1,0:T(8,128)(2,1)S(1)}, bf16[528,128]{1,0:T(8,128)(2,1)S(1)}, u32[]{:S(2)}, u32[]{:S(2)}) collective-permute-start(bf16[528,128]{1,0:T(8,128)(2,1)S(1)} %get-tuple-element.54), channel_id=1, source_target_pairs={{0,2},{1,3},{2,0},{3,1},{4,6},{5,7},{6,4},{7,5},{8,10},{9,11},{10,... | collective-permute-start | bytes 405512 | tf_op jit(solution)/shard_map/ppermute | solution.py:273
  36.6 10.8 %collective-permute-start.10 = (bf16[528,128]{1,0:T(8,128)(2,1)S(1)}, bf16[528,128]{1,0:T(8,128)(2,1)S(1)}, u32[]{:S(2)}, u32[]{:S(2)}) collective-permute-start(bf16[528,128]{1,0:T(8,128)(2,1)S(1)} %get-tuple-element.54), channel_id=1, source_target_pairs={{0,1},{1,0},{2,3},{3,2},{4,5},{5,4},{6,7},{7,6},{8,9},{9,8},{10,11... | collective-permute-start | bytes 405512 | tf_op jit(solution)/shard_map/ppermute | solution.py:273
  38.8 4.3 %collective-permute-start.13 = (bf16[128,256]{1,0:T(8,128)(2,1)S(1)}, bf16[128,256]{1,0:T(8,128)(2,1)S(1)}, u32[]{:S(2)}, u32[]{:S(2)}) collective-permute-start(bf16[128,256]{1,0:T(8,128)(2,1)S(1)} %collective-permute-done.8.refs_6_), channel_id=1, source_target_pairs={{0,16},{16,0},{1,17},{17,1},{2,18},{18,2},{3,19},{19,3},{4,20},{20... | collective-permute-start | bytes 196616 | tf_op jit(solution)/shard_map/ppermute | solution.py:301
  40.3 4.3 %collective-permute-start.14 = (bf16[128,256]{1,0:T(8,128)(2,1)S(1)}, bf16[128,256]{1,0:T(8,128)(2,1)S(1)}, u32[]{:S(2)}, u32[]{:S(2)}) collective-permute-start(bf16[128,256]{1,0:T(8,128)(2,1)S(1)} %collective-permute-done.9.refs_8_), channel_id=1, source_target_pairs={{0,16},{16,0},{1,17},{17,1},{2,18},{18,2},{3,19},{19,3},{4,20},{20... | collective-permute-start | bytes 196616 | tf_op jit(solution)/shard_map/ppermute | solution.py:301
  48.2 8.4 %collective-permute-start.17 = (bf16[528,128]{1,0:T(8,128)(2,1)S(1)}, bf16[528,128]{1,0:T(8,128)(2,1)S(1)}, u32[]{:S(2)}, u32[]{:S(2)}) collective-permute-start(bf16[528,128]{1,0:T(8,128)(2,1)S(1)} %get-tuple-element.65), channel_id=1, source_target_pairs={{0,3},{1,2},{2,1},{3,0},{4,7},{5,6},{6,5},{7,4},{8,11},{9,10},{10,... | collective-permute-start | bytes 405512 | tf_op jit(solution)/shard_map/ppermute | solution.py:273
  49.9 10.9 %collective-permute-start.16 = (bf16[528,128]{1,0:T(8,128)(2,1)S(1)}, bf16[528,128]{1,0:T(8,128)(2,1)S(1)}, u32[]{:S(2)}, u32[]{:S(2)}) collective-permute-start(bf16[528,128]{1,0:T(8,128)(2,1)S(1)} %get-tuple-element.65), channel_id=1, source_target_pairs={{0,2},{1,3},{2,0},{3,1},{4,6},{5,7},{6,4},{7,5},{8,10},{9,11},{10,... | collective-permute-start | bytes 405512 | tf_op jit(solution)/shard_map/ppermute | solution.py:273
  49.9 10.9 %collective-permute-start.15 = (bf16[528,128]{1,0:T(8,128)(2,1)S(1)}, bf16[528,128]{1,0:T(8,128)(2,1)S(1)}, u32[]{:S(2)}, u32[]{:S(2)}) collective-permute-start(bf16[528,128]{1,0:T(8,128)(2,1)S(1)} %get-tuple-element.65), channel_id=1, source_target_pairs={{0,1},{1,0},{2,3},{3,2},{4,5},{5,4},{6,7},{7,6},{8,9},{9,8},{10,11... | collective-permute-start | bytes 405512 | tf_op jit(solution)/shard_map/ppermute | solution.py:273
  62.5 1.6 %collective-permute-start.19 = (bf16[128,1024]{1,0:T(8,128)(2,1)S(1)}, bf16[128,1024]{1,0:T(8,128)(2,1)S(1)}, u32[]{:S(2)}, u32[]{:S(2)}) collective-permute-start(bf16[128,1024]{1,0:T(8,128)(2,1)S(1)} %get-tuple-element.72), channel_id=1, source_target_pairs={{0,4},{4,0},{8,12},{12,8},{1,5},{5,1},{9,13},{13,9},{2,6},{6,2},{1... | collective-permute-start | bytes 786440 | tf_op jit(solution)/shard_map/ppermute | solution.py:258
  62.6 2.9 %collective-permute-start.18 = (bf16[128,1024]{1,0:T(8,128)(2,1)S(1)}, bf16[128,1024]{1,0:T(8,128)(2,1)S(1)}, u32[]{:S(2)}, u32[]{:S(2)}) collective-permute-start(bf16[128,1024]{1,0:T(8,128)(2,1)S(1)} %get-tuple-element.71), channel_id=1, source_target_pairs={{0,4},{4,0},{8,12},{12,8},{1,5},{5,1},{9,13},{13,9},{2,6},{6,2},{1... | collective-permute-start | bytes 786440 | tf_op jit(solution)/shard_map/ppermute | solution.py:258
  64.2 8.4 %collective-permute-start.20 = (bf16[128,1024]{1,0:T(8,128)(2,1)S(1)}, bf16[128,1024]{1,0:T(8,128)(2,1)S(1)}, u32[]{:S(2)}, u32[]{:S(2)}) collective-permute-start(bf16[128,1024]{1,0:T(8,128)(2,1)S(1)} %add_convert_fusion.1), channel_id=1, source_target_pairs={{0,8},{4,12},{8,0},{12,4},{1,9},{5,13},{9,1},{13,5},{2,10},{6,14},... | collective-permute-start | bytes 786440 | tf_op jit(solution)/shard_map/ppermute | solution.py:258
  (1 other events, 0.7 us)

commit v9 on v8

--- a/solution.py
+++ b/solution.py
@@ -132,7 +132,7 @@
 
 def key_value_kernel(g, n, nw, hp, width, *refs):
     xs, ws, om = refs[:g], refs[g : g + nw], refs[g + nw]
-    w_full, feat, sig, val, own, send = refs[g + nw + 1 :]
+    w_full, feat, sig, val, total = refs[g + nw + 1 :]
     hd, m = om.shape[1], om.shape[2]
     cols = hp * hd
     place_rows(w_full, ws, n, 0)
@@ -144,6 +144,11 @@
         for h in range(hp):
             soft = features(act, om, h, i, feat, sig)
             sums[h] = sums[h] + jnp.sum(soft.astype(F32), axis=0, keepdims=True)
+    total[...] = jnp.concatenate(sums, axis=1)
+
+
+def summary_kernel(hp, feat, val, total, own, send):
+    m, hd = feat.shape[1] // hp, val.shape[1] // hp
     base = hp * m
     own[base:, :] = jnp.zeros_like(own[base:, :])
     send[base:, :] = jnp.zeros_like(send[base:, :])
@@ -151,7 +156,7 @@
         s = dot(feat[:, h * m : (h + 1) * m], val[:, h * hd : (h + 1) * hd], 0, 0)
         own[h * m : (h + 1) * m, :] = s
         send[h * m : (h + 1) * m, :] = s.astype(BF16)
-    put_total(own, send, base, hp * m // hd, jnp.concatenate(sums, axis=1))
+    put_total(own, send, base, hp * m // hd, total[...])
 
 
 def query_kernel(g, n, nw, hp, width, *refs):
@@ -312,17 +317,18 @@
         xs[k] = over_seq(xs[k ^ 1], 1)
     far_query, _ = lax.optimization_barrier((far_query, arrived + xs[1:2]))
     query_rows = [over_sub(far_query, k) for k in range(2, n_sub)]
-    kvs, _ = lax.optimization_barrier((kvs, query_rows))
     om = lax.dynamic_slice_in_dim(omega, (lax.axis_index("seq") % g) * hp, hp, 0)
 
     flop = 2 * t * width * cols
     summary_out = [((srows, hd), F32), ((srows, hd), BF16)]
-    wkv_full, key_feat, key_sig, val, own, send = call(
+    wkv_full, key_feat, key_sig, val, total = call(
         functools.partial(key_value_kernel, g, n_sub, len(kvs), hp, width),
-        [((width, 2 * cols), BF16), ((t, hp * m), BF16), ((t, hp * m), F32), ((t, cols), BF16)] + summary_out,
+        [((width, 2 * cols), BF16), ((t, hp * m), BF16), ((t, hp * m), F32), ((t, cols), BF16), ((1, hp * m), F32)],
         [*xs, *kvs, om],
         8 * flop,
     )
+    total, _ = lax.optimization_barrier((total, query_rows))
+    own, send = call(functools.partial(summary_kernel, hp), summary_out, [key_feat, val, total], 0)
     summary = to_all(own, send)
     query_rows, _ = lax.optimization_barrier((query_rows, val))
     qs = [near, nearest] + swapped(query_rows)

time: 73.6 us -> 71.9 us (0.977)
  waiting for transfers between devices: 37.5 us -> 35.7 us
    ppermute x5, waiting for transfers between devices: 13.1 us -> 11.4 us  [over_sub(): return lax.ppermute(x, 'sub', [(i, i ^ k) for i in range(n_sub)])]
    pallas_call x9 -> x10, Pallas kernels: 10.1 us -> 10.1 us  [call(): pl.pallas_call(body, out_shape=[jax.ShapeDtypeStruct(s, d) for s, d in ou...]
  transfers between devices with their start and end apart: 21 -> 21, of which waited for: 12 -> 12; matrix products, arithmetic and copies ran while one was open for 0% -> 0% of each run, Pallas kernels for 4% -> 7%
where the time goes in v9:
time: 71.9 us; the launch traced here: 71.7 us
  waiting for transfers between devices  35.7 us (50%)
  starting transfers between devices  24.2 us (34%)
  Pallas kernels  10.1 us (14%)
  other arithmetic  0.88 us (1%)
    ppermute x5, waiting for transfers between devices, over_sub(): return lax.ppermute(x, 'sub', [(i, i ^ k) for i in range(n_sub)])  11.4 us
    pallas_call x10, Pallas kernels, call(): pl.pallas_call(body, out_shape=[jax.ShapeDtypeStruct(s, d) for s, d in ou...  10.1 us
    ppermute x6, waiting for transfers between devices, to_all(): parts.append(lax.ppermute(send, ('seq', 'sub'), perm))  8.99 us
    ppermute x6, starting transfers between devices, to_all(): parts.append(lax.ppermute(send, ('seq', 'sub'), perm))  8.91 us
    ppermute x4, waiting for transfers between devices, swapped(): lax.ppermute(part, 'grp', [(0, 1), (1, 0)])  7.78 us
    ppermute x6, waiting for transfers between devices, over_seq(): return lax.ppermute(x, 'seq', [(i, i ^ k) for i in range(n_seq)])  7.56 us
    ppermute x5, starting transfers between devices, over_sub(): return lax.ppermute(x, 'sub', [(i, i ^ k) for i in range(n_sub)])  7.02 us
    ppermute x6, starting transfers between devices, over_seq(): return lax.ppermute(x, 'seq', [(i, i ^ k) for i in range(n_seq)])  4.17 us
  transfers between devices with their start and end apart: 21, of which 12 were waited for; matrix products, arithmetic and copies ran while one was open for 0% of the time, Pallas kernels for 7%

profile of v9, /device:TPU:0, one launch (start us, length us, event | category | flops | bytes accessed | tf_op | source)
XLA Modules:
  0.0 71.7 jit_solution(7462724915678438426)
XLA Ops:
  0.0 1.2 %shard_map.73 = (bf16[256,768]{1,0:T(8,128)(2,1)S(1)}, bf16[128,512]{1,0:T(8,128)(2,1)S(1)}, bf16[128,256]{1,0:T(8,128)(2,1)S(1)}) custom-call(bf16[256,1024]{1,0:T(8,128)(2,1)} %refs_0_.1, bf16[256,1024]{1,0:T(8,128)(2,1)} %refs_1_.1, bf16[256,1024]{1,0:T(8,128)(2,1)} %refs_2_.1), custom_call_target="tpu_custom_call" | custom-call | tf_op jit(solution)/shard_map/pallas_call | solution.py:30
  3.1 3.0 %collective-permute-start.1 = (bf16[128,1536]{1,0:T(8,128)(2,1)S(1)}, bf16[128,1536]{1,0:T(8,128)(2,1)S(1)}, u32[]{:S(2)}, u32[]{:S(2)}) collective-permute-start(bf16[128,1536]{1,0:T(8,128)(2,1)S(1)} %get-tuple-element.38), channel_id=1, source_target_pairs={{0,8},{4,12},{8,0},{12,4},{1,9},{5,13},{9,1},{13,5},{2,10},{6,14},... | collective-permute-start | bytes 1179656 | tf_op jit(solution)/shard_map/ppermute | solution.py:263
  6.1 3.6 %collective-permute-start.3 = (bf16[128,512]{1,0:T(8,128)(2,1)S(1)}, bf16[128,512]{1,0:T(8,128)(2,1)S(1)}, u32[]{:S(2)}, u32[]{:S(2)}) collective-permute-start(bf16[128,512]{1,0:T(8,128)(2,1)S(1)} %get-tuple-element.39), channel_id=1, source_target_pairs={{0,3},{1,2},{2,1},{3,0},{4,7},{5,6},{6,5},{7,4},{8,11},{9,10},{10,... | collective-permute-start | bytes 393224 | tf_op jit(solution)/shard_map/ppermute | solution.py:266
  10.5 3.9 %collective-permute-done.3.refs_8_ = bf16[128,512]{1,0:T(8,128)(2,1)S(1)} collective-permute-done((bf16[128,512]{1,0:T(8,128)(2,1)S(1)}, bf16[128,512]{1,0:T(8,128)(2,1)S(1)}, u32[]{:S(2)}, u32[]{:S(2)}) %collective-permute-start.3) | collective-permute-done | bytes 131104 | tf_op jit(solution)/shard_map/ppermute | solution.py:266
  14.4 6.2 %collective-permute-done.2.refs_6_ = bf16[128,512]{1,0:T(8,128)(2,1)S(1)} collective-permute-done((bf16[128,512]{1,0:T(8,128)(2,1)S(1)}, bf16[128,512]{1,0:T(8,128)(2,1)S(1)}, u32[]{:S(2)}, u32[]{:S(2)}) %collective-permute-start.2) | collective-permute-done | bytes 131104 | tf_op jit(solution)/shard_map/ppermute | solution.py:266
  20.6 1.5 %collective-permute-start.7 = (bf16[128,512]{1,0:T(8,128)(2,1)S(1)}, bf16[128,512]{1,0:T(8,128)(2,1)S(1)}, u32[]{:S(2)}, u32[]{:S(2)}) collective-permute-start(bf16[128,512]{1,0:T(8,128)(2,1)S(1)} %collective-permute-done.3.refs_8_), channel_id=1, source_target_pairs={{0,16},{16,0},{1,17},{17,1},{2,18},{18,2},{3,19},{19,3},{4,20},{20... | collective-permute-start | bytes 393224 | tf_op jit(solution)/shard_map/ppermute | solution.py:306
  22.6 2.5 %collective-permute-start.9 = (bf16[128,256]{1,0:T(8,128)(2,1)S(1)}, bf16[128,256]{1,0:T(8,128)(2,1)S(1)}, u32[]{:S(2)}, u32[]{:S(2)}) collective-permute-start(bf16[128,256]{1,0:T(8,128)(2,1)S(1)} %get-tuple-element.45), channel_id=1, source_target_pairs={{0,3},{1,2},{2,1},{3,0},{4,7},{5,6},{6,5},{7,4},{8,11},{9,10},{10,... | collective-permute-start | bytes 196616 | tf_op jit(solution)/shard_map/ppermute | solution.py:266
  25.1 1.7 %collective-permute-done.7.refs_9_ = bf16[128,512]{1,0:T(8,128)(2,1)S(1)} collective-permute-done((bf16[128,512]{1,0:T(8,128)(2,1)S(1)}, bf16[128,512]{1,0:T(8,128)(2,1)S(1)}, u32[]{:S(2)}, u32[]{:S(2)}) %collective-permute-start.7) | collective-permute-done | bytes 131104 | tf_op jit(solution)/shard_map/ppermute | solution.py:306
  27.0 2.3 %collective-permute-done.6.refs_7_ = bf16[128,512]{1,0:T(8,128)(2,1)S(1)} collective-permute-done((bf16[128,512]{1,0:T(8,128)(2,1)S(1)}, bf16[128,512]{1,0:T(8,128)(2,1)S(1)}, u32[]{:S(2)}, u32[]{:S(2)}) %collective-permute-start.6) | collective-permute-done | bytes 131104 | tf_op jit(solution)/shard_map/ppermute | solution.py:306
  29.3 1.7 %shard_map.75 = (bf16[1024,512]{1,0:T(8,128)(2,1)S(1)}, bf16[512,512]{1,0:T(8,128)(2,1)S(1)}, f32[512,512]{1,0:T(8,128)S(1)}, bf16[512,256]{1,0:T(8,128)(2,1)S(1)}, f32[1,512]{1,0:T(1,128)S(1)}) custom-call(bf16[128,1536]{1,0:T(8,128)(2,1)S(1)} %get-tuple-element.37.refs_0_.refs_4_, bf16[128,1536]{1,0:T(8,128)(2,1)S(1)} %collective-permute-done.refs_1_.refs_5_, ...), custom_call_target="tpu_custom_call" | custom-call | flops 2147483648 | bytes 3014656 | tf_op jit(solution)/shard_map/pallas_call | solution.py:30
  31.0 1.3 %collective-permute-done.8.refs_6_ = bf16[128,256]{1,0:T(8,128)(2,1)S(1)} collective-permute-done((bf16[128,256]{1,0:T(8,128)(2,1)S(1)}, bf16[128,256]{1,0:T(8,128)(2,1)S(1)}, u32[]{:S(2)}, u32[]{:S(2)}) %collective-permute-start.8) | collective-permute-done | bytes 65568 | tf_op jit(solution)/shard_map/ppermute | solution.py:266
  32.7 2.2 %collective-permute-start.12 = (bf16[528,128]{1,0:T(8,128)(2,1)S(1)}, bf16[528,128]{1,0:T(8,128)(2,1)S(1)}, u32[]{:S(2)}, u32[]{:S(2)}) collective-permute-start(bf16[528,128]{1,0:T(8,128)(2,1)S(1)} %get-tuple-element.48), channel_id=1, source_target_pairs={{0,3},{1,2},{2,1},{3,0},{4,7},{5,6},{6,5},{7,4},{8,11},{9,10},{10,... | collective-permute-start | bytes 405512 | tf_op jit(solution)/shard_map/ppermute | solution.py:278
  34.9 2.2 %collective-permute-start.10 = (bf16[528,128]{1,0:T(8,128)(2,1)S(1)}, bf16[528,128]{1,0:T(8,128)(2,1)S(1)}, u32[]{:S(2)}, u32[]{:S(2)}) collective-permute-start(bf16[528,128]{1,0:T(8,128)(2,1)S(1)} %get-tuple-element.48), channel_id=1, source_target_pairs={{0,1},{1,0},{2,3},{3,2},{4,5},{5,4},{6,7},{7,6},{8,9},{9,8},{10,11... | collective-permute-start | bytes 405512 | tf_op jit(solution)/shard_map/ppermute | solution.py:278
  37.1 1.5 %collective-permute-start.13 = (bf16[128,256]{1,0:T(8,128)(2,1)S(1)}, bf16[128,256]{1,0:T(8,128)(2,1)S(1)}, u32[]{:S(2)}, u32[]{:S(2)}) collective-permute-start(bf16[128,256]{1,0:T(8,128)(2,1)S(1)} %collective-permute-done.8.refs_6_), channel_id=1, source_target_pairs={{0,16},{16,0},{1,17},{17,1},{2,18},{18,2},{3,19},{19,3},{4,20},{20... | collective-permute-start | bytes 196616 | tf_op jit(solution)/shard_map/ppermute | solution.py:306
  39.1 2.2 %collective-permute-done.13.refs_7_ = bf16[128,256]{1,0:T(8,128)(2,1)S(1)} collective-permute-done((bf16[128,256]{1,0:T(8,128)(2,1)S(1)}, bf16[128,256]{1,0:T(8,128)(2,1)S(1)}, u32[]{:S(2)}, u32[]{:S(2)}) %collective-permute-start.13) | collective-permute-done | bytes 65568 | tf_op jit(solution)/shard_map/ppermute | solution.py:306
  41.4 1.5 %collective-permute-done.14.refs_9_ = bf16[128,256]{1,0:T(8,128)(2,1)S(1)} collective-permute-done((bf16[128,256]{1,0:T(8,128)(2,1)S(1)}, bf16[128,256]{1,0:T(8,128)(2,1)S(1)}, u32[]{:S(2)}, u32[]{:S(2)}) %collective-permute-start.14) | collective-permute-done | bytes 65568 | tf_op jit(solution)/shard_map/ppermute | solution.py:306
  42.9 1.4 %shard_map.77 = (bf16[1024,256]{1,0:T(8,128)(2,1)S(1)}, bf16[512,512]{1,0:T(8,128)(2,1)S(1)}, f32[512,512]{1,0:T(8,128)S(1)}) custom-call(bf16[128,1536]{1,0:T(8,128)(2,1)S(1)} %get-tuple-element.37.refs_0_.refs_4_, bf16[128,1536]{1,0:T(8,128)(2,1)S(1)} %collective-permute-done.refs_1_.refs_5_, bf16[128,1536]{1,0:T(8,128)(2,1)S(1)} %collective-permute-done.1.refs_2_.refs_6_, ...), custom_call_target="tpu_custom_call" | custom-call | tf_op jit(solution)/shard_map/pallas_call | solution.py:30
  44.3 1.4 %collective-permute-done.11.refs_2_ = bf16[528,128]{1,0:T(8,128)(2,1)S(1)} collective-permute-done((bf16[528,128]{1,0:T(8,128)(2,1)S(1)}, bf16[528,128]{1,0:T(8,128)(2,1)S(1)}, u32[]{:S(2)}, u32[]{:S(2)}) %collective-permute-start.11) | collective-permute-done | bytes 135200 | tf_op jit(solution)/shard_map/ppermute | solution.py:278
  46.6 1.6 %collective-permute-start.17 = (bf16[528,128]{1,0:T(8,128)(2,1)S(1)}, bf16[528,128]{1,0:T(8,128)(2,1)S(1)}, u32[]{:S(2)}, u32[]{:S(2)}) collective-permute-start(bf16[528,128]{1,0:T(8,128)(2,1)S(1)} %get-tuple-element.58), channel_id=1, source_target_pairs={{0,3},{1,2},{2,1},{3,0},{4,7},{5,6},{6,5},{7,4},{8,11},{9,10},{10,... | collective-permute-start | bytes 405512 | tf_op jit(solution)/shard_map/ppermute | solution.py:278
  48.2 2.8 %collective-permute-start.15 = (bf16[528,128]{1,0:T(8,128)(2,1)S(1)}, bf16[528,128]{1,0:T(8,128)(2,1)S(1)}, u32[]{:S(2)}, u32[]{:S(2)}) collective-permute-start(bf16[528,128]{1,0:T(8,128)(2,1)S(1)} %get-tuple-element.58), channel_id=1, source_target_pairs={{0,1},{1,0},{2,3},{3,2},{4,5},{5,4},{6,7},{7,6},{8,9},{9,8},{10,11... | collective-permute-start | bytes 405512 | tf_op jit(solution)/shard_map/ppermute | solution.py:278
  51.6 3.4 %collective-permute-done.17.refs_3_ = bf16[528,128]{1,0:T(8,128)(2,1)S(1)} collective-permute-done((bf16[528,128]{1,0:T(8,128)(2,1)S(1)}, bf16[528,128]{1,0:T(8,128)(2,1)S(1)}, u32[]{:S(2)}, u32[]{:S(2)}) %collective-permute-start.17) | collective-permute-done | bytes 135200 | tf_op jit(solution)/shard_map/ppermute | solution.py:278
  55.0 4.2 %collective-permute-done.16.refs_2_ = bf16[528,128]{1,0:T(8,128)(2,1)S(1)} collective-permute-done((bf16[528,128]{1,0:T(8,128)(2,1)S(1)}, bf16[528,128]{1,0:T(8,128)(2,1)S(1)}, u32[]{:S(2)}, u32[]{:S(2)}) %collective-permute-start.16) | collective-permute-done | bytes 135200 | tf_op jit(solution)/shard_map/ppermute | solution.py:278
  59.2 1.7 %shard_map.80 = (bf16[128,1024]{1,0:T(8,128)(2,1)S(1)}, bf16[128,1024]{1,0:T(8,128)(2,1)S(1)}, bf16[512,512]{1,0:T(8,128)(2,1)S(1)}) custom-call(f32[528,128]{1,0:T(8,128)S(1)} %get-tuple-element.57.refs_0_, bf16[528,128]{1,0:T(8,128)(2,1)S(1)} %collective-permute-done.15.refs_1_, bf16[528,128]{1,0:T(8,128)(2,1)S(1)} %collective-permute-done.16.refs_2_, ...), custom_call_target="tpu_custom_call" | custom-call | flops 2147483648 | bytes 4476928 | tf_op jit(solution)/shard_map/pallas_call | solution.py:30
  63.8 7.2 %collective-permute-done.20 = bf16[128,1024]{1,0:T(8,128)(2,1)S(1)} collective-permute-done((bf16[128,1024]{1,0:T(8,128)(2,1)S(1)}, bf16[128,1024]{1,0:T(8,128)(2,1)S(1)}, u32[]{:S(2)}, u32[]{:S(2)}) %collective-permute-start.20) | collective-permute-done | bytes 262176 | tf_op jit(solution)/shard_map/ppermute | solution.py:263
  (40 shorter events, 9.2 us)
Async XLA Ops:
  0.0 22.6 %copy-start = (bf16[8,128,256]{2,1,0:T(8,128)(2,1)S(1)}, bf16[8,128,256]{2,1,0:T(8,128)(2,1)}, u32[]{:S(2)}) copy-start(bf16[8,128,256]{2,1,0:T(8,128)(2,1)} %param.13) | copy-start | bytes 1572868
  0.0 1.3 %copy-start.1 = (bf16[128,1024]{1,0:T(8,128)(2,1)S(1)}, bf16[128,1024]{1,0:T(8,128)(2,1)}, u32[]{:S(2)}) copy-start(bf16[128,1024]{1,0:T(8,128)(2,1)} %events.1) | copy-start | bytes 786436
  0.0 1.4 %copy-start.2 = (bf16[128,1024]{1,0:T(8,128)(2,1)S(1)}, bf16[128,1024]{1,0:T(8,128)(2,1)}, u32[]{:S(2)}) copy-start(bf16[128,1024]{1,0:T(8,128)(2,1)} %cot.1) | copy-start | bytes 786436
  3.1 17.5 %collective-permute-start.1 = (bf16[128,1536]{1,0:T(8,128)(2,1)S(1)}, bf16[128,1536]{1,0:T(8,128)(2,1)S(1)}, u32[]{:S(2)}, u32[]{:S(2)}) collective-permute-start(bf16[128,1536]{1,0:T(8,128)(2,1)S(1)} %get-tuple-element.38), channel_id=1, source_target_pairs={{0,8},{4,12},{8,0},{12,4},{1,9},{5,13},{9,1},{13,5},{2,10},{6,14},... | collective-permute-start | bytes 1179656 | tf_op jit(solution)/shard_map/ppermute | solution.py:263
  6.1 8.3 %collective-permute-start.3 = (bf16[128,512]{1,0:T(8,128)(2,1)S(1)}, bf16[128,512]{1,0:T(8,128)(2,1)S(1)}, u32[]{:S(2)}, u32[]{:S(2)}) collective-permute-start(bf16[128,512]{1,0:T(8,128)(2,1)S(1)} %get-tuple-element.39), channel_id=1, source_target_pairs={{0,3},{1,2},{2,1},{3,0},{4,7},{5,6},{6,5},{7,4},{8,11},{9,10},{10,... | collective-permute-start | bytes 393224 | tf_op jit(solution)/shard_map/ppermute | solution.py:266
  9.7 10.9 %collective-permute-start.2 = (bf16[128,512]{1,0:T(8,128)(2,1)S(1)}, bf16[128,512]{1,0:T(8,128)(2,1)S(1)}, u32[]{:S(2)}, u32[]{:S(2)}) collective-permute-start(bf16[128,512]{1,0:T(8,128)(2,1)S(1)} %get-tuple-element.39), channel_id=1, source_target_pairs={{0,2},{1,3},{2,0},{3,1},{4,6},{5,7},{6,4},{7,5},{8,10},{9,11},{10,... | collective-permute-start | bytes 393224 | tf_op jit(solution)/shard_map/ppermute | solution.py:266
  9.7 13.0 %collective-permute-start = (bf16[128,1536]{1,0:T(8,128)(2,1)S(1)}, bf16[128,1536]{1,0:T(8,128)(2,1)S(1)}, u32[]{:S(2)}, u32[]{:S(2)}) collective-permute-start(bf16[128,1536]{1,0:T(8,128)(2,1)S(1)} %get-tuple-element.37.refs_0_.refs_4_), channel_id=1, source_target_pairs={{0,4},{4,0},{8,12},{12,8},{1,5},{5,1},{9,13},{13,9},{2,6},{6,2},{1... | collective-permute-start | bytes 1179656 | tf_op jit(solution)/shard_map/ppermute | solution.py:263
  9.7 19.6 %collective-permute-start.5 = (bf16[256,768]{1,0:T(8,128)(2,1)S(1)}, bf16[256,768]{1,0:T(8,128)(2,1)S(1)}, u32[]{:S(2)}, u32[]{:S(2)}) collective-permute-start(bf16[256,768]{1,0:T(8,128)(2,1)S(1)} %get-tuple-element.35.refs_4_), channel_id=1, source_target_pairs={{0,1},{1,0},{2,3},{3,2},{4,5},{5,4},{6,7},{7,6},{8,9},{9,8},{10,11... | collective-permute-start | bytes 1179656 | tf_op jit(solution)/shard_map/ppermute | solution.py:266
  20.6 8.7 %collective-permute-start.4 = (bf16[128,1536]{1,0:T(8,128)(2,1)S(1)}, bf16[128,1536]{1,0:T(8,128)(2,1)S(1)}, u32[]{:S(2)}, u32[]{:S(2)}) collective-permute-start(bf16[128,1536]{1,0:T(8,128)(2,1)S(1)} %collective-permute-done.1.refs_2_.refs_6_), channel_id=1, source_target_pairs={{0,4},{4,0},{8,12},{12,8},{1,5},{5,1},{9,13},{13,9},{2,6},{6,2},{1... | collective-permute-start | bytes 1179656 | tf_op jit(solution)/shard_map/ppermute | solution.py:263
  20.6 6.3 %collective-permute-start.7 = (bf16[128,512]{1,0:T(8,128)(2,1)S(1)}, bf16[128,512]{1,0:T(8,128)(2,1)S(1)}, u32[]{:S(2)}, u32[]{:S(2)}) collective-permute-start(bf16[128,512]{1,0:T(8,128)(2,1)S(1)} %collective-permute-done.3.refs_8_), channel_id=1, source_target_pairs={{0,16},{16,0},{1,17},{17,1},{2,18},{18,2},{3,19},{19,3},{4,20},{20... | collective-permute-start | bytes 393224 | tf_op jit(solution)/shard_map/ppermute | solution.py:306
  22.1 7.2 %collective-permute-start.6 = (bf16[128,512]{1,0:T(8,128)(2,1)S(1)}, bf16[128,512]{1,0:T(8,128)(2,1)S(1)}, u32[]{:S(2)}, u32[]{:S(2)}) collective-permute-start(bf16[128,512]{1,0:T(8,128)(2,1)S(1)} %collective-permute-done.2.refs_6_), channel_id=1, source_target_pairs={{0,16},{16,0},{1,17},{17,1},{2,18},{18,2},{3,19},{19,3},{4,20},{20... | collective-permute-start | bytes 393224 | tf_op jit(solution)/shard_map/ppermute | solution.py:306
  22.6 8.4 %collective-permute-start.9 = (bf16[128,256]{1,0:T(8,128)(2,1)S(1)}, bf16[128,256]{1,0:T(8,128)(2,1)S(1)}, u32[]{:S(2)}, u32[]{:S(2)}) collective-permute-start(bf16[128,256]{1,0:T(8,128)(2,1)S(1)} %get-tuple-element.45), channel_id=1, source_target_pairs={{0,3},{1,2},{2,1},{3,0},{4,7},{5,6},{6,5},{7,4},{8,11},{9,10},{10,... | collective-permute-start | bytes 196616 | tf_op jit(solution)/shard_map/ppermute | solution.py:266
  26.9 5.4 %collective-permute-start.8 = (bf16[128,256]{1,0:T(8,128)(2,1)S(1)}, bf16[128,256]{1,0:T(8,128)(2,1)S(1)}, u32[]{:S(2)}, u32[]{:S(2)}) collective-permute-start(bf16[128,256]{1,0:T(8,128)(2,1)S(1)} %get-tuple-element.45), channel_id=1, source_target_pairs={{0,2},{1,3},{2,0},{3,1},{4,6},{5,7},{6,4},{7,5},{8,10},{9,11},{10,... | collective-permute-start | bytes 196616 | tf_op jit(solution)/shard_map/ppermute | solution.py:266
  32.7 11.7 %collective-permute-start.12 = (bf16[528,128]{1,0:T(8,128)(2,1)S(1)}, bf16[528,128]{1,0:T(8,128)(2,1)S(1)}, u32[]{:S(2)}, u32[]{:S(2)}) collective-permute-start(bf16[528,128]{1,0:T(8,128)(2,1)S(1)} %get-tuple-element.48), channel_id=1, source_target_pairs={{0,3},{1,2},{2,1},{3,0},{4,7},{5,6},{6,5},{7,4},{8,11},{9,10},{10,... | collective-permute-start | bytes 405512 | tf_op jit(solution)/shard_map/ppermute | solution.py:278
  34.9 10.8 %collective-permute-start.11 = (bf16[528,128]{1,0:T(8,128)(2,1)S(1)}, bf16[528,128]{1,0:T(8,128)(2,1)S(1)}, u32[]{:S(2)}, u32[]{:S(2)}) collective-permute-start(bf16[528,128]{1,0:T(8,128)(2,1)S(1)} %get-tuple-element.48), channel_id=1, source_target_pairs={{0,2},{1,3},{2,0},{3,1},{4,6},{5,7},{6,4},{7,5},{8,10},{9,11},{10,... | collective-permute-start | bytes 405512 | tf_op jit(solution)/shard_map/ppermute | solution.py:278
  34.9 10.8 %collective-permute-start.10 = (bf16[528,128]{1,0:T(8,128)(2,1)S(1)}, bf16[528,128]{1,0:T(8,128)(2,1)S(1)}, u32[]{:S(2)}, u32[]{:S(2)}) collective-permute-start(bf16[528,128]{1,0:T(8,128)(2,1)S(1)} %get-tuple-element.48), channel_id=1, source_target_pairs={{0,1},{1,0},{2,3},{3,2},{4,5},{5,4},{6,7},{7,6},{8,9},{9,8},{10,11... | collective-permute-start | bytes 405512 | tf_op jit(solution)/shard_map/ppermute | solution.py:278
  37.1 4.3 %collective-permute-start.13 = (bf16[128,256]{1,0:T(8,128)(2,1)S(1)}, bf16[128,256]{1,0:T(8,128)(2,1)S(1)}, u32[]{:S(2)}, u32[]{:S(2)}) collective-permute-start(bf16[128,256]{1,0:T(8,128)(2,1)S(1)} %collective-permute-done.8.refs_6_), channel_id=1, source_target_pairs={{0,16},{16,0},{1,17},{17,1},{2,18},{18,2},{3,19},{19,3},{4,20},{20... | collective-permute-start | bytes 196616 | tf_op jit(solution)/shard_map/ppermute | solution.py:306
  38.6 4.3 %collective-permute-start.14 = (bf16[128,256]{1,0:T(8,128)(2,1)S(1)}, bf16[128,256]{1,0:T(8,128)(2,1)S(1)}, u32[]{:S(2)}, u32[]{:S(2)}) collective-permute-start(bf16[128,256]{1,0:T(8,128)(2,1)S(1)} %collective-permute-done.9.refs_8_), channel_id=1, source_target_pairs={{0,16},{16,0},{1,17},{17,1},{2,18},{18,2},{3,19},{19,3},{4,20},{20... | collective-permute-start | bytes 196616 | tf_op jit(solution)/shard_map/ppermute | solution.py:306
  46.6 8.4 %collective-permute-start.17 = (bf16[528,128]{1,0:T(8,128)(2,1)S(1)}, bf16[528,128]{1,0:T(8,128)(2,1)S(1)}, u32[]{:S(2)}, u32[]{:S(2)}) collective-permute-start(bf16[528,128]{1,0:T(8,128)(2,1)S(1)} %get-tuple-element.58), channel_id=1, source_target_pairs={{0,3},{1,2},{2,1},{3,0},{4,7},{5,6},{6,5},{7,4},{8,11},{9,10},{10,... | collective-permute-start | bytes 405512 | tf_op jit(solution)/shard_map/ppermute | solution.py:278
  48.2 10.9 %collective-permute-start.16 = (bf16[528,128]{1,0:T(8,128)(2,1)S(1)}, bf16[528,128]{1,0:T(8,128)(2,1)S(1)}, u32[]{:S(2)}, u32[]{:S(2)}) collective-permute-start(bf16[528,128]{1,0:T(8,128)(2,1)S(1)} %get-tuple-element.58), channel_id=1, source_target_pairs={{0,2},{1,3},{2,0},{3,1},{4,6},{5,7},{6,4},{7,5},{8,10},{9,11},{10,... | collective-permute-start | bytes 405512 | tf_op jit(solution)/shard_map/ppermute | solution.py:278
  48.2 10.9 %collective-permute-start.15 = (bf16[528,128]{1,0:T(8,128)(2,1)S(1)}, bf16[528,128]{1,0:T(8,128)(2,1)S(1)}, u32[]{:S(2)}, u32[]{:S(2)}) collective-permute-start(bf16[528,128]{1,0:T(8,128)(2,1)S(1)} %get-tuple-element.58), channel_id=1, source_target_pairs={{0,1},{1,0},{2,3},{3,2},{4,5},{5,4},{6,7},{7,6},{8,9},{9,8},{10,11... | collective-permute-start | bytes 405512 | tf_op jit(solution)/shard_map/ppermute | solution.py:278
  60.9 1.6 %collective-permute-start.19 = (bf16[128,1024]{1,0:T(8,128)(2,1)S(1)}, bf16[128,1024]{1,0:T(8,128)(2,1)S(1)}, u32[]{:S(2)}, u32[]{:S(2)}) collective-permute-start(bf16[128,1024]{1,0:T(8,128)(2,1)S(1)} %get-tuple-element.64), channel_id=1, source_target_pairs={{0,4},{4,0},{8,12},{12,8},{1,5},{5,1},{9,13},{13,9},{2,6},{6,2},{1... | collective-permute-start | bytes 786440 | tf_op jit(solution)/shard_map/ppermute | solution.py:263
  60.9 2.8 %collective-permute-start.18 = (bf16[128,1024]{1,0:T(8,128)(2,1)S(1)}, bf16[128,1024]{1,0:T(8,128)(2,1)S(1)}, u32[]{:S(2)}, u32[]{:S(2)}) collective-permute-start(bf16[128,1024]{1,0:T(8,128)(2,1)S(1)} %get-tuple-element.63), channel_id=1, source_target_pairs={{0,4},{4,0},{8,12},{12,8},{1,5},{5,1},{9,13},{13,9},{2,6},{6,2},{1... | collective-permute-start | bytes 786440 | tf_op jit(solution)/shard_map/ppermute | solution.py:263
  62.5 8.4 %collective-permute-start.20 = (bf16[128,1024]{1,0:T(8,128)(2,1)S(1)}, bf16[128,1024]{1,0:T(8,128)(2,1)S(1)}, u32[]{:S(2)}, u32[]{:S(2)}) collective-permute-start(bf16[128,1024]{1,0:T(8,128)(2,1)S(1)} %add_convert_fusion.1), channel_id=1, source_target_pairs={{0,8},{4,12},{8,0},{12,4},{1,9},{5,13},{9,1},{13,5},{2,10},{6,14},... | collective-permute-start | bytes 786440 | tf_op jit(solution)/shard_map/ppermute | solution.py:263
  (1 other events, 0.7 us)

commit v10 on v9

--- a/solution.py
+++ b/solution.py
@@ -226,7 +226,7 @@
 def key_side_kernel(g, p, hp, *refs):
     parts = refs[:p]
     val, feat, sig, om, qg, wq, wkv = refs[p : p + 7]
-    odd, one, kvg = refs[p + 7 :]
+    odd, kvg = refs[p + 7 :]
     hd, m = om.shape[1], om.shape[2]
     base = hp * m
     cols = hp * hd
@@ -239,11 +239,20 @@
         pg = (fg * sig[:, h * m : (h + 1) * m]).astype(BF16)
         kvg[:, col] = dot(pg, om[h], 1, 1).astype(BF16)
     products(g, range(3, g, 2), qg, kvg, wq, wkv, odd)
-    products(g, [1], qg, kvg, wq, wkv, one)
-
-
-def even_kernel(g, blocks, qg, kvg, wq, wkv, even):
-    products(g, blocks, qg, kvg, wq, wkv, even)
+
+
+def even_kernel(g, qg, kvg, wq, wkv, even):
+    products(g, range(2, g, 2), qg, kvg, wq, wkv, even)
+
+
+def near_kernel(g, qg, kvg, wq, wkv, top, bottom, zero):
+    rows = zero.shape[0]
+    half = rows // 2
+    for start, out in ((rows, top), (rows + half, bottom)):
+        tok = slice(start, start + half)
+        o = dot(qg[tok, :], wq[...], 1, 1) + dot(kvg[tok, :], wkv[...], 1, 1)
+        out[...] = o.astype(out.dtype)
+    products(g, [0], qg, kvg, wq, wkv, zero)
 
 
 def local(events, offsets, cotangent, query_weight, key_weight, value_weight, omega):
@@ -292,7 +301,7 @@
         in_specs=[HBM] * 3,
         scratch_shapes=[pltpu.SemaphoreType.DMA((6,))],
     )
-    offsets, _ = lax.optimization_barrier((offsets, near))
+    frequency, _ = lax.optimization_barrier((frequency, near))
     bufs = call(
         functools.partial(input_kernel, g, cols),
         [((rows, width + 2 * cols), BF16)] * (g // 2),
@@ -352,25 +361,24 @@
         4 * flop,
     )
     others = g // 2 - 1
-    odd, one, key_value_grad = call(
+    odd, key_value_grad = call(
         functools.partial(key_side_kernel, g, p, hp),
-        [((others * rows, width), BF16), ((rows, width), BF16), ((t, 2 * cols), BF16)],
+        [((others * rows, width), BF16), ((t, 2 * cols), BF16)],
         [*summary_grad, val, key_feat, key_sig, om, query_grad, wq_full, wkv_full],
         8 * flop,
     )
     got = over_seq(odd, 1)
-    got_one = over_seq(one, 1)
-
-    def even_blocks(blocks):
-        return call(
-            functools.partial(even_kernel, g, blocks),
-            [((len(blocks) * rows, width), F32)],
-            [query_grad, key_value_grad, wq_full, wkv_full],
-            8 * flop,
-        )[0]
-
-    both = (even_blocks(range(2, g, 2)) + got.astype(F32)).astype(BF16)
-    out = even_blocks([0]) + got_one.astype(F32)
+    grads = [query_grad, key_value_grad, wq_full, wkv_full]
+    (even,) = call(functools.partial(even_kernel, g), [((others * rows, width), F32)], grads, 8 * flop)
+    both = (even + got.astype(F32)).astype(BF16)
+    top, bottom, zero = call(
+        functools.partial(near_kernel, g),
+        [((rows // 2, width), BF16), ((rows // 2, width), BF16), ((rows, width), F32)],
+        grads,
+        0,
+    )
+    near_sum = jnp.concatenate([over_seq(top, 1), over_seq(bottom, 1)], axis=0)
+    out = zero + near_sum.astype(F32)
     for k in range(2, g, 2):
         at = (k // 2 - 1) * rows
         out = out + over_seq(both[at : at + rows], k).astype(F32)

time: 71.9 us -> 71.4 us (level)
  waiting for transfers between devices: 35.7 us -> 34.7 us
    ppermute x6 -> x7, waiting for transfers between devices: 7.56 us -> 6.53 us  [over_seq(): return lax.ppermute(x, 'seq', [(i, i ^ k) for i in range(n_seq)])]
    ppermute x6 -> x7, starting transfers between devices: 4.17 us -> 4.25 us  [over_seq(): return lax.ppermute(x, 'seq', [(i, i ^ k) for i in range(n_seq)])]
  transfers between devices with their start and end apart: 21 -> 22, of which waited for: 12 -> 14; matrix products, arithmetic and copies ran while one was open for 0% -> 0% of each run, Pallas kernels for 7% -> 8%
where the time goes in v10:
time: 71.4 us; the launch traced here: 71.2 us
  waiting for transfers between devices  34.7 us (49%)
  starting transfers between devices  24.2 us (34%)
  Pallas kernels  10.6 us (15%)
  other arithmetic  0.86 us (1%)
    ppermute x5, waiting for transfers between devices, over_sub(): return lax.ppermute(x, 'sub', [(i, i ^ k) for i in range(n_sub)])  11.4 us
    pallas_call x10, Pallas kernels, call(): pl.pallas_call(body, out_shape=[jax.ShapeDtypeStruct(s, d) for s, d in ou...  10.6 us
    ppermute x6, waiting for transfers between devices, to_all(): parts.append(lax.ppermute(send, ('seq', 'sub'), perm))  8.99 us
    ppermute x6, starting transfers between devices, to_all(): parts.append(lax.ppermute(send, ('seq', 'sub'), perm))  8.91 us
    ppermute x4, waiting for transfers between devices, swapped(): lax.ppermute(part, 'grp', [(0, 1), (1, 0)])  7.78 us
    ppermute x5, starting transfers between devices, over_sub(): return lax.ppermute(x, 'sub', [(i, i ^ k) for i in range(n_sub)])  7.02 us
    ppermute x7, waiting for transfers between devices, over_seq(): return lax.ppermute(x, 'seq', [(i, i ^ k) for i in range(n_seq)])  6.53 us
    ppermute x7, starting transfers between devices, over_seq(): return lax.ppermute(x, 'seq', [(i, i ^ k) for i in range(n_seq)])  4.25 us
  transfers between devices with their start and end apart: 22, of which 14 were waited for; matrix products, arithmetic and copies ran while one was open for 0% of the time, Pallas kernels for 8%

profile of v10, /device:TPU:0, one launch (start us, length us, event | category | flops | bytes accessed | tf_op | source)
XLA Modules:
  0.0 71.2 jit_solution(16386576215220695016)
XLA Ops:
  0.0 1.2 %shard_map.73 = (bf16[256,768]{1,0:T(8,128)(2,1)S(1)}, bf16[128,512]{1,0:T(8,128)(2,1)S(1)}, bf16[128,256]{1,0:T(8,128)(2,1)S(1)}) custom-call(bf16[256,1024]{1,0:T(8,128)(2,1)} %refs_0_.1, bf16[256,1024]{1,0:T(8,128)(2,1)} %refs_1_.1, bf16[256,1024]{1,0:T(8,128)(2,1)} %refs_2_.1), custom_call_target="tpu_custom_call" | custom-call | tf_op jit(solution)/shard_map/pallas_call | solution.py:30
  3.1 3.0 %collective-permute-start.1 = (bf16[128,1536]{1,0:T(8,128)(2,1)S(1)}, bf16[128,1536]{1,0:T(8,128)(2,1)S(1)}, u32[]{:S(2)}, u32[]{:S(2)}) collective-permute-start(bf16[128,1536]{1,0:T(8,128)(2,1)S(1)} %get-tuple-element.40), channel_id=1, source_target_pairs={{0,8},{4,12},{8,0},{12,4},{1,9},{5,13},{9,1},{13,5},{2,10},{6,14},... | collective-permute-start | bytes 1179656 | tf_op jit(solution)/shard_map/ppermute | solution.py:272
  6.1 3.6 %collective-permute-start.3 = (bf16[128,512]{1,0:T(8,128)(2,1)S(1)}, bf16[128,512]{1,0:T(8,128)(2,1)S(1)}, u32[]{:S(2)}, u32[]{:S(2)}) collective-permute-start(bf16[128,512]{1,0:T(8,128)(2,1)S(1)} %get-tuple-element.41), channel_id=1, source_target_pairs={{0,3},{1,2},{2,1},{3,0},{4,7},{5,6},{6,5},{7,4},{8,11},{9,10},{10,... | collective-permute-start | bytes 393224 | tf_op jit(solution)/shard_map/ppermute | solution.py:275
  10.5 3.9 %collective-permute-done.3.refs_8_ = bf16[128,512]{1,0:T(8,128)(2,1)S(1)} collective-permute-done((bf16[128,512]{1,0:T(8,128)(2,1)S(1)}, bf16[128,512]{1,0:T(8,128)(2,1)S(1)}, u32[]{:S(2)}, u32[]{:S(2)}) %collective-permute-start.3) | collective-permute-done | bytes 131104 | tf_op jit(solution)/shard_map/ppermute | solution.py:275
  14.3 6.2 %collective-permute-done.2.refs_6_ = bf16[128,512]{1,0:T(8,128)(2,1)S(1)} collective-permute-done((bf16[128,512]{1,0:T(8,128)(2,1)S(1)}, bf16[128,512]{1,0:T(8,128)(2,1)S(1)}, u32[]{:S(2)}, u32[]{:S(2)}) %collective-permute-start.2) | collective-permute-done | bytes 131104 | tf_op jit(solution)/shard_map/ppermute | solution.py:275
  20.6 1.5 %collective-permute-start.7 = (bf16[128,512]{1,0:T(8,128)(2,1)S(1)}, bf16[128,512]{1,0:T(8,128)(2,1)S(1)}, u32[]{:S(2)}, u32[]{:S(2)}) collective-permute-start(bf16[128,512]{1,0:T(8,128)(2,1)S(1)} %collective-permute-done.3.refs_8_), channel_id=1, source_target_pairs={{0,16},{16,0},{1,17},{17,1},{2,18},{18,2},{3,19},{19,3},{4,20},{20... | collective-permute-start | bytes 393224 | tf_op jit(solution)/shard_map/ppermute | solution.py:315
  22.6 2.5 %collective-permute-start.9 = (bf16[128,256]{1,0:T(8,128)(2,1)S(1)}, bf16[128,256]{1,0:T(8,128)(2,1)S(1)}, u32[]{:S(2)}, u32[]{:S(2)}) collective-permute-start(bf16[128,256]{1,0:T(8,128)(2,1)S(1)} %get-tuple-element.47), channel_id=1, source_target_pairs={{0,3},{1,2},{2,1},{3,0},{4,7},{5,6},{6,5},{7,4},{8,11},{9,10},{10,... | collective-permute-start | bytes 196616 | tf_op jit(solution)/shard_map/ppermute | solution.py:275
  25.1 1.7 %collective-permute-done.7.refs_9_ = bf16[128,512]{1,0:T(8,128)(2,1)S(1)} collective-permute-done((bf16[128,512]{1,0:T(8,128)(2,1)S(1)}, bf16[128,512]{1,0:T(8,128)(2,1)S(1)}, u32[]{:S(2)}, u32[]{:S(2)}) %collective-permute-start.7) | collective-permute-done | bytes 131104 | tf_op jit(solution)/shard_map/ppermute | solution.py:315
  27.0 2.3 %collective-permute-done.6.refs_7_ = bf16[128,512]{1,0:T(8,128)(2,1)S(1)} collective-permute-done((bf16[128,512]{1,0:T(8,128)(2,1)S(1)}, bf16[128,512]{1,0:T(8,128)(2,1)S(1)}, u32[]{:S(2)}, u32[]{:S(2)}) %collective-permute-start.6) | collective-permute-done | bytes 131104 | tf_op jit(solution)/shard_map/ppermute | solution.py:315
  29.3 1.7 %shard_map.75 = (bf16[1024,512]{1,0:T(8,128)(2,1)S(1)}, bf16[512,512]{1,0:T(8,128)(2,1)S(1)}, f32[512,512]{1,0:T(8,128)S(1)}, bf16[512,256]{1,0:T(8,128)(2,1)S(1)}, f32[1,512]{1,0:T(1,128)S(1)}) custom-call(bf16[128,1536]{1,0:T(8,128)(2,1)S(1)} %get-tuple-element.39.refs_0_.refs_4_, bf16[128,1536]{1,0:T(8,128)(2,1)S(1)} %collective-permute-done.refs_1_.refs_5_, ...), custom_call_target="tpu_custom_call" | custom-call | flops 2147483648 | bytes 3014656 | tf_op jit(solution)/shard_map/pallas_call | solution.py:30
  31.0 1.3 %collective-permute-done.8.refs_6_ = bf16[128,256]{1,0:T(8,128)(2,1)S(1)} collective-permute-done((bf16[128,256]{1,0:T(8,128)(2,1)S(1)}, bf16[128,256]{1,0:T(8,128)(2,1)S(1)}, u32[]{:S(2)}, u32[]{:S(2)}) %collective-permute-start.8) | collective-permute-done | bytes 65568 | tf_op jit(solution)/shard_map/ppermute | solution.py:275
  32.7 2.2 %collective-permute-start.12 = (bf16[528,128]{1,0:T(8,128)(2,1)S(1)}, bf16[528,128]{1,0:T(8,128)(2,1)S(1)}, u32[]{:S(2)}, u32[]{:S(2)}) collective-permute-start(bf16[528,128]{1,0:T(8,128)(2,1)S(1)} %get-tuple-element.50), channel_id=1, source_target_pairs={{0,3},{1,2},{2,1},{3,0},{4,7},{5,6},{6,5},{7,4},{8,11},{9,10},{10,... | collective-permute-start | bytes 405512 | tf_op jit(solution)/shard_map/ppermute | solution.py:287
  34.9 2.2 %collective-permute-start.10 = (bf16[528,128]{1,0:T(8,128)(2,1)S(1)}, bf16[528,128]{1,0:T(8,128)(2,1)S(1)}, u32[]{:S(2)}, u32[]{:S(2)}) collective-permute-start(bf16[528,128]{1,0:T(8,128)(2,1)S(1)} %get-tuple-element.50), channel_id=1, source_target_pairs={{0,1},{1,0},{2,3},{3,2},{4,5},{5,4},{6,7},{7,6},{8,9},{9,8},{10,11... | collective-permute-start | bytes 405512 | tf_op jit(solution)/shard_map/ppermute | solution.py:287
  37.1 1.5 %collective-permute-start.13 = (bf16[128,256]{1,0:T(8,128)(2,1)S(1)}, bf16[128,256]{1,0:T(8,128)(2,1)S(1)}, u32[]{:S(2)}, u32[]{:S(2)}) collective-permute-start(bf16[128,256]{1,0:T(8,128)(2,1)S(1)} %collective-permute-done.8.refs_6_), channel_id=1, source_target_pairs={{0,16},{16,0},{1,17},{17,1},{2,18},{18,2},{3,19},{19,3},{4,20},{20... | collective-permute-start | bytes 196616 | tf_op jit(solution)/shard_map/ppermute | solution.py:315
  39.1 2.2 %collective-permute-done.13.refs_7_ = bf16[128,256]{1,0:T(8,128)(2,1)S(1)} collective-permute-done((bf16[128,256]{1,0:T(8,128)(2,1)S(1)}, bf16[128,256]{1,0:T(8,128)(2,1)S(1)}, u32[]{:S(2)}, u32[]{:S(2)}) %collective-permute-start.13) | collective-permute-done | bytes 65568 | tf_op jit(solution)/shard_map/ppermute | solution.py:315
  41.4 1.5 %collective-permute-done.14.refs_9_ = bf16[128,256]{1,0:T(8,128)(2,1)S(1)} collective-permute-done((bf16[128,256]{1,0:T(8,128)(2,1)S(1)}, bf16[128,256]{1,0:T(8,128)(2,1)S(1)}, u32[]{:S(2)}, u32[]{:S(2)}) %collective-permute-start.14) | collective-permute-done | bytes 65568 | tf_op jit(solution)/shard_map/ppermute | solution.py:315
  42.9 1.4 %shard_map.77 = (bf16[1024,256]{1,0:T(8,128)(2,1)S(1)}, bf16[512,512]{1,0:T(8,128)(2,1)S(1)}, f32[512,512]{1,0:T(8,128)S(1)}) custom-call(bf16[128,1536]{1,0:T(8,128)(2,1)S(1)} %get-tuple-element.39.refs_0_.refs_4_, bf16[128,1536]{1,0:T(8,128)(2,1)S(1)} %collective-permute-done.refs_1_.refs_5_, bf16[128,1536]{1,0:T(8,128)(2,1)S(1)} %collective-permute-done.1.refs_2_.refs_6_, ...), custom_call_target="tpu_custom_call" | custom-call | tf_op jit(solution)/shard_map/pallas_call | solution.py:30
  44.3 1.4 %collective-permute-done.11.refs_2_ = bf16[528,128]{1,0:T(8,128)(2,1)S(1)} collective-permute-done((bf16[528,128]{1,0:T(8,128)(2,1)S(1)}, bf16[528,128]{1,0:T(8,128)(2,1)S(1)}, u32[]{:S(2)}, u32[]{:S(2)}) %collective-permute-start.11) | collective-permute-done | bytes 135200 | tf_op jit(solution)/shard_map/ppermute | solution.py:287
  46.6 1.6 %collective-permute-start.17 = (bf16[528,128]{1,0:T(8,128)(2,1)S(1)}, bf16[528,128]{1,0:T(8,128)(2,1)S(1)}, u32[]{:S(2)}, u32[]{:S(2)}) collective-permute-start(bf16[528,128]{1,0:T(8,128)(2,1)S(1)} %get-tuple-element.60), channel_id=1, source_target_pairs={{0,3},{1,2},{2,1},{3,0},{4,7},{5,6},{6,5},{7,4},{8,11},{9,10},{10,... | collective-permute-start | bytes 405512 | tf_op jit(solution)/shard_map/ppermute | solution.py:287
  48.2 2.8 %collective-permute-start.15 = (bf16[528,128]{1,0:T(8,128)(2,1)S(1)}, bf16[528,128]{1,0:T(8,128)(2,1)S(1)}, u32[]{:S(2)}, u32[]{:S(2)}) collective-permute-start(bf16[528,128]{1,0:T(8,128)(2,1)S(1)} %get-tuple-element.60), channel_id=1, source_target_pairs={{0,1},{1,0},{2,3},{3,2},{4,5},{5,4},{6,7},{7,6},{8,9},{9,8},{10,11... | collective-permute-start | bytes 405512 | tf_op jit(solution)/shard_map/ppermute | solution.py:287
  51.6 3.4 %collective-permute-done.17.refs_3_ = bf16[528,128]{1,0:T(8,128)(2,1)S(1)} collective-permute-done((bf16[528,128]{1,0:T(8,128)(2,1)S(1)}, bf16[528,128]{1,0:T(8,128)(2,1)S(1)}, u32[]{:S(2)}, u32[]{:S(2)}) %collective-permute-start.17) | collective-permute-done | bytes 135200 | tf_op jit(solution)/shard_map/ppermute | solution.py:287
  55.0 4.2 %collective-permute-done.16.refs_2_ = bf16[528,128]{1,0:T(8,128)(2,1)S(1)} collective-permute-done((bf16[528,128]{1,0:T(8,128)(2,1)S(1)}, bf16[528,128]{1,0:T(8,128)(2,1)S(1)}, u32[]{:S(2)}, u32[]{:S(2)}) %collective-permute-start.16) | collective-permute-done | bytes 135200 | tf_op jit(solution)/shard_map/ppermute | solution.py:287
  62.6 1.6 %shard_map.81 = (bf16[64,1024]{1,0:T(8,128)(2,1)S(1)}, bf16[64,1024]{1,0:T(8,128)(2,1)S(1)}, f32[128,1024]{1,0:T(8,128)S(1)}) custom-call(bf16[512,256]{1,0:T(8,128)(2,1)S(1)} %shard_map.79.refs_8_.qg, bf16[512,512]{1,0:T(8,128)(2,1)S(1)} %get-tuple-element.64.kvg, bf16[1024,256]{1,0:T(8,128)(2,1)S(1)} %get-tuple-element.62.refs_9_.wq, ...), custom_call_target="tpu_custom_call" | custom-call | tf_op jit(solution)/shard_map/pallas_call | solution.py:30
  65.8 4.6 %collective-permute-done.21 = bf16[128,1024]{1,0:T(8,128)(2,1)S(1)} collective-permute-done((bf16[128,1024]{1,0:T(8,128)(2,1)S(1)}, bf16[128,1024]{1,0:T(8,128)(2,1)S(1)}, u32[]{:S(2)}, u32[]{:S(2)}) %collective-permute-start.21) | collective-permute-done | bytes 262176 | tf_op jit(solution)/shard_map/ppermute | solution.py:272
  (42 shorter events, 11.3 us)
Async XLA Ops:
  0.0 22.6 %copy-start = (bf16[8,128,256]{2,1,0:T(8,128)(2,1)S(1)}, bf16[8,128,256]{2,1,0:T(8,128)(2,1)}, u32[]{:S(2)}) copy-start(bf16[8,128,256]{2,1,0:T(8,128)(2,1)} %param.13) | copy-start | bytes 1572868
  0.0 1.4 %copy-start.2 = (bf16[128,1024]{1,0:T(8,128)(2,1)S(1)}, bf16[128,1024]{1,0:T(8,128)(2,1)}, u32[]{:S(2)}) copy-start(bf16[128,1024]{1,0:T(8,128)(2,1)} %cot.1) | copy-start | bytes 786436
  3.1 17.5 %collective-permute-start.1 = (bf16[128,1536]{1,0:T(8,128)(2,1)S(1)}, bf16[128,1536]{1,0:T(8,128)(2,1)S(1)}, u32[]{:S(2)}, u32[]{:S(2)}) collective-permute-start(bf16[128,1536]{1,0:T(8,128)(2,1)S(1)} %get-tuple-element.40), channel_id=1, source_target_pairs={{0,8},{4,12},{8,0},{12,4},{1,9},{5,13},{9,1},{13,5},{2,10},{6,14},... | collective-permute-start | bytes 1179656 | tf_op jit(solution)/shard_map/ppermute | solution.py:272
  6.1 8.3 %collective-permute-start.3 = (bf16[128,512]{1,0:T(8,128)(2,1)S(1)}, bf16[128,512]{1,0:T(8,128)(2,1)S(1)}, u32[]{:S(2)}, u32[]{:S(2)}) collective-permute-start(bf16[128,512]{1,0:T(8,128)(2,1)S(1)} %get-tuple-element.41), channel_id=1, source_target_pairs={{0,3},{1,2},{2,1},{3,0},{4,7},{5,6},{6,5},{7,4},{8,11},{9,10},{10,... | collective-permute-start | bytes 393224 | tf_op jit(solution)/shard_map/ppermute | solution.py:275
  9.7 10.9 %collective-permute-start.2 = (bf16[128,512]{1,0:T(8,128)(2,1)S(1)}, bf16[128,512]{1,0:T(8,128)(2,1)S(1)}, u32[]{:S(2)}, u32[]{:S(2)}) collective-permute-start(bf16[128,512]{1,0:T(8,128)(2,1)S(1)} %get-tuple-element.41), channel_id=1, source_target_pairs={{0,2},{1,3},{2,0},{3,1},{4,6},{5,7},{6,4},{7,5},{8,10},{9,11},{10,... | collective-permute-start | bytes 393224 | tf_op jit(solution)/shard_map/ppermute | solution.py:275
  9.7 13.0 %collective-permute-start = (bf16[128,1536]{1,0:T(8,128)(2,1)S(1)}, bf16[128,1536]{1,0:T(8,128)(2,1)S(1)}, u32[]{:S(2)}, u32[]{:S(2)}) collective-permute-start(bf16[128,1536]{1,0:T(8,128)(2,1)S(1)} %get-tuple-element.39.refs_0_.refs_4_), channel_id=1, source_target_pairs={{0,4},{4,0},{8,12},{12,8},{1,5},{5,1},{9,13},{13,9},{2,6},{6,2},{1... | collective-permute-start | bytes 1179656 | tf_op jit(solution)/shard_map/ppermute | solution.py:272
  9.7 19.6 %collective-permute-start.5 = (bf16[256,768]{1,0:T(8,128)(2,1)S(1)}, bf16[256,768]{1,0:T(8,128)(2,1)S(1)}, u32[]{:S(2)}, u32[]{:S(2)}) collective-permute-start(bf16[256,768]{1,0:T(8,128)(2,1)S(1)} %get-tuple-element.37.refs_4_), channel_id=1, source_target_pairs={{0,1},{1,0},{2,3},{3,2},{4,5},{5,4},{6,7},{7,6},{8,9},{9,8},{10,11... | collective-permute-start | bytes 1179656 | tf_op jit(solution)/shard_map/ppermute | solution.py:275
  20.6 8.7 %collective-permute-start.4 = (bf16[128,1536]{1,0:T(8,128)(2,1)S(1)}, bf16[128,1536]{1,0:T(8,128)(2,1)S(1)}, u32[]{:S(2)}, u32[]{:S(2)}) collective-permute-start(bf16[128,1536]{1,0:T(8,128)(2,1)S(1)} %collective-permute-done.1.refs_2_.refs_6_), channel_id=1, source_target_pairs={{0,4},{4,0},{8,12},{12,8},{1,5},{5,1},{9,13},{13,9},{2,6},{6,2},{1... | collective-permute-start | bytes 1179656 | tf_op jit(solution)/shard_map/ppermute | solution.py:272
  20.6 6.3 %collective-permute-start.7 = (bf16[128,512]{1,0:T(8,128)(2,1)S(1)}, bf16[128,512]{1,0:T(8,128)(2,1)S(1)}, u32[]{:S(2)}, u32[]{:S(2)}) collective-permute-start(bf16[128,512]{1,0:T(8,128)(2,1)S(1)} %collective-permute-done.3.refs_8_), channel_id=1, source_target_pairs={{0,16},{16,0},{1,17},{17,1},{2,18},{18,2},{3,19},{19,3},{4,20},{20... | collective-permute-start | bytes 393224 | tf_op jit(solution)/shard_map/ppermute | solution.py:315
  22.1 7.2 %collective-permute-start.6 = (bf16[128,512]{1,0:T(8,128)(2,1)S(1)}, bf16[128,512]{1,0:T(8,128)(2,1)S(1)}, u32[]{:S(2)}, u32[]{:S(2)}) collective-permute-start(bf16[128,512]{1,0:T(8,128)(2,1)S(1)} %collective-permute-done.2.refs_6_), channel_id=1, source_target_pairs={{0,16},{16,0},{1,17},{17,1},{2,18},{18,2},{3,19},{19,3},{4,20},{20... | collective-permute-start | bytes 393224 | tf_op jit(solution)/shard_map/ppermute | solution.py:315
  22.6 8.4 %collective-permute-start.9 = (bf16[128,256]{1,0:T(8,128)(2,1)S(1)}, bf16[128,256]{1,0:T(8,128)(2,1)S(1)}, u32[]{:S(2)}, u32[]{:S(2)}) collective-permute-start(bf16[128,256]{1,0:T(8,128)(2,1)S(1)} %get-tuple-element.47), channel_id=1, source_target_pairs={{0,3},{1,2},{2,1},{3,0},{4,7},{5,6},{6,5},{7,4},{8,11},{9,10},{10,... | collective-permute-start | bytes 196616 | tf_op jit(solution)/shard_map/ppermute | solution.py:275
  26.9 5.4 %collective-permute-start.8 = (bf16[128,256]{1,0:T(8,128)(2,1)S(1)}, bf16[128,256]{1,0:T(8,128)(2,1)S(1)}, u32[]{:S(2)}, u32[]{:S(2)}) collective-permute-start(bf16[128,256]{1,0:T(8,128)(2,1)S(1)} %get-tuple-element.47), channel_id=1, source_target_pairs={{0,2},{1,3},{2,0},{3,1},{4,6},{5,7},{6,4},{7,5},{8,10},{9,11},{10,... | collective-permute-start | bytes 196616 | tf_op jit(solution)/shard_map/ppermute | solution.py:275
  32.7 11.7 %collective-permute-start.12 = (bf16[528,128]{1,0:T(8,128)(2,1)S(1)}, bf16[528,128]{1,0:T(8,128)(2,1)S(1)}, u32[]{:S(2)}, u32[]{:S(2)}) collective-permute-start(bf16[528,128]{1,0:T(8,128)(2,1)S(1)} %get-tuple-element.50), channel_id=1, source_target_pairs={{0,3},{1,2},{2,1},{3,0},{4,7},{5,6},{6,5},{7,4},{8,11},{9,10},{10,... | collective-permute-start | bytes 405512 | tf_op jit(solution)/shard_map/ppermute | solution.py:287
  34.9 10.8 %collective-permute-start.11 = (bf16[528,128]{1,0:T(8,128)(2,1)S(1)}, bf16[528,128]{1,0:T(8,128)(2,1)S(1)}, u32[]{:S(2)}, u32[]{:S(2)}) collective-permute-start(bf16[528,128]{1,0:T(8,128)(2,1)S(1)} %get-tuple-element.50), channel_id=1, source_target_pairs={{0,2},{1,3},{2,0},{3,1},{4,6},{5,7},{6,4},{7,5},{8,10},{9,11},{10,... | collective-permute-start | bytes 405512 | tf_op jit(solution)/shard_map/ppermute | solution.py:287
  34.9 10.8 %collective-permute-start.10 = (bf16[528,128]{1,0:T(8,128)(2,1)S(1)}, bf16[528,128]{1,0:T(8,128)(2,1)S(1)}, u32[]{:S(2)}, u32[]{:S(2)}) collective-permute-start(bf16[528,128]{1,0:T(8,128)(2,1)S(1)} %get-tuple-element.50), channel_id=1, source_target_pairs={{0,1},{1,0},{2,3},{3,2},{4,5},{5,4},{6,7},{7,6},{8,9},{9,8},{10,11... | collective-permute-start | bytes 405512 | tf_op jit(solution)/shard_map/ppermute | solution.py:287
  37.1 4.3 %collective-permute-start.13 = (bf16[128,256]{1,0:T(8,128)(2,1)S(1)}, bf16[128,256]{1,0:T(8,128)(2,1)S(1)}, u32[]{:S(2)}, u32[]{:S(2)}) collective-permute-start(bf16[128,256]{1,0:T(8,128)(2,1)S(1)} %collective-permute-done.8.refs_6_), channel_id=1, source_target_pairs={{0,16},{16,0},{1,17},{17,1},{2,18},{18,2},{3,19},{19,3},{4,20},{20... | collective-permute-start | bytes 196616 | tf_op jit(solution)/shard_map/ppermute | solution.py:315
  38.6 4.3 %collective-permute-start.14 = (bf16[128,256]{1,0:T(8,128)(2,1)S(1)}, bf16[128,256]{1,0:T(8,128)(2,1)S(1)}, u32[]{:S(2)}, u32[]{:S(2)}) collective-permute-start(bf16[128,256]{1,0:T(8,128)(2,1)S(1)} %collective-permute-done.9.refs_8_), channel_id=1, source_target_pairs={{0,16},{16,0},{1,17},{17,1},{2,18},{18,2},{3,19},{19,3},{4,20},{20... | collective-permute-start | bytes 196616 | tf_op jit(solution)/shard_map/ppermute | solution.py:315
  46.6 8.4 %collective-permute-start.17 = (bf16[528,128]{1,0:T(8,128)(2,1)S(1)}, bf16[528,128]{1,0:T(8,128)(2,1)S(1)}, u32[]{:S(2)}, u32[]{:S(2)}) collective-permute-start(bf16[528,128]{1,0:T(8,128)(2,1)S(1)} %get-tuple-element.60), channel_id=1, source_target_pairs={{0,3},{1,2},{2,1},{3,0},{4,7},{5,6},{6,5},{7,4},{8,11},{9,10},{10,... | collective-permute-start | bytes 405512 | tf_op jit(solution)/shard_map/ppermute | solution.py:287
  48.2 10.9 %collective-permute-start.16 = (bf16[528,128]{1,0:T(8,128)(2,1)S(1)}, bf16[528,128]{1,0:T(8,128)(2,1)S(1)}, u32[]{:S(2)}, u32[]{:S(2)}) collective-permute-start(bf16[528,128]{1,0:T(8,128)(2,1)S(1)} %get-tuple-element.60), channel_id=1, source_target_pairs={{0,2},{1,3},{2,0},{3,1},{4,6},{5,7},{6,4},{7,5},{8,10},{9,11},{10,... | collective-permute-start | bytes 405512 | tf_op jit(solution)/shard_map/ppermute | solution.py:287
  48.2 10.9 %collective-permute-start.15 = (bf16[528,128]{1,0:T(8,128)(2,1)S(1)}, bf16[528,128]{1,0:T(8,128)(2,1)S(1)}, u32[]{:S(2)}, u32[]{:S(2)}) collective-permute-start(bf16[528,128]{1,0:T(8,128)(2,1)S(1)} %get-tuple-element.60), channel_id=1, source_target_pairs={{0,1},{1,0},{2,3},{3,2},{4,5},{5,4},{6,7},{7,6},{8,9},{9,8},{10,11... | collective-permute-start | bytes 405512 | tf_op jit(solution)/shard_map/ppermute | solution.py:287
  60.3 1.6 %collective-permute-start.20 = (bf16[128,1024]{1,0:T(8,128)(2,1)S(1)}, bf16[128,1024]{1,0:T(8,128)(2,1)S(1)}, u32[]{:S(2)}, u32[]{:S(2)}) collective-permute-start(bf16[128,1024]{1,0:T(8,128)(2,1)S(1)} %get-tuple-element.68), channel_id=1, source_target_pairs={{0,4},{4,0},{8,12},{12,8},{1,5},{5,1},{9,13},{13,9},{2,6},{6,2},{1... | collective-permute-start | bytes 786440 | tf_op jit(solution)/shard_map/ppermute | solution.py:272
  62.0 8.4 %collective-permute-start.21 = (bf16[128,1024]{1,0:T(8,128)(2,1)S(1)}, bf16[128,1024]{1,0:T(8,128)(2,1)S(1)}, u32[]{:S(2)}, u32[]{:S(2)}) collective-permute-start(bf16[128,1024]{1,0:T(8,128)(2,1)S(1)} %add_convert_fusion.1), channel_id=1, source_target_pairs={{0,8},{4,12},{8,0},{12,4},{1,9},{5,13},{9,1},{13,5},{2,10},{6,14},... | collective-permute-start | bytes 786440 | tf_op jit(solution)/shard_map/ppermute | solution.py:272
  64.2 1.4 %collective-permute-start.18 = (bf16[64,1024]{1,0:T(8,128)(2,1)S(1)}, bf16[64,1024]{1,0:T(8,128)(2,1)S(1)}, u32[]{:S(2)}, u32[]{:S(2)}) collective-permute-start(bf16[64,1024]{1,0:T(8,128)(2,1)S(1)} %get-tuple-element.66), channel_id=1, source_target_pairs={{0,4},{4,0},{8,12},{12,8},{1,5},{5,1},{9,13},{13,9},{2,6},{6,2},{1... | collective-permute-start | bytes 393224 | tf_op jit(solution)/shard_map/ppermute | solution.py:272
  64.3 1.5 %collective-permute-start.19 = (bf16[64,1024]{1,0:T(8,128)(2,1)S(1)}, bf16[64,1024]{1,0:T(8,128)(2,1)S(1)}, u32[]{:S(2)}, u32[]{:S(2)}) collective-permute-start(bf16[64,1024]{1,0:T(8,128)(2,1)S(1)} %get-tuple-element.67), channel_id=1, source_target_pairs={{0,4},{4,0},{8,12},{12,8},{1,5},{5,1},{9,13},{13,9},{2,6},{6,2},{1... | collective-permute-start | bytes 393224 | tf_op jit(solution)/shard_map/ppermute | solution.py:272
  (2 other events, 2.0 us)

commit v11 on v10

--- a/solution.py
+++ b/solution.py
@@ -275,9 +275,10 @@
         return lax.ppermute(x, "sub", [(i, i ^ k) for i in range(n_sub)])
 
     def to_all(own, send):
+        order = [*range(n_sub - 2, -1, -1), n_sub - 1]
         parts = [own]
         for j in range(r):
-            for k in range(n_sub):
+            for k in order:
                 if j or k:
                     perm = [
                         (a * n_sub + b, (a ^ (j * g)) * n_sub + (b ^ k))

time: 71.4 us -> 70.7 us (level)
  transfers between devices with their start and end apart: 22 -> 22, of which waited for: 14 -> 15; matrix products, arithmetic and copies ran while one was open for 0% -> 0% of each run, Pallas kernels for 8% -> 8%
where the time goes in v11:
time: 70.7 us; the launch traced here: 70.5 us
  waiting for transfers between devices  34 us (48%)
  starting transfers between devices  24.2 us (34%)
  Pallas kernels  10.6 us (15%)
  other arithmetic  0.86 us (1%)
    ppermute x5, waiting for transfers between devices, over_sub(): return lax.ppermute(x, 'sub', [(i, i ^ k) for i in range(n_sub)])  11.4 us
    pallas_call x10, Pallas kernels, call(): pl.pallas_call(body, out_shape=[jax.ShapeDtypeStruct(s, d) for s, d in ou...  10.6 us
    ppermute x6, starting transfers between devices, to_all(): parts.append(lax.ppermute(send, ('seq', 'sub'), perm))  8.91 us
    ppermute x6, waiting for transfers between devices, to_all(): parts.append(lax.ppermute(send, ('seq', 'sub'), perm))  8.32 us
    ppermute x4, waiting for transfers between devices, swapped(): lax.ppermute(part, 'grp', [(0, 1), (1, 0)])  7.78 us
    ppermute x5, starting transfers between devices, over_sub(): return lax.ppermute(x, 'sub', [(i, i ^ k) for i in range(n_sub)])  7.02 us
    ppermute x7, waiting for transfers between devices, over_seq(): return lax.ppermute(x, 'seq', [(i, i ^ k) for i in range(n_seq)])  6.53 us
    ppermute x7, starting transfers between devices, over_seq(): return lax.ppermute(x, 'seq', [(i, i ^ k) for i in range(n_seq)])  4.25 us
  transfers between devices with their start and end apart: 22, of which 15 were waited for; matrix products, arithmetic and copies ran while one was open for 0% of the time, Pallas kernels for 8%

profile of v11, /device:TPU:0, one launch (start us, length us, event | category | flops | bytes accessed | tf_op | source)
XLA Modules:
  0.0 70.5 jit_solution(4250985611792634196)
XLA Ops:
  0.0 1.2 %shard_map.73 = (bf16[256,768]{1,0:T(8,128)(2,1)S(1)}, bf16[128,512]{1,0:T(8,128)(2,1)S(1)}, bf16[128,256]{1,0:T(8,128)(2,1)S(1)}) custom-call(bf16[256,1024]{1,0:T(8,128)(2,1)} %refs_0_.1, bf16[256,1024]{1,0:T(8,128)(2,1)} %refs_1_.1, bf16[256,1024]{1,0:T(8,128)(2,1)} %refs_2_.1), custom_call_target="tpu_custom_call" | custom-call | tf_op jit(solution)/shard_map/pallas_call | solution.py:30
  3.1 3.0 %collective-permute-start.1 = (bf16[128,1536]{1,0:T(8,128)(2,1)S(1)}, bf16[128,1536]{1,0:T(8,128)(2,1)S(1)}, u32[]{:S(2)}, u32[]{:S(2)}) collective-permute-start(bf16[128,1536]{1,0:T(8,128)(2,1)S(1)} %get-tuple-element.40), channel_id=1, source_target_pairs={{0,8},{4,12},{8,0},{12,4},{1,9},{5,13},{9,1},{13,5},{2,10},{6,14},... | collective-permute-start | bytes 1179656 | tf_op jit(solution)/shard_map/ppermute | solution.py:272
  6.1 3.6 %collective-permute-start.3 = (bf16[128,512]{1,0:T(8,128)(2,1)S(1)}, bf16[128,512]{1,0:T(8,128)(2,1)S(1)}, u32[]{:S(2)}, u32[]{:S(2)}) collective-permute-start(bf16[128,512]{1,0:T(8,128)(2,1)S(1)} %get-tuple-element.41), channel_id=1, source_target_pairs={{0,3},{1,2},{2,1},{3,0},{4,7},{5,6},{6,5},{7,4},{8,11},{9,10},{10,... | collective-permute-start | bytes 393224 | tf_op jit(solution)/shard_map/ppermute | solution.py:275
  10.5 3.9 %collective-permute-done.3.refs_8_ = bf16[128,512]{1,0:T(8,128)(2,1)S(1)} collective-permute-done((bf16[128,512]{1,0:T(8,128)(2,1)S(1)}, bf16[128,512]{1,0:T(8,128)(2,1)S(1)}, u32[]{:S(2)}, u32[]{:S(2)}) %collective-permute-start.3) | collective-permute-done | bytes 131104 | tf_op jit(solution)/shard_map/ppermute | solution.py:275
  14.3 6.2 %collective-permute-done.2.refs_6_ = bf16[128,512]{1,0:T(8,128)(2,1)S(1)} collective-permute-done((bf16[128,512]{1,0:T(8,128)(2,1)S(1)}, bf16[128,512]{1,0:T(8,128)(2,1)S(1)}, u32[]{:S(2)}, u32[]{:S(2)}) %collective-permute-start.2) | collective-permute-done | bytes 131104 | tf_op jit(solution)/shard_map/ppermute | solution.py:275
  20.6 1.5 %collective-permute-start.7 = (bf16[128,512]{1,0:T(8,128)(2,1)S(1)}, bf16[128,512]{1,0:T(8,128)(2,1)S(1)}, u32[]{:S(2)}, u32[]{:S(2)}) collective-permute-start(bf16[128,512]{1,0:T(8,128)(2,1)S(1)} %collective-permute-done.3.refs_8_), channel_id=1, source_target_pairs={{0,16},{16,0},{1,17},{17,1},{2,18},{18,2},{3,19},{19,3},{4,20},{20... | collective-permute-start | bytes 393224 | tf_op jit(solution)/shard_map/ppermute | solution.py:316
  22.6 2.5 %collective-permute-start.9 = (bf16[128,256]{1,0:T(8,128)(2,1)S(1)}, bf16[128,256]{1,0:T(8,128)(2,1)S(1)}, u32[]{:S(2)}, u32[]{:S(2)}) collective-permute-start(bf16[128,256]{1,0:T(8,128)(2,1)S(1)} %get-tuple-element.47), channel_id=1, source_target_pairs={{0,3},{1,2},{2,1},{3,0},{4,7},{5,6},{6,5},{7,4},{8,11},{9,10},{10,... | collective-permute-start | bytes 196616 | tf_op jit(solution)/shard_map/ppermute | solution.py:275
  25.1 1.7 %collective-permute-done.7.refs_9_ = bf16[128,512]{1,0:T(8,128)(2,1)S(1)} collective-permute-done((bf16[128,512]{1,0:T(8,128)(2,1)S(1)}, bf16[128,512]{1,0:T(8,128)(2,1)S(1)}, u32[]{:S(2)}, u32[]{:S(2)}) %collective-permute-start.7) | collective-permute-done | bytes 131104 | tf_op jit(solution)/shard_map/ppermute | solution.py:316
  27.0 2.3 %collective-permute-done.6.refs_7_ = bf16[128,512]{1,0:T(8,128)(2,1)S(1)} collective-permute-done((bf16[128,512]{1,0:T(8,128)(2,1)S(1)}, bf16[128,512]{1,0:T(8,128)(2,1)S(1)}, u32[]{:S(2)}, u32[]{:S(2)}) %collective-permute-start.6) | collective-permute-done | bytes 131104 | tf_op jit(solution)/shard_map/ppermute | solution.py:316
  29.3 1.7 %shard_map.75 = (bf16[1024,512]{1,0:T(8,128)(2,1)S(1)}, bf16[512,512]{1,0:T(8,128)(2,1)S(1)}, f32[512,512]{1,0:T(8,128)S(1)}, bf16[512,256]{1,0:T(8,128)(2,1)S(1)}, f32[1,512]{1,0:T(1,128)S(1)}) custom-call(bf16[128,1536]{1,0:T(8,128)(2,1)S(1)} %get-tuple-element.39.refs_0_.refs_4_, bf16[128,1536]{1,0:T(8,128)(2,1)S(1)} %collective-permute-done.refs_1_.refs_5_, ...), custom_call_target="tpu_custom_call" | custom-call | flops 2147483648 | bytes 3014656 | tf_op jit(solution)/shard_map/pallas_call | solution.py:30
  31.0 1.3 %collective-permute-done.8.refs_6_ = bf16[128,256]{1,0:T(8,128)(2,1)S(1)} collective-permute-done((bf16[128,256]{1,0:T(8,128)(2,1)S(1)}, bf16[128,256]{1,0:T(8,128)(2,1)S(1)}, u32[]{:S(2)}, u32[]{:S(2)}) %collective-permute-start.8) | collective-permute-done | bytes 65568 | tf_op jit(solution)/shard_map/ppermute | solution.py:275
  32.7 2.2 %collective-permute-start.12 = (bf16[528,128]{1,0:T(8,128)(2,1)S(1)}, bf16[528,128]{1,0:T(8,128)(2,1)S(1)}, u32[]{:S(2)}, u32[]{:S(2)}) collective-permute-start(bf16[528,128]{1,0:T(8,128)(2,1)S(1)} %get-tuple-element.50), channel_id=1, source_target_pairs={{0,3},{1,2},{2,1},{3,0},{4,7},{5,6},{6,5},{7,4},{8,11},{9,10},{10,... | collective-permute-start | bytes 405512 | tf_op jit(solution)/shard_map/ppermute | solution.py:288
  34.9 2.2 %collective-permute-start.10 = (bf16[528,128]{1,0:T(8,128)(2,1)S(1)}, bf16[528,128]{1,0:T(8,128)(2,1)S(1)}, u32[]{:S(2)}, u32[]{:S(2)}) collective-permute-start(bf16[528,128]{1,0:T(8,128)(2,1)S(1)} %get-tuple-element.50), channel_id=1, source_target_pairs={{0,2},{1,3},{2,0},{3,1},{4,6},{5,7},{6,4},{7,5},{8,10},{9,11},{10,... | collective-permute-start | bytes 405512 | tf_op jit(solution)/shard_map/ppermute | solution.py:288
  37.1 1.5 %collective-permute-start.13 = (bf16[128,256]{1,0:T(8,128)(2,1)S(1)}, bf16[128,256]{1,0:T(8,128)(2,1)S(1)}, u32[]{:S(2)}, u32[]{:S(2)}) collective-permute-start(bf16[128,256]{1,0:T(8,128)(2,1)S(1)} %collective-permute-done.8.refs_6_), channel_id=1, source_target_pairs={{0,16},{16,0},{1,17},{17,1},{2,18},{18,2},{3,19},{19,3},{4,20},{20... | collective-permute-start | bytes 196616 | tf_op jit(solution)/shard_map/ppermute | solution.py:316
  39.1 2.2 %collective-permute-done.13.refs_7_ = bf16[128,256]{1,0:T(8,128)(2,1)S(1)} collective-permute-done((bf16[128,256]{1,0:T(8,128)(2,1)S(1)}, bf16[128,256]{1,0:T(8,128)(2,1)S(1)}, u32[]{:S(2)}, u32[]{:S(2)}) %collective-permute-start.13) | collective-permute-done | bytes 65568 | tf_op jit(solution)/shard_map/ppermute | solution.py:316
  41.4 1.5 %collective-permute-done.14.refs_9_ = bf16[128,256]{1,0:T(8,128)(2,1)S(1)} collective-permute-done((bf16[128,256]{1,0:T(8,128)(2,1)S(1)}, bf16[128,256]{1,0:T(8,128)(2,1)S(1)}, u32[]{:S(2)}, u32[]{:S(2)}) %collective-permute-start.14) | collective-permute-done | bytes 65568 | tf_op jit(solution)/shard_map/ppermute | solution.py:316
  42.9 1.4 %shard_map.77 = (bf16[1024,256]{1,0:T(8,128)(2,1)S(1)}, bf16[512,512]{1,0:T(8,128)(2,1)S(1)}, f32[512,512]{1,0:T(8,128)S(1)}) custom-call(bf16[128,1536]{1,0:T(8,128)(2,1)S(1)} %get-tuple-element.39.refs_0_.refs_4_, bf16[128,1536]{1,0:T(8,128)(2,1)S(1)} %collective-permute-done.refs_1_.refs_5_, bf16[128,1536]{1,0:T(8,128)(2,1)S(1)} %collective-permute-done.1.refs_2_.refs_6_, ...), custom_call_target="tpu_custom_call" | custom-call | tf_op jit(solution)/shard_map/pallas_call | solution.py:30
  44.3 1.5 %collective-permute-done.10.refs_1_ = bf16[528,128]{1,0:T(8,128)(2,1)S(1)} collective-permute-done((bf16[528,128]{1,0:T(8,128)(2,1)S(1)}, bf16[528,128]{1,0:T(8,128)(2,1)S(1)}, u32[]{:S(2)}, u32[]{:S(2)}) %collective-permute-start.10) | collective-permute-done | bytes 135200 | tf_op jit(solution)/shard_map/ppermute | solution.py:288
  46.7 1.5 %collective-permute-start.17 = (bf16[528,128]{1,0:T(8,128)(2,1)S(1)}, bf16[528,128]{1,0:T(8,128)(2,1)S(1)}, u32[]{:S(2)}, u32[]{:S(2)}) collective-permute-start(bf16[528,128]{1,0:T(8,128)(2,1)S(1)} %get-tuple-element.60), channel_id=1, source_target_pairs={{0,3},{1,2},{2,1},{3,0},{4,7},{5,6},{6,5},{7,4},{8,11},{9,10},{10,... | collective-permute-start | bytes 405512 | tf_op jit(solution)/shard_map/ppermute | solution.py:288
  48.2 2.9 %collective-permute-start.15 = (bf16[528,128]{1,0:T(8,128)(2,1)S(1)}, bf16[528,128]{1,0:T(8,128)(2,1)S(1)}, u32[]{:S(2)}, u32[]{:S(2)}) collective-permute-start(bf16[528,128]{1,0:T(8,128)(2,1)S(1)} %get-tuple-element.60), channel_id=1, source_target_pairs={{0,2},{1,3},{2,0},{3,1},{4,6},{5,7},{6,4},{7,5},{8,10},{9,11},{10,... | collective-permute-start | bytes 405512 | tf_op jit(solution)/shard_map/ppermute | solution.py:288
  51.7 2.7 %collective-permute-done.17.refs_3_ = bf16[528,128]{1,0:T(8,128)(2,1)S(1)} collective-permute-done((bf16[528,128]{1,0:T(8,128)(2,1)S(1)}, bf16[528,128]{1,0:T(8,128)(2,1)S(1)}, u32[]{:S(2)}, u32[]{:S(2)}) %collective-permute-start.17) | collective-permute-done | bytes 135200 | tf_op jit(solution)/shard_map/ppermute | solution.py:288
  55.6 2.9 %collective-permute-done.15.refs_1_ = bf16[528,128]{1,0:T(8,128)(2,1)S(1)} collective-permute-done((bf16[528,128]{1,0:T(8,128)(2,1)S(1)}, bf16[528,128]{1,0:T(8,128)(2,1)S(1)}, u32[]{:S(2)}, u32[]{:S(2)}) %collective-permute-start.15) | collective-permute-done | bytes 135200 | tf_op jit(solution)/shard_map/ppermute | solution.py:288
  61.9 1.6 %shard_map.81 = (bf16[64,1024]{1,0:T(8,128)(2,1)S(1)}, bf16[64,1024]{1,0:T(8,128)(2,1)S(1)}, f32[128,1024]{1,0:T(8,128)S(1)}) custom-call(bf16[512,256]{1,0:T(8,128)(2,1)S(1)} %shard_map.79.refs_8_.qg, bf16[512,512]{1,0:T(8,128)(2,1)S(1)} %get-tuple-element.64.kvg, bf16[1024,256]{1,0:T(8,128)(2,1)S(1)} %get-tuple-element.62.refs_9_.wq, ...), custom_call_target="tpu_custom_call" | custom-call | tf_op jit(solution)/shard_map/pallas_call | solution.py:30
  65.1 4.6 %collective-permute-done.21 = bf16[128,1024]{1,0:T(8,128)(2,1)S(1)} collective-permute-done((bf16[128,1024]{1,0:T(8,128)(2,1)S(1)}, bf16[128,1024]{1,0:T(8,128)(2,1)S(1)}, u32[]{:S(2)}, u32[]{:S(2)}) %collective-permute-start.21) | collective-permute-done | bytes 262176 | tf_op jit(solution)/shard_map/ppermute | solution.py:272
  (42 shorter events, 12.5 us)
Async XLA Ops:
  0.0 22.6 %copy-start = (bf16[8,128,256]{2,1,0:T(8,128)(2,1)S(1)}, bf16[8,128,256]{2,1,0:T(8,128)(2,1)}, u32[]{:S(2)}) copy-start(bf16[8,128,256]{2,1,0:T(8,128)(2,1)} %param.13) | copy-start | bytes 1572868
  0.0 1.4 %copy-start.2 = (bf16[128,1024]{1,0:T(8,128)(2,1)S(1)}, bf16[128,1024]{1,0:T(8,128)(2,1)}, u32[]{:S(2)}) copy-start(bf16[128,1024]{1,0:T(8,128)(2,1)} %cot.1) | copy-start | bytes 786436
  3.1 17.5 %collective-permute-start.1 = (bf16[128,1536]{1,0:T(8,128)(2,1)S(1)}, bf16[128,1536]{1,0:T(8,128)(2,1)S(1)}, u32[]{:S(2)}, u32[]{:S(2)}) collective-permute-start(bf16[128,1536]{1,0:T(8,128)(2,1)S(1)} %get-tuple-element.40), channel_id=1, source_target_pairs={{0,8},{4,12},{8,0},{12,4},{1,9},{5,13},{9,1},{13,5},{2,10},{6,14},... | collective-permute-start | bytes 1179656 | tf_op jit(solution)/shard_map/ppermute | solution.py:272
  6.1 8.3 %collective-permute-start.3 = (bf16[128,512]{1,0:T(8,128)(2,1)S(1)}, bf16[128,512]{1,0:T(8,128)(2,1)S(1)}, u32[]{:S(2)}, u32[]{:S(2)}) collective-permute-start(bf16[128,512]{1,0:T(8,128)(2,1)S(1)} %get-tuple-element.41), channel_id=1, source_target_pairs={{0,3},{1,2},{2,1},{3,0},{4,7},{5,6},{6,5},{7,4},{8,11},{9,10},{10,... | collective-permute-start | bytes 393224 | tf_op jit(solution)/shard_map/ppermute | solution.py:275
  9.7 10.9 %collective-permute-start.2 = (bf16[128,512]{1,0:T(8,128)(2,1)S(1)}, bf16[128,512]{1,0:T(8,128)(2,1)S(1)}, u32[]{:S(2)}, u32[]{:S(2)}) collective-permute-start(bf16[128,512]{1,0:T(8,128)(2,1)S(1)} %get-tuple-element.41), channel_id=1, source_target_pairs={{0,2},{1,3},{2,0},{3,1},{4,6},{5,7},{6,4},{7,5},{8,10},{9,11},{10,... | collective-permute-start | bytes 393224 | tf_op jit(solution)/shard_map/ppermute | solution.py:275
  9.7 13.0 %collective-permute-start = (bf16[128,1536]{1,0:T(8,128)(2,1)S(1)}, bf16[128,1536]{1,0:T(8,128)(2,1)S(1)}, u32[]{:S(2)}, u32[]{:S(2)}) collective-permute-start(bf16[128,1536]{1,0:T(8,128)(2,1)S(1)} %get-tuple-element.39.refs_0_.refs_4_), channel_id=1, source_target_pairs={{0,4},{4,0},{8,12},{12,8},{1,5},{5,1},{9,13},{13,9},{2,6},{6,2},{1... | collective-permute-start | bytes 1179656 | tf_op jit(solution)/shard_map/ppermute | solution.py:272
  9.7 19.6 %collective-permute-start.5 = (bf16[256,768]{1,0:T(8,128)(2,1)S(1)}, bf16[256,768]{1,0:T(8,128)(2,1)S(1)}, u32[]{:S(2)}, u32[]{:S(2)}) collective-permute-start(bf16[256,768]{1,0:T(8,128)(2,1)S(1)} %get-tuple-element.37.refs_4_), channel_id=1, source_target_pairs={{0,1},{1,0},{2,3},{3,2},{4,5},{5,4},{6,7},{7,6},{8,9},{9,8},{10,11... | collective-permute-start | bytes 1179656 | tf_op jit(solution)/shard_map/ppermute | solution.py:275
  20.6 8.7 %collective-permute-start.4 = (bf16[128,1536]{1,0:T(8,128)(2,1)S(1)}, bf16[128,1536]{1,0:T(8,128)(2,1)S(1)}, u32[]{:S(2)}, u32[]{:S(2)}) collective-permute-start(bf16[128,1536]{1,0:T(8,128)(2,1)S(1)} %collective-permute-done.1.refs_2_.refs_6_), channel_id=1, source_target_pairs={{0,4},{4,0},{8,12},{12,8},{1,5},{5,1},{9,13},{13,9},{2,6},{6,2},{1... | collective-permute-start | bytes 1179656 | tf_op jit(solution)/shard_map/ppermute | solution.py:272
  20.6 6.3 %collective-permute-start.7 = (bf16[128,512]{1,0:T(8,128)(2,1)S(1)}, bf16[128,512]{1,0:T(8,128)(2,1)S(1)}, u32[]{:S(2)}, u32[]{:S(2)}) collective-permute-start(bf16[128,512]{1,0:T(8,128)(2,1)S(1)} %collective-permute-done.3.refs_8_), channel_id=1, source_target_pairs={{0,16},{16,0},{1,17},{17,1},{2,18},{18,2},{3,19},{19,3},{4,20},{20... | collective-permute-start | bytes 393224 | tf_op jit(solution)/shard_map/ppermute | solution.py:316
  22.1 7.2 %collective-permute-start.6 = (bf16[128,512]{1,0:T(8,128)(2,1)S(1)}, bf16[128,512]{1,0:T(8,128)(2,1)S(1)}, u32[]{:S(2)}, u32[]{:S(2)}) collective-permute-start(bf16[128,512]{1,0:T(8,128)(2,1)S(1)} %collective-permute-done.2.refs_6_), channel_id=1, source_target_pairs={{0,16},{16,0},{1,17},{17,1},{2,18},{18,2},{3,19},{19,3},{4,20},{20... | collective-permute-start | bytes 393224 | tf_op jit(solution)/shard_map/ppermute | solution.py:316
  22.6 8.4 %collective-permute-start.9 = (bf16[128,256]{1,0:T(8,128)(2,1)S(1)}, bf16[128,256]{1,0:T(8,128)(2,1)S(1)}, u32[]{:S(2)}, u32[]{:S(2)}) collective-permute-start(bf16[128,256]{1,0:T(8,128)(2,1)S(1)} %get-tuple-element.47), channel_id=1, source_target_pairs={{0,3},{1,2},{2,1},{3,0},{4,7},{5,6},{6,5},{7,4},{8,11},{9,10},{10,... | collective-permute-start | bytes 196616 | tf_op jit(solution)/shard_map/ppermute | solution.py:275
  26.9 5.4 %collective-permute-start.8 = (bf16[128,256]{1,0:T(8,128)(2,1)S(1)}, bf16[128,256]{1,0:T(8,128)(2,1)S(1)}, u32[]{:S(2)}, u32[]{:S(2)}) collective-permute-start(bf16[128,256]{1,0:T(8,128)(2,1)S(1)} %get-tuple-element.47), channel_id=1, source_target_pairs={{0,2},{1,3},{2,0},{3,1},{4,6},{5,7},{6,4},{7,5},{8,10},{9,11},{10,... | collective-permute-start | bytes 196616 | tf_op jit(solution)/shard_map/ppermute | solution.py:275
  32.7 11.7 %collective-permute-start.12 = (bf16[528,128]{1,0:T(8,128)(2,1)S(1)}, bf16[528,128]{1,0:T(8,128)(2,1)S(1)}, u32[]{:S(2)}, u32[]{:S(2)}) collective-permute-start(bf16[528,128]{1,0:T(8,128)(2,1)S(1)} %get-tuple-element.50), channel_id=1, source_target_pairs={{0,3},{1,2},{2,1},{3,0},{4,7},{5,6},{6,5},{7,4},{8,11},{9,10},{10,... | collective-permute-start | bytes 405512 | tf_op jit(solution)/shard_map/ppermute | solution.py:288
  34.9 9.4 %collective-permute-start.11 = (bf16[528,128]{1,0:T(8,128)(2,1)S(1)}, bf16[528,128]{1,0:T(8,128)(2,1)S(1)}, u32[]{:S(2)}, u32[]{:S(2)}) collective-permute-start(bf16[528,128]{1,0:T(8,128)(2,1)S(1)} %get-tuple-element.50), channel_id=1, source_target_pairs={{0,1},{1,0},{2,3},{3,2},{4,5},{5,4},{6,7},{7,6},{8,9},{9,8},{10,11... | collective-permute-start | bytes 405512 | tf_op jit(solution)/shard_map/ppermute | solution.py:288
  34.9 10.9 %collective-permute-start.10 = (bf16[528,128]{1,0:T(8,128)(2,1)S(1)}, bf16[528,128]{1,0:T(8,128)(2,1)S(1)}, u32[]{:S(2)}, u32[]{:S(2)}) collective-permute-start(bf16[528,128]{1,0:T(8,128)(2,1)S(1)} %get-tuple-element.50), channel_id=1, source_target_pairs={{0,2},{1,3},{2,0},{3,1},{4,6},{5,7},{6,4},{7,5},{8,10},{9,11},{10,... | collective-permute-start | bytes 405512 | tf_op jit(solution)/shard_map/ppermute | solution.py:288
  37.1 4.3 %collective-permute-start.13 = (bf16[128,256]{1,0:T(8,128)(2,1)S(1)}, bf16[128,256]{1,0:T(8,128)(2,1)S(1)}, u32[]{:S(2)}, u32[]{:S(2)}) collective-permute-start(bf16[128,256]{1,0:T(8,128)(2,1)S(1)} %collective-permute-done.8.refs_6_), channel_id=1, source_target_pairs={{0,16},{16,0},{1,17},{17,1},{2,18},{18,2},{3,19},{19,3},{4,20},{20... | collective-permute-start | bytes 196616 | tf_op jit(solution)/shard_map/ppermute | solution.py:316
  38.6 4.3 %collective-permute-start.14 = (bf16[128,256]{1,0:T(8,128)(2,1)S(1)}, bf16[128,256]{1,0:T(8,128)(2,1)S(1)}, u32[]{:S(2)}, u32[]{:S(2)}) collective-permute-start(bf16[128,256]{1,0:T(8,128)(2,1)S(1)} %collective-permute-done.9.refs_8_), channel_id=1, source_target_pairs={{0,16},{16,0},{1,17},{17,1},{2,18},{18,2},{3,19},{19,3},{4,20},{20... | collective-permute-start | bytes 196616 | tf_op jit(solution)/shard_map/ppermute | solution.py:316
  46.7 7.7 %collective-permute-start.17 = (bf16[528,128]{1,0:T(8,128)(2,1)S(1)}, bf16[528,128]{1,0:T(8,128)(2,1)S(1)}, u32[]{:S(2)}, u32[]{:S(2)}) collective-permute-start(bf16[528,128]{1,0:T(8,128)(2,1)S(1)} %get-tuple-element.60), channel_id=1, source_target_pairs={{0,3},{1,2},{2,1},{3,0},{4,7},{5,6},{6,5},{7,4},{8,11},{9,10},{10,... | collective-permute-start | bytes 405512 | tf_op jit(solution)/shard_map/ppermute | solution.py:288
  48.2 7.3 %collective-permute-start.16 = (bf16[528,128]{1,0:T(8,128)(2,1)S(1)}, bf16[528,128]{1,0:T(8,128)(2,1)S(1)}, u32[]{:S(2)}, u32[]{:S(2)}) collective-permute-start(bf16[528,128]{1,0:T(8,128)(2,1)S(1)} %get-tuple-element.60), channel_id=1, source_target_pairs={{0,1},{1,0},{2,3},{3,2},{4,5},{5,4},{6,7},{7,6},{8,9},{9,8},{10,11... | collective-permute-start | bytes 405512 | tf_op jit(solution)/shard_map/ppermute | solution.py:288
  48.2 10.3 %collective-permute-start.15 = (bf16[528,128]{1,0:T(8,128)(2,1)S(1)}, bf16[528,128]{1,0:T(8,128)(2,1)S(1)}, u32[]{:S(2)}, u32[]{:S(2)}) collective-permute-start(bf16[528,128]{1,0:T(8,128)(2,1)S(1)} %get-tuple-element.60), channel_id=1, source_target_pairs={{0,2},{1,3},{2,0},{3,1},{4,6},{5,7},{6,4},{7,5},{8,10},{9,11},{10,... | collective-permute-start | bytes 405512 | tf_op jit(solution)/shard_map/ppermute | solution.py:288
  59.7 1.6 %collective-permute-start.20 = (bf16[128,1024]{1,0:T(8,128)(2,1)S(1)}, bf16[128,1024]{1,0:T(8,128)(2,1)S(1)}, u32[]{:S(2)}, u32[]{:S(2)}) collective-permute-start(bf16[128,1024]{1,0:T(8,128)(2,1)S(1)} %get-tuple-element.68), channel_id=1, source_target_pairs={{0,4},{4,0},{8,12},{12,8},{1,5},{5,1},{9,13},{13,9},{2,6},{6,2},{1... | collective-permute-start | bytes 786440 | tf_op jit(solution)/shard_map/ppermute | solution.py:272
  61.3 8.4 %collective-permute-start.21 = (bf16[128,1024]{1,0:T(8,128)(2,1)S(1)}, bf16[128,1024]{1,0:T(8,128)(2,1)S(1)}, u32[]{:S(2)}, u32[]{:S(2)}) collective-permute-start(bf16[128,1024]{1,0:T(8,128)(2,1)S(1)} %add_convert_fusion.1), channel_id=1, source_target_pairs={{0,8},{4,12},{8,0},{12,4},{1,9},{5,13},{9,1},{13,5},{2,10},{6,14},... | collective-permute-start | bytes 786440 | tf_op jit(solution)/shard_map/ppermute | solution.py:272
  63.5 1.4 %collective-permute-start.18 = (bf16[64,1024]{1,0:T(8,128)(2,1)S(1)}, bf16[64,1024]{1,0:T(8,128)(2,1)S(1)}, u32[]{:S(2)}, u32[]{:S(2)}) collective-permute-start(bf16[64,1024]{1,0:T(8,128)(2,1)S(1)} %get-tuple-element.66), channel_id=1, source_target_pairs={{0,4},{4,0},{8,12},{12,8},{1,5},{5,1},{9,13},{13,9},{2,6},{6,2},{1... | collective-permute-start | bytes 393224 | tf_op jit(solution)/shard_map/ppermute | solution.py:272
  63.6 1.5 %collective-permute-start.19 = (bf16[64,1024]{1,0:T(8,128)(2,1)S(1)}, bf16[64,1024]{1,0:T(8,128)(2,1)S(1)}, u32[]{:S(2)}, u32[]{:S(2)}) collective-permute-start(bf16[64,1024]{1,0:T(8,128)(2,1)S(1)} %get-tuple-element.67), channel_id=1, source_target_pairs={{0,4},{4,0},{8,12},{12,8},{1,5},{5,1},{9,13},{13,9},{2,6},{6,2},{1... | collective-permute-start | bytes 393224 | tf_op jit(solution)/shard_map/ppermute | solution.py:272
  (2 other events, 2.0 us)

commit v12 on v11

--- a/solution.py
+++ b/solution.py
@@ -274,8 +274,10 @@
     def over_sub(x, k):
         return lax.ppermute(x, "sub", [(i, i ^ k) for i in range(n_sub)])
 
-    def to_all(own, send):
-        order = [*range(n_sub - 2, -1, -1), n_sub - 1]
+    far_first = [*range(n_sub - 2, -1, -1), n_sub - 1]
+    far_last = [n_sub - 1, *range(n_sub - 1)]
+
+    def to_all(own, send, order):
         parts = [own]
         for j in range(r):
             for k in order:
@@ -339,7 +341,7 @@
     )
     total, _ = lax.optimization_barrier((total, query_rows))
     own, send = call(functools.partial(summary_kernel, hp), summary_out, [key_feat, val, total], 0)
-    summary = to_all(own, send)
+    summary = to_all(own, send, far_first)
     query_rows, _ = lax.optimization_barrier((query_rows, val))
     qs = [near, nearest] + swapped(query_rows)
     wq_full, query_feat, query_sig = call(
@@ -354,7 +356,7 @@
         [*summary, *xs, query_feat],
         8 * flop,
     )
-    summary_grad = to_all(own, send)
+    summary_grad = to_all(own, send, far_last)
     (query_grad,) = call(
         functools.partial(query_grad_kernel, hp),
         [((t, cols), BF16)],

time: 70.7 us -> 69.5 us (0.983)
  waiting for transfers between devices: 34 us -> 32.8 us
    ppermute x6, waiting for transfers between devices: 8.32 us -> 7.08 us  [to_all(): parts.append(lax.ppermute(send, ('seq', 'sub'), perm))]
  transfers between devices with their start and end apart: 22 -> 22, of which waited for: 15 -> 13; matrix products, arithmetic and copies ran while one was open for 0% -> 0% of each run, Pallas kernels for 8% -> 9%
where the time goes in v12:
time: 69.5 us; the launch traced here: 69.3 us
  waiting for transfers between devices  32.8 us (47%)
  starting transfers between devices  24.2 us (35%)
  Pallas kernels  10.6 us (15%)
  other arithmetic  0.86 us (1%)
    ppermute x5, waiting for transfers between devices, over_sub(): return lax.ppermute(x, 'sub', [(i, i ^ k) for i in range(n_sub)])  11.4 us
    pallas_call x10, Pallas kernels, call(): pl.pallas_call(body, out_shape=[jax.ShapeDtypeStruct(s, d) for s, d in ou...  10.6 us
    ppermute x6, starting transfers between devices, to_all(): parts.append(lax.ppermute(send, ('seq', 'sub'), perm))  8.9 us
    ppermute x4, waiting for transfers between devices, swapped(): lax.ppermute(part, 'grp', [(0, 1), (1, 0)])  7.78 us
    ppermute x6, waiting for transfers between devices, to_all(): parts.append(lax.ppermute(send, ('seq', 'sub'), perm))  7.08 us
    ppermute x5, starting transfers between devices, over_sub(): return lax.ppermute(x, 'sub', [(i, i ^ k) for i in range(n_sub)])  7.02 us
    ppermute x7, waiting for transfers between devices, over_seq(): return lax.ppermute(x, 'seq', [(i, i ^ k) for i in range(n_seq)])  6.53 us
    ppermute x7, starting transfers between devices, over_seq(): return lax.ppermute(x, 'seq', [(i, i ^ k) for i in range(n_seq)])  4.25 us
  transfers between devices with their start and end apart: 22, of which 13 were waited for; matrix products, arithmetic and copies ran while one was open for 0% of the time, Pallas kernels for 9%

profile of v12, /device:TPU:0, one launch (start us, length us, event | category | flops | bytes accessed | tf_op | source)
XLA Modules:
  0.0 69.3 jit_solution(3535328232078345587)
XLA Ops:
  0.0 1.2 %shard_map.73 = (bf16[256,768]{1,0:T(8,128)(2,1)S(1)}, bf16[128,512]{1,0:T(8,128)(2,1)S(1)}, bf16[128,256]{1,0:T(8,128)(2,1)S(1)}) custom-call(bf16[256,1024]{1,0:T(8,128)(2,1)} %refs_0_.1, bf16[256,1024]{1,0:T(8,128)(2,1)} %refs_1_.1, bf16[256,1024]{1,0:T(8,128)(2,1)} %refs_2_.1), custom_call_target="tpu_custom_call" | custom-call | tf_op jit(solution)/shard_map/pallas_call | solution.py:30
  3.1 3.0 %collective-permute-start.1 = (bf16[128,1536]{1,0:T(8,128)(2,1)S(1)}, bf16[128,1536]{1,0:T(8,128)(2,1)S(1)}, u32[]{:S(2)}, u32[]{:S(2)}) collective-permute-start(bf16[128,1536]{1,0:T(8,128)(2,1)S(1)} %get-tuple-element.40), channel_id=1, source_target_pairs={{0,8},{4,12},{8,0},{12,4},{1,9},{5,13},{9,1},{13,5},{2,10},{6,14},... | collective-permute-start | bytes 1179656 | tf_op jit(solution)/shard_map/ppermute | solution.py:272
  6.1 3.6 %collective-permute-start.3 = (bf16[128,512]{1,0:T(8,128)(2,1)S(1)}, bf16[128,512]{1,0:T(8,128)(2,1)S(1)}, u32[]{:S(2)}, u32[]{:S(2)}) collective-permute-start(bf16[128,512]{1,0:T(8,128)(2,1)S(1)} %get-tuple-element.41), channel_id=1, source_target_pairs={{0,3},{1,2},{2,1},{3,0},{4,7},{5,6},{6,5},{7,4},{8,11},{9,10},{10,... | collective-permute-start | bytes 393224 | tf_op jit(solution)/shard_map/ppermute | solution.py:275
  10.5 3.9 %collective-permute-done.3.refs_8_ = bf16[128,512]{1,0:T(8,128)(2,1)S(1)} collective-permute-done((bf16[128,512]{1,0:T(8,128)(2,1)S(1)}, bf16[128,512]{1,0:T(8,128)(2,1)S(1)}, u32[]{:S(2)}, u32[]{:S(2)}) %collective-permute-start.3) | collective-permute-done | bytes 131104 | tf_op jit(solution)/shard_map/ppermute | solution.py:275
  14.3 6.2 %collective-permute-done.2.refs_6_ = bf16[128,512]{1,0:T(8,128)(2,1)S(1)} collective-permute-done((bf16[128,512]{1,0:T(8,128)(2,1)S(1)}, bf16[128,512]{1,0:T(8,128)(2,1)S(1)}, u32[]{:S(2)}, u32[]{:S(2)}) %collective-permute-start.2) | collective-permute-done | bytes 131104 | tf_op jit(solution)/shard_map/ppermute | solution.py:275
  20.6 1.5 %collective-permute-start.7 = (bf16[128,512]{1,0:T(8,128)(2,1)S(1)}, bf16[128,512]{1,0:T(8,128)(2,1)S(1)}, u32[]{:S(2)}, u32[]{:S(2)}) collective-permute-start(bf16[128,512]{1,0:T(8,128)(2,1)S(1)} %collective-permute-done.3.refs_8_), channel_id=1, source_target_pairs={{0,16},{16,0},{1,17},{17,1},{2,18},{18,2},{3,19},{19,3},{4,20},{20... | collective-permute-start | bytes 393224 | tf_op jit(solution)/shard_map/ppermute | solution.py:318
  22.6 2.5 %collective-permute-start.9 = (bf16[128,256]{1,0:T(8,128)(2,1)S(1)}, bf16[128,256]{1,0:T(8,128)(2,1)S(1)}, u32[]{:S(2)}, u32[]{:S(2)}) collective-permute-start(bf16[128,256]{1,0:T(8,128)(2,1)S(1)} %get-tuple-element.47), channel_id=1, source_target_pairs={{0,3},{1,2},{2,1},{3,0},{4,7},{5,6},{6,5},{7,4},{8,11},{9,10},{10,... | collective-permute-start | bytes 196616 | tf_op jit(solution)/shard_map/ppermute | solution.py:275
  25.1 1.7 %collective-permute-done.7.refs_9_ = bf16[128,512]{1,0:T(8,128)(2,1)S(1)} collective-permute-done((bf16[128,512]{1,0:T(8,128)(2,1)S(1)}, bf16[128,512]{1,0:T(8,128)(2,1)S(1)}, u32[]{:S(2)}, u32[]{:S(2)}) %collective-permute-start.7) | collective-permute-done | bytes 131104 | tf_op jit(solution)/shard_map/ppermute | solution.py:318
  27.0 2.3 %collective-permute-done.6.refs_7_ = bf16[128,512]{1,0:T(8,128)(2,1)S(1)} collective-permute-done((bf16[128,512]{1,0:T(8,128)(2,1)S(1)}, bf16[128,512]{1,0:T(8,128)(2,1)S(1)}, u32[]{:S(2)}, u32[]{:S(2)}) %collective-permute-start.6) | collective-permute-done | bytes 131104 | tf_op jit(solution)/shard_map/ppermute | solution.py:318
  29.3 1.7 %shard_map.75 = (bf16[1024,512]{1,0:T(8,128)(2,1)S(1)}, bf16[512,512]{1,0:T(8,128)(2,1)S(1)}, f32[512,512]{1,0:T(8,128)S(1)}, bf16[512,256]{1,0:T(8,128)(2,1)S(1)}, f32[1,512]{1,0:T(1,128)S(1)}) custom-call(bf16[128,1536]{1,0:T(8,128)(2,1)S(1)} %get-tuple-element.39.refs_0_.refs_4_, bf16[128,1536]{1,0:T(8,128)(2,1)S(1)} %collective-permute-done.refs_1_.refs_5_, ...), custom_call_target="tpu_custom_call" | custom-call | flops 2147483648 | bytes 3014656 | tf_op jit(solution)/shard_map/pallas_call | solution.py:30
  31.0 1.3 %collective-permute-done.8.refs_6_ = bf16[128,256]{1,0:T(8,128)(2,1)S(1)} collective-permute-done((bf16[128,256]{1,0:T(8,128)(2,1)S(1)}, bf16[128,256]{1,0:T(8,128)(2,1)S(1)}, u32[]{:S(2)}, u32[]{:S(2)}) %collective-permute-start.8) | collective-permute-done | bytes 65568 | tf_op jit(solution)/shard_map/ppermute | solution.py:275
  32.7 2.2 %collective-permute-start.12 = (bf16[528,128]{1,0:T(8,128)(2,1)S(1)}, bf16[528,128]{1,0:T(8,128)(2,1)S(1)}, u32[]{:S(2)}, u32[]{:S(2)}) collective-permute-start(bf16[528,128]{1,0:T(8,128)(2,1)S(1)} %get-tuple-element.50), channel_id=1, source_target_pairs={{0,3},{1,2},{2,1},{3,0},{4,7},{5,6},{6,5},{7,4},{8,11},{9,10},{10,... | collective-permute-start | bytes 405512 | tf_op jit(solution)/shard_map/ppermute | solution.py:290
  34.9 2.2 %collective-permute-start.10 = (bf16[528,128]{1,0:T(8,128)(2,1)S(1)}, bf16[528,128]{1,0:T(8,128)(2,1)S(1)}, u32[]{:S(2)}, u32[]{:S(2)}) collective-permute-start(bf16[528,128]{1,0:T(8,128)(2,1)S(1)} %get-tuple-element.50), channel_id=1, source_target_pairs={{0,2},{1,3},{2,0},{3,1},{4,6},{5,7},{6,4},{7,5},{8,10},{9,11},{10,... | collective-permute-start | bytes 405512 | tf_op jit(solution)/shard_map/ppermute | solution.py:290
  37.1 1.5 %collective-permute-start.13 = (bf16[128,256]{1,0:T(8,128)(2,1)S(1)}, bf16[128,256]{1,0:T(8,128)(2,1)S(1)}, u32[]{:S(2)}, u32[]{:S(2)}) collective-permute-start(bf16[128,256]{1,0:T(8,128)(2,1)S(1)} %collective-permute-done.8.refs_6_), channel_id=1, source_target_pairs={{0,16},{16,0},{1,17},{17,1},{2,18},{18,2},{3,19},{19,3},{4,20},{20... | collective-permute-start | bytes 196616 | tf_op jit(solution)/shard_map/ppermute | solution.py:318
  39.1 2.2 %collective-permute-done.13.refs_7_ = bf16[128,256]{1,0:T(8,128)(2,1)S(1)} collective-permute-done((bf16[128,256]{1,0:T(8,128)(2,1)S(1)}, bf16[128,256]{1,0:T(8,128)(2,1)S(1)}, u32[]{:S(2)}, u32[]{:S(2)}) %collective-permute-start.13) | collective-permute-done | bytes 65568 | tf_op jit(solution)/shard_map/ppermute | solution.py:318
  41.4 1.5 %collective-permute-done.14.refs_9_ = bf16[128,256]{1,0:T(8,128)(2,1)S(1)} collective-permute-done((bf16[128,256]{1,0:T(8,128)(2,1)S(1)}, bf16[128,256]{1,0:T(8,128)(2,1)S(1)}, u32[]{:S(2)}, u32[]{:S(2)}) %collective-permute-start.14) | collective-permute-done | bytes 65568 | tf_op jit(solution)/shard_map/ppermute | solution.py:318
  42.9 1.4 %shard_map.77 = (bf16[1024,256]{1,0:T(8,128)(2,1)S(1)}, bf16[512,512]{1,0:T(8,128)(2,1)S(1)}, f32[512,512]{1,0:T(8,128)S(1)}) custom-call(bf16[128,1536]{1,0:T(8,128)(2,1)S(1)} %get-tuple-element.39.refs_0_.refs_4_, bf16[128,1536]{1,0:T(8,128)(2,1)S(1)} %collective-permute-done.refs_1_.refs_5_, bf16[128,1536]{1,0:T(8,128)(2,1)S(1)} %collective-permute-done.1.refs_2_.refs_6_, ...), custom_call_target="tpu_custom_call" | custom-call | tf_op jit(solution)/shard_map/pallas_call | solution.py:30
  44.3 1.4 %collective-permute-done.10.refs_1_ = bf16[528,128]{1,0:T(8,128)(2,1)S(1)} collective-permute-done((bf16[528,128]{1,0:T(8,128)(2,1)S(1)}, bf16[528,128]{1,0:T(8,128)(2,1)S(1)}, u32[]{:S(2)}, u32[]{:S(2)}) %collective-permute-start.10) | collective-permute-done | bytes 135200 | tf_op jit(solution)/shard_map/ppermute | solution.py:290
  47.1 1.7 %collective-permute-start.16 = (bf16[528,128]{1,0:T(8,128)(2,1)S(1)}, bf16[528,128]{1,0:T(8,128)(2,1)S(1)}, u32[]{:S(2)}, u32[]{:S(2)}) collective-permute-start(bf16[528,128]{1,0:T(8,128)(2,1)S(1)} %get-tuple-element.60), channel_id=1, source_target_pairs={{0,1},{1,0},{2,3},{3,2},{4,5},{5,4},{6,7},{7,6},{8,9},{9,8},{10,11... | collective-permute-start | bytes 405512 | tf_op jit(solution)/shard_map/ppermute | solution.py:290
  48.8 2.2 %collective-permute-start.15 = (bf16[528,128]{1,0:T(8,128)(2,1)S(1)}, bf16[528,128]{1,0:T(8,128)(2,1)S(1)}, u32[]{:S(2)}, u32[]{:S(2)}) collective-permute-start(bf16[528,128]{1,0:T(8,128)(2,1)S(1)} %get-tuple-element.60), channel_id=1, source_target_pairs={{0,3},{1,2},{2,1},{3,0},{4,7},{5,6},{6,5},{7,4},{8,11},{9,10},{10,... | collective-permute-start | bytes 405512 | tf_op jit(solution)/shard_map/ppermute | solution.py:290
  51.6 5.7 %collective-permute-done.17.refs_3_ = bf16[528,128]{1,0:T(8,128)(2,1)S(1)} collective-permute-done((bf16[528,128]{1,0:T(8,128)(2,1)S(1)}, bf16[528,128]{1,0:T(8,128)(2,1)S(1)}, u32[]{:S(2)}, u32[]{:S(2)}) %collective-permute-start.17) | collective-permute-done | bytes 135200 | tf_op jit(solution)/shard_map/ppermute | solution.py:290
  57.3 1.2 %shard_map.80 = (bf16[128,1024]{1,0:T(8,128)(2,1)S(1)}, bf16[512,512]{1,0:T(8,128)(2,1)S(1)}) custom-call(f32[528,128]{1,0:T(8,128)S(1)} %get-tuple-element.59.refs_0_, bf16[528,128]{1,0:T(8,128)(2,1)S(1)} %collective-permute-done.15.refs_1_, bf16[528,128]{1,0:T(8,128)(2,1)S(1)} %collective-permute-done.16.refs_2_, ...), custom_call_target="tpu_custom_call" | custom-call | flops 2147483648 | bytes 4476928 | tf_op jit(solution)/shard_map/pallas_call | solution.py:30
  60.7 1.6 %shard_map.81 = (bf16[64,1024]{1,0:T(8,128)(2,1)S(1)}, bf16[64,1024]{1,0:T(8,128)(2,1)S(1)}, f32[128,1024]{1,0:T(8,128)S(1)}) custom-call(bf16[512,256]{1,0:T(8,128)(2,1)S(1)} %shard_map.79.refs_8_.qg, bf16[512,512]{1,0:T(8,128)(2,1)S(1)} %get-tuple-element.64.kvg, bf16[1024,256]{1,0:T(8,128)(2,1)S(1)} %get-tuple-element.62.refs_9_.wq, ...), custom_call_target="tpu_custom_call" | custom-call | tf_op jit(solution)/shard_map/pallas_call | solution.py:30
  63.9 4.6 %collective-permute-done.21 = bf16[128,1024]{1,0:T(8,128)(2,1)S(1)} collective-permute-done((bf16[128,1024]{1,0:T(8,128)(2,1)S(1)}, bf16[128,1024]{1,0:T(8,128)(2,1)S(1)}, u32[]{:S(2)}, u32[]{:S(2)}) %collective-permute-start.21) | collective-permute-done | bytes 262176 | tf_op jit(solution)/shard_map/ppermute | solution.py:272
  (42 shorter events, 10.6 us)
Async XLA Ops:
  0.0 22.6 %copy-start = (bf16[8,128,256]{2,1,0:T(8,128)(2,1)S(1)}, bf16[8,128,256]{2,1,0:T(8,128)(2,1)}, u32[]{:S(2)}) copy-start(bf16[8,128,256]{2,1,0:T(8,128)(2,1)} %param.13) | copy-start | bytes 1572868
  0.0 1.4 %copy-start.2 = (bf16[128,1024]{1,0:T(8,128)(2,1)S(1)}, bf16[128,1024]{1,0:T(8,128)(2,1)}, u32[]{:S(2)}) copy-start(bf16[128,1024]{1,0:T(8,128)(2,1)} %cot.1) | copy-start | bytes 786436
  3.1 17.5 %collective-permute-start.1 = (bf16[128,1536]{1,0:T(8,128)(2,1)S(1)}, bf16[128,1536]{1,0:T(8,128)(2,1)S(1)}, u32[]{:S(2)}, u32[]{:S(2)}) collective-permute-start(bf16[128,1536]{1,0:T(8,128)(2,1)S(1)} %get-tuple-element.40), channel_id=1, source_target_pairs={{0,8},{4,12},{8,0},{12,4},{1,9},{5,13},{9,1},{13,5},{2,10},{6,14},... | collective-permute-start | bytes 1179656 | tf_op jit(solution)/shard_map/ppermute | solution.py:272
  6.1 8.3 %collective-permute-start.3 = (bf16[128,512]{1,0:T(8,128)(2,1)S(1)}, bf16[128,512]{1,0:T(8,128)(2,1)S(1)}, u32[]{:S(2)}, u32[]{:S(2)}) collective-permute-start(bf16[128,512]{1,0:T(8,128)(2,1)S(1)} %get-tuple-element.41), channel_id=1, source_target_pairs={{0,3},{1,2},{2,1},{3,0},{4,7},{5,6},{6,5},{7,4},{8,11},{9,10},{10,... | collective-permute-start | bytes 393224 | tf_op jit(solution)/shard_map/ppermute | solution.py:275
  9.7 10.9 %collective-permute-start.2 = (bf16[128,512]{1,0:T(8,128)(2,1)S(1)}, bf16[128,512]{1,0:T(8,128)(2,1)S(1)}, u32[]{:S(2)}, u32[]{:S(2)}) collective-permute-start(bf16[128,512]{1,0:T(8,128)(2,1)S(1)} %get-tuple-element.41), channel_id=1, source_target_pairs={{0,2},{1,3},{2,0},{3,1},{4,6},{5,7},{6,4},{7,5},{8,10},{9,11},{10,... | collective-permute-start | bytes 393224 | tf_op jit(solution)/shard_map/ppermute | solution.py:275
  9.7 13.0 %collective-permute-start = (bf16[128,1536]{1,0:T(8,128)(2,1)S(1)}, bf16[128,1536]{1,0:T(8,128)(2,1)S(1)}, u32[]{:S(2)}, u32[]{:S(2)}) collective-permute-start(bf16[128,1536]{1,0:T(8,128)(2,1)S(1)} %get-tuple-element.39.refs_0_.refs_4_), channel_id=1, source_target_pairs={{0,4},{4,0},{8,12},{12,8},{1,5},{5,1},{9,13},{13,9},{2,6},{6,2},{1... | collective-permute-start | bytes 1179656 | tf_op jit(solution)/shard_map/ppermute | solution.py:272
  9.7 19.6 %collective-permute-start.5 = (bf16[256,768]{1,0:T(8,128)(2,1)S(1)}, bf16[256,768]{1,0:T(8,128)(2,1)S(1)}, u32[]{:S(2)}, u32[]{:S(2)}) collective-permute-start(bf16[256,768]{1,0:T(8,128)(2,1)S(1)} %get-tuple-element.37.refs_4_), channel_id=1, source_target_pairs={{0,1},{1,0},{2,3},{3,2},{4,5},{5,4},{6,7},{7,6},{8,9},{9,8},{10,11... | collective-permute-start | bytes 1179656 | tf_op jit(solution)/shard_map/ppermute | solution.py:275
  20.6 8.7 %collective-permute-start.4 = (bf16[128,1536]{1,0:T(8,128)(2,1)S(1)}, bf16[128,1536]{1,0:T(8,128)(2,1)S(1)}, u32[]{:S(2)}, u32[]{:S(2)}) collective-permute-start(bf16[128,1536]{1,0:T(8,128)(2,1)S(1)} %collective-permute-done.1.refs_2_.refs_6_), channel_id=1, source_target_pairs={{0,4},{4,0},{8,12},{12,8},{1,5},{5,1},{9,13},{13,9},{2,6},{6,2},{1... | collective-permute-start | bytes 1179656 | tf_op jit(solution)/shard_map/ppermute | solution.py:272
  20.6 6.3 %collective-permute-start.7 = (bf16[128,512]{1,0:T(8,128)(2,1)S(1)}, bf16[128,512]{1,0:T(8,128)(2,1)S(1)}, u32[]{:S(2)}, u32[]{:S(2)}) collective-permute-start(bf16[128,512]{1,0:T(8,128)(2,1)S(1)} %collective-permute-done.3.refs_8_), channel_id=1, source_target_pairs={{0,16},{16,0},{1,17},{17,1},{2,18},{18,2},{3,19},{19,3},{4,20},{20... | collective-permute-start | bytes 393224 | tf_op jit(solution)/shard_map/ppermute | solution.py:318
  22.1 7.2 %collective-permute-start.6 = (bf16[128,512]{1,0:T(8,128)(2,1)S(1)}, bf16[128,512]{1,0:T(8,128)(2,1)S(1)}, u32[]{:S(2)}, u32[]{:S(2)}) collective-permute-start(bf16[128,512]{1,0:T(8,128)(2,1)S(1)} %collective-permute-done.2.refs_6_), channel_id=1, source_target_pairs={{0,16},{16,0},{1,17},{17,1},{2,18},{18,2},{3,19},{19,3},{4,20},{20... | collective-permute-start | bytes 393224 | tf_op jit(solution)/shard_map/ppermute | solution.py:318
  22.6 8.4 %collective-permute-start.9 = (bf16[128,256]{1,0:T(8,128)(2,1)S(1)}, bf16[128,256]{1,0:T(8,128)(2,1)S(1)}, u32[]{:S(2)}, u32[]{:S(2)}) collective-permute-start(bf16[128,256]{1,0:T(8,128)(2,1)S(1)} %get-tuple-element.47), channel_id=1, source_target_pairs={{0,3},{1,2},{2,1},{3,0},{4,7},{5,6},{6,5},{7,4},{8,11},{9,10},{10,... | collective-permute-start | bytes 196616 | tf_op jit(solution)/shard_map/ppermute | solution.py:275
  26.9 5.4 %collective-permute-start.8 = (bf16[128,256]{1,0:T(8,128)(2,1)S(1)}, bf16[128,256]{1,0:T(8,128)(2,1)S(1)}, u32[]{:S(2)}, u32[]{:S(2)}) collective-permute-start(bf16[128,256]{1,0:T(8,128)(2,1)S(1)} %get-tuple-element.47), channel_id=1, source_target_pairs={{0,2},{1,3},{2,0},{3,1},{4,6},{5,7},{6,4},{7,5},{8,10},{9,11},{10,... | collective-permute-start | bytes 196616 | tf_op jit(solution)/shard_map/ppermute | solution.py:275
  32.7 11.7 %collective-permute-start.12 = (bf16[528,128]{1,0:T(8,128)(2,1)S(1)}, bf16[528,128]{1,0:T(8,128)(2,1)S(1)}, u32[]{:S(2)}, u32[]{:S(2)}) collective-permute-start(bf16[528,128]{1,0:T(8,128)(2,1)S(1)} %get-tuple-element.50), channel_id=1, source_target_pairs={{0,3},{1,2},{2,1},{3,0},{4,7},{5,6},{6,5},{7,4},{8,11},{9,10},{10,... | collective-permute-start | bytes 405512 | tf_op jit(solution)/shard_map/ppermute | solution.py:290
  34.9 9.4 %collective-permute-start.11 = (bf16[528,128]{1,0:T(8,128)(2,1)S(1)}, bf16[528,128]{1,0:T(8,128)(2,1)S(1)}, u32[]{:S(2)}, u32[]{:S(2)}) collective-permute-start(bf16[528,128]{1,0:T(8,128)(2,1)S(1)} %get-tuple-element.50), channel_id=1, source_target_pairs={{0,1},{1,0},{2,3},{3,2},{4,5},{5,4},{6,7},{7,6},{8,9},{9,8},{10,11... | collective-permute-start | bytes 405512 | tf_op jit(solution)/shard_map/ppermute | solution.py:290
  34.9 10.8 %collective-permute-start.10 = (bf16[528,128]{1,0:T(8,128)(2,1)S(1)}, bf16[528,128]{1,0:T(8,128)(2,1)S(1)}, u32[]{:S(2)}, u32[]{:S(2)}) collective-permute-start(bf16[528,128]{1,0:T(8,128)(2,1)S(1)} %get-tuple-element.50), channel_id=1, source_target_pairs={{0,2},{1,3},{2,0},{3,1},{4,6},{5,7},{6,4},{7,5},{8,10},{9,11},{10,... | collective-permute-start | bytes 405512 | tf_op jit(solution)/shard_map/ppermute | solution.py:290
  37.1 4.3 %collective-permute-start.13 = (bf16[128,256]{1,0:T(8,128)(2,1)S(1)}, bf16[128,256]{1,0:T(8,128)(2,1)S(1)}, u32[]{:S(2)}, u32[]{:S(2)}) collective-permute-start(bf16[128,256]{1,0:T(8,128)(2,1)S(1)} %collective-permute-done.8.refs_6_), channel_id=1, source_target_pairs={{0,16},{16,0},{1,17},{17,1},{2,18},{18,2},{3,19},{19,3},{4,20},{20... | collective-permute-start | bytes 196616 | tf_op jit(solution)/shard_map/ppermute | solution.py:318
  38.6 4.3 %collective-permute-start.14 = (bf16[128,256]{1,0:T(8,128)(2,1)S(1)}, bf16[128,256]{1,0:T(8,128)(2,1)S(1)}, u32[]{:S(2)}, u32[]{:S(2)}) collective-permute-start(bf16[128,256]{1,0:T(8,128)(2,1)S(1)} %collective-permute-done.9.refs_8_), channel_id=1, source_target_pairs={{0,16},{16,0},{1,17},{17,1},{2,18},{18,2},{3,19},{19,3},{4,20},{20... | collective-permute-start | bytes 196616 | tf_op jit(solution)/shard_map/ppermute | solution.py:318
  46.6 10.7 %collective-permute-start.17 = (bf16[528,128]{1,0:T(8,128)(2,1)S(1)}, bf16[528,128]{1,0:T(8,128)(2,1)S(1)}, u32[]{:S(2)}, u32[]{:S(2)}) collective-permute-start(bf16[528,128]{1,0:T(8,128)(2,1)S(1)} %get-tuple-element.60), channel_id=1, source_target_pairs={{0,2},{1,3},{2,0},{3,1},{4,6},{5,7},{6,4},{7,5},{8,10},{9,11},{10,... | collective-permute-start | bytes 405512 | tf_op jit(solution)/shard_map/ppermute | solution.py:290
  47.1 10.2 %collective-permute-start.16 = (bf16[528,128]{1,0:T(8,128)(2,1)S(1)}, bf16[528,128]{1,0:T(8,128)(2,1)S(1)}, u32[]{:S(2)}, u32[]{:S(2)}) collective-permute-start(bf16[528,128]{1,0:T(8,128)(2,1)S(1)} %get-tuple-element.60), channel_id=1, source_target_pairs={{0,1},{1,0},{2,3},{3,2},{4,5},{5,4},{6,7},{7,6},{8,9},{9,8},{10,11... | collective-permute-start | bytes 405512 | tf_op jit(solution)/shard_map/ppermute | solution.py:290
  48.8 8.5 %collective-permute-start.15 = (bf16[528,128]{1,0:T(8,128)(2,1)S(1)}, bf16[528,128]{1,0:T(8,128)(2,1)S(1)}, u32[]{:S(2)}, u32[]{:S(2)}) collective-permute-start(bf16[528,128]{1,0:T(8,128)(2,1)S(1)} %get-tuple-element.60), channel_id=1, source_target_pairs={{0,3},{1,2},{2,1},{3,0},{4,7},{5,6},{6,5},{7,4},{8,11},{9,10},{10,... | collective-permute-start | bytes 405512 | tf_op jit(solution)/shard_map/ppermute | solution.py:290
  58.4 1.6 %collective-permute-start.20 = (bf16[128,1024]{1,0:T(8,128)(2,1)S(1)}, bf16[128,1024]{1,0:T(8,128)(2,1)S(1)}, u32[]{:S(2)}, u32[]{:S(2)}) collective-permute-start(bf16[128,1024]{1,0:T(8,128)(2,1)S(1)} %get-tuple-element.68), channel_id=1, source_target_pairs={{0,4},{4,0},{8,12},{12,8},{1,5},{5,1},{9,13},{13,9},{2,6},{6,2},{1... | collective-permute-start | bytes 786440 | tf_op jit(solution)/shard_map/ppermute | solution.py:272
  60.1 8.4 %collective-permute-start.21 = (bf16[128,1024]{1,0:T(8,128)(2,1)S(1)}, bf16[128,1024]{1,0:T(8,128)(2,1)S(1)}, u32[]{:S(2)}, u32[]{:S(2)}) collective-permute-start(bf16[128,1024]{1,0:T(8,128)(2,1)S(1)} %add_convert_fusion.1), channel_id=1, source_target_pairs={{0,8},{4,12},{8,0},{12,4},{1,9},{5,13},{9,1},{13,5},{2,10},{6,14},... | collective-permute-start | bytes 786440 | tf_op jit(solution)/shard_map/ppermute | solution.py:272
  62.3 1.4 %collective-permute-start.18 = (bf16[64,1024]{1,0:T(8,128)(2,1)S(1)}, bf16[64,1024]{1,0:T(8,128)(2,1)S(1)}, u32[]{:S(2)}, u32[]{:S(2)}) collective-permute-start(bf16[64,1024]{1,0:T(8,128)(2,1)S(1)} %get-tuple-element.66), channel_id=1, source_target_pairs={{0,4},{4,0},{8,12},{12,8},{1,5},{5,1},{9,13},{13,9},{2,6},{6,2},{1... | collective-permute-start | bytes 393224 | tf_op jit(solution)/shard_map/ppermute | solution.py:272
  62.4 1.5 %collective-permute-start.19 = (bf16[64,1024]{1,0:T(8,128)(2,1)S(1)}, bf16[64,1024]{1,0:T(8,128)(2,1)S(1)}, u32[]{:S(2)}, u32[]{:S(2)}) collective-permute-start(bf16[64,1024]{1,0:T(8,128)(2,1)S(1)} %get-tuple-element.67), channel_id=1, source_target_pairs={{0,4},{4,0},{8,12},{12,8},{1,5},{5,1},{9,13},{13,9},{2,6},{6,2},{1... | collective-permute-start | bytes 393224 | tf_op jit(solution)/shard_map/ppermute | solution.py:272
  (2 other events, 2.0 us)

commit v13 on v12

--- a/solution.py
+++ b/solution.py
@@ -206,13 +206,14 @@
     put_total(own, send, base, extra, jnp.concatenate(sums, axis=1))
 
 
-def query_grad_kernel(hp, scaled_half, summary_half, norm, total_half, sig, om, out):
+def query_grad_kernel(g, hp, scaled_half, summary_half, norm, total_half, sig, om, wq, out, part):
     hd, m = om.shape[1], om.shape[2]
     for h in range(hp):
         fg = dot(scaled_half[:, h * hd : (h + 1) * hd], summary_half[h * m : (h + 1) * m, :], 1, 1)
         fg = fg + norm[:, h : h + 1] * total_half[:, h * m : (h + 1) * m].astype(F32)
         pg = (fg * sig[:, h * m : (h + 1) * m]).astype(BF16)
         out[:, h * hd : (h + 1) * hd] = dot(pg, om[h], 1, 1).astype(BF16)
+    part[...] = dot(out[out.shape[0] // g * 2 :, :], wq[...], 1, 1)
 
 
 def products(g, blocks, qg, kvg, wq, wkv, out):
@@ -223,10 +224,17 @@
         out[j * rows : (j + 1) * rows, :] = o.astype(out.dtype)
 
 
+def far_products(g, blocks, part, kvg, wkv, out):
+    rows = kvg.shape[0] // g
+    for j, i in enumerate(blocks):
+        o = part[(i - 2) * rows : (i - 1) * rows, :] + dot(kvg[i * rows : (i + 1) * rows, :], wkv[...], 1, 1)
+        out[j * rows : (j + 1) * rows, :] = o.astype(out.dtype)
+
+
 def key_side_kernel(g, p, hp, *refs):
     parts = refs[:p]
-    val, feat, sig, om, qg, wq, wkv = refs[p : p + 7]
-    odd, kvg = refs[p + 7 :]
+    val, feat, sig, om, part, wkv = refs[p : p + 6]
+    odd, kvg = refs[p + 6 :]
     hd, m = om.shape[1], om.shape[2]
     base = hp * m
     cols = hp * hd
@@ -238,11 +246,11 @@
         kvg[:, cols + h * hd : cols + (h + 1) * hd] = dot(feat[:, h * m : (h + 1) * m], gh).astype(BF16)
         pg = (fg * sig[:, h * m : (h + 1) * m]).astype(BF16)
         kvg[:, col] = dot(pg, om[h], 1, 1).astype(BF16)
-    products(g, range(3, g, 2), qg, kvg, wq, wkv, odd)
-
-
-def even_kernel(g, qg, kvg, wq, wkv, even):
-    products(g, range(2, g, 2), qg, kvg, wq, wkv, even)
+    far_products(g, range(3, g, 2), part, kvg, wkv, odd)
+
+
+def even_kernel(g, part, kvg, wkv, even):
+    far_products(g, range(2, g, 2), part, kvg, wkv, even)
 
 
 def near_kernel(g, qg, kvg, wq, wkv, top, bottom, zero):
@@ -357,22 +365,27 @@
         8 * flop,
     )
     summary_grad = to_all(own, send, far_last)
-    (query_grad,) = call(
-        functools.partial(query_grad_kernel, hp),
-        [((t, cols), BF16)],
-        [scaled_half, summary_half, norm, total_half, query_sig, om],
+    query_grad, query_part = call(
+        functools.partial(query_grad_kernel, g, hp),
+        [((t, cols), BF16), ((t - 2 * rows, width), F32)],
+        [scaled_half, summary_half, norm, total_half, query_sig, om, wq_full],
         4 * flop,
     )
     others = g // 2 - 1
     odd, key_value_grad = call(
         functools.partial(key_side_kernel, g, p, hp),
         [((others * rows, width), BF16), ((t, 2 * cols), BF16)],
-        [*summary_grad, val, key_feat, key_sig, om, query_grad, wq_full, wkv_full],
+        [*summary_grad, val, key_feat, key_sig, om, query_part, wkv_full],
         8 * flop,
     )
     got = over_seq(odd, 1)
     grads = [query_grad, key_value_grad, wq_full, wkv_full]
-    (even,) = call(functools.partial(even_kernel, g), [((others * rows, width), F32)], grads, 8 * flop)
+    (even,) = call(
+        functools.partial(even_kernel, g),
+        [((others * rows, width), F32)],
+        [query_part, key_value_grad, wkv_full],
+        8 * flop,
+    )
     both = (even + got.astype(F32)).astype(BF16)
     top, bottom, zero = call(
         functools.partial(near_kernel, g),

time: 69.5 us -> 69.3 us (level)
  no operation moved by 1% of the time
where the time goes in v13:
time: 69.3 us; the launch traced here: 69.2 us
  waiting for transfers between devices  32.7 us (47%)
  starting transfers between devices  24.2 us (35%)
  Pallas kernels  10.5 us (15%)
  other arithmetic  0.89 us (1%)
    ppermute x5, waiting for transfers between devices, over_sub(): return lax.ppermute(x, 'sub', [(i, i ^ k) for i in range(n_sub)])  11.4 us
    pallas_call x10, Pallas kernels, call(): pl.pallas_call(body, out_shape=[jax.ShapeDtypeStruct(s, d) for s, d in ou...  10.5 us
    ppermute x6, starting transfers between devices, to_all(): parts.append(lax.ppermute(send, ('seq', 'sub'), perm))  8.9 us
    ppermute x4, waiting for transfers between devices, swapped(): lax.ppermute(part, 'grp', [(0, 1), (1, 0)])  7.78 us
    ppermute x5, starting transfers between devices, over_sub(): return lax.ppermute(x, 'sub', [(i, i ^ k) for i in range(n_sub)])  7.02 us
    ppermute x6, waiting for transfers between devices, to_all(): parts.append(lax.ppermute(send, ('seq', 'sub'), perm))  6.86 us
    ppermute x7, waiting for transfers between devices, over_seq(): return lax.ppermute(x, 'seq', [(i, i ^ k) for i in range(n_seq)])  6.68 us
    ppermute x7, starting transfers between devices, over_seq(): return lax.ppermute(x, 'seq', [(i, i ^ k) for i in range(n_seq)])  4.25 us
  transfers between devices with their start and end apart: 22, of which 13 were waited for; matrix products, arithmetic and copies ran while one was open for 0% of the time, Pallas kernels for 9%

profile of v13, /device:TPU:0, one launch (start us, length us, event | category | flops | bytes accessed | tf_op | source)
XLA Modules:
  0.0 69.2 jit_solution(12250051587647824309)
XLA Ops:
  0.0 1.2 %shard_map.73 = (bf16[256,768]{1,0:T(8,128)(2,1)S(1)}, bf16[128,512]{1,0:T(8,128)(2,1)S(1)}, bf16[128,256]{1,0:T(8,128)(2,1)S(1)}) custom-call(bf16[256,1024]{1,0:T(8,128)(2,1)} %refs_0_.1, bf16[256,1024]{1,0:T(8,128)(2,1)} %refs_1_.1, bf16[256,1024]{1,0:T(8,128)(2,1)} %refs_2_.1), custom_call_target="tpu_custom_call" | custom-call | tf_op jit(solution)/shard_map/pallas_call | solution.py:30
  2.0 1.1 %shard_map.74 = (bf16[128,1536]{1,0:T(8,128)(2,1)S(1)}, bf16[128,1536]{1,0:T(8,128)(2,1)S(1)}) custom-call(bf16[128,1024]{1,0:T(8,128)(2,1)S(1)} %copy-done.1, s32[1,128]{1,0:T(1,128)S(1)} %bitcast.3, f32[1,512]{1,0:T(1,128)S(1)} %bitcast.2, bf16[128,1024]{1,0:T(8,128)(2,1)S(1)} %copy-done.2), custom_call_target="tpu_custom_call" | custom-call | tf_op jit(solution)/shard_map/pallas_call | solution.py:30
  3.1 3.0 %collective-permute-start.1 = (bf16[128,1536]{1,0:T(8,128)(2,1)S(1)}, bf16[128,1536]{1,0:T(8,128)(2,1)S(1)}, u32[]{:S(2)}, u32[]{:S(2)}) collective-permute-start(bf16[128,1536]{1,0:T(8,128)(2,1)S(1)} %get-tuple-element.42), channel_id=1, source_target_pairs={{0,8},{4,12},{8,0},{12,4},{1,9},{5,13},{9,1},{13,5},{2,10},{6,14},... | collective-permute-start | bytes 1179656 | tf_op jit(solution)/shard_map/ppermute | solution.py:280
  6.1 3.6 %collective-permute-start.3 = (bf16[128,512]{1,0:T(8,128)(2,1)S(1)}, bf16[128,512]{1,0:T(8,128)(2,1)S(1)}, u32[]{:S(2)}, u32[]{:S(2)}) collective-permute-start(bf16[128,512]{1,0:T(8,128)(2,1)S(1)} %get-tuple-element.43), channel_id=1, source_target_pairs={{0,3},{1,2},{2,1},{3,0},{4,7},{5,6},{6,5},{7,4},{8,11},{9,10},{10,... | collective-permute-start | bytes 393224 | tf_op jit(solution)/shard_map/ppermute | solution.py:283
  10.5 3.9 %collective-permute-done.3.refs_8_ = bf16[128,512]{1,0:T(8,128)(2,1)S(1)} collective-permute-done((bf16[128,512]{1,0:T(8,128)(2,1)S(1)}, bf16[128,512]{1,0:T(8,128)(2,1)S(1)}, u32[]{:S(2)}, u32[]{:S(2)}) %collective-permute-start.3) | collective-permute-done | bytes 131104 | tf_op jit(solution)/shard_map/ppermute | solution.py:283
  14.3 6.2 %collective-permute-done.2.refs_6_ = bf16[128,512]{1,0:T(8,128)(2,1)S(1)} collective-permute-done((bf16[128,512]{1,0:T(8,128)(2,1)S(1)}, bf16[128,512]{1,0:T(8,128)(2,1)S(1)}, u32[]{:S(2)}, u32[]{:S(2)}) %collective-permute-start.2) | collective-permute-done | bytes 131104 | tf_op jit(solution)/shard_map/ppermute | solution.py:283
  20.6 1.5 %collective-permute-start.7 = (bf16[128,512]{1,0:T(8,128)(2,1)S(1)}, bf16[128,512]{1,0:T(8,128)(2,1)S(1)}, u32[]{:S(2)}, u32[]{:S(2)}) collective-permute-start(bf16[128,512]{1,0:T(8,128)(2,1)S(1)} %collective-permute-done.3.refs_8_), channel_id=1, source_target_pairs={{0,16},{16,0},{1,17},{17,1},{2,18},{18,2},{3,19},{19,3},{4,20},{20... | collective-permute-start | bytes 393224 | tf_op jit(solution)/shard_map/ppermute | solution.py:326
  22.6 2.5 %collective-permute-start.9 = (bf16[128,256]{1,0:T(8,128)(2,1)S(1)}, bf16[128,256]{1,0:T(8,128)(2,1)S(1)}, u32[]{:S(2)}, u32[]{:S(2)}) collective-permute-start(bf16[128,256]{1,0:T(8,128)(2,1)S(1)} %get-tuple-element.49), channel_id=1, source_target_pairs={{0,3},{1,2},{2,1},{3,0},{4,7},{5,6},{6,5},{7,4},{8,11},{9,10},{10,... | collective-permute-start | bytes 196616 | tf_op jit(solution)/shard_map/ppermute | solution.py:283
  25.1 1.7 %collective-permute-done.7.refs_9_ = bf16[128,512]{1,0:T(8,128)(2,1)S(1)} collective-permute-done((bf16[128,512]{1,0:T(8,128)(2,1)S(1)}, bf16[128,512]{1,0:T(8,128)(2,1)S(1)}, u32[]{:S(2)}, u32[]{:S(2)}) %collective-permute-start.7) | collective-permute-done | bytes 131104 | tf_op jit(solution)/shard_map/ppermute | solution.py:326
  27.0 2.3 %collective-permute-done.6.refs_7_ = bf16[128,512]{1,0:T(8,128)(2,1)S(1)} collective-permute-done((bf16[128,512]{1,0:T(8,128)(2,1)S(1)}, bf16[128,512]{1,0:T(8,128)(2,1)S(1)}, u32[]{:S(2)}, u32[]{:S(2)}) %collective-permute-start.6) | collective-permute-done | bytes 131104 | tf_op jit(solution)/shard_map/ppermute | solution.py:326
  29.3 1.7 %shard_map.75 = (bf16[1024,512]{1,0:T(8,128)(2,1)S(1)}, bf16[512,512]{1,0:T(8,128)(2,1)S(1)}, f32[512,512]{1,0:T(8,128)S(1)}, bf16[512,256]{1,0:T(8,128)(2,1)S(1)}, f32[1,512]{1,0:T(1,128)S(1)}) custom-call(bf16[128,1536]{1,0:T(8,128)(2,1)S(1)} %get-tuple-element.41.refs_0_.refs_4_, bf16[128,1536]{1,0:T(8,128)(2,1)S(1)} %collective-permute-done.refs_1_.refs_5_, ...), custom_call_target="tpu_custom_call" | custom-call | flops 2147483648 | bytes 3014656 | tf_op jit(solution)/shard_map/pallas_call | solution.py:30
  31.0 1.3 %collective-permute-done.8.refs_6_ = bf16[128,256]{1,0:T(8,128)(2,1)S(1)} collective-permute-done((bf16[128,256]{1,0:T(8,128)(2,1)S(1)}, bf16[128,256]{1,0:T(8,128)(2,1)S(1)}, u32[]{:S(2)}, u32[]{:S(2)}) %collective-permute-start.8) | collective-permute-done | bytes 65568 | tf_op jit(solution)/shard_map/ppermute | solution.py:283
  32.7 2.2 %collective-permute-start.12 = (bf16[528,128]{1,0:T(8,128)(2,1)S(1)}, bf16[528,128]{1,0:T(8,128)(2,1)S(1)}, u32[]{:S(2)}, u32[]{:S(2)}) collective-permute-start(bf16[528,128]{1,0:T(8,128)(2,1)S(1)} %get-tuple-element.52), channel_id=1, source_target_pairs={{0,3},{1,2},{2,1},{3,0},{4,7},{5,6},{6,5},{7,4},{8,11},{9,10},{10,... | collective-permute-start | bytes 405512 | tf_op jit(solution)/shard_map/ppermute | solution.py:298
  34.9 2.2 %collective-permute-start.10 = (bf16[528,128]{1,0:T(8,128)(2,1)S(1)}, bf16[528,128]{1,0:T(8,128)(2,1)S(1)}, u32[]{:S(2)}, u32[]{:S(2)}) collective-permute-start(bf16[528,128]{1,0:T(8,128)(2,1)S(1)} %get-tuple-element.52), channel_id=1, source_target_pairs={{0,2},{1,3},{2,0},{3,1},{4,6},{5,7},{6,4},{7,5},{8,10},{9,11},{10,... | collective-permute-start | bytes 405512 | tf_op jit(solution)/shard_map/ppermute | solution.py:298
  37.1 1.5 %collective-permute-start.13 = (bf16[128,256]{1,0:T(8,128)(2,1)S(1)}, bf16[128,256]{1,0:T(8,128)(2,1)S(1)}, u32[]{:S(2)}, u32[]{:S(2)}) collective-permute-start(bf16[128,256]{1,0:T(8,128)(2,1)S(1)} %collective-permute-done.8.refs_6_), channel_id=1, source_target_pairs={{0,16},{16,0},{1,17},{17,1},{2,18},{18,2},{3,19},{19,3},{4,20},{20... | collective-permute-start | bytes 196616 | tf_op jit(solution)/shard_map/ppermute | solution.py:326
  39.1 2.2 %collective-permute-done.13.refs_7_ = bf16[128,256]{1,0:T(8,128)(2,1)S(1)} collective-permute-done((bf16[128,256]{1,0:T(8,128)(2,1)S(1)}, bf16[128,256]{1,0:T(8,128)(2,1)S(1)}, u32[]{:S(2)}, u32[]{:S(2)}) %collective-permute-start.13) | collective-permute-done | bytes 65568 | tf_op jit(solution)/shard_map/ppermute | solution.py:326
  41.4 1.5 %collective-permute-done.14.refs_9_ = bf16[128,256]{1,0:T(8,128)(2,1)S(1)} collective-permute-done((bf16[128,256]{1,0:T(8,128)(2,1)S(1)}, bf16[128,256]{1,0:T(8,128)(2,1)S(1)}, u32[]{:S(2)}, u32[]{:S(2)}) %collective-permute-start.14) | collective-permute-done | bytes 65568 | tf_op jit(solution)/shard_map/ppermute | solution.py:326
  42.9 1.4 %shard_map.77 = (bf16[1024,256]{1,0:T(8,128)(2,1)S(1)}, bf16[512,512]{1,0:T(8,128)(2,1)S(1)}, f32[512,512]{1,0:T(8,128)S(1)}) custom-call(bf16[128,1536]{1,0:T(8,128)(2,1)S(1)} %get-tuple-element.41.refs_0_.refs_4_, bf16[128,1536]{1,0:T(8,128)(2,1)S(1)} %collective-permute-done.refs_1_.refs_5_, bf16[128,1536]{1,0:T(8,128)(2,1)S(1)} %collective-permute-done.1.refs_2_.refs_6_, ...), custom_call_target="tpu_custom_call" | custom-call | tf_op jit(solution)/shard_map/pallas_call | solution.py:30
  44.3 1.4 %collective-permute-done.10.refs_1_ = bf16[528,128]{1,0:T(8,128)(2,1)S(1)} collective-permute-done((bf16[528,128]{1,0:T(8,128)(2,1)S(1)}, bf16[528,128]{1,0:T(8,128)(2,1)S(1)}, u32[]{:S(2)}, u32[]{:S(2)}) %collective-permute-start.10) | collective-permute-done | bytes 135200 | tf_op jit(solution)/shard_map/ppermute | solution.py:298
  47.1 1.7 %collective-permute-start.16 = (bf16[528,128]{1,0:T(8,128)(2,1)S(1)}, bf16[528,128]{1,0:T(8,128)(2,1)S(1)}, u32[]{:S(2)}, u32[]{:S(2)}) collective-permute-start(bf16[528,128]{1,0:T(8,128)(2,1)S(1)} %get-tuple-element.64), channel_id=1, source_target_pairs={{0,1},{1,0},{2,3},{3,2},{4,5},{5,4},{6,7},{7,6},{8,9},{9,8},{10,11... | collective-permute-start | bytes 405512 | tf_op jit(solution)/shard_map/ppermute | solution.py:298
  48.8 2.2 %collective-permute-start.15 = (bf16[528,128]{1,0:T(8,128)(2,1)S(1)}, bf16[528,128]{1,0:T(8,128)(2,1)S(1)}, u32[]{:S(2)}, u32[]{:S(2)}) collective-permute-start(bf16[528,128]{1,0:T(8,128)(2,1)S(1)} %get-tuple-element.64), channel_id=1, source_target_pairs={{0,3},{1,2},{2,1},{3,0},{4,7},{5,6},{6,5},{7,4},{8,11},{9,10},{10,... | collective-permute-start | bytes 405512 | tf_op jit(solution)/shard_map/ppermute | solution.py:298
  51.8 5.5 %collective-permute-done.17.refs_3_ = bf16[528,128]{1,0:T(8,128)(2,1)S(1)} collective-permute-done((bf16[528,128]{1,0:T(8,128)(2,1)S(1)}, bf16[528,128]{1,0:T(8,128)(2,1)S(1)}, u32[]{:S(2)}, u32[]{:S(2)}) %collective-permute-start.17) | collective-permute-done | bytes 135200 | tf_op jit(solution)/shard_map/ppermute | solution.py:298
  60.6 1.6 %shard_map.81 = (bf16[64,1024]{1,0:T(8,128)(2,1)S(1)}, bf16[64,1024]{1,0:T(8,128)(2,1)S(1)}, f32[128,1024]{1,0:T(8,128)S(1)}) custom-call(bf16[512,256]{1,0:T(8,128)(2,1)S(1)} %get-tuple-element.62.qg, bf16[512,512]{1,0:T(8,128)(2,1)S(1)} %get-tuple-element.68.kvg, bf16[1024,256]{1,0:T(8,128)(2,1)S(1)} %get-tuple-element.61.wq, ...), custom_call_target="tpu_custom_call" | custom-call | tf_op jit(solution)/shard_map/pallas_call | solution.py:30
  63.8 4.6 %collective-permute-done.21 = bf16[128,1024]{1,0:T(8,128)(2,1)S(1)} collective-permute-done((bf16[128,1024]{1,0:T(8,128)(2,1)S(1)}, bf16[128,1024]{1,0:T(8,128)(2,1)S(1)}, u32[]{:S(2)}, u32[]{:S(2)}) %collective-permute-start.21) | collective-permute-done | bytes 262176 | tf_op jit(solution)/shard_map/ppermute | solution.py:280
  (42 shorter events, 10.8 us)
Async XLA Ops:
  0.0 22.6 %copy-start = (bf16[8,128,256]{2,1,0:T(8,128)(2,1)S(1)}, bf16[8,128,256]{2,1,0:T(8,128)(2,1)}, u32[]{:S(2)}) copy-start(bf16[8,128,256]{2,1,0:T(8,128)(2,1)} %param.13) | copy-start | bytes 1572868
  0.0 1.4 %copy-start.2 = (bf16[128,1024]{1,0:T(8,128)(2,1)S(1)}, bf16[128,1024]{1,0:T(8,128)(2,1)}, u32[]{:S(2)}) copy-start(bf16[128,1024]{1,0:T(8,128)(2,1)} %cot.1) | copy-start | bytes 786436
  3.1 17.5 %collective-permute-start.1 = (bf16[128,1536]{1,0:T(8,128)(2,1)S(1)}, bf16[128,1536]{1,0:T(8,128)(2,1)S(1)}, u32[]{:S(2)}, u32[]{:S(2)}) collective-permute-start(bf16[128,1536]{1,0:T(8,128)(2,1)S(1)} %get-tuple-element.42), channel_id=1, source_target_pairs={{0,8},{4,12},{8,0},{12,4},{1,9},{5,13},{9,1},{13,5},{2,10},{6,14},... | collective-permute-start | bytes 1179656 | tf_op jit(solution)/shard_map/ppermute | solution.py:280
  6.1 8.3 %collective-permute-start.3 = (bf16[128,512]{1,0:T(8,128)(2,1)S(1)}, bf16[128,512]{1,0:T(8,128)(2,1)S(1)}, u32[]{:S(2)}, u32[]{:S(2)}) collective-permute-start(bf16[128,512]{1,0:T(8,128)(2,1)S(1)} %get-tuple-element.43), channel_id=1, source_target_pairs={{0,3},{1,2},{2,1},{3,0},{4,7},{5,6},{6,5},{7,4},{8,11},{9,10},{10,... | collective-permute-start | bytes 393224 | tf_op jit(solution)/shard_map/ppermute | solution.py:283
  9.7 10.9 %collective-permute-start.2 = (bf16[128,512]{1,0:T(8,128)(2,1)S(1)}, bf16[128,512]{1,0:T(8,128)(2,1)S(1)}, u32[]{:S(2)}, u32[]{:S(2)}) collective-permute-start(bf16[128,512]{1,0:T(8,128)(2,1)S(1)} %get-tuple-element.43), channel_id=1, source_target_pairs={{0,2},{1,3},{2,0},{3,1},{4,6},{5,7},{6,4},{7,5},{8,10},{9,11},{10,... | collective-permute-start | bytes 393224 | tf_op jit(solution)/shard_map/ppermute | solution.py:283
  9.7 13.0 %collective-permute-start = (bf16[128,1536]{1,0:T(8,128)(2,1)S(1)}, bf16[128,1536]{1,0:T(8,128)(2,1)S(1)}, u32[]{:S(2)}, u32[]{:S(2)}) collective-permute-start(bf16[128,1536]{1,0:T(8,128)(2,1)S(1)} %get-tuple-element.41.refs_0_.refs_4_), channel_id=1, source_target_pairs={{0,4},{4,0},{8,12},{12,8},{1,5},{5,1},{9,13},{13,9},{2,6},{6,2},{1... | collective-permute-start | bytes 1179656 | tf_op jit(solution)/shard_map/ppermute | solution.py:280
  9.7 19.6 %collective-permute-start.5 = (bf16[256,768]{1,0:T(8,128)(2,1)S(1)}, bf16[256,768]{1,0:T(8,128)(2,1)S(1)}, u32[]{:S(2)}, u32[]{:S(2)}) collective-permute-start(bf16[256,768]{1,0:T(8,128)(2,1)S(1)} %get-tuple-element.39.refs_4_), channel_id=1, source_target_pairs={{0,1},{1,0},{2,3},{3,2},{4,5},{5,4},{6,7},{7,6},{8,9},{9,8},{10,11... | collective-permute-start | bytes 1179656 | tf_op jit(solution)/shard_map/ppermute | solution.py:283
  20.6 8.7 %collective-permute-start.4 = (bf16[128,1536]{1,0:T(8,128)(2,1)S(1)}, bf16[128,1536]{1,0:T(8,128)(2,1)S(1)}, u32[]{:S(2)}, u32[]{:S(2)}) collective-permute-start(bf16[128,1536]{1,0:T(8,128)(2,1)S(1)} %collective-permute-done.1.refs_2_.refs_6_), channel_id=1, source_target_pairs={{0,4},{4,0},{8,12},{12,8},{1,5},{5,1},{9,13},{13,9},{2,6},{6,2},{1... | collective-permute-start | bytes 1179656 | tf_op jit(solution)/shard_map/ppermute | solution.py:280
  20.6 6.3 %collective-permute-start.7 = (bf16[128,512]{1,0:T(8,128)(2,1)S(1)}, bf16[128,512]{1,0:T(8,128)(2,1)S(1)}, u32[]{:S(2)}, u32[]{:S(2)}) collective-permute-start(bf16[128,512]{1,0:T(8,128)(2,1)S(1)} %collective-permute-done.3.refs_8_), channel_id=1, source_target_pairs={{0,16},{16,0},{1,17},{17,1},{2,18},{18,2},{3,19},{19,3},{4,20},{20... | collective-permute-start | bytes 393224 | tf_op jit(solution)/shard_map/ppermute | solution.py:326
  22.1 7.2 %collective-permute-start.6 = (bf16[128,512]{1,0:T(8,128)(2,1)S(1)}, bf16[128,512]{1,0:T(8,128)(2,1)S(1)}, u32[]{:S(2)}, u32[]{:S(2)}) collective-permute-start(bf16[128,512]{1,0:T(8,128)(2,1)S(1)} %collective-permute-done.2.refs_6_), channel_id=1, source_target_pairs={{0,16},{16,0},{1,17},{17,1},{2,18},{18,2},{3,19},{19,3},{4,20},{20... | collective-permute-start | bytes 393224 | tf_op jit(solution)/shard_map/ppermute | solution.py:326
  22.6 8.4 %collective-permute-start.9 = (bf16[128,256]{1,0:T(8,128)(2,1)S(1)}, bf16[128,256]{1,0:T(8,128)(2,1)S(1)}, u32[]{:S(2)}, u32[]{:S(2)}) collective-permute-start(bf16[128,256]{1,0:T(8,128)(2,1)S(1)} %get-tuple-element.49), channel_id=1, source_target_pairs={{0,3},{1,2},{2,1},{3,0},{4,7},{5,6},{6,5},{7,4},{8,11},{9,10},{10,... | collective-permute-start | bytes 196616 | tf_op jit(solution)/shard_map/ppermute | solution.py:283
  26.9 5.4 %collective-permute-start.8 = (bf16[128,256]{1,0:T(8,128)(2,1)S(1)}, bf16[128,256]{1,0:T(8,128)(2,1)S(1)}, u32[]{:S(2)}, u32[]{:S(2)}) collective-permute-start(bf16[128,256]{1,0:T(8,128)(2,1)S(1)} %get-tuple-element.49), channel_id=1, source_target_pairs={{0,2},{1,3},{2,0},{3,1},{4,6},{5,7},{6,4},{7,5},{8,10},{9,11},{10,... | collective-permute-start | bytes 196616 | tf_op jit(solution)/shard_map/ppermute | solution.py:283
  32.7 11.7 %collective-permute-start.12 = (bf16[528,128]{1,0:T(8,128)(2,1)S(1)}, bf16[528,128]{1,0:T(8,128)(2,1)S(1)}, u32[]{:S(2)}, u32[]{:S(2)}) collective-permute-start(bf16[528,128]{1,0:T(8,128)(2,1)S(1)} %get-tuple-element.52), channel_id=1, source_target_pairs={{0,3},{1,2},{2,1},{3,0},{4,7},{5,6},{6,5},{7,4},{8,11},{9,10},{10,... | collective-permute-start | bytes 405512 | tf_op jit(solution)/shard_map/ppermute | solution.py:298
  34.9 9.4 %collective-permute-start.11 = (bf16[528,128]{1,0:T(8,128)(2,1)S(1)}, bf16[528,128]{1,0:T(8,128)(2,1)S(1)}, u32[]{:S(2)}, u32[]{:S(2)}) collective-permute-start(bf16[528,128]{1,0:T(8,128)(2,1)S(1)} %get-tuple-element.52), channel_id=1, source_target_pairs={{0,1},{1,0},{2,3},{3,2},{4,5},{5,4},{6,7},{7,6},{8,9},{9,8},{10,11... | collective-permute-start | bytes 405512 | tf_op jit(solution)/shard_map/ppermute | solution.py:298
  34.9 10.8 %collective-permute-start.10 = (bf16[528,128]{1,0:T(8,128)(2,1)S(1)}, bf16[528,128]{1,0:T(8,128)(2,1)S(1)}, u32[]{:S(2)}, u32[]{:S(2)}) collective-permute-start(bf16[528,128]{1,0:T(8,128)(2,1)S(1)} %get-tuple-element.52), channel_id=1, source_target_pairs={{0,2},{1,3},{2,0},{3,1},{4,6},{5,7},{6,4},{7,5},{8,10},{9,11},{10,... | collective-permute-start | bytes 405512 | tf_op jit(solution)/shard_map/ppermute | solution.py:298
  37.1 4.3 %collective-permute-start.13 = (bf16[128,256]{1,0:T(8,128)(2,1)S(1)}, bf16[128,256]{1,0:T(8,128)(2,1)S(1)}, u32[]{:S(2)}, u32[]{:S(2)}) collective-permute-start(bf16[128,256]{1,0:T(8,128)(2,1)S(1)} %collective-permute-done.8.refs_6_), channel_id=1, source_target_pairs={{0,16},{16,0},{1,17},{17,1},{2,18},{18,2},{3,19},{19,3},{4,20},{20... | collective-permute-start | bytes 196616 | tf_op jit(solution)/shard_map/ppermute | solution.py:326
  38.6 4.3 %collective-permute-start.14 = (bf16[128,256]{1,0:T(8,128)(2,1)S(1)}, bf16[128,256]{1,0:T(8,128)(2,1)S(1)}, u32[]{:S(2)}, u32[]{:S(2)}) collective-permute-start(bf16[128,256]{1,0:T(8,128)(2,1)S(1)} %collective-permute-done.9.refs_8_), channel_id=1, source_target_pairs={{0,16},{16,0},{1,17},{17,1},{2,18},{18,2},{3,19},{19,3},{4,20},{20... | collective-permute-start | bytes 196616 | tf_op jit(solution)/shard_map/ppermute | solution.py:326
  46.6 10.7 %collective-permute-start.17 = (bf16[528,128]{1,0:T(8,128)(2,1)S(1)}, bf16[528,128]{1,0:T(8,128)(2,1)S(1)}, u32[]{:S(2)}, u32[]{:S(2)}) collective-permute-start(bf16[528,128]{1,0:T(8,128)(2,1)S(1)} %get-tuple-element.64), channel_id=1, source_target_pairs={{0,2},{1,3},{2,0},{3,1},{4,6},{5,7},{6,4},{7,5},{8,10},{9,11},{10,... | collective-permute-start | bytes 405512 | tf_op jit(solution)/shard_map/ppermute | solution.py:298
  47.1 10.2 %collective-permute-start.16 = (bf16[528,128]{1,0:T(8,128)(2,1)S(1)}, bf16[528,128]{1,0:T(8,128)(2,1)S(1)}, u32[]{:S(2)}, u32[]{:S(2)}) collective-permute-start(bf16[528,128]{1,0:T(8,128)(2,1)S(1)} %get-tuple-element.64), channel_id=1, source_target_pairs={{0,1},{1,0},{2,3},{3,2},{4,5},{5,4},{6,7},{7,6},{8,9},{9,8},{10,11... | collective-permute-start | bytes 405512 | tf_op jit(solution)/shard_map/ppermute | solution.py:298
  48.8 8.5 %collective-permute-start.15 = (bf16[528,128]{1,0:T(8,128)(2,1)S(1)}, bf16[528,128]{1,0:T(8,128)(2,1)S(1)}, u32[]{:S(2)}, u32[]{:S(2)}) collective-permute-start(bf16[528,128]{1,0:T(8,128)(2,1)S(1)} %get-tuple-element.64), channel_id=1, source_target_pairs={{0,3},{1,2},{2,1},{3,0},{4,7},{5,6},{6,5},{7,4},{8,11},{9,10},{10,... | collective-permute-start | bytes 405512 | tf_op jit(solution)/shard_map/ppermute | solution.py:298
  58.3 1.6 %collective-permute-start.20 = (bf16[128,1024]{1,0:T(8,128)(2,1)S(1)}, bf16[128,1024]{1,0:T(8,128)(2,1)S(1)}, u32[]{:S(2)}, u32[]{:S(2)}) collective-permute-start(bf16[128,1024]{1,0:T(8,128)(2,1)S(1)} %get-tuple-element.72), channel_id=1, source_target_pairs={{0,4},{4,0},{8,12},{12,8},{1,5},{5,1},{9,13},{13,9},{2,6},{6,2},{1... | collective-permute-start | bytes 786440 | tf_op jit(solution)/shard_map/ppermute | solution.py:280
  60.0 8.4 %collective-permute-start.21 = (bf16[128,1024]{1,0:T(8,128)(2,1)S(1)}, bf16[128,1024]{1,0:T(8,128)(2,1)S(1)}, u32[]{:S(2)}, u32[]{:S(2)}) collective-permute-start(bf16[128,1024]{1,0:T(8,128)(2,1)S(1)} %add_convert_fusion.1), channel_id=1, source_target_pairs={{0,8},{4,12},{8,0},{12,4},{1,9},{5,13},{9,1},{13,5},{2,10},{6,14},... | collective-permute-start | bytes 786440 | tf_op jit(solution)/shard_map/ppermute | solution.py:280
  62.2 1.4 %collective-permute-start.18 = (bf16[64,1024]{1,0:T(8,128)(2,1)S(1)}, bf16[64,1024]{1,0:T(8,128)(2,1)S(1)}, u32[]{:S(2)}, u32[]{:S(2)}) collective-permute-start(bf16[64,1024]{1,0:T(8,128)(2,1)S(1)} %get-tuple-element.70), channel_id=1, source_target_pairs={{0,4},{4,0},{8,12},{12,8},{1,5},{5,1},{9,13},{13,9},{2,6},{6,2},{1... | collective-permute-start | bytes 393224 | tf_op jit(solution)/shard_map/ppermute | solution.py:280
  62.2 1.5 %collective-permute-start.19 = (bf16[64,1024]{1,0:T(8,128)(2,1)S(1)}, bf16[64,1024]{1,0:T(8,128)(2,1)S(1)}, u32[]{:S(2)}, u32[]{:S(2)}) collective-permute-start(bf16[64,1024]{1,0:T(8,128)(2,1)S(1)} %get-tuple-element.71), channel_id=1, source_target_pairs={{0,4},{4,0},{8,12},{12,8},{1,5},{5,1},{9,13},{13,9},{2,6},{6,2},{1... | collective-permute-start | bytes 393224 | tf_op jit(solution)/shard_map/ppermute | solution.py:280
  (2 other events, 2.0 us)
